TPU v7x, 256 devices: a whole 4x4x8 slice. The times are simulated.
256 devices in a mesh: dp: 8 (over x, core), seq: 32 (over y, z).
Axes of the slice: x: 4, y: 4, z: 8, core: 2. Of those that a mesh axis runs over, the one named last changes fastest.
Arguments:
- node_feats: bfloat16 [8, 8192, 1024], P('dp', 'seq'), may hold values from -11 to 11
- w_qkv: bfloat16 [1024, 3072], replicated, may hold values from -1 to 1
- w_out: bfloat16 [1024, 1024], replicated, may hold values from -6 to 6
- cotangent: bfloat16 [8, 8192, 1024], P('dp', 'seq'), may hold values from -0.1796875 to 0.1796875
- block_neighbors: int32 [8, 64, 8], P('dp'), may hold values from 0 to 63, as said below
- block_counts: int32 [8, 64], P('dp'), may hold values from 1 to 8, as said below
- global_blocks: int32 [8, 4], P('dp'), may hold values from 1 to 62, as said below
Outputs:
- attn_update: bfloat16 [8, 8192, 1024], P('dp', 'seq')
- grad_nodes: bfloat16 [8, 8192, 1024], P('dp', 'seq')
- grad_weights: float32 [1024, 3072], P(('dp', 'seq'))
Inputs may be any that keep to these rules, and one draw needn't show every extreme that they name: `block_neighbors`: each row holds 8 distinct block ids, none of them one of the graph's global blocks; the first block_counts of them are the row's neighbour blocks and the rest are to be ignored. A block row that is not global lists itself among its neighbour blocks. `block_counts`: in every subgraph some block row has exactly 8. `global_blocks`: the 4 ids of a subgraph are distinct, and include blocks 1 and 62.
All inputs are finite; a program needn't handle non-finite values.
Results may differ from a plain program's by a relative error of at most 0.017.
The roundings to bfloat16 on the way count: a program that leaves them out, or rounds other values in their place, can miss the bound.
Values may be sent and summed in bfloat16 or wider, within the bound.
No kernel may reach another device: no remote copies, remote signals or barrier semaphores. Data moves between devices by JAX's collectives and lax.ppermute only.
A program may use at most 128 MiB of HBM per device.

v0:
```python
import math

import jax
import jax.numpy as jnp
from jax import lax
from jax.sharding import PartitionSpec as P

H = 16
BLOCK = 128
MAXNB = 8
NGLOB = 4


def to_items(values, qsplit):
    node_count, head_count, inner_dim = values.shape
    part_rows = node_count // qsplit
    grouped = values.reshape(qsplit, part_rows, head_count, inner_dim).transpose(2, 0, 1, 3)
    return grouped.reshape(head_count * qsplit, part_rows, inner_dim)


def from_items(values, head_count):
    item_total, part_rows, inner_dim = values.shape
    qsplit = item_total // head_count
    grouped = values.reshape(head_count, qsplit, part_rows, inner_dim).transpose(1, 2, 0, 3)
    return grouped.reshape(qsplit * part_rows, head_count, inner_dim)


def block_probs(queries, key_vecs, key_valid, score_scale):
    scores = (
        jnp.einsum("istd,iskd->istk", queries, key_vecs, preferred_element_type=jnp.float32)
        * score_scale
    )
    scores = jnp.where(key_valid[None, :, None, :], scores, -jnp.inf)
    scores = scores - jnp.max(scores, axis=-1, keepdims=True)
    weights = jnp.exp(scores)
    return weights / jnp.sum(weights, axis=-1, keepdims=True)


def on_device(node_feats, w_qkv, w_out, cotangent, block_neighbors, block_counts, global_blocks):
    features = node_feats[0]
    grad_out = cotangent[0]
    neighbors = block_neighbors[0]
    counts = block_counts[0]
    global_ids = global_blocks[0]
    node_dev, model_dim = features.shape
    head_dim = model_dim // H
    score_scale = head_dim ** (-0.5)
    seq_size = lax.axis_size("seq")
    seq_rank = lax.axis_index("seq")
    qsplit = max(1, seq_size // H)
    part_rows = node_dev // qsplit
    item_count = H * qsplit // seq_size
    block_total = neighbors.shape[0]
    slot_count = MAXNB + NGLOB
    key_span = slot_count * BLOCK
    group_rank = seq_rank * item_count % qsplit
    pair_dim = 2 * head_dim
    projected = jnp.dot(features, w_qkv, preferred_element_type=jnp.float32).astype(jnp.bfloat16)
    projected = projected.reshape(node_dev, 3, H, head_dim)
    query_items = to_items(projected[:, 0], qsplit)
    kv_nodes = projected[:, 1:].transpose(0, 2, 1, 3).reshape(node_dev, H, pair_dim)
    kv_items = jnp.broadcast_to(
        kv_nodes.transpose(1, 0, 2)[:, None], (H, qsplit, node_dev, pair_dim)
    )
    kv_items = kv_items.reshape(H * qsplit, node_dev, pair_dim)
    query_heads, kv_heads = (
        lax.all_to_all(query_items, "seq", split_axis=0, concat_axis=1, tiled=True),
        lax.all_to_all(kv_items, "seq", split_axis=0, concat_axis=1, tiled=True),
    )
    grad_attended = jnp.einsum(
        "nc,dc->nd", grad_out, w_out, preferred_element_type=jnp.float32
    ).astype(jnp.bfloat16)
    grad_heads = lax.all_to_all(
        to_items(grad_attended.reshape(node_dev, H, head_dim), qsplit),
        "seq",
        split_axis=0,
        concat_axis=1,
        tiled=True,
    )
    kv_blocks = kv_heads.reshape(item_count, block_total, BLOCK, pair_dim)
    per_part = part_rows // BLOCK
    query_count = seq_size * per_part
    source = jnp.arange(seq_size, dtype=jnp.int32)[:, None]
    offset = jnp.arange(per_part, dtype=jnp.int32)[None, :]
    query_ids = (source * (node_dev // BLOCK) + group_rank * per_part + offset).reshape(query_count)
    slot_index = jnp.arange(slot_count, dtype=jnp.int32)
    id_table = jnp.concatenate(
        [neighbors, jnp.broadcast_to(global_ids[None, :], (block_total, NGLOB))], axis=1
    )
    valid_table = ((slot_index[None, :] < counts[:, None]) | (slot_index[None, :] >= MAXNB)).astype(
        jnp.int32
    )
    selector = (query_ids[:, None] == jnp.arange(block_total, dtype=jnp.int32)[None, :]).astype(
        jnp.int32
    )
    key_ids = jnp.dot(selector, id_table)
    key_mask = jnp.repeat(jnp.dot(selector, valid_table) > 0, BLOCK, axis=1)
    group_size = math.gcd(query_count, 4)
    group_total = query_count // group_size
    query_groups = query_heads.reshape(
        item_count, group_total, group_size, BLOCK, head_dim
    ).transpose(1, 0, 2, 3, 4)
    grad_groups = grad_heads.reshape(
        item_count, group_total, group_size, BLOCK, head_dim
    ).transpose(1, 0, 2, 3, 4)
    id_groups = key_ids.reshape(group_total, group_size, slot_count)
    mask_groups = key_mask.reshape(group_total, group_size, key_span)

    def attend_group(running, inputs):
        queries, grad_rows, key_rows, key_valid = inputs
        flat_rows = key_rows.reshape(-1)
        pair_vecs = kv_blocks[:, flat_rows].reshape(item_count, group_size, key_span, pair_dim)
        zero_half = jnp.zeros(queries.shape, jnp.bfloat16)
        query_wide = jnp.concatenate([queries, zero_half], axis=-1)
        grad_wide = jnp.concatenate([zero_half, grad_rows], axis=-1)
        probs = block_probs(query_wide, pair_vecs, key_valid, score_scale)
        probs_low = probs.astype(jnp.bfloat16)
        mixed = jnp.einsum(
            "istk,iskd->istd", probs_low, pair_vecs, preferred_element_type=jnp.float32
        )
        attended_rows = mixed[..., head_dim:].astype(jnp.bfloat16)
        grad_probs = jnp.einsum(
            "istd,iskd->istk", grad_wide, pair_vecs, preferred_element_type=jnp.float32
        )
        row_delta = jnp.sum(probs * grad_probs, axis=-1, keepdims=True)
        dscore = (probs * (grad_probs - row_delta) * score_scale).astype(jnp.bfloat16)
        grad_both = jnp.einsum(
            "istk,iskd->istd", dscore, pair_vecs, preferred_element_type=jnp.float32
        )
        grad_q = grad_both[..., :head_dim].astype(jnp.bfloat16)
        grad_kv = jnp.einsum(
            "istk,istd->iskd", dscore, query_wide, preferred_element_type=jnp.float32
        )
        grad_kv = grad_kv + jnp.einsum(
            "istk,istd->iskd", probs_low, grad_wide, preferred_element_type=jnp.float32
        )
        grad_kv = grad_kv.reshape(item_count, group_size * slot_count, BLOCK, pair_dim)
        return (running.at[:, flat_rows].add(grad_kv), (attended_rows, grad_q))

    zeros_start = jnp.zeros((item_count, block_total, BLOCK, pair_dim), jnp.float32)
    kv_total, group_outputs = lax.scan(
        attend_group, zeros_start, (query_groups, grad_groups, id_groups, mask_groups)
    )
    attended_groups, grad_q_groups = group_outputs
    attended_heads = attended_groups.transpose(1, 0, 2, 3, 4).reshape(
        item_count, query_count * BLOCK, head_dim
    )
    attended = from_items(
        lax.all_to_all(attended_heads, "seq", split_axis=1, concat_axis=0, tiled=True), H
    ).reshape(node_dev, model_dim)
    attn_update = jnp.dot(attended, w_out, preferred_element_type=jnp.float32).astype(jnp.bfloat16)
    grad_q_heads = grad_q_groups.transpose(1, 0, 2, 3, 4).reshape(
        item_count, query_count * BLOCK, head_dim
    )
    kv_part = kv_total.astype(jnp.bfloat16).reshape(item_count, block_total * BLOCK, pair_dim)
    grad_q_items, kv_back = (
        lax.all_to_all(grad_q_heads, "seq", split_axis=1, concat_axis=0, tiled=True),
        lax.all_to_all(kv_part, "seq", split_axis=1, concat_axis=0, tiled=True),
    )
    kv_summed = jnp.sum(kv_back.reshape(H, qsplit, node_dev, pair_dim).astype(jnp.float32), axis=1)
    grad_kv_nodes = kv_summed.astype(jnp.bfloat16).transpose(1, 0, 2)
    grad_q_nodes = from_items(grad_q_items, H).reshape(node_dev, model_dim)
    grad_kv_flat = (
        grad_kv_nodes.reshape(node_dev, H, 2, head_dim)
        .transpose(0, 2, 1, 3)
        .reshape(node_dev, 2 * model_dim)
    )
    grad_qkv = jnp.concatenate([grad_q_nodes, grad_kv_flat], axis=1)
    grad_nodes = jnp.einsum(
        "nc,dc->nd", grad_qkv, w_qkv, preferred_element_type=jnp.float32
    ).astype(jnp.bfloat16)
    grad_weights = lax.psum_scatter(
        jnp.einsum("nc,nd->cd", features, grad_qkv, preferred_element_type=jnp.float32),
        ("dp", "seq"),
        scatter_dimension=0,
        tiled=True,
    )
    return (attn_update[None], grad_nodes[None], grad_weights)


def solution(mesh):
    in_specs = (
        P("dp", "seq", None),
        P(),
        P(),
        P("dp", "seq", None),
        P("dp", None, None),
        P("dp", None),
        P("dp", None),
    )
    out_specs = (P("dp", "seq", None), P("dp", "seq", None), P(("dp", "seq"), None))
    return jax.shard_map(
        on_device, mesh=mesh, in_specs=in_specs, out_specs=out_specs, check_vma=False
    )
```

profile of v0, /device:TPU:8, one launch (start us, length us, event | category | flops | bytes accessed | tf_op | source)
XLA Modules:
  0.0 1061.3 jit_solution(8046751909578580185)
XLA Ops:
  7.2 6.0 convolution_convert_fusion.1
  17.9 11.8 %all-to-all-start = ((bf16[32,128,64]{1,2,0:T(8,128)(2,1)}), bf16[32,128,64]{1,2,0:T(8,128)(2,1)}, u32[]{:S(2)}, u32[]{:S(2)}) async-start(bf16[32,128,64]{1,2,0:T(8,128)(2,1)} %bitcast.22), calls=%async_computation | async-start | bytes 1048576 | tf_op jit(solution)/shard_map/all_to_all | solution.py:67
  32.8 12.5 %all-to-all-done = bf16[32,128,64]{1,2,0:T(8,128)(2,1)} async-done(((bf16[32,128,64]{1,2,0:T(8,128)(2,1)}), bf16[32,128,64]{1,2,0:T(8,128)(2,1)}, u32[]{:S(2)}, u32[]{:S(2)}) %all-to-all-start) | async-done | bytes 524320 | tf_op jit(solution)/shard_map/all_to_all | solution.py:67
  45.3 7.0 all-to-all-start.2
  56.3 10.9 %all-to-all-done.2 = bf16[32,128,64]{1,2,0:T(8,128)(2,1)} async-done(((bf16[32,128,64]{1,2,0:T(8,128)(2,1)}), bf16[32,128,64]{1,2,0:T(8,128)(2,1)}, u32[]{:S(2)}, u32[]{:S(2)}) %all-to-all-start.2) | async-done | bytes 524320 | tf_op jit(solution)/shard_map/all_to_all | solution.py:73
  69.0 7.7 all-to-all-start.1
  77.7 45.8 %all-to-all-done.1 = bf16[32,256,128]{2,1,0:T(8,128)(2,1)} async-done(((bf16[32,256,128]{2,1,0:T(8,128)(2,1)}), bf16[32,256,128]{2,1,0:T(8,128)(2,1)}, u32[]{:S(2)}, u32[]{:S(2)}) %all-to-all-start.1) | async-done | bytes 2097184 | tf_op jit(solution)/shard_map/all_to_all | solution.py:68
  125.9 417.7 %while.14 = (s32[]{:T(128)}, f32[1,64,128,128]{3,2,1,0:T(8,128)}, bf16[8,1,4,128,64]{3,4,2,1,0:T(8,128)(2,1)}, bf16[8,1,4,128,64]{3,4,2,1,0:T(8,128)(2,1)}, s32[...) while((s32[]{:T(128)}, f32[1,64,128,128]{3,2,1,0:T(8,128)}, ...), condition=%wide.region_5.6_spmd, body=%wide.region_0.5_spmd.sunk | while | flops 1226971776 | bytes 54822720 | solution.py:141
  139.3 10.3 fusion.123
  149.5 5.5 convolution_add_fusion.2
  155.0 10.3 scatter_fusion
  165.3 9.0 fusion.124
  191.5 10.3 fusion.123
  207.2 10.3 scatter_fusion
  217.5 9.0 fusion.124
  243.7 10.3 fusion.123
  259.4 10.3 scatter_fusion
  269.7 9.0 fusion.124
  295.9 10.3 fusion.123
  311.7 10.3 scatter_fusion
  322.0 9.0 fusion.124
  348.2 10.3 fusion.123
  363.9 10.3 scatter_fusion
  374.2 9.0 fusion.124
  400.4 10.3 fusion.123
  416.1 10.3 scatter_fusion
  426.4 9.0 fusion.124
  452.6 10.3 fusion.123
  468.4 10.2 scatter_fusion
  478.6 9.0 fusion.124
  504.8 10.3 fusion.123
  520.5 10.2 scatter_fusion
  530.8 9.0 fusion.124
  548.8 23.6 %reduce.9 = bf16[4096,64]{1,0:T(8,128)(2,1)S(1)} reduce(bf16[4096,1,64]{2,1,0:T(2,128)(2,1)} %bitcast.188, bf16[]{:T(256)} %broadcast.98), dimensions={1}, to_apply=%bitcast.117.reduce_sub_computation | reduce | bytes 1048578
  573.9 8.9 all-to-all-start.4
  585.4 33.3 %copy.128 = bf16[1,8192,128]{2,0,1:T(2,128)(2,1)} copy(bf16[1,8192,128]{2,1,0:T(8,128)(2,1)S(1)} %bitcast.183) | data formatting | bytes 4194304 | tf_op jit(solution)/shard_map/reshape | solution.py:155
  618.7 46.5 %reduce.8 = bf16[8192,128]{1,0:T(8,128)(2,1)} reduce(bf16[8192,1,128]{2,1,0:T(2,128)(2,1)} %bitcast.179, bf16[]{:T(256)} %broadcast.98), dimensions={1}, to_apply=%bitcast.131.reduce_sub_computation | reduce | bytes 4194306
  669.1 9.8 all-to-all-start.5
  689.2 36.6 %all-to-all-done.5 = bf16[32,2,16384]{2,1,0:T(2,128)(2,1)} async-done(((bf16[32,2,16384]{2,1,0:T(2,128)(2,1)}), bf16[32,2,16384]{2,1,0:T(2,128)(2,1)}, u32[]{:S(2)}, u32[]{:S(2)}) %all-to-all-start.5) | async-done | bytes 2097184 | tf_op jit(solution)/shard_map/all_to_all | solution.py:158
  725.9 10.5 reshape.228
  744.8 7.5 convolution_bitcast_fusion
  754.6 6.9 reshape.220
  761.5 24.6 %reduce.7 = bf16[4096,64]{1,0:T(8,128)(2,1)} reduce(bf16[4096,1,64]{2,1,0:T(2,128)(2,1)} %bitcast.189, bf16[]{:T(256)} %broadcast.98), dimensions={1}, to_apply=%bitcast.113.reduce_sub_computation | reduce | bytes 1048578
  789.1 8.4 all-to-all-start.3
  797.5 18.1 %all-to-all-done.3 = bf16[32,2,4096]{2,1,0:T(2,128)(2,1)} async-done(((bf16[32,2,4096]{2,1,0:T(2,128)(2,1)}), bf16[32,2,4096]{2,1,0:T(2,128)(2,1)}, u32[]{:S(2)}, u32[]{:S(2)}) %all-to-all-start.3) | async-done | bytes 524320 | tf_op jit(solution)/shard_map/all_to_all | solution.py:149
  815.6 5.6 reshape.226
  831.7 5.5 fusion.59
  837.2 211.2 %all-reduce.5.cloned.1.call-done = f32[1024,3072]{0,1:T(8,128)} async-done(((f32[1024,3072]{0,1:T(8,128)}), f32[1024,3072]{0,1:T(8,128)}) %all-reduce.5.cloned.1.call-update) | async-done | bytes 12582928
  (178 shorter events, 245.9 us)
Async XLA Ops:
  7.2 22.5 %copy-start = (bf16[1024,1024]{1,0:T(8,128)(2,1)S(1)}, bf16[1024,1024]{1,0:T(8,128)(2,1)}, u32[]{:S(2)}) copy-start(bf16[1024,1024]{1,0:T(8,128)(2,1)} %param.11) | copy-start | bytes 6291460
  17.9 27.3 %all-to-all-start = ((bf16[32,128,64]{1,2,0:T(8,128)(2,1)}), bf16[32,128,64]{1,2,0:T(8,128)(2,1)}, u32[]{:S(2)}, u32[]{:S(2)}) async-start(bf16[32,128,64]{1,2,0:T(8,128)(2,1)} %bitcast.22), calls=%async_computation | async-start | bytes 1048576 | tf_op jit(solution)/shard_map/all_to_all | solution.py:67
  45.3 21.9 %all-to-all-start.2 = ((bf16[32,128,64]{1,2,0:T(8,128)(2,1)}), bf16[32,128,64]{1,2,0:T(8,128)(2,1)}, u32[]{:S(2)}, u32[]{:S(2)}) async-start(bf16[32,128,64]{1,2,0:T(8,128)(2,1)} %bitcast.31), calls=%async_computation.2 | async-start | bytes 1048576 | tf_op jit(solution)/shard_map/all_to_all | solution.py:73
  56.3 20.5 %copy-start.3 = (s32[1,4]{1,0:T(1,128)S(1)}, s32[1,4]{1,0:T(1,128)}, u32[]{:S(2)}) copy-start(s32[1,4]{1,0:T(1,128)} %param.15) | copy-start | bytes 52
  56.3 20.6 %copy-start.4 = (s32[1,64]{1,0:T(1,128)S(1)}, s32[1,64]{1,0:T(1,128)}, u32[]{:S(2)}) copy-start(s32[1,64]{1,0:T(1,128)} %param.14) | copy-start | bytes 772
  56.3 21.1 %copy-start.2 = (s32[1,64,8]{1,2,0:T(8,128)S(1)}, s32[1,64,8]{1,2,0:T(8,128)}, u32[]{:S(2)}) copy-start(s32[1,64,8]{1,2,0:T(8,128)} %param.13) | copy-start | bytes 6148
  69.0 54.4 %all-to-all-start.1 = ((bf16[32,256,128]{2,1,0:T(8,128)(2,1)}), bf16[32,256,128]{2,1,0:T(8,128)(2,1)}, u32[]{:S(2)}, u32[]{:S(2)}) async-start(bf16[32,256,128]{2,1,0:T(8,128)(2,1)} %bitcast.187), calls=%async_computation.1 | async-start | bytes 4194304 | tf_op jit(solution)/shard_map/all_to_all | solution.py:68
  573.9 95.2 %all-to-all-start.4 = ((bf16[32,2,4096]{2,1,0:T(2,128)(2,1)}), bf16[32,2,4096]{2,1,0:T(2,128)(2,1)S(1)}, u32[]{:S(2)}, u32[]{:S(2)}) async-start(bf16[32,2,4096]{2,1,0:T(2,128)(2,1)} %reshape.229), calls=%async_computation.4 | async-start | bytes 1048576 | tf_op jit(solution)/shard_map/all_to_all | solution.py:157
  669.1 56.7 %all-to-all-start.5 = ((bf16[32,2,16384]{2,1,0:T(2,128)(2,1)}), bf16[32,2,16384]{2,1,0:T(2,128)(2,1)}, u32[]{:S(2)}, u32[]{:S(2)}) async-start(bf16[32,2,16384]{2,1,0:T(2,128)(2,1)} %reshape.227), calls=%async_computation.5 | async-start | bytes 4194304 | tf_op jit(solution)/shard_map/all_to_all | solution.py:158
  679.0 369.4 %all-reduce.5.cloned.1.call-start = ((), (), s32[]{:S(2)}) async-start(), calls=%async_computation.6 | async-start | bytes 25165824
  789.1 26.5 %all-to-all-start.3 = ((bf16[32,2,4096]{2,1,0:T(2,128)(2,1)}), bf16[32,2,4096]{2,1,0:T(2,128)(2,1)}, u32[]{:S(2)}, u32[]{:S(2)}) async-start(bf16[32,2,4096]{2,1,0:T(2,128)(2,1)} %reshape.225), calls=%async_computation.3 | async-start | bytes 1048576 | tf_op jit(solution)/shard_map/all_to_all | solution.py:149
  828.6 3.1 copy-start.1
Sparse Core Ops, SparseCore 0:
  752.4 295.9 all-reduce.4
where the time goes:
time: 1070 us; the launch traced here: 1060 us
  waiting for transfers between devices  335 us (31%)
  matrix products  308 us (29%)
  other arithmetic  182 us (17%)
  local copies, waits for them, and re-layouts  168 us (16%)
  starting transfers between devices  53.7 us (5%)
  between operations  14.8 us (1%)
    unnamed x2, waiting for transfers between devices  211 us
    unnamed x3, other arithmetic  94.7 us
    scatter-add x8, other arithmetic, attend_group(): return (running.at[:, flat_rows].add(grad_kv), (attended_rows, grad_q))  82.2 us
    dot_general x8, matrix products, attend_group(): jnp.einsum('istk,istd->iskd', dscore, query_wide, preferred_element_type=...  82.1 us
    dot_general x8, matrix products, attend_group(): jnp.einsum('istk,iskd->istd', dscore, pair_vecs, preferred_element_type=j...  72 us
    all_to_all x1, waiting for transfers between devices, on_device(): lax.all_to_all(kv_items, 'seq', split_axis=0, concat_axis=1, tiled=True)  45.8 us
    dot_general x8, matrix products, attend_group(): jnp.einsum('istk,istd->iskd', probs_low, grad_wide, preferred_element_typ...  43.6 us
    unnamed x21, local copies, waits for them, and re-layouts  39.2 us
  transfers between devices with their start and end apart: 7, of which 6 were waited for; matrix products, arithmetic and copies ran while one was open for 15% of the time, Pallas kernels for 0%

commit v1 on v0

v1 whole, which is shorter than its diff:
```python
import functools
import math

import jax
import jax.numpy as jnp
import numpy as np
from jax import lax
from jax.experimental import pallas as pl
from jax.experimental.pallas import tpu as pltpu
from jax.sharding import Mesh
from jax.sharding import PartitionSpec as P

H = 16
HD = 64
BLOCK = 128
MAXNB = 8
NGLOB = 4
SLOTS = MAXNB + NGLOB
YS = 4
ZS = 8
NODE_DEV = 256
ROW = NODE_DEV * ZS
QBLK = ROW // BLOCK
NODES = ROW * YS
HALF = ROW // 2
SCALE = HD**-0.5
LOG2E = math.log2(math.e)
MASKED = -3.0e38
VMEM = pltpu.CompilerParams(vmem_limit_bytes=48 * 1024 * 1024)

bf16 = jnp.bfloat16
f32 = jnp.float32


def low_half(shape):
    return lax.broadcasted_iota(jnp.int32, shape, 1) < HD


def pair_up(first, second):
    low = low_half(first.shape)
    return (
        jnp.where(low, first, pltpu.roll(second, HD, 1)),
        jnp.where(low, pltpu.roll(first, HD, 1), second),
    )


def nt(a, b):
    return lax.dot_general(a, b, (((1,), (1,)), ((), ())), preferred_element_type=f32)


def nn(a, b):
    return lax.dot_general(a, b, (((1,), (0,)), ((), ())), preferred_element_type=f32)


def kv_kernel(f_ref, wk_ref, wv_ref, a_ref, b_ref):
    both = nn(f_ref[...], jnp.concatenate([wk_ref[...], wv_ref[...]], axis=1))
    a, b = pair_up(both[:, :128], both[:, 128:])
    a_ref[0] = a.astype(bf16)
    b_ref[0] = b.astype(bf16)


def qg_kernel(f_ref, c_ref, wq_ref, wo_ref, a_ref, b_ref):
    a, b = pair_up(nn(f_ref[...], wq_ref[...]), nt(c_ref[...], wo_ref[...]))
    a_ref[0] = a.astype(bf16)
    b_ref[0] = b.astype(bf16)


def whole(shape):
    return pl.BlockSpec(shape, lambda i: (0,) * len(shape))


def project_kv(feats, w_qkv):
    d = feats.shape[1]
    out = jax.ShapeDtypeStruct((ZS, NODE_DEV, 128), bf16)
    tile = pl.BlockSpec((1, NODE_DEV, 128), lambda i: (i, 0, 0))
    return pl.pallas_call(
        kv_kernel,
        grid=(ZS,),
        in_specs=[
            whole((NODE_DEV, d)),
            pl.BlockSpec((d, 128), lambda i: (0, ZS + i)),
            pl.BlockSpec((d, 128), lambda i: (0, 2 * ZS + i)),
        ],
        out_specs=[tile, tile],
        out_shape=[out, out],
        compiler_params=VMEM,
        name="project_kv",
    )(feats, w_qkv, w_qkv)


def project_qg(feats, cot, w_qkv, w_out):
    d = feats.shape[1]
    out = jax.ShapeDtypeStruct((ZS, NODE_DEV, 128), bf16)
    tile = pl.BlockSpec((1, NODE_DEV, 128), lambda i: (i, 0, 0))
    return pl.pallas_call(
        qg_kernel,
        grid=(ZS,),
        in_specs=[
            whole((NODE_DEV, d)),
            whole((NODE_DEV, d)),
            pl.BlockSpec((d, 128), lambda i: (0, i)),
            pl.BlockSpec((128, d), lambda i: (i, 0)),
        ],
        out_specs=[tile, tile],
        out_shape=[out, out],
        compiler_params=VMEM,
        name="project_qg",
    )(feats, cot, w_qkv, w_out)


def attend_kernel(
    tab_ref, cnt_ref, y_ref, own_ref, left_ref, right_ref, opp_lo_ref, opp_hi_ref, qg_ref,
    od_ref, sum_own_ref, sum_right_ref, sum_left_ref, sum_opp_ref,
    kv_s, acc, sc, xs,
):
    y = y_ref[0]
    at = lambda step: lax.rem(y + step, YS) * ROW

    kv_s[pl.ds(pl.multiple_of(at(0), ROW), ROW), :] = own_ref[...]
    kv_s[pl.ds(pl.multiple_of(at(YS - 1), ROW), ROW), :] = left_ref[...]
    kv_s[pl.ds(pl.multiple_of(at(1), ROW), ROW), :] = right_ref[...]
    kv_s[pl.ds(pl.multiple_of(at(2), ROW), HALF), :] = opp_lo_ref[...]
    kv_s[pl.ds(pl.multiple_of(at(2) + HALF, HALF), HALF), :] = opp_hi_ref[...]

    @pl.loop(0, NODES // 512)
    def _(t):
        acc[:, pl.ds(pl.multiple_of(t * 512, 512), 512)] = jnp.zeros((128, 512), f32)

    def keys(ids, t):
        rows = [kv_s[pl.ds(pl.multiple_of(ids[2 * t + u] * BLOCK, BLOCK), BLOCK), :] for u in (0, 1)]
        return jnp.concatenate(rows, axis=0)

    def row_block(i, pairs):
        width = pairs * 256
        ids = [tab_ref[i * SLOTS + t] for t in range(2 * pairs)]
        odd = lax.rem(cnt_ref[i], 2) == 1
        rows = pl.ds(pl.multiple_of(i * BLOCK, BLOCK), BLOCK)
        qg = qg_ref[rows, :].astype(f32)
        low = low_half(qg.shape)
        zero = jnp.zeros_like(qg)
        wide32 = jnp.concatenate([jnp.where(low, qg, zero), jnp.where(low, zero, qg)], axis=0)
        wide = wide32.astype(bf16)
        for t in range(pairs):
            sc[:, t * 256 : (t + 1) * 256] = nt(wide, keys(ids, t))
        step = 16
        for r in range(BLOCK // step):
            s = sc[r * step : (r + 1) * step, :width]
            dp = sc[BLOCK + r * step : BLOCK + (r + 1) * step, :width]
            last = jnp.where(odd, MASKED, s[:, width - BLOCK :])
            s = jnp.concatenate([s[:, : width - BLOCK], last], axis=1)
            e = jnp.exp2((s - jnp.max(s, axis=1, keepdims=True)) * (SCALE * LOG2E))
            p = e * (1.0 / jnp.sum(e, axis=1, keepdims=True))
            delta = jnp.sum(p * dp, axis=1, keepdims=True)
            ds = p * (dp - delta) * SCALE
            xs[r * step : (r + 1) * step, :width] = ds.astype(bf16)
            xs[BLOCK + r * step : BLOCK + (r + 1) * step, :width] = p.astype(bf16)
        every = jnp.concatenate([keys(ids, t) for t in range(pairs)], axis=0)
        mixed = nn(xs[:, :width], every)
        od_ref[rows, :] = jnp.where(low, mixed[:BLOCK], mixed[BLOCK:]).astype(bf16)
        wide_t = wide32.T.astype(bf16)
        for t in range(pairs):
            part = nn(wide_t, xs[:, t * 256 : (t + 1) * 256])
            for u in (0, 1):
                at_key = pl.ds(pl.multiple_of(ids[2 * t + u] * BLOCK, BLOCK), BLOCK)
                acc[:, at_key] += part[:, u * BLOCK : (u + 1) * BLOCK]

    @pl.loop(0, QBLK)
    def _(i):
        pairs = NGLOB // 2 + (cnt_ref[i] + 1) // 2
        for v in range(NGLOB // 2 + 1, SLOTS // 2 + 1):
            pl.when(pairs == v)(functools.partial(row_block, i, v))

    for step, out in ((0, sum_own_ref), (1, sum_right_ref), (YS - 1, sum_left_ref), (2, sum_opp_ref)):
        start = at(step)

        @pl.loop(0, ROW // 256)
        def _(t):
            cols = pl.ds(pl.multiple_of(start + t * 256, 256), 256)
            out[pl.ds(pl.multiple_of(t * 256, 256), 256), :] = acc[:, cols].T.astype(bf16)


def attend(table, counts, y, kv_parts, qg):
    vmem = pl.BlockSpec(memory_space=pltpu.VMEM)
    smem = pl.BlockSpec(memory_space=pltpu.SMEM)
    row = jax.ShapeDtypeStruct((ROW, 128), bf16)
    return pl.pallas_call(
        attend_kernel,
        in_specs=[smem] * 3 + [vmem] * 6,
        out_specs=[vmem] * 5,
        out_shape=[row] * 5,
        scratch_shapes=[
            pltpu.VMEM((NODES, 128), bf16),
            pltpu.VMEM((128, NODES), f32),
            pltpu.VMEM((256, SLOTS * BLOCK), f32),
            pltpu.VMEM((256, SLOTS * BLOCK), bf16),
        ],
        compiler_params=VMEM,
        cost_estimate=pl.CostEstimate(
            flops=6 * QBLK * BLOCK * 1152 * 128 * 2, bytes_accessed=6 << 20, transcendentals=0
        ),
        name="attend",
    )(table, counts, y, *kv_parts, qg)


def out_kernel(a_ref, b_ref, wo_ref, o_ref, total):
    step = pl.program_id(0)

    @pl.when(step == 0)
    def _():
        total[...] = jnp.zeros_like(total)

    cols = [pair_up(a_ref[u].astype(f32), b_ref[u].astype(f32))[1] for u in (0, 1)]
    total[...] += nn(jnp.concatenate(cols, axis=1).astype(bf16), wo_ref[...])

    @pl.when(step == pl.num_programs(0) - 1)
    def _():
        o_ref[...] = total[...].astype(bf16)


def project_out(od_a, od_b, w_out):
    d = w_out.shape[1]
    tile = pl.BlockSpec((2, NODE_DEV, 128), lambda i: (i, 0, 0))
    return pl.pallas_call(
        out_kernel,
        grid=(ZS // 2,),
        in_specs=[tile, tile, pl.BlockSpec((256, d), lambda i: (i, 0))],
        out_specs=whole((NODE_DEV, d)),
        out_shape=jax.ShapeDtypeStruct((NODE_DEV, d), bf16),
        scratch_shapes=[pltpu.VMEM((NODE_DEV, d), f32)],
        compiler_params=VMEM,
        name="project_out",
    )(od_a, od_b, w_out)


def nodes_kernel(oa_ref, ob_ref, ka_ref, kb_ref, wq_ref, wk_ref, wv_ref, o_ref, total):
    step = pl.program_id(0)

    @pl.when(step == 0)
    def _():
        total[...] = jnp.zeros_like(total)

    dq, dk, dv = [], [], []
    for u in (0, 1):
        dq.append(pair_up(oa_ref[u].astype(f32), ob_ref[u].astype(f32))[0])
        k, v = pair_up(ka_ref[u].astype(f32), kb_ref[u].astype(f32))
        dk.append(k)
        dv.append(v)
    add = nt(jnp.concatenate(dq, axis=1).astype(bf16), wq_ref[...])
    add += nt(jnp.concatenate(dk, axis=1).astype(bf16), wk_ref[...])
    add += nt(jnp.concatenate(dv, axis=1).astype(bf16), wv_ref[...])
    total[...] += add

    @pl.when(step == pl.num_programs(0) - 1)
    def _():
        o_ref[...] = total[...].astype(bf16)


def node_grads(od_a, od_b, kv_a, kv_b, w_qkv):
    d = w_qkv.shape[0]
    tile = pl.BlockSpec((2, NODE_DEV, 128), lambda i: (i, 0, 0))
    steps = ZS // 2
    return pl.pallas_call(
        nodes_kernel,
        grid=(steps,),
        in_specs=[tile] * 4
        + [pl.BlockSpec((d, 256), functools.partial(lambda i, third: (0, third * steps + i), third=k)) for k in range(3)],
        out_specs=whole((NODE_DEV, d)),
        out_shape=jax.ShapeDtypeStruct((NODE_DEV, d), bf16),
        scratch_shapes=[pltpu.VMEM((NODE_DEV, d), f32)],
        compiler_params=VMEM,
        name="node_grads",
    )(od_a, od_b, kv_a, kv_b, w_qkv, w_qkv, w_qkv)


def swap(values, axis):
    return lax.all_to_all(values, axis, split_axis=0, concat_axis=0, tiled=True)


RIGHT = [(i, (i + 1) % YS) for i in range(YS)]
LEFT = [(i, (i - 1) % YS) for i in range(YS)]


def gather_row(own):
    left = lax.ppermute(own, "y", RIGHT)
    right = lax.ppermute(own, "y", LEFT)
    opp_lo = lax.ppermute(left[:HALF], "y", RIGHT)
    opp_hi = lax.ppermute(right[HALF:], "y", LEFT)
    return own, left, right, opp_lo, opp_hi


def sum_row(own, to_right, to_left, opp):
    lo = lax.ppermute(opp[:HALF], "y", RIGHT)
    hi = lax.ppermute(opp[HALF:], "y", LEFT)
    add = lambda *v: sum(x.astype(f32) for x in v)
    to_right = jnp.concatenate([add(to_right[:HALF], lo).astype(bf16), to_right[HALF:]], axis=0)
    to_left = jnp.concatenate([to_left[:HALF], add(to_left[HALF:], hi).astype(bf16)], axis=0)
    return add(own, lax.ppermute(to_right, "y", RIGHT), lax.ppermute(to_left, "y", LEFT)).astype(bf16)


def on_device(node_feats, w_qkv, w_out, cotangent, block_neighbors, block_counts, global_blocks):
    feats = node_feats[0]
    cot = cotangent[0]
    y = lax.axis_index("y")
    neighbors = lax.dynamic_slice_in_dim(block_neighbors[0], y * QBLK, QBLK, 0)
    counts = lax.dynamic_slice_in_dim(block_counts[0], y * QBLK, QBLK, 0)
    table = jnp.concatenate([jnp.broadcast_to(global_blocks[0][None], (QBLK, NGLOB)), neighbors], axis=1).reshape(-1)
    y_arr = y.reshape(1).astype(jnp.int32)

    kv = project_kv(feats, w_qkv)
    qg = project_qg(feats, cot, w_qkv, w_out)
    feats_row = lax.all_gather(feats, "z", axis=0, tiled=True)
    od, kv_sum = [], []
    for p in (0, 1):
        kv_row = swap(kv[p], "z").reshape(ROW, 128)
        qg_row = swap(qg[p], "z").reshape(ROW, 128)
        outs = attend(table, counts, y_arr, gather_row(kv_row), qg_row)
        od.append(outs[0])
        kv_sum.append(sum_row(*outs[1:]))
    od_nodes = [swap(v.reshape(ZS, NODE_DEV, 128), "z") for v in od]
    kv_nodes = [swap(v.reshape(ZS, NODE_DEV, 128), "z") for v in kv_sum]
    attn_update = project_out(od_nodes[0], od_nodes[1], w_out)
    grad_nodes = node_grads(od_nodes[0], od_nodes[1], kv_nodes[0], kv_nodes[1], w_qkv)

    grads = jnp.concatenate([od[0][:, :HD], od[1][:, :HD], kv_sum[0], kv_sum[1]], axis=1)
    share = lax.dot_general(feats_row, grads, (((0,), (0,)), ((), ())), preferred_element_type=f32)
    rows = share.shape[0] // 32
    share = swap(share.astype(bf16).reshape(32, rows, 6 * HD), ("x", "c", "y"))
    share = jnp.sum(share.astype(f32), axis=0)
    share = swap(share.reshape(ZS, rows // ZS, 6, HD), "z")
    pick = lambda a, b: jnp.stack([share[:, :, a], share[:, :, b]], axis=2)
    grad_weights = jnp.stack([pick(0, 1), pick(2, 4), pick(3, 5)], axis=0)
    grad_weights = grad_weights.transpose(2, 0, 1, 3, 4).reshape(rows // ZS, 3 * H * HD)
    return attn_update[None], grad_nodes[None], grad_weights


def solution(mesh):
    fine = Mesh(np.asarray(mesh.devices).reshape(4, 2, YS, ZS), ("x", "c", "y", "z"))
    dp, seq = ("x", "c"), ("y", "z")
    in_specs = (P(dp, seq, None), P(), P(), P(dp, seq, None), P(dp, None, None), P(dp, None), P(dp, None))
    out_specs = (P(dp, seq, None), P(dp, seq, None), P(dp + seq, None))
    return jax.shard_map(on_device, mesh=fine, in_specs=in_specs, out_specs=out_specs, check_vma=False)
```

time: 1070 us -> 297 us (0.28)
  matrix products: 308 us -> 5.65 us
  waiting for transfers between devices: 335 us -> 54.8 us
  other arithmetic: 182 us -> 16.5 us
  local copies, waits for them, and re-layouts: 168 us -> 22.2 us
  Pallas kernels: 0 us -> 65.1 us
  blocking collectives: 0 us -> 55.1 us
    dot_general x47 -> x1, matrix products: 276 us -> 5.65 us  [on_device(): lax.dot_general(feats_row, grads, (((0,), (0,)), ((), ())), preferred_ele...]
    unnamed x2 -> x1, waiting for transfers between devices: 211 us -> 0.68 us
    unnamed x3 -> x0, other arithmetic: 94.7 us -> none
    scatter-add x8 -> x0, other arithmetic: 82.2 us -> none  [attend_group(): return (running.at[:, flat_rows].add(grad_kv), (attended_rows, grad_q))]
    all_to_all x6 -> x8, waiting for transfers between devices: 124 us -> 43 us  [swap(): return lax.all_to_all(values, axis, split_axis=0, concat_axis=0, tiled=True)]
    pallas_call x0 -> x6, Pallas kernels: none -> 65.1 us  [the longest x2 44.1 us: attend(): pl.pallas_call(attend_kernel, in_specs=[smem] * 3 + [vmem] * 6, out_specs...]
    all_to_all x0 -> x2, blocking collectives: none -> 55.1 us  [swap(): return lax.all_to_all(values, axis, split_axis=0, concat_axis=0, tiled=True)]
    reshape x11 -> x4, local copies, waits for them, and re-layouts: 36.6 us -> 0.95 us  [the longest x1 0.76 us: on_device(): grad_weights.transpose(2, 0, 1, 3, 4).reshape(rows // ZS, 3 * H * HD)]
  transfers between devices with their start and end apart: 7 -> 25, of which waited for: 6 -> 7; matrix products, arithmetic and copies ran while one was open for 15% -> 12% of each run, Pallas kernels for 0% -> 22%
where the time goes in v1:
time: 297 us; the launch traced here: 293 us
  Pallas kernels  65.1 us (22%)
  starting transfers between devices  59.1 us (20%)
  blocking collectives  55.1 us (19%)
  waiting for transfers between devices  54.8 us (18%)
  local copies, waits for them, and re-layouts  22.2 us (7%)
  other arithmetic  16.5 us (6%)
  between operations  14.4 us (5%)
  matrix products  5.65 us (2%)
    all_to_all x2, blocking collectives, swap(): return lax.all_to_all(values, axis, split_axis=0, concat_axis=0, tiled=True)  55.1 us
    pallas_call x2, Pallas kernels, attend(): pl.pallas_call(attend_kernel, in_specs=[smem] * 3 + [vmem] * 6, out_specs...  44.1 us
    all_to_all x8, waiting for transfers between devices, swap(): return lax.all_to_all(values, axis, split_axis=0, concat_axis=0, tiled=True)  43 us
    all_to_all x8, starting transfers between devices, swap(): return lax.all_to_all(values, axis, split_axis=0, concat_axis=0, tiled=True)  36.7 us
    ppermute x2, waiting for transfers between devices, gather_row(): left = lax.ppermute(own, 'y', RIGHT)  11 us
    unnamed x50, local copies, waits for them, and re-layouts  8.32 us
    ppermute x2, starting transfers between devices, sum_row(): lax.ppermute(to_left, 'y', LEFT)  6.47 us
    pallas_call x1, Pallas kernels, project_qg(): pl.pallas_call(qg_kernel, grid=(ZS,), in_specs=[whole((NODE_DEV, d)), who...  6.43 us
  transfers between devices with their start and end apart: 25, of which 7 were waited for; matrix products, arithmetic and copies ran while one was open for 12% of the time, Pallas kernels for 22%

profile of v1, /device:TPU:8, one launch (start us, length us, event | category | flops | bytes accessed | tf_op | source)
XLA Modules:
  0.0 292.9 jit_solution(14679753699555936368)
XLA Ops:
  9.0 6.3 %project_kv.1 = (bf16[8,256,128]{2,1,0:T(8,128)(2,1)S(1)}, bf16[8,256,128]{2,1,0:T(8,128)(2,1)S(1)}) custom-call(bf16[256,1024]{1,0:T(8,128)(2,1)S(1)} %bitcast.42, bf16[1024,3072]{1,0:T(8,128)(2,1)} %wv_ref.3, bf16[1024,3072]{1,0:T(8,128)(2,1)} %wv_ref.3), custom_call_target="tpu_custom_call" | custom-call | tf_op jit(solution)/shard_map/project_kv/pallas_call | solution.py:76
  16.1 31.9 %all_to_all.50 = bf16[8,256,128]{2,1,0:T(8,128)(2,1)} all-to-all(bf16[8,256,128]{2,1,0:T(8,128)(2,1)S(1)} %get-tuple-element.20), channel_id=1, replica_groups=mesh['x'=4,'c'=2,'y'=4,'z'=8] {'z'}, dimensions={0} | all-to-all | bytes 1048576 | tf_op jit(solution)/shard_map/all_to_all | solution.py:276
  48.0 4.1 %all-to-all-start = ((bf16[8,256,128]{2,1,0:T(8,128)(2,1)}), bf16[8,256,128]{2,1,0:T(8,128)(2,1)}, u32[]{:S(2)}, u32[]{:S(2)}) async-start(bf16[8,256,128]{2,1,0:T(8,128)(2,1)} %copy-done.16), calls=%async_computation | async-start | bytes 1048576 | tf_op jit(solution)/shard_map/all_to_all | solution.py:276
  52.2 6.4 %project_qg.1 = (bf16[8,256,128]{2,1,0:T(8,128)(2,1)S(1)}, bf16[8,256,128]{2,1,0:T(8,128)(2,1)S(1)}) custom-call(bf16[256,1024]{1,0:T(8,128)(2,1)S(1)} %bitcast.43, bf16[256,1024]{1,0:T(8,128)(2,1)S(1)} %bitcast.44, bf16[1024,3072]{1,0:T(8,128)(2,1)} %wv_ref.3, bf16[1024,1024]{1,0:T(8,128)(2,1)S(1)} %copy-done.1), custom_call_target="tpu_custom_call" | custom-call | tf_op jit(solution)/shard_map/project_qg/pallas_call | solution.py:95
  60.2 14.9 %all-to-all-done = bf16[8,256,128]{2,1,0:T(8,128)(2,1)} async-done(((bf16[8,256,128]{2,1,0:T(8,128)(2,1)}), bf16[8,256,128]{2,1,0:T(8,128)(2,1)}, u32[]{:S(2)}, u32[]{:S(2)}) %all-to-all-start) | async-done | bytes 524320 | tf_op jit(solution)/shard_map/all_to_all | solution.py:276
  75.1 3.5 %all-to-all-start.4 = ((bf16[8,256,128]{2,1,0:T(8,128)(2,1)}), bf16[8,256,128]{2,1,0:T(8,128)(2,1)S(1)}, u32[]{:S(2)}, u32[]{:S(2)}) async-start(bf16[8,256,128]{2,1,0:T(8,128)(2,1)} %copy-done.15), calls=%async_computation.4 | async-start | bytes 1048576 | tf_op jit(solution)/shard_map/all_to_all | solution.py:276
  78.6 1.7 collective-permute-start.4
  80.7 1.6 collective-permute-start
  82.8 11.0 %collective-permute-done.4.left_ref = bf16[2048,128]{1,0:T(8,128)(2,1)} collective-permute-done((bf16[2048,128]{1,0:T(8,128)(2,1)}, bf16[2048,128]{1,0:T(8,128)(2,1)}, u32[]{:S(2)}, u32[]{:S(2)}) %collective-permute-start.4) | collective-permute-done | bytes 524320 | tf_op jit(solution)/shard_map/ppermute | solution.py:284
  93.9 1.7 slice.93
  95.5 1.6 collective-permute-start.6
  97.2 1.7 slice.94
  99.3 2.0 all-to-all-done.4
  101.3 5.1 %all-to-all-start.1 = ((bf16[8,256,128]{2,1,0:T(8,128)(2,1)}), bf16[8,256,128]{2,1,0:T(8,128)(2,1)}, u32[]{:S(2)}, u32[]{:S(2)}) async-start(bf16[8,256,128]{2,1,0:T(8,128)(2,1)} %copy-done.11), calls=%async_computation.1 | async-start | bytes 1048576 | tf_op jit(solution)/shard_map/all_to_all | solution.py:276
  107.4 1.6 collective-permute-start.2
  109.0 1.7 slice.92
  110.7 1.3 collective-permute-start.3
  113.1 1.0 copy-done.14
  114.1 21.9 %attend.3 = (bf16[2048,128]{1,0:T(8,128)(2,1)S(1)}, bf16[2048,128]{1,0:T(8,128)(2,1)S(1)}, bf16[2048,128]{1,0:T(8,128)(2,1)S(1)}, bf16[2048,128]{1,0:T(8,128)(2,1)S(1)}, bf16[2048,128]{1,0:T(8,128)(2,1)S(1)}) custom-call(s32[192]{0:T(256)S(1)} %reshape.47.tab_ref, s32[16]{0:T(128)S(1)} %dynamic-slice_bitcast_fusion.1.cnt_ref, s32[1]{0:T(128)} %bitcast.3.y_ref, ...), custom_call_target="tpu_custom_call" | custom-call | flops 3623878656 | bytes 6291456 | tf_op jit(solution)/shard_map/attend/pallas_call | solution.py:186
  137.8 1.1 collective-permute-start.12
  140.0 22.2 %attend.2 = (bf16[2048,128]{1,0:T(8,128)(2,1)S(1)}, bf16[2048,128]{1,0:T(8,128)(2,1)S(1)}, bf16[2048,128]{1,0:T(8,128)(2,1)S(1)}, bf16[2048,128]{1,0:T(8,128)(2,1)S(1)}, bf16[2048,128]{1,0:T(8,128)(2,1)S(1)}) custom-call(s32[192]{0:T(256)S(1)} %reshape.47.tab_ref, s32[16]{0:T(128)S(1)} %dynamic-slice_bitcast_fusion.1.cnt_ref, s32[1]{0:T(128)} %bitcast.3.y_ref, ...), custom_call_target="tpu_custom_call" | custom-call | flops 3623878656 | bytes 6291456 | tf_op jit(solution)/shard_map/attend/pallas_call | solution.py:186
  163.1 2.6 collective-permute-start.14
  168.0 3.0 %collective-permute-start.10 = (bf16[1024,128]{1,0:T(8,128)(2,1)}, bf16[1024,128]{1,0:T(8,128)(2,1)}, u32[]{:S(2)}, u32[]{:S(2)}) collective-permute-start(bf16[1024,128]{1,0:T(8,128)(2,1)} %get-tuple-element.34), channel_id=1, source_target_pairs={{0,24},{8,0},{16,8},{24,16},{1,25},{9,1},{17,9},{25,17},{2,26},{10... | collective-permute-start | bytes 786440 | tf_op jit(solution)/shard_map/ppermute | solution.py:293
  171.1 7.2 %all-to-all-start.5 = ((bf16[8,256,128]{2,1,0:T(8,128)(2,1)}), bf16[8,256,128]{2,1,0:T(8,128)(2,1)S(1)}, u32[]{:S(2)}, u32[]{:S(2)}) async-start(bf16[8,256,128]{2,1,0:T(8,128)(2,1)} %bitcast.45), calls=%async_computation.5 | async-start | bytes 1048576 | tf_op jit(solution)/shard_map/all_to_all | solution.py:276
  178.4 1.2 add_convert_fusion.3
  179.5 1.8 pad_maximum_fusion.2
  181.4 1.0 add_convert_fusion.2
  182.4 1.8 pad_maximum_fusion.3
  184.2 3.2 %collective-permute-start.15 = (bf16[2048,128]{1,0:T(8,128)(2,1)}, bf16[2048,128]{1,0:T(8,128)(2,1)}, u32[]{:S(2)}, u32[]{:S(2)}) collective-permute-start(bf16[2048,128]{1,0:T(8,128)(2,1)} %pad_maximum_fusion.3), channel_id=1, source_target_pairs={{0,24},{8,0},{16,8},{24,16},{1,25},{9,1},{17,9},{25,17},{2,26},{10... | collective-permute-start | bytes 1572872 | tf_op jit(solution)/shard_map/ppermute | solution.py:297
  187.4 1.0 add_convert_fusion.5
  189.3 2.3 all-to-all-done.5.b_ref.ob_ref
  191.6 4.9 %all-to-all-start.2 = ((bf16[8,256,128]{2,1,0:T(8,128)(2,1)}), bf16[8,256,128]{2,1,0:T(8,128)(2,1)S(1)}, u32[]{:S(2)}, u32[]{:S(2)}) async-start(bf16[8,256,128]{2,1,0:T(8,128)(2,1)} %bitcast.47), calls=%async_computation.2 | async-start | bytes 1048576 | tf_op jit(solution)/shard_map/all_to_all | solution.py:276
  196.5 1.1 add_convert_fusion.4
  198.5 3.2 %collective-permute-start.11 = (bf16[2048,128]{1,0:T(8,128)(2,1)}, bf16[2048,128]{1,0:T(8,128)(2,1)}, u32[]{:S(2)}, u32[]{:S(2)}) collective-permute-start(bf16[2048,128]{1,0:T(8,128)(2,1)} %pad_maximum_fusion.1), channel_id=1, source_target_pairs={{0,24},{8,0},{16,8},{24,16},{1,25},{9,1},{17,9},{25,17},{2,26},{10... | collective-permute-start | bytes 1572872 | tf_op jit(solution)/shard_map/ppermute | solution.py:297
  201.7 2.4 add_convert_fusion
  204.1 5.0 %all-to-all-done.2.a_ref.oa_ref = bf16[8,256,128]{2,1,0:T(8,128)(2,1)S(1)} async-done(((bf16[8,256,128]{2,1,0:T(8,128)(2,1)}), bf16[8,256,128]{2,1,0:T(8,128)(2,1)S(1)}, u32[]{:S(2)}, u32[]{:S(2)}) %all-to-all-start.2) | async-done | bytes 524320 | tf_op jit(solution)/shard_map/all_to_all | solution.py:276
  209.1 4.4 %all-to-all-start.7 = ((bf16[8,256,128]{2,1,0:T(8,128)(2,1)}), bf16[8,256,128]{2,1,0:T(8,128)(2,1)}, u32[]{:S(2)}, u32[]{:S(2)}) async-start(bf16[8,256,128]{2,1,0:T(8,128)(2,1)} %bitcast.54), calls=%async_computation.7 | async-start | bytes 1048576 | tf_op jit(solution)/shard_map/all_to_all | solution.py:276
  213.5 2.4 add_convert_fusion.1
  215.9 5.7 %fusion.14 = bf16[1024,384]{0,1:T(8,128)(2,1)} fusion(bf16[1,2048,1024]{2,1,0:T(8,128)(2,1)} %all-gather.3.cloned.1.call-done, bf16[2048,128]{1,0:T(8,128)(2,1)} %add_convert_fusion, bf16[2048,128]{1,0:T(8,128)(2,1)} %add_convert_fusion.1, bf16[2048,64]{1,0:T(8,128)(2,1)} %bitcast.46, bf16[2048,64]{1,0:T(8,128)(2,1)} %bitcast.48), kind=kOutput, calls=%fused_computation.11 | convolution fusion | flops 1617297408 | bytes 6553600 | tf_op jit(solution)/shard_map/dot_general | solution.py:325
  221.5 2.3 copy.18
  223.8 2.7 all-to-all-done.7.kb_ref
  226.5 23.2 %all_to_all.51 = bf16[32,32,384]{2,1,0:T(8,128)(2,1)} all-to-all(bf16[32,32,384]{2,1,0:T(8,128)(2,1)} %bitcast.53), channel_id=1, replica_groups=mesh['x'=4,'c'=2,'y'=4,'z'=8] {'x','c','y'}, dimensions={0} | all-to-all | bytes 1572864 | tf_op jit(solution)/shard_map/all_to_all | solution.py:276
  249.8 4.2 %all-to-all-start.6 = ((bf16[8,256,128]{2,1,0:T(8,128)(2,1)}), bf16[8,256,128]{2,1,0:T(8,128)(2,1)}, u32[]{:S(2)}, u32[]{:S(2)}) async-start(bf16[8,256,128]{2,1,0:T(8,128)(2,1)} %bitcast.55), calls=%async_computation.6 | async-start | bytes 1048576 | tf_op jit(solution)/shard_map/all_to_all | solution.py:276
  253.9 1.3 convert_reduce_fusion
  256.0 16.1 %all-to-all-done.6.ka_ref = bf16[8,256,128]{2,1,0:T(8,128)(2,1)} async-done(((bf16[8,256,128]{2,1,0:T(8,128)(2,1)}), bf16[8,256,128]{2,1,0:T(8,128)(2,1)}, u32[]{:S(2)}, u32[]{:S(2)}) %all-to-all-start.6) | async-done | bytes 524320 | tf_op jit(solution)/shard_map/all_to_all | solution.py:276
  272.1 3.3 %all-to-all-start.9 = ((f32[8,1,1536]{2,1,0:T(1,128)}), f32[8,1,1536]{2,1,0:T(1,128)S(1)}, u32[]{:S(2)}, u32[]{:S(2)}) async-start(f32[8,1,1536]{2,1,0:T(1,128)} %reshape.62), calls=%async_computation.9 | async-start | bytes 98304 | tf_op jit(solution)/shard_map/all_to_all | solution.py:276
  275.5 2.3 project_out.1
  277.8 5.9 %node_grads.1 = bf16[256,1024]{1,0:T(8,128)(2,1)} custom-call(bf16[8,256,128]{2,1,0:T(8,128)(2,1)S(1)} %all-to-all-done.2.a_ref.oa_ref, bf16[8,256,128]{2,1,0:T(8,128)(2,1)S(1)} %all-to-all-done.5.b_ref.ob_ref, bf16[8,256,128]{2,1,0:T(8,128)(2,1)} %all-to-all-done.6.ka_ref, bf16[8,256,128]{2,1,0:T(8,128)(2,1)} %all-to-all-done.7.kb_ref, ...), custom_call_target="tpu_custom_call" | custom-call | tf_op jit(solution)/shard_map/node_grads/pallas_call | solution.py:262
  (100 shorter events, 18.4 us)
Async XLA Ops:
  7.2 75.6 %copy-start = (s32[1,64,8]{1,2,0:T(8,128)S(1)}, s32[1,64,8]{1,2,0:T(8,128)}, u32[]{:S(2)}) copy-start(s32[1,64,8]{1,2,0:T(8,128)} %param.11) | copy-start | bytes 6148
  7.2 208.7 %all-gather.3.cloned.1.call-start = ((), (), s32[]{:S(2)}) async-start(), calls=%async_computation.10 | async-start | bytes 4718592 | tf_op jit(solution)/shard_map/all_gather | solution.py:311
  7.9 1.0 copy-start.2
  9.0 43.2 %copy-start.3 = (bf16[1,256,1024]{2,1,0:T(8,128)(2,1)S(1)}, bf16[1,256,1024]{2,1,0:T(8,128)(2,1)}, u32[]{:S(2)}) copy-start(bf16[1,256,1024]{2,1,0:T(8,128)(2,1)} %param.7) | copy-start | bytes 1572868
  9.0 43.2 %copy-start.4 = (bf16[1,256,1024]{2,1,0:T(8,128)(2,1)S(1)}, bf16[1,256,1024]{2,1,0:T(8,128)(2,1)}, u32[]{:S(2)}) copy-start(bf16[1,256,1024]{2,1,0:T(8,128)(2,1)} %param.10) | copy-start | bytes 1572868
  15.3 0.8 copy-start.16
  16.1 36.1 %copy-start.1 = (bf16[1024,1024]{1,0:T(8,128)(2,1)S(1)}, bf16[1024,1024]{1,0:T(8,128)(2,1)}, u32[]{:S(2)}) copy-start(bf16[1024,1024]{1,0:T(8,128)(2,1)} %wo_ref.3) | copy-start | bytes 6291460
  48.0 27.1 %all-to-all-start = ((bf16[8,256,128]{2,1,0:T(8,128)(2,1)}), bf16[8,256,128]{2,1,0:T(8,128)(2,1)}, u32[]{:S(2)}, u32[]{:S(2)}) async-start(bf16[8,256,128]{2,1,0:T(8,128)(2,1)} %copy-done.16), calls=%async_computation | async-start | bytes 1048576 | tf_op jit(solution)/shard_map/all_to_all | solution.py:276
  52.2 30.6 %copy-start.22 = (s32[1,4]{1,0:T(1,128)S(1)}, s32[1,4]{1,0:T(1,128)}, u32[]{:S(2)}) copy-start(s32[1,4]{1,0:T(1,128)} %param.13) | copy-start | bytes 52
  58.6 0.8 copy-start.11
  60.2 46.3 %copy-start.23 = (s32[1,64]{1,0:T(1,128)S(1)}, s32[1,64]{1,0:T(1,128)}, u32[]{:S(2)}) copy-start(s32[1,64]{1,0:T(1,128)} %param.12) | copy-start | bytes 772
  75.1 26.1 %all-to-all-start.4 = ((bf16[8,256,128]{2,1,0:T(8,128)(2,1)}), bf16[8,256,128]{2,1,0:T(8,128)(2,1)S(1)}, u32[]{:S(2)}, u32[]{:S(2)}) async-start(bf16[8,256,128]{2,1,0:T(8,128)(2,1)} %copy-done.15), calls=%async_computation.4 | async-start | bytes 1048576 | tf_op jit(solution)/shard_map/all_to_all | solution.py:276
  78.6 15.3 %collective-permute-start.4 = (bf16[2048,128]{1,0:T(8,128)(2,1)}, bf16[2048,128]{1,0:T(8,128)(2,1)}, u32[]{:S(2)}, u32[]{:S(2)}) collective-permute-start(bf16[2048,128]{1,0:T(8,128)(2,1)} %bitcast.49), channel_id=1, source_target_pairs={{0,8},{8,16},{16,24},{24,0},{1,9},{9,17},{17,25},{25,1},{2,10},{10... | collective-permute-start | bytes 1572872 | tf_op jit(solution)/shard_map/ppermute | solution.py:284
  80.3 16.9 %collective-permute-start.5 = (bf16[2048,128]{1,0:T(8,128)(2,1)}, bf16[2048,128]{1,0:T(8,128)(2,1)}, u32[]{:S(2)}, u32[]{:S(2)}) collective-permute-start(bf16[2048,128]{1,0:T(8,128)(2,1)} %bitcast.50), channel_id=1, source_target_pairs={{0,24},{8,0},{16,8},{24,16},{1,25},{9,1},{17,9},{25,17},{2,26},{10... | collective-permute-start | bytes 1572872 | tf_op jit(solution)/shard_map/ppermute | solution.py:285
  80.7 25.9 %collective-permute-start = (bf16[2048,128]{1,0:T(8,128)(2,1)}, bf16[2048,128]{1,0:T(8,128)(2,1)S(1)}, u32[]{:S(2)}, u32[]{:S(2)}) collective-permute-start(bf16[2048,128]{1,0:T(8,128)(2,1)} %bitcast.5.own_ref), channel_id=1, source_target_pairs={{0,8},{8,16},{16,24},{24,0},{1,9},{9,17},{17,25},{25,1},{2,10},{10... | collective-permute-start | bytes 1572872 | tf_op jit(solution)/shard_map/ppermute | solution.py:284
  82.3 26.7 %collective-permute-start.1 = (bf16[2048,128]{1,0:T(8,128)(2,1)}, bf16[2048,128]{1,0:T(8,128)(2,1)}, u32[]{:S(2)}, u32[]{:S(2)}) collective-permute-start(bf16[2048,128]{1,0:T(8,128)(2,1)} %bitcast.5.own_ref), channel_id=1, source_target_pairs={{0,24},{8,0},{16,8},{24,16},{1,25},{9,1},{17,9},{25,17},{2,26},{10... | collective-permute-start | bytes 1572872 | tf_op jit(solution)/shard_map/ppermute | solution.py:285
  95.5 16.5 %collective-permute-start.6 = (bf16[1024,128]{1,0:T(8,128)(2,1)}, bf16[1024,128]{1,0:T(8,128)(2,1)S(1)}, u32[]{:S(2)}, u32[]{:S(2)}) collective-permute-start(bf16[1024,128]{1,0:T(8,128)(2,1)} %slice.93), channel_id=1, source_target_pairs={{0,8},{8,16},{16,24},{24,0},{1,9},{9,17},{17,25},{25,1},{2,10},{10... | collective-permute-start | bytes 786440 | tf_op jit(solution)/shard_map/ppermute | solution.py:286
  98.9 13.2 %collective-permute-start.7 = (bf16[1024,128]{1,0:T(8,128)(2,1)}, bf16[1024,128]{1,0:T(8,128)(2,1)}, u32[]{:S(2)}, u32[]{:S(2)}) collective-permute-start(bf16[1024,128]{1,0:T(8,128)(2,1)} %slice.94), channel_id=1, source_target_pairs={{0,24},{8,0},{16,8},{24,16},{1,25},{9,1},{17,9},{25,17},{2,26},{10... | collective-permute-start | bytes 786440 | tf_op jit(solution)/shard_map/ppermute | solution.py:287
  101.3 10.8 %copy-start.13 = (bf16[8,256,128]{2,1,0:T(8,128)(2,1)}, bf16[8,256,128]{2,1,0:T(8,128)(2,1)S(1)}, u32[]{:S(2)}) copy-start(bf16[8,256,128]{2,1,0:T(8,128)(2,1)S(1)} %all-to-all-done.4) | copy-start | bytes 1572868
  101.3 37.7 %all-to-all-start.1 = ((bf16[8,256,128]{2,1,0:T(8,128)(2,1)}), bf16[8,256,128]{2,1,0:T(8,128)(2,1)}, u32[]{:S(2)}, u32[]{:S(2)}) async-start(bf16[8,256,128]{2,1,0:T(8,128)(2,1)} %copy-done.11), calls=%async_computation.1 | async-start | bytes 1048576 | tf_op jit(solution)/shard_map/all_to_all | solution.py:276
  106.7 5.4 %copy-start.19 = (bf16[2048,128]{1,0:T(8,128)(2,1)}, bf16[2048,128]{1,0:T(8,128)(2,1)S(1)}, u32[]{:S(2)}) copy-start(bf16[2048,128]{1,0:T(8,128)(2,1)S(1)} %collective-permute-done.left_ref) | copy-start | bytes 1572868
  107.4 31.6 %collective-permute-start.2 = (bf16[1024,128]{1,0:T(8,128)(2,1)}, bf16[1024,128]{1,0:T(8,128)(2,1)}, u32[]{:S(2)}, u32[]{:S(2)}) collective-permute-start(bf16[1024,128]{1,0:T(8,128)(2,1)} %slice.91), channel_id=1, source_target_pairs={{0,8},{8,16},{16,24},{24,0},{1,9},{9,17},{17,25},{25,1},{2,10},{10... | collective-permute-start | bytes 786440 | tf_op jit(solution)/shard_map/ppermute | solution.py:286
  110.7 28.3 %collective-permute-start.3 = (bf16[1024,128]{1,0:T(8,128)(2,1)}, bf16[1024,128]{1,0:T(8,128)(2,1)}, u32[]{:S(2)}, u32[]{:S(2)}) collective-permute-start(bf16[1024,128]{1,0:T(8,128)(2,1)} %slice.92), channel_id=1, source_target_pairs={{0,24},{8,0},{16,8},{24,16},{1,25},{9,1},{17,9},{25,17},{2,26},{10... | collective-permute-start | bytes 786440 | tf_op jit(solution)/shard_map/ppermute | solution.py:287
  112.0 1.0 copy-start.12
  113.1 1.0 copy-start.14
  136.0 0.8 copy-start.9
  136.8 1.0 copy-start.17
  136.8 25.4 %copy-start.6 = (bf16[2048,128]{1,0:T(8,128)(2,1)}, bf16[2048,128]{1,0:T(8,128)(2,1)S(1)}, u32[]{:S(2)}) copy-start(bf16[2048,128]{1,0:T(8,128)(2,1)S(1)} %get-tuple-element.28) | copy-start | bytes 1572868
  137.8 40.5 %collective-permute-start.12 = (bf16[1024,128]{1,0:T(8,128)(2,1)}, bf16[1024,128]{1,0:T(8,128)(2,1)}, u32[]{:S(2)}, u32[]{:S(2)}) collective-permute-start(bf16[1024,128]{1,0:T(8,128)(2,1)} %get-tuple-element.31), channel_id=1, source_target_pairs={{0,8},{8,16},{16,24},{24,0},{1,9},{9,17},{17,25},{25,1},{2,10},{10... | collective-permute-start | bytes 786440 | tf_op jit(solution)/shard_map/ppermute | solution.py:292
  139.0 1.0 copy-start.20
  162.2 8.8 %copy-start.5 = (bf16[2048,128]{1,0:T(8,128)(2,1)}, bf16[2048,128]{1,0:T(8,128)(2,1)S(1)}, u32[]{:S(2)}) copy-start(bf16[2048,128]{1,0:T(8,128)(2,1)S(1)} %get-tuple-element.26) | copy-start | bytes 1572868
  162.2 8.9 %copy-start.7 = (bf16[2048,128]{1,0:T(8,128)(2,1)}, bf16[2048,128]{1,0:T(8,128)(2,1)S(1)}, u32[]{:S(2)}) copy-start(bf16[2048,128]{1,0:T(8,128)(2,1)S(1)} %get-tuple-element.24) | copy-start | bytes 1572868
  162.2 8.9 %copy-start.10 = (bf16[2048,128]{1,0:T(8,128)(2,1)}, bf16[2048,128]{1,0:T(8,128)(2,1)S(1)}, u32[]{:S(2)}) copy-start(bf16[2048,128]{1,0:T(8,128)(2,1)S(1)} %get-tuple-element.19) | copy-start | bytes 1572868
  162.2 8.9 %copy-start.18 = (bf16[2048,128]{1,0:T(8,128)(2,1)}, bf16[2048,128]{1,0:T(8,128)(2,1)S(1)}, u32[]{:S(2)}) copy-start(bf16[2048,128]{1,0:T(8,128)(2,1)S(1)} %get-tuple-element.23) | copy-start | bytes 1572868
  163.1 18.3 %collective-permute-start.14 = (bf16[1024,128]{1,0:T(8,128)(2,1)}, bf16[1024,128]{1,0:T(8,128)(2,1)}, u32[]{:S(2)}, u32[]{:S(2)}) collective-permute-start(bf16[1024,128]{1,0:T(8,128)(2,1)} %get-tuple-element.32), channel_id=1, source_target_pairs={{0,24},{8,0},{16,8},{24,16},{1,25},{9,1},{17,9},{25,17},{2,26},{10... | collective-permute-start | bytes 786440 | tf_op jit(solution)/shard_map/ppermute | solution.py:293
  167.3 20.1 %collective-permute-start.8 = (bf16[1024,128]{1,0:T(8,128)(2,1)}, bf16[1024,128]{1,0:T(8,128)(2,1)}, u32[]{:S(2)}, u32[]{:S(2)}) collective-permute-start(bf16[1024,128]{1,0:T(8,128)(2,1)} %get-tuple-element.33), channel_id=1, source_target_pairs={{0,8},{8,16},{16,24},{24,0},{1,9},{9,17},{17,25},{25,1},{2,10},{10... | collective-permute-start | bytes 786440 | tf_op jit(solution)/shard_map/ppermute | solution.py:292
  168.0 28.5 %collective-permute-start.10 = (bf16[1024,128]{1,0:T(8,128)(2,1)}, bf16[1024,128]{1,0:T(8,128)(2,1)}, u32[]{:S(2)}, u32[]{:S(2)}) collective-permute-start(bf16[1024,128]{1,0:T(8,128)(2,1)} %get-tuple-element.34), channel_id=1, source_target_pairs={{0,24},{8,0},{16,8},{24,16},{1,25},{9,1},{17,9},{25,17},{2,26},{10... | collective-permute-start | bytes 786440 | tf_op jit(solution)/shard_map/ppermute | solution.py:293
  171.1 20.5 %all-to-all-start.5 = ((bf16[8,256,128]{2,1,0:T(8,128)(2,1)}), bf16[8,256,128]{2,1,0:T(8,128)(2,1)S(1)}, u32[]{:S(2)}, u32[]{:S(2)}) async-start(bf16[8,256,128]{2,1,0:T(8,128)(2,1)} %bitcast.45), calls=%async_computation.5 | async-start | bytes 1048576 | tf_op jit(solution)/shard_map/all_to_all | solution.py:276
  178.3 9.1 %copy-start.8 = (bf16[2048,128]{1,0:T(8,128)(2,1)S(1)}, bf16[2048,128]{1,0:T(8,128)(2,1)}, u32[]{:S(2)}) copy-start(bf16[2048,128]{1,0:T(8,128)(2,1)} %copy-done.7) | copy-start | bytes 1572868
  178.3 10.1 %copy-start.21 = (bf16[1024,128]{1,0:T(8,128)(2,1)S(1)}, bf16[1024,128]{1,0:T(8,128)(2,1)}, u32[]{:S(2)}) copy-start(bf16[1024,128]{1,0:T(8,128)(2,1)} %slice.75) | copy-start | bytes 786436
  181.3 20.3 %collective-permute-start.13 = (bf16[2048,128]{1,0:T(8,128)(2,1)}, bf16[2048,128]{1,0:T(8,128)(2,1)}, u32[]{:S(2)}, u32[]{:S(2)}) collective-permute-start(bf16[2048,128]{1,0:T(8,128)(2,1)} %pad_maximum_fusion.2), channel_id=1, source_target_pairs={{0,8},{8,16},{16,24},{24,0},{1,9},{9,17},{17,25},{25,1},{2,10},{10... | collective-permute-start | bytes 1572872 | tf_op jit(solution)/shard_map/ppermute | solution.py:297
  184.2 17.5 %collective-permute-start.15 = (bf16[2048,128]{1,0:T(8,128)(2,1)}, bf16[2048,128]{1,0:T(8,128)(2,1)}, u32[]{:S(2)}, u32[]{:S(2)}) collective-permute-start(bf16[2048,128]{1,0:T(8,128)(2,1)} %pad_maximum_fusion.3), channel_id=1, source_target_pairs={{0,24},{8,0},{16,8},{24,16},{1,25},{9,1},{17,9},{25,17},{2,26},{10... | collective-permute-start | bytes 1572872 | tf_op jit(solution)/shard_map/ppermute | solution.py:297
  189.3 24.2 %collective-permute-start.9 = (bf16[2048,128]{1,0:T(8,128)(2,1)}, bf16[2048,128]{1,0:T(8,128)(2,1)}, u32[]{:S(2)}, u32[]{:S(2)}) collective-permute-start(bf16[2048,128]{1,0:T(8,128)(2,1)} %pad_maximum_fusion), channel_id=1, source_target_pairs={{0,8},{8,16},{16,24},{24,0},{1,9},{9,17},{17,25},{25,1},{2,10},{10... | collective-permute-start | bytes 1572872 | tf_op jit(solution)/shard_map/ppermute | solution.py:297
  191.6 17.5 %all-to-all-start.2 = ((bf16[8,256,128]{2,1,0:T(8,128)(2,1)}), bf16[8,256,128]{2,1,0:T(8,128)(2,1)S(1)}, u32[]{:S(2)}, u32[]{:S(2)}) async-start(bf16[8,256,128]{2,1,0:T(8,128)(2,1)} %bitcast.47), calls=%async_computation.2 | async-start | bytes 1048576 | tf_op jit(solution)/shard_map/all_to_all | solution.py:276
  198.5 15.0 %collective-permute-start.11 = (bf16[2048,128]{1,0:T(8,128)(2,1)}, bf16[2048,128]{1,0:T(8,128)(2,1)}, u32[]{:S(2)}, u32[]{:S(2)}) collective-permute-start(bf16[2048,128]{1,0:T(8,128)(2,1)} %pad_maximum_fusion.1), channel_id=1, source_target_pairs={{0,24},{8,0},{16,8},{24,16},{1,25},{9,1},{17,9},{25,17},{2,26},{10... | collective-permute-start | bytes 1572872 | tf_op jit(solution)/shard_map/ppermute | solution.py:297
  209.1 17.4 %all-to-all-start.7 = ((bf16[8,256,128]{2,1,0:T(8,128)(2,1)}), bf16[8,256,128]{2,1,0:T(8,128)(2,1)}, u32[]{:S(2)}, u32[]{:S(2)}) async-start(bf16[8,256,128]{2,1,0:T(8,128)(2,1)} %bitcast.54), calls=%async_computation.7 | async-start | bytes 1048576 | tf_op jit(solution)/shard_map/all_to_all | solution.py:276
  249.8 22.3 %all-to-all-start.6 = ((bf16[8,256,128]{2,1,0:T(8,128)(2,1)}), bf16[8,256,128]{2,1,0:T(8,128)(2,1)}, u32[]{:S(2)}, u32[]{:S(2)}) async-start(bf16[8,256,128]{2,1,0:T(8,128)(2,1)} %bitcast.55), calls=%async_computation.6 | async-start | bytes 1048576 | tf_op jit(solution)/shard_map/all_to_all | solution.py:276
  272.1 11.6 %all-to-all-start.9 = ((f32[8,1,1536]{2,1,0:T(1,128)}), f32[8,1,1536]{2,1,0:T(1,128)S(1)}, u32[]{:S(2)}, u32[]{:S(2)}) async-start(f32[8,1,1536]{2,1,0:T(1,128)} %reshape.62), calls=%async_computation.9 | async-start | bytes 98304 | tf_op jit(solution)/shard_map/all_to_all | solution.py:276
  (1 other events, 0.8 us)
Sparse Core Ops, SparseCore 0:
  9.8 91.1 all-gather.2

commit v2 on v1

--- a/solution.py
+++ b/solution.py
@@ -26,7 +26,7 @@
 SCALE = HD**-0.5
 LOG2E = math.log2(math.e)
 MASKED = -3.0e38
-VMEM = pltpu.CompilerParams(vmem_limit_bytes=48 * 1024 * 1024)
+VMEM = pltpu.CompilerParams(vmem_limit_bytes=60 * 1024 * 1024)
 
 bf16 = jnp.bfloat16
 f32 = jnp.float32
@@ -52,17 +52,20 @@
     return lax.dot_general(a, b, (((1,), (0,)), ((), ())), preferred_element_type=f32)
 
 
+def put_pairs(first, second, a_ref, b_ref):
+    for u in (0, 1):
+        cols = slice(u * 128, (u + 1) * 128)
+        a, b = pair_up(first[:, cols], second[:, cols])
+        a_ref[u] = a.astype(bf16)
+        b_ref[u] = b.astype(bf16)
+
+
 def kv_kernel(f_ref, wk_ref, wv_ref, a_ref, b_ref):
-    both = nn(f_ref[...], jnp.concatenate([wk_ref[...], wv_ref[...]], axis=1))
-    a, b = pair_up(both[:, :128], both[:, 128:])
-    a_ref[0] = a.astype(bf16)
-    b_ref[0] = b.astype(bf16)
+    put_pairs(nn(f_ref[...], wk_ref[...]), nn(f_ref[...], wv_ref[...]), a_ref, b_ref)
 
 
 def qg_kernel(f_ref, c_ref, wq_ref, wo_ref, a_ref, b_ref):
-    a, b = pair_up(nn(f_ref[...], wq_ref[...]), nt(c_ref[...], wo_ref[...]))
-    a_ref[0] = a.astype(bf16)
-    b_ref[0] = b.astype(bf16)
+    put_pairs(nn(f_ref[...], wq_ref[...]), nt(c_ref[...], wo_ref[...]), a_ref, b_ref)
 
 
 def whole(shape):
@@ -72,14 +75,14 @@
 def project_kv(feats, w_qkv):
     d = feats.shape[1]
     out = jax.ShapeDtypeStruct((ZS, NODE_DEV, 128), bf16)
-    tile = pl.BlockSpec((1, NODE_DEV, 128), lambda i: (i, 0, 0))
+    tile = pl.BlockSpec((2, NODE_DEV, 128), lambda i: (i, 0, 0))
     return pl.pallas_call(
         kv_kernel,
-        grid=(ZS,),
+        grid=(ZS // 2,),
         in_specs=[
             whole((NODE_DEV, d)),
-            pl.BlockSpec((d, 128), lambda i: (0, ZS + i)),
-            pl.BlockSpec((d, 128), lambda i: (0, 2 * ZS + i)),
+            pl.BlockSpec((d, 256), lambda i: (0, ZS // 2 + i)),
+            pl.BlockSpec((d, 256), lambda i: (0, ZS + i)),
         ],
         out_specs=[tile, tile],
         out_shape=[out, out],
@@ -91,15 +94,15 @@
 def project_qg(feats, cot, w_qkv, w_out):
     d = feats.shape[1]
     out = jax.ShapeDtypeStruct((ZS, NODE_DEV, 128), bf16)
-    tile = pl.BlockSpec((1, NODE_DEV, 128), lambda i: (i, 0, 0))
+    tile = pl.BlockSpec((2, NODE_DEV, 128), lambda i: (i, 0, 0))
     return pl.pallas_call(
         qg_kernel,
-        grid=(ZS,),
+        grid=(ZS // 2,),
         in_specs=[
             whole((NODE_DEV, d)),
             whole((NODE_DEV, d)),
-            pl.BlockSpec((d, 128), lambda i: (0, i)),
-            pl.BlockSpec((128, d), lambda i: (i, 0)),
+            pl.BlockSpec((d, 256), lambda i: (0, i)),
+            pl.BlockSpec((256, d), lambda i: (i, 0)),
         ],
         out_specs=[tile, tile],
         out_shape=[out, out],
@@ -109,7 +112,7 @@
 
 
 def attend_kernel(
-    tab_ref, cnt_ref, y_ref, own_ref, left_ref, right_ref, opp_lo_ref, opp_hi_ref, qg_ref,
+    tab_ref, cnt_ref, y_ref, own_ref, left_ref, right_ref, opp_lo_ref, opp_hi_ref, qg_ref, after_ref,
     od_ref, sum_own_ref, sum_right_ref, sum_left_ref, sum_opp_ref,
     kv_s, acc, sc, xs,
 ):
@@ -179,13 +182,13 @@
             out[pl.ds(pl.multiple_of(t * 256, 256), 256), :] = acc[:, cols].T.astype(bf16)
 
 
-def attend(table, counts, y, kv_parts, qg):
+def attend(table, counts, y, kv_parts, qg, after):
     vmem = pl.BlockSpec(memory_space=pltpu.VMEM)
     smem = pl.BlockSpec(memory_space=pltpu.SMEM)
     row = jax.ShapeDtypeStruct((ROW, 128), bf16)
     return pl.pallas_call(
         attend_kernel,
-        in_specs=[smem] * 3 + [vmem] * 6,
+        in_specs=[smem] * 3 + [vmem] * 6 + [pl.BlockSpec(memory_space=pl.ANY)],
         out_specs=[vmem] * 5,
         out_shape=[row] * 5,
         scratch_shapes=[
@@ -196,10 +199,10 @@
         ],
         compiler_params=VMEM,
         cost_estimate=pl.CostEstimate(
-            flops=6 * QBLK * BLOCK * 1152 * 128 * 2, bytes_accessed=6 << 20, transcendentals=0
+            flops=26 * 10**9, bytes_accessed=6 << 20, transcendentals=0
         ),
         name="attend",
-    )(table, counts, y, *kv_parts, qg)
+    )(table, counts, y, *kv_parts, qg, after)
 
 
 def out_kernel(a_ref, b_ref, wo_ref, o_ref, total):
@@ -217,19 +220,22 @@
         o_ref[...] = total[...].astype(bf16)
 
 
-def project_out(od_a, od_b, w_out):
+SECOND = pl.BlockSpec((2, NODE_DEV, 128), lambda i: (i, 1, 0))
+
+
+def project_out(od_a, joint, w_out):
     d = w_out.shape[1]
     tile = pl.BlockSpec((2, NODE_DEV, 128), lambda i: (i, 0, 0))
     return pl.pallas_call(
         out_kernel,
         grid=(ZS // 2,),
-        in_specs=[tile, tile, pl.BlockSpec((256, d), lambda i: (i, 0))],
+        in_specs=[tile, SECOND, pl.BlockSpec((256, d), lambda i: (i, 0))],
         out_specs=whole((NODE_DEV, d)),
         out_shape=jax.ShapeDtypeStruct((NODE_DEV, d), bf16),
         scratch_shapes=[pltpu.VMEM((NODE_DEV, d), f32)],
         compiler_params=VMEM,
         name="project_out",
-    )(od_a, od_b, w_out)
+    )(od_a, joint, w_out)
 
 
 def nodes_kernel(oa_ref, ob_ref, ka_ref, kb_ref, wq_ref, wk_ref, wv_ref, o_ref, total):
@@ -255,21 +261,21 @@
         o_ref[...] = total[...].astype(bf16)
 
 
-def node_grads(od_a, od_b, kv_a, kv_b, w_qkv):
+def node_grads(od_a, joint, kv_b, w_qkv):
     d = w_qkv.shape[0]
     tile = pl.BlockSpec((2, NODE_DEV, 128), lambda i: (i, 0, 0))
     steps = ZS // 2
     return pl.pallas_call(
         nodes_kernel,
         grid=(steps,),
-        in_specs=[tile] * 4
+        in_specs=[tile, SECOND, tile, tile]
         + [pl.BlockSpec((d, 256), functools.partial(lambda i, third: (0, third * steps + i), third=k)) for k in range(3)],
         out_specs=whole((NODE_DEV, d)),
         out_shape=jax.ShapeDtypeStruct((NODE_DEV, d), bf16),
         scratch_shapes=[pltpu.VMEM((NODE_DEV, d), f32)],
         compiler_params=VMEM,
         name="node_grads",
-    )(od_a, od_b, kv_a, kv_b, w_qkv, w_qkv, w_qkv)
+    )(od_a, joint, joint, kv_b, w_qkv, w_qkv, w_qkv)
 
 
 def swap(values, axis):
@@ -278,6 +284,7 @@
 
 RIGHT = [(i, (i + 1) % YS) for i in range(YS)]
 LEFT = [(i, (i - 1) % YS) for i in range(YS)]
+OPPOSITE = [(i, (i + 2) % YS) for i in range(YS)]
 
 
 def gather_row(own):
@@ -288,13 +295,116 @@
     return own, left, right, opp_lo, opp_hi
 
 
-def sum_row(own, to_right, to_left, opp):
-    lo = lax.ppermute(opp[:HALF], "y", RIGHT)
-    hi = lax.ppermute(opp[HALF:], "y", LEFT)
-    add = lambda *v: sum(x.astype(f32) for x in v)
-    to_right = jnp.concatenate([add(to_right[:HALF], lo).astype(bf16), to_right[HALF:]], axis=0)
-    to_left = jnp.concatenate([to_left[:HALF], add(to_left[HALF:], hi).astype(bf16)], axis=0)
-    return add(own, lax.ppermute(to_right, "y", RIGHT), lax.ppermute(to_left, "y", LEFT)).astype(bf16)
+def sum_kernel(count, *refs):
+    parts = (r[...].astype(f32) for r in refs[:count])
+    refs[-1][...] = sum(parts).astype(bf16)
+
+
+def sum_parts(parts, after):
+    rows, cols = parts[0].shape
+    tile = pl.BlockSpec((rows // 2, cols), lambda i: (i, 0))
+    return pl.pallas_call(
+        functools.partial(sum_kernel, len(parts)),
+        grid=(2,),
+        in_specs=[tile] * len(parts) + [pl.BlockSpec(memory_space=pl.ANY)] * len(after),
+        out_specs=tile,
+        out_shape=jax.ShapeDtypeStruct((rows, cols), bf16),
+        compiler_params=VMEM,
+        name="sum_parts",
+    )(*parts, *after)
+
+
+def sum_join_kernel(a_ref, b_ref, c_ref, d_ref, od_ref, o_ref):
+    total = sum(r[...].astype(f32) for r in (a_ref, b_ref, c_ref, d_ref)).astype(bf16)
+    pieces = o_ref.shape[0]
+    for u in range(pieces):
+        rows = slice(u * NODE_DEV, (u + 1) * NODE_DEV)
+        o_ref[u, :NODE_DEV, :] = total[rows]
+        o_ref[u, NODE_DEV:, :] = od_ref[rows, :]
+
+
+def sum_join(parts, od):
+    tile = pl.BlockSpec((HALF, 128), lambda i: (i, 0))
+    return pl.pallas_call(
+        sum_join_kernel,
+        grid=(2,),
+        in_specs=[tile] * 5,
+        out_specs=pl.BlockSpec((ZS // 2, 2 * NODE_DEV, 128), lambda i: (i, 0, 0)),
+        out_shape=jax.ShapeDtypeStruct((ZS, 2 * NODE_DEV, 128), bf16),
+        compiler_params=VMEM,
+        name="sum_join",
+    )(*parts, od)
+
+
+def send_row(own, to_right, to_left, opp):
+    return [
+        own,
+        lax.ppermute(to_right, "y", RIGHT),
+        lax.ppermute(to_left, "y", LEFT),
+        lax.ppermute(opp, "y", OPPOSITE),
+    ]
+
+
+def hold_kernel(x_ref, after_ref, o_ref):
+    o_ref[...] = x_ref[...]
+
+
+def hold(values, after):
+    vmem = pl.BlockSpec(memory_space=pltpu.VMEM)
+    return pl.pallas_call(
+        hold_kernel,
+        in_specs=[vmem, pl.BlockSpec(memory_space=pl.ANY)],
+        out_specs=vmem,
+        out_shape=jax.ShapeDtypeStruct(values.shape, values.dtype),
+        compiler_params=VMEM,
+        name="hold",
+    )(values, after)
+
+
+def gate_kernel(*refs):
+    pass
+
+
+def gate(values, after):
+    anywhere = pl.BlockSpec(memory_space=pl.ANY)
+    return pl.pallas_call(
+        gate_kernel,
+        in_specs=[anywhere] * (len(values) + len(after)),
+        out_specs=[anywhere] * len(values),
+        out_shape=[jax.ShapeDtypeStruct(v.shape, v.dtype) for v in values],
+        input_output_aliases={i: i for i in range(len(values))},
+        compiler_params=VMEM,
+        name="gate",
+    )(*values, *after)
+
+
+def weight_kernel(oa_ref, ob_ref, ka_ref, kb_ref, f_ref, o_ref, grads):
+    @pl.when(pl.program_id(0) == 0)
+    def _():
+        @pl.loop(0, ZS)
+        def _(t):
+            rows = pl.ds(pl.multiple_of(t * NODE_DEV, NODE_DEV), NODE_DEV)
+            dq = pair_up(oa_ref[rows, :].astype(f32), ob_ref[rows, :].astype(f32))[0]
+            dk, dv = pair_up(ka_ref[t, :NODE_DEV, :].astype(f32), kb_ref[rows, :].astype(f32))
+            for k, part in enumerate((dq, dk, dv)):
+                grads[k * 128 : (k + 1) * 128, rows] = part.T.astype(bf16)
+
+    o_ref[...] = nn(grads[...], f_ref[...]).T.astype(bf16)
+
+
+def weight_share(od_a, od_b, joint, kv_b, feats_row):
+    d = feats_row.shape[1]
+    part = whole((ROW, 128))
+    return pl.pallas_call(
+        weight_kernel,
+        grid=(d // 256,),
+        in_specs=[part, part, whole(joint.shape), part, pl.BlockSpec((ROW, 256), lambda i: (0, i))],
+        out_specs=pl.BlockSpec((256, 384), lambda i: (i, 0)),
+        out_shape=jax.ShapeDtypeStruct((d, 384), bf16),
+        scratch_shapes=[pltpu.VMEM((384, ROW), bf16)],
+        compiler_params=VMEM,
+        name="weight_share",
+    )(od_a, od_b, joint, kv_b, feats_row)
 
 
 def on_device(node_feats, w_qkv, w_out, cotangent, block_neighbors, block_counts, global_blocks):
@@ -308,28 +418,37 @@
 
     kv = project_kv(feats, w_qkv)
     qg = project_qg(feats, cot, w_qkv, w_out)
-    feats_row = lax.all_gather(feats, "z", axis=0, tiled=True)
-    od, kv_sum = [], []
-    for p in (0, 1):
-        kv_row = swap(kv[p], "z").reshape(ROW, 128)
-        qg_row = swap(qg[p], "z").reshape(ROW, 128)
-        outs = attend(table, counts, y_arr, gather_row(kv_row), qg_row)
-        od.append(outs[0])
-        kv_sum.append(sum_row(*outs[1:]))
-    od_nodes = [swap(v.reshape(ZS, NODE_DEV, 128), "z") for v in od]
-    kv_nodes = [swap(v.reshape(ZS, NODE_DEV, 128), "z") for v in kv_sum]
-    attn_update = project_out(od_nodes[0], od_nodes[1], w_out)
-    grad_nodes = node_grads(od_nodes[0], od_nodes[1], kv_nodes[0], kv_nodes[1], w_qkv)
-
-    grads = jnp.concatenate([od[0][:, :HD], od[1][:, :HD], kv_sum[0], kv_sum[1]], axis=1)
-    share = lax.dot_general(feats_row, grads, (((0,), (0,)), ((), ())), preferred_element_type=f32)
-    rows = share.shape[0] // 32
-    share = swap(share.astype(bf16).reshape(32, rows, 6 * HD), ("x", "c", "y"))
-    share = jnp.sum(share.astype(f32), axis=0)
-    share = swap(share.reshape(ZS, rows // ZS, 6, HD), "z")
-    pick = lambda a, b: jnp.stack([share[:, :, a], share[:, :, b]], axis=2)
-    grad_weights = jnp.stack([pick(0, 1), pick(2, 4), pick(3, 5)], axis=0)
-    grad_weights = grad_weights.transpose(2, 0, 1, 3, 4).reshape(rows // ZS, 3 * H * HD)
+    kv_row = [gather_row(swap(v, "z").reshape(ROW, 128)) for v in kv]
+    qg_row = [swap(v, "z").reshape(ROW, 128) for v in qg]
+    feats_late = hold(feats, qg_row[0])
+    feats_row = lax.all_gather(feats_late, "z", axis=0, tiled=True)
+    od_a, *kv_a = attend(table, counts, y_arr, kv_row[0], qg_row[0], feats_late)
+    to_nodes = lambda v: swap(v.reshape(ZS, NODE_DEV, 128), "z")
+    (od_a_late,) = gate([od_a], [qg_row[1]])
+    od_nodes_a = to_nodes(od_a_late)
+    parts_a = send_row(*kv_a)
+    late = attend(table, counts, y_arr, kv_row[1], qg_row[1], od_a_late)
+    od_b, *kv_b = gate(late, parts_a[1:] + [od_nodes_a])
+    parts_b = send_row(*kv_b)
+    joint = sum_join(parts_a, od_b)
+    joint_nodes = swap(joint, "z")
+    sum_b = sum_parts(parts_b, (joint_nodes,))
+    kv_nodes_b = to_nodes(sum_b)
+    attn_update = project_out(od_nodes_a, joint_nodes, w_out)
+    grad_nodes = node_grads(od_nodes_a, joint_nodes, kv_nodes_b, w_qkv)
+
+    share = weight_share(od_a_late, od_b, joint, sum_b, feats_row)
+    d = share.shape[0]
+    share = share.reshape(4, 2, d // 8, 384)
+    c = lax.axis_index("c")
+    mine, theirs = (lax.dynamic_index_in_dim(share, k, 1, keepdims=False) for k in (c, 1 - c))
+    theirs = lax.ppermute(theirs, "c", [(0, 1), (1, 0)])
+    share = sum_parts([v.reshape(d // 2, 384) for v in (mine, theirs)], (kv_nodes_b,))
+    share = share.reshape(16, d // 32, 384)
+    share = jnp.sum(swap(share, ("x", "y")).astype(f32), axis=0)
+    share = swap(share.reshape(ZS, d // 256, 384), "z")
+    share = share.reshape(ZS, d // 256, 3, 128).transpose(1, 2, 0, 3)
+    grad_weights = share.reshape(d // 256, 3 * H * HD)
     return attn_update[None], grad_nodes[None], grad_weights
 
 

time: 297 us -> 256 us (0.86)
  Pallas kernels: 65.1 us -> 85.1 us
  other arithmetic: 16.5 us -> 0.13 us
  blocking collectives: 55.1 us -> 40.8 us
  local copies, waits for them, and re-layouts: 22.2 us -> 12.9 us
  starting transfers between devices: 59.1 us -> 52 us
  waiting for transfers between devices: 54.8 us -> 47.8 us
  matrix products: 5.65 us -> 0 us
    pallas_call x6 -> x13, Pallas kernels: 65.1 us -> 85.1 us  [the longest x2 47.3 us: attend(): pl.pallas_call(attend_kernel, in_specs=[smem] * 3 + [vmem] * 6 + [pl.Bloc...]
    ppermute x8 -> x7, waiting for transfers between devices: 0.02 us -> 16.7 us  [the longest x2 10.4 us: send_row(): lax.ppermute(to_right, 'y', RIGHT)]
    all_to_all x8 -> x7, waiting for transfers between devices: 43 us -> 27.3 us  [swap(): return lax.all_to_all(values, axis, split_axis=0, concat_axis=0, tiled=True)]
    all_to_all x2, blocking collectives: 55.1 us -> 40.8 us  [swap(): return lax.all_to_all(values, axis, split_axis=0, concat_axis=0, tiled=True)]
    ppermute x2, waiting for transfers between devices: 11 us -> 0.01 us  [gather_row(): left = lax.ppermute(own, 'y', RIGHT)]
    convert_element_type x6 -> x0, other arithmetic: 9.1 us -> none  [the longest x2 4.75 us: sum_row(): add(own, lax.ppermute(to_right, 'y', RIGHT), lax.ppermute(to_left, 'y', L...]
    dot_general x1 -> x0, matrix products: 5.65 us -> none  [on_device(): lax.dot_general(feats_row, grads, (((0,), (0,)), ((), ())), preferred_ele...]
    ppermute x8 -> x7, starting transfers between devices: 13.3 us -> 7.81 us  [the longest x2 3.67 us: send_row(): lax.ppermute(opp, 'y', OPPOSITE)]
  transfers between devices with their start and end apart: 25 -> 23, of which waited for: 7 -> 10; matrix products, arithmetic and copies ran while one was open for 12% -> 2% of each run, Pallas kernels for 22% -> 31%
where the time goes in v2:
time: 256 us; the launch traced here: 253 us
  Pallas kernels  85.1 us (33%)
  starting transfers between devices  52 us (20%)
  waiting for transfers between devices  47.8 us (19%)
  blocking collectives  40.8 us (16%)
  between operations  14.3 us (6%)
  local copies, waits for them, and re-layouts  12.9 us (5%)
    pallas_call x2, Pallas kernels, attend(): pl.pallas_call(attend_kernel, in_specs=[smem] * 3 + [vmem] * 6 + [pl.Bloc...  47.3 us
    all_to_all x2, blocking collectives, swap(): return lax.all_to_all(values, axis, split_axis=0, concat_axis=0, tiled=True)  40.8 us
    all_to_all x7, starting transfers between devices, swap(): return lax.all_to_all(values, axis, split_axis=0, concat_axis=0, tiled=True)  35.6 us
    all_to_all x7, waiting for transfers between devices, swap(): return lax.all_to_all(values, axis, split_axis=0, concat_axis=0, tiled=True)  27.3 us
    ppermute x2, waiting for transfers between devices, send_row(): lax.ppermute(to_right, 'y', RIGHT)  10.4 us
    pallas_call x1, Pallas kernels, weight_share(): pl.pallas_call(weight_kernel, grid=(d // 256,), in_specs=[part, part, who...  7.81 us
    unnamed x47, local copies, waits for them, and re-layouts  6.87 us
    pallas_call x1, Pallas kernels, node_grads(): pl.pallas_call(nodes_kernel, grid=(steps,), in_specs=[tile, SECOND, tile,...  6.27 us
  transfers between devices with their start and end apart: 23, of which 10 were waited for; matrix products, arithmetic and copies ran while one was open for 2% of the time, Pallas kernels for 31%

profile of v2, /device:TPU:8, one launch (start us, length us, event | category | flops | bytes accessed | tf_op | source)
XLA Modules:
  0.0 252.9 jit_solution(4858614288313118032)
XLA Ops:
  7.2 5.1 %project_kv.1 = (bf16[8,256,128]{2,1,0:T(8,128)(2,1)}, bf16[8,256,128]{2,1,0:T(8,128)(2,1)}) custom-call(bf16[256,1024]{1,0:T(8,128)(2,1)} %bitcast.34, bf16[1024,3072]{1,0:T(8,128)(2,1)} %wv_ref.3, bf16[1024,3072]{1,0:T(8,128)(2,1)} %wv_ref.3), custom_call_target="tpu_custom_call" | custom-call | tf_op jit(solution)/shard_map/project_kv/pallas_call | solution.py:79
  12.3 26.0 %all_to_all.45 = bf16[8,256,128]{2,1,0:T(8,128)(2,1)S(1)} all-to-all(bf16[8,256,128]{2,1,0:T(8,128)(2,1)} %get-tuple-element.22), channel_id=1, replica_groups=mesh['x'=4,'c'=2,'y'=4,'z'=8] {'z'}, dimensions={0} | all-to-all | bytes 1048576 | tf_op jit(solution)/shard_map/all_to_all | solution.py:282
  38.3 3.5 %all-to-all-start.4 = ((bf16[8,256,128]{2,1,0:T(8,128)(2,1)}), bf16[8,256,128]{2,1,0:T(8,128)(2,1)S(1)}, u32[]{:S(2)}, u32[]{:S(2)}) async-start(bf16[8,256,128]{2,1,0:T(8,128)(2,1)} %get-tuple-element.30), calls=%async_computation.4 | async-start | bytes 1048576 | tf_op jit(solution)/shard_map/all_to_all | solution.py:282
  41.8 5.3 %project_qg.1 = (bf16[8,256,128]{2,1,0:T(8,128)(2,1)}, bf16[8,256,128]{2,1,0:T(8,128)(2,1)}) custom-call(bf16[256,1024]{1,0:T(8,128)(2,1)} %bitcast.35, bf16[256,1024]{1,0:T(8,128)(2,1)} %bitcast.46, bf16[1024,3072]{1,0:T(8,128)(2,1)} %wv_ref.3, bf16[1024,1024]{1,0:T(8,128)(2,1)} %wo_ref.3), custom_call_target="tpu_custom_call" | custom-call | tf_op jit(solution)/shard_map/project_qg/pallas_call | solution.py:98
  47.1 10.6 %all-to-all-done.4 = bf16[8,256,128]{2,1,0:T(8,128)(2,1)S(1)} async-done(((bf16[8,256,128]{2,1,0:T(8,128)(2,1)}), bf16[8,256,128]{2,1,0:T(8,128)(2,1)S(1)}, u32[]{:S(2)}, u32[]{:S(2)}) %all-to-all-start.4) | async-done | bytes 524320 | tf_op jit(solution)/shard_map/all_to_all | solution.py:282
  57.7 3.5 %all-to-all-start.1 = ((bf16[8,256,128]{2,1,0:T(8,128)(2,1)}), bf16[8,256,128]{2,1,0:T(8,128)(2,1)S(1)}, u32[]{:S(2)}, u32[]{:S(2)}) async-start(bf16[8,256,128]{2,1,0:T(8,128)(2,1)} %get-tuple-element.23), calls=%async_computation.1 | async-start | bytes 1048576 | tf_op jit(solution)/shard_map/all_to_all | solution.py:282
  61.2 1.6 collective-permute-start
  63.3 1.7 collective-permute-start.8
  65.4 10.7 %all-to-all-done.1 = bf16[8,256,128]{2,1,0:T(8,128)(2,1)S(1)} async-done(((bf16[8,256,128]{2,1,0:T(8,128)(2,1)}), bf16[8,256,128]{2,1,0:T(8,128)(2,1)S(1)}, u32[]{:S(2)}, u32[]{:S(2)}) %all-to-all-start.1) | async-done | bytes 524320 | tf_op jit(solution)/shard_map/all_to_all | solution.py:282
  76.1 3.5 %all-to-all-start.2 = ((bf16[8,256,128]{2,1,0:T(8,128)(2,1)}), bf16[8,256,128]{2,1,0:T(8,128)(2,1)S(1)}, u32[]{:S(2)}, u32[]{:S(2)}) async-start(bf16[8,256,128]{2,1,0:T(8,128)(2,1)} %get-tuple-element.25), calls=%async_computation.2 | async-start | bytes 1048576 | tf_op jit(solution)/shard_map/all_to_all | solution.py:282
  79.7 1.9 hold.1.after_ref
  81.6 1.6 collective-permute-start.2
  83.3 1.0 slice.17
  86.5 1.5 collective-permute-start.10
  87.9 1.0 slice.18
  89.6 1.4 collective-permute-done.2.opp_lo_ref
  91.0 2.1 collective-permute-done.3.opp_hi_ref
  93.1 0.7 copy-done.20
  93.8 23.7 %attend.2 = (bf16[2048,128]{1,0:T(8,128)(2,1)}, bf16[2048,128]{1,0:T(8,128)(2,1)}, bf16[2048,128]{1,0:T(8,128)(2,1)}, bf16[2048,128]{1,0:T(8,128)(2,1)}, bf16[2048,128]{1,0:T(8,128)(2,1)}) custom-call(s32[192]{0:T(256)} %reshape.54.tab_ref, s32[16]{0:T(128)} %fusion.cnt_ref, s32[1]{0:T(128)} %bitcast.3.y_ref, bf16[2048,128]{1,0:T(8,128)(2,1)} %bitcast.53, ...), custom_call_target="tpu_custom_call" | custom-call | flops 25999998976 | bytes 6291456 | tf_op jit(solution)/shard_map/attend/pallas_call | solution.py:189
  117.5 0.8 copy-done.7
  118.3 6.7 %all-to-all-start.3 = ((bf16[8,256,128]{2,1,0:T(8,128)(2,1)}), bf16[8,256,128]{2,1,0:T(8,128)(2,1)S(1)}, u32[]{:S(2)}, u32[]{:S(2)}) async-start(bf16[8,256,128]{2,1,0:T(8,128)(2,1)} %bitcast.38), calls=%async_computation.3 | async-start | bytes 1048576 | tf_op jit(solution)/shard_map/all_to_all | solution.py:282
  125.0 1.3 collective-permute-start.4
  127.0 2.3 collective-permute-start.6
  129.3 0.7 copy-done.19
  130.0 23.6 %attend.3 = (bf16[2048,128]{1,0:T(8,128)(2,1)}, bf16[2048,128]{1,0:T(8,128)(2,1)}, bf16[2048,128]{1,0:T(8,128)(2,1)}, bf16[2048,128]{1,0:T(8,128)(2,1)}, bf16[2048,128]{1,0:T(8,128)(2,1)}) custom-call(s32[192]{0:T(256)} %reshape.54.tab_ref, s32[16]{0:T(128)} %fusion.cnt_ref, s32[1]{0:T(128)} %bitcast.3.y_ref, bf16[2048,128]{1,0:T(8,128)(2,1)} %bitcast.50, ...), custom_call_target="tpu_custom_call" | custom-call | flops 25999998976 | bytes 6291456 | tf_op jit(solution)/shard_map/attend/pallas_call | solution.py:189
  153.8 0.7 copy-done.4
  155.0 2.7 %sum_join.1.ka_ref = bf16[8,512,128]{2,1,0:T(8,128)(2,1)} custom-call(bf16[2048,128]{1,0:T(8,128)(2,1)} %get-tuple-element.26.a_ref, bf16[2048,128]{1,0:T(8,128)(2,1)} %copy-done.4, bf16[2048,128]{1,0:T(8,128)(2,1)} %copy-done.5, bf16[2048,128]{1,0:T(8,128)(2,1)} %copy-done.6, bf16[2048,128]{1,0:T(8,128)(2,1)} %get-tuple-element.36.od_ref.ob_ref), custom_call_target="tpu_custom_call" | custom-call | tf_op jit(solution)/shard_map/sum_join/pallas_call | solution.py:328
  157.7 7.2 %all-to-all-start.5 = ((bf16[8,512,128]{2,1,0:T(8,128)(2,1)}), bf16[8,512,128]{2,1,0:T(8,128)(2,1)S(1)}, u32[]{:S(2)}, u32[]{:S(2)}) async-start(bf16[8,512,128]{2,1,0:T(8,128)(2,1)} %sum_join.1.ka_ref), calls=%async_computation.5 | async-start | bytes 2097152 | tf_op jit(solution)/shard_map/all_to_all | solution.py:282
  164.9 1.1 collective-permute-start.11
  166.1 1.0 collective-permute-start.12
  167.1 1.4 collective-permute-start.13
  168.4 10.4 %collective-permute-done.11.refs_1_ = bf16[2048,128]{1,0:T(8,128)(2,1)S(1)} collective-permute-done((bf16[2048,128]{1,0:T(8,128)(2,1)S(1)}, bf16[2048,128]{1,0:T(8,128)(2,1)S(1)}, u32[]{:S(2)}, u32[]{:S(2)}) %collective-permute-start.11) | collective-permute-done | bytes 524320 | tf_op jit(solution)/shard_map/ppermute | solution.py:342
  178.8 1.4 collective-permute-done.12.refs_2_
  180.2 0.8 copy-done.13
  181.0 4.9 %collective-permute-done.13.refs_3_ = bf16[2048,128]{1,0:T(8,128)(2,1)} collective-permute-done((bf16[2048,128]{1,0:T(8,128)(2,1)S(1)}, bf16[2048,128]{1,0:T(8,128)(2,1)}, u32[]{:S(2)}, u32[]{:S(2)}) %collective-permute-start.13) | collective-permute-done | bytes 524320 | tf_op jit(solution)/shard_map/ppermute | solution.py:344
  185.9 2.5 all-to-all-done.5.b_ref.refs_4_.ob_ref.ka_ref
  188.4 1.0 copy-done.1
  189.5 2.3 sum_parts.2.kb_ref
  191.8 4.4 %all-to-all-start.6 = ((bf16[8,256,128]{2,1,0:T(8,128)(2,1)}), bf16[8,256,128]{2,1,0:T(8,128)(2,1)S(1)}, u32[]{:S(2)}, u32[]{:S(2)}) async-start(bf16[8,256,128]{2,1,0:T(8,128)(2,1)} %bitcast.37), calls=%async_computation.6 | async-start | bytes 1048576 | tf_op jit(solution)/shard_map/all_to_all | solution.py:282
  196.2 7.8 %weight_share.1 = bf16[1024,384]{1,0:T(8,128)(2,1)} custom-call(bf16[2048,128]{1,0:T(8,128)(2,1)} %gate.2.after_ref.oa_ref, bf16[2048,128]{1,0:T(8,128)(2,1)} %get-tuple-element.36.od_ref.ob_ref, bf16[8,512,128]{2,1,0:T(8,128)(2,1)} %sum_join.1.ka_ref, bf16[2048,128]{1,0:T(8,128)(2,1)} %sum_parts.2.kb_ref, bf16[2048,1024]{1,0:T(8,128)(2,1)} %all-gather.2.cloned.1.call-done.f_ref), custom_call_target="tpu_custom_call" | custom-call | tf_op jit(solution)/shard_map/weight_share/pallas_call | solution.py:398
  204.0 1.9 dynamic-slice_bitcast_fusion
  205.9 3.5 %all-to-all-done.6.kb_ref.refs_2_ = bf16[8,256,128]{2,1,0:T(8,128)(2,1)S(1)} async-done(((bf16[8,256,128]{2,1,0:T(8,128)(2,1)}), bf16[8,256,128]{2,1,0:T(8,128)(2,1)S(1)}, u32[]{:S(2)}, u32[]{:S(2)}) %all-to-all-start.6) | async-done | bytes 524320 | tf_op jit(solution)/shard_map/all_to_all | solution.py:282
  209.5 0.8 copy-done.3
  210.4 1.9 sum_parts.3
  212.3 14.8 %all_to_all.46 = bf16[16,32,384]{2,1,0:T(8,128)(2,1)S(1)} all-to-all(bf16[16,32,384]{2,1,0:T(8,128)(2,1)} %bitcast.44), channel_id=1, replica_groups=mesh['x'=4,'c'=2,'y'=4,'z'=8] {'x','y'}, dimensions={0} | all-to-all | bytes 786432 | tf_op jit(solution)/shard_map/all_to_all | solution.py:282
  227.8 6.9 %all-to-all-start.8 = ((f32[8,4,384]{2,1,0:T(4,128)}), f32[8,4,384]{2,1,0:T(4,128)S(1)}, u32[]{:S(2)}, u32[]{:S(2)}) async-start(f32[8,4,384]{2,1,0:T(4,128)} %reshape.66), calls=%async_computation.8 | async-start | bytes 98304 | tf_op jit(solution)/shard_map/all_to_all | solution.py:282
  234.7 4.4 %project_out.1 = bf16[256,1024]{1,0:T(8,128)(2,1)} custom-call(bf16[8,256,128]{2,1,0:T(8,128)(2,1)} %copy-done.2, bf16[8,512,128]{2,1,0:T(8,128)(2,1)} %copy-done.1, bf16[1024,1024]{1,0:T(8,128)(2,1)} %wo_ref.3), custom_call_target="tpu_custom_call" | custom-call | tf_op jit(solution)/shard_map/project_out/pallas_call | solution.py:229
  239.1 6.3 %node_grads.1 = bf16[256,1024]{1,0:T(8,128)(2,1)} custom-call(bf16[8,256,128]{2,1,0:T(8,128)(2,1)} %copy-done.2, bf16[8,512,128]{2,1,0:T(8,128)(2,1)} %copy-done.1, bf16[8,512,128]{2,1,0:T(8,128)(2,1)} %copy-done.1, bf16[8,256,128]{2,1,0:T(8,128)(2,1)} %copy-done.3, bf16[1024,3072]{1,0:T(8,128)(2,1)} %wv_ref.3, bf16[1024,3072]{1,0:T(8,128)(2,1)} %wv_ref.3, ...), custom_call_target="tpu_custom_call" | custom-call | tf_op jit(solution)/shard_map/node_grads/pallas_call | solution.py:268
  (77 shorter events, 6.7 us)
Async XLA Ops:
  7.2 58.2 %copy-start = (s32[1,64,8]{1,2,0:T(8,128)S(1)}, s32[1,64,8]{1,2,0:T(8,128)}, u32[]{:S(2)}) copy-start(s32[1,64,8]{1,2,0:T(8,128)} %param.11) | copy-start | bytes 6148
  38.3 24.6 %copy-start.15 = (bf16[8,256,128]{2,1,0:T(8,128)(2,1)}, bf16[8,256,128]{2,1,0:T(8,128)(2,1)S(1)}, u32[]{:S(2)}) copy-start(bf16[8,256,128]{2,1,0:T(8,128)(2,1)S(1)} %all_to_all.45) | copy-start | bytes 1572868
  38.3 19.4 %all-to-all-start.4 = ((bf16[8,256,128]{2,1,0:T(8,128)(2,1)}), bf16[8,256,128]{2,1,0:T(8,128)(2,1)S(1)}, u32[]{:S(2)}, u32[]{:S(2)}) async-start(bf16[8,256,128]{2,1,0:T(8,128)(2,1)} %get-tuple-element.30), calls=%async_computation.4 | async-start | bytes 1048576 | tf_op jit(solution)/shard_map/all_to_all | solution.py:282
  41.8 23.5 %copy-start.21 = (s32[1,4]{1,0:T(1,128)S(1)}, s32[1,4]{1,0:T(1,128)}, u32[]{:S(2)}) copy-start(s32[1,4]{1,0:T(1,128)} %param.13) | copy-start | bytes 52
  47.1 38.5 %copy-start.22 = (s32[1,64]{1,0:T(1,128)S(1)}, s32[1,64]{1,0:T(1,128)}, u32[]{:S(2)}) copy-start(s32[1,64]{1,0:T(1,128)} %param.12) | copy-start | bytes 772
  57.7 59.8 %copy-start.14 = (bf16[8,256,128]{2,1,0:T(8,128)(2,1)}, bf16[8,256,128]{2,1,0:T(8,128)(2,1)S(1)}, u32[]{:S(2)}) copy-start(bf16[8,256,128]{2,1,0:T(8,128)(2,1)S(1)} %all-to-all-done.4) | copy-start | bytes 1572868
  57.7 18.4 %all-to-all-start.1 = ((bf16[8,256,128]{2,1,0:T(8,128)(2,1)}), bf16[8,256,128]{2,1,0:T(8,128)(2,1)S(1)}, u32[]{:S(2)}, u32[]{:S(2)}) async-start(bf16[8,256,128]{2,1,0:T(8,128)(2,1)} %get-tuple-element.23), calls=%async_computation.1 | async-start | bytes 1048576 | tf_op jit(solution)/shard_map/all_to_all | solution.py:282
  61.2 20.4 %collective-permute-start = (bf16[2048,128]{1,0:T(8,128)(2,1)S(1)}, bf16[2048,128]{1,0:T(8,128)(2,1)S(1)}, u32[]{:S(2)}, u32[]{:S(2)}) collective-permute-start(bf16[2048,128]{1,0:T(8,128)(2,1)S(1)} %bitcast.51), channel_id=1, source_target_pairs={{0,8},{8,16},{16,24},{24,0},{1,9},{9,17},{17,25},{25,1},{2,10},{10... | collective-permute-start | bytes 1572872 | tf_op jit(solution)/shard_map/ppermute | solution.py:291
  62.8 20.4 %collective-permute-start.1 = (bf16[2048,128]{1,0:T(8,128)(2,1)S(1)}, bf16[2048,128]{1,0:T(8,128)(2,1)}, u32[]{:S(2)}, u32[]{:S(2)}) collective-permute-start(bf16[2048,128]{1,0:T(8,128)(2,1)S(1)} %bitcast.52), channel_id=1, source_target_pairs={{0,24},{8,0},{16,8},{24,16},{1,25},{9,1},{17,9},{25,17},{2,26},{10... | collective-permute-start | bytes 1572872 | tf_op jit(solution)/shard_map/ppermute | solution.py:292
  63.3 23.1 %collective-permute-start.8 = (bf16[2048,128]{1,0:T(8,128)(2,1)S(1)}, bf16[2048,128]{1,0:T(8,128)(2,1)S(1)}, u32[]{:S(2)}, u32[]{:S(2)}) collective-permute-start(bf16[2048,128]{1,0:T(8,128)(2,1)S(1)} %bitcast.48), channel_id=1, source_target_pairs={{0,24},{8,0},{16,8},{24,16},{1,25},{9,1},{17,9},{25,17},{2,26},{10... | collective-permute-start | bytes 1572872 | tf_op jit(solution)/shard_map/ppermute | solution.py:292
  64.9 23.0 %collective-permute-start.7 = (bf16[2048,128]{1,0:T(8,128)(2,1)S(1)}, bf16[2048,128]{1,0:T(8,128)(2,1)}, u32[]{:S(2)}, u32[]{:S(2)}) collective-permute-start(bf16[2048,128]{1,0:T(8,128)(2,1)S(1)} %bitcast.49), channel_id=1, source_target_pairs={{0,8},{8,16},{16,24},{24,0},{1,9},{9,17},{17,25},{25,1},{2,10},{10... | collective-permute-start | bytes 1572872 | tf_op jit(solution)/shard_map/ppermute | solution.py:291
  76.1 3.6 %copy-start.8 = (bf16[8,256,128]{2,1,0:T(8,128)(2,1)}, bf16[8,256,128]{2,1,0:T(8,128)(2,1)S(1)}, u32[]{:S(2)}) copy-start(bf16[8,256,128]{2,1,0:T(8,128)(2,1)S(1)} %all-to-all-done.1) | copy-start | bytes 1572868
  76.1 41.4 %all-to-all-start.2 = ((bf16[8,256,128]{2,1,0:T(8,128)(2,1)}), bf16[8,256,128]{2,1,0:T(8,128)(2,1)S(1)}, u32[]{:S(2)}, u32[]{:S(2)}) async-start(bf16[8,256,128]{2,1,0:T(8,128)(2,1)} %get-tuple-element.25), calls=%async_computation.2 | async-start | bytes 1048576 | tf_op jit(solution)/shard_map/all_to_all | solution.py:282
  79.6 116.5 %all-gather.2.cloned.1.call-start = ((), (), s32[]{:S(2)}) async-start(), calls=%async_computation.9 | async-start | bytes 4718592 | tf_op jit(solution)/shard_map/all_gather | solution.py:424
  81.6 4.6 %copy-start.18 = (bf16[2048,128]{1,0:T(8,128)(2,1)}, bf16[2048,128]{1,0:T(8,128)(2,1)S(1)}, u32[]{:S(2)}) copy-start(bf16[2048,128]{1,0:T(8,128)(2,1)S(1)} %collective-permute-done.left_ref) | copy-start | bytes 1572868
  81.6 9.4 %collective-permute-start.2 = (bf16[1024,128]{1,0:T(8,128)(2,1)S(1)}, bf16[1024,128]{1,0:T(8,128)(2,1)}, u32[]{:S(2)}, u32[]{:S(2)}) collective-permute-start(bf16[1024,128]{1,0:T(8,128)(2,1)S(1)} %slice.16), channel_id=1, source_target_pairs={{0,8},{8,16},{16,24},{24,0},{1,9},{9,17},{17,25},{25,1},{2,10},{10... | collective-permute-start | bytes 786440 | tf_op jit(solution)/shard_map/ppermute | solution.py:293
  84.2 8.9 %collective-permute-start.3 = (bf16[1024,128]{1,0:T(8,128)(2,1)S(1)}, bf16[1024,128]{1,0:T(8,128)(2,1)S(1)}, u32[]{:S(2)}, u32[]{:S(2)}) collective-permute-start(bf16[1024,128]{1,0:T(8,128)(2,1)S(1)} %slice.17), channel_id=1, source_target_pairs={{0,24},{8,0},{16,8},{24,16},{1,25},{9,1},{17,9},{25,17},{2,26},{10... | collective-permute-start | bytes 786440 | tf_op jit(solution)/shard_map/ppermute | solution.py:294
  86.4 31.1 %copy-start.17 = (bf16[2048,128]{1,0:T(8,128)(2,1)}, bf16[2048,128]{1,0:T(8,128)(2,1)S(1)}, u32[]{:S(2)}) copy-start(bf16[2048,128]{1,0:T(8,128)(2,1)S(1)} %collective-permute-done.8.right_ref) | copy-start | bytes 1572868
  86.5 42.9 %collective-permute-start.10 = (bf16[1024,128]{1,0:T(8,128)(2,1)S(1)}, bf16[1024,128]{1,0:T(8,128)(2,1)S(1)}, u32[]{:S(2)}, u32[]{:S(2)}) collective-permute-start(bf16[1024,128]{1,0:T(8,128)(2,1)S(1)} %slice.19), channel_id=1, source_target_pairs={{0,24},{8,0},{16,8},{24,16},{1,25},{9,1},{17,9},{25,17},{2,26},{10... | collective-permute-start | bytes 786440 | tf_op jit(solution)/shard_map/ppermute | solution.py:294
  88.9 40.4 %collective-permute-start.9 = (bf16[1024,128]{1,0:T(8,128)(2,1)S(1)}, bf16[1024,128]{1,0:T(8,128)(2,1)}, u32[]{:S(2)}, u32[]{:S(2)}) collective-permute-start(bf16[1024,128]{1,0:T(8,128)(2,1)S(1)} %slice.18), channel_id=1, source_target_pairs={{0,8},{8,16},{16,24},{24,0},{1,9},{9,17},{17,25},{25,1},{2,10},{10... | collective-permute-start | bytes 786440 | tf_op jit(solution)/shard_map/ppermute | solution.py:293
  93.1 0.7 copy-start.20
  117.5 0.8 copy-start.7
  118.3 35.4 %all-to-all-start.3 = ((bf16[8,256,128]{2,1,0:T(8,128)(2,1)}), bf16[8,256,128]{2,1,0:T(8,128)(2,1)S(1)}, u32[]{:S(2)}, u32[]{:S(2)}) async-start(bf16[8,256,128]{2,1,0:T(8,128)(2,1)} %bitcast.38), calls=%async_computation.3 | async-start | bytes 1048576 | tf_op jit(solution)/shard_map/all_to_all | solution.py:282
  125.0 28.7 %collective-permute-start.4 = (bf16[2048,128]{1,0:T(8,128)(2,1)}, bf16[2048,128]{1,0:T(8,128)(2,1)S(1)}, u32[]{:S(2)}, u32[]{:S(2)}) collective-permute-start(bf16[2048,128]{1,0:T(8,128)(2,1)} %get-tuple-element.27), channel_id=1, source_target_pairs={{0,8},{8,16},{16,24},{24,0},{1,9},{9,17},{17,25},{25,1},{2,10},{10... | collective-permute-start | bytes 1572872 | tf_op jit(solution)/shard_map/ppermute | solution.py:342
  126.3 27.4 %collective-permute-start.5 = (bf16[2048,128]{1,0:T(8,128)(2,1)}, bf16[2048,128]{1,0:T(8,128)(2,1)S(1)}, u32[]{:S(2)}, u32[]{:S(2)}) collective-permute-start(bf16[2048,128]{1,0:T(8,128)(2,1)} %get-tuple-element.28), channel_id=1, source_target_pairs={{0,24},{8,0},{16,8},{24,16},{1,25},{9,1},{17,9},{25,17},{2,26},{10... | collective-permute-start | bytes 1572872 | tf_op jit(solution)/shard_map/ppermute | solution.py:343
  127.0 26.7 %collective-permute-start.6 = (bf16[2048,128]{1,0:T(8,128)(2,1)}, bf16[2048,128]{1,0:T(8,128)(2,1)S(1)}, u32[]{:S(2)}, u32[]{:S(2)}) collective-permute-start(bf16[2048,128]{1,0:T(8,128)(2,1)} %get-tuple-element.29), channel_id=1, source_target_pairs={{0,16},{8,24},{16,0},{24,8},{1,17},{9,25},{17,1},{25,9},{2,18},{10... | collective-permute-start | bytes 1572872 | tf_op jit(solution)/shard_map/ppermute | solution.py:344
  129.3 0.7 copy-start.19
  153.7 0.8 copy-start.4
  153.7 0.9 copy-start.5
  153.7 1.2 copy-start.6
  153.8 1.3 copy-start.2
  155.0 9.9 %copy-start.9 = (bf16[2048,128]{1,0:T(8,128)(2,1)S(1)}, bf16[2048,128]{1,0:T(8,128)(2,1)}, u32[]{:S(2)}) copy-start(bf16[2048,128]{1,0:T(8,128)(2,1)} %get-tuple-element.38) | copy-start | bytes 1572868
  155.0 11.1 %copy-start.10 = (bf16[2048,128]{1,0:T(8,128)(2,1)S(1)}, bf16[2048,128]{1,0:T(8,128)(2,1)}, u32[]{:S(2)}) copy-start(bf16[2048,128]{1,0:T(8,128)(2,1)} %get-tuple-element.39) | copy-start | bytes 1572868
  155.0 12.0 %copy-start.11 = (bf16[2048,128]{1,0:T(8,128)(2,1)S(1)}, bf16[2048,128]{1,0:T(8,128)(2,1)}, u32[]{:S(2)}) copy-start(bf16[2048,128]{1,0:T(8,128)(2,1)} %get-tuple-element.40) | copy-start | bytes 1572868
  157.7 30.7 %all-to-all-start.5 = ((bf16[8,512,128]{2,1,0:T(8,128)(2,1)}), bf16[8,512,128]{2,1,0:T(8,128)(2,1)S(1)}, u32[]{:S(2)}, u32[]{:S(2)}) async-start(bf16[8,512,128]{2,1,0:T(8,128)(2,1)} %sum_join.1.ka_ref), calls=%async_computation.5 | async-start | bytes 2097152 | tf_op jit(solution)/shard_map/all_to_all | solution.py:282
  164.9 13.8 %collective-permute-start.11 = (bf16[2048,128]{1,0:T(8,128)(2,1)S(1)}, bf16[2048,128]{1,0:T(8,128)(2,1)S(1)}, u32[]{:S(2)}, u32[]{:S(2)}) collective-permute-start(bf16[2048,128]{1,0:T(8,128)(2,1)S(1)} %copy-done.9), channel_id=1, source_target_pairs={{0,8},{8,16},{16,24},{24,0},{1,9},{9,17},{17,25},{25,1},{2,10},{10... | collective-permute-start | bytes 1572872 | tf_op jit(solution)/shard_map/ppermute | solution.py:342
  166.1 14.1 %collective-permute-start.12 = (bf16[2048,128]{1,0:T(8,128)(2,1)S(1)}, bf16[2048,128]{1,0:T(8,128)(2,1)S(1)}, u32[]{:S(2)}, u32[]{:S(2)}) collective-permute-start(bf16[2048,128]{1,0:T(8,128)(2,1)S(1)} %copy-done.10), channel_id=1, source_target_pairs={{0,24},{8,0},{16,8},{24,16},{1,25},{9,1},{17,9},{25,17},{2,26},{10... | collective-permute-start | bytes 1572872 | tf_op jit(solution)/shard_map/ppermute | solution.py:343
  167.1 18.9 %collective-permute-start.13 = (bf16[2048,128]{1,0:T(8,128)(2,1)S(1)}, bf16[2048,128]{1,0:T(8,128)(2,1)}, u32[]{:S(2)}, u32[]{:S(2)}) collective-permute-start(bf16[2048,128]{1,0:T(8,128)(2,1)S(1)} %copy-done.11), channel_id=1, source_target_pairs={{0,16},{8,24},{16,0},{24,8},{1,17},{9,25},{17,1},{25,9},{2,18},{10... | collective-permute-start | bytes 1572872 | tf_op jit(solution)/shard_map/ppermute | solution.py:344
  178.8 9.6 %copy-start.12 = (bf16[2048,128]{1,0:T(8,128)(2,1)}, bf16[2048,128]{1,0:T(8,128)(2,1)S(1)}, u32[]{:S(2)}) copy-start(bf16[2048,128]{1,0:T(8,128)(2,1)S(1)} %collective-permute-done.11.refs_1_) | copy-start | bytes 1572868
  180.2 0.8 copy-start.13
  188.4 1.0 copy-start.1
  191.8 17.6 %all-to-all-start.6 = ((bf16[8,256,128]{2,1,0:T(8,128)(2,1)}), bf16[8,256,128]{2,1,0:T(8,128)(2,1)S(1)}, u32[]{:S(2)}, u32[]{:S(2)}) async-start(bf16[8,256,128]{2,1,0:T(8,128)(2,1)} %bitcast.37), calls=%async_computation.6 | async-start | bytes 1048576 | tf_op jit(solution)/shard_map/all_to_all | solution.py:282
  205.9 3.5 %collective-permute-start.14 = (bf16[4,128,384]{2,1,0:T(8,128)(2,1)S(1)}, bf16[4,128,384]{2,1,0:T(8,128)(2,1)S(1)}, u32[]{:S(2)}, u32[]{:S(2)}) collective-permute-start(bf16[4,128,384]{2,1,0:T(8,128)(2,1)S(1)} %get-tuple-element.41), channel_id=1, source_target_pairs={{0,32},{32,0},{1,33},{33,1},{2,34},{34,2},{3,35},{35,3},{4,36},{36... | collective-permute-start | bytes 1179656 | tf_op jit(solution)/shard_map/ppermute | solution.py:445
  209.5 0.8 copy-start.3
  209.5 0.9 copy-start.16
  227.8 17.5 %all-to-all-start.8 = ((f32[8,4,384]{2,1,0:T(4,128)}), f32[8,4,384]{2,1,0:T(4,128)S(1)}, u32[]{:S(2)}, u32[]{:S(2)}) async-start(f32[8,4,384]{2,1,0:T(4,128)} %reshape.66), calls=%async_computation.8 | async-start | bytes 98304 | tf_op jit(solution)/shard_map/all_to_all | solution.py:282
Sparse Core Ops, SparseCore 0:
  82.3 67.6 all-gather.1

commit v3 on v2

--- a/solution.py
+++ b/solution.py
@@ -60,8 +60,29 @@
         b_ref[u] = b.astype(bf16)
 
 
-def kv_kernel(f_ref, wk_ref, wv_ref, a_ref, b_ref):
+def kv_kernel(f_ref, wk_ref, wv_ref, o_ref):
+    a_ref, b_ref = o_ref.at[:, :NODE_DEV], o_ref.at[:, NODE_DEV:]
     put_pairs(nn(f_ref[...], wk_ref[...]), nn(f_ref[...], wv_ref[...]), a_ref, b_ref)
+
+
+def split_kernel(x_ref, a_ref, b_ref):
+    for u in range(x_ref.shape[0]):
+        rows = slice(u * NODE_DEV, (u + 1) * NODE_DEV)
+        a_ref[rows, :] = x_ref[u, :NODE_DEV, :]
+        b_ref[rows, :] = x_ref[u, NODE_DEV:, :]
+
+
+def split_heads(both):
+    tile = pl.BlockSpec((HALF, 128), lambda i: (i, 0))
+    return pl.pallas_call(
+        split_kernel,
+        grid=(2,),
+        in_specs=[pl.BlockSpec((ZS // 2, 2 * NODE_DEV, 128), lambda i: (i, 0, 0))],
+        out_specs=[tile, tile],
+        out_shape=[jax.ShapeDtypeStruct((ROW, 128), bf16)] * 2,
+        compiler_params=VMEM,
+        name="split_heads",
+    )(both)
 
 
 def qg_kernel(f_ref, c_ref, wq_ref, wo_ref, a_ref, b_ref):
@@ -74,8 +95,6 @@
 
 def project_kv(feats, w_qkv):
     d = feats.shape[1]
-    out = jax.ShapeDtypeStruct((ZS, NODE_DEV, 128), bf16)
-    tile = pl.BlockSpec((2, NODE_DEV, 128), lambda i: (i, 0, 0))
     return pl.pallas_call(
         kv_kernel,
         grid=(ZS // 2,),
@@ -84,8 +103,8 @@
             pl.BlockSpec((d, 256), lambda i: (0, ZS // 2 + i)),
             pl.BlockSpec((d, 256), lambda i: (0, ZS + i)),
         ],
-        out_specs=[tile, tile],
-        out_shape=[out, out],
+        out_specs=pl.BlockSpec((2, 2 * NODE_DEV, 128), lambda i: (i, 0, 0)),
+        out_shape=jax.ShapeDtypeStruct((ZS, 2 * NODE_DEV, 128), bf16),
         compiler_params=VMEM,
         name="project_kv",
     )(feats, w_qkv, w_qkv)
@@ -112,7 +131,7 @@
 
 
 def attend_kernel(
-    tab_ref, cnt_ref, y_ref, own_ref, left_ref, right_ref, opp_lo_ref, opp_hi_ref, qg_ref, after_ref,
+    tab_ref, cnt_ref, y_ref, own_ref, left_ref, right_ref, opp_ref, qg_ref, after_ref,
     od_ref, sum_own_ref, sum_right_ref, sum_left_ref, sum_opp_ref,
     kv_s, acc, sc, xs,
 ):
@@ -122,8 +141,7 @@
     kv_s[pl.ds(pl.multiple_of(at(0), ROW), ROW), :] = own_ref[...]
     kv_s[pl.ds(pl.multiple_of(at(YS - 1), ROW), ROW), :] = left_ref[...]
     kv_s[pl.ds(pl.multiple_of(at(1), ROW), ROW), :] = right_ref[...]
-    kv_s[pl.ds(pl.multiple_of(at(2), ROW), HALF), :] = opp_lo_ref[...]
-    kv_s[pl.ds(pl.multiple_of(at(2) + HALF, HALF), HALF), :] = opp_hi_ref[...]
+    kv_s[pl.ds(pl.multiple_of(at(2), ROW), ROW), :] = opp_ref[...]
 
     @pl.loop(0, NODES // 512)
     def _(t):
@@ -188,7 +206,7 @@
     row = jax.ShapeDtypeStruct((ROW, 128), bf16)
     return pl.pallas_call(
         attend_kernel,
-        in_specs=[smem] * 3 + [vmem] * 6 + [pl.BlockSpec(memory_space=pl.ANY)],
+        in_specs=[smem] * 3 + [vmem] * 5 + [pl.BlockSpec(memory_space=pl.ANY)],
         out_specs=[vmem] * 5,
         out_shape=[row] * 5,
         scratch_shapes=[
@@ -278,6 +296,25 @@
     )(od_a, joint, joint, kv_b, w_qkv, w_qkv, w_qkv)
 
 
+def spread_kernel(x_ref, o_ref):
+    for z in range(ZS):
+        for third in range(3):
+            cols = third * H * HD + z * 128
+            o_ref[:, cols : cols + 128] = x_ref[z, :, third * 128 : (third + 1) * 128]
+
+
+def spread(share):
+    vmem = pl.BlockSpec(memory_space=pltpu.VMEM)
+    return pl.pallas_call(
+        spread_kernel,
+        in_specs=[vmem],
+        out_specs=vmem,
+        out_shape=jax.ShapeDtypeStruct((share.shape[1], 3 * H * HD), f32),
+        compiler_params=VMEM,
+        name="spread",
+    )(share)
+
+
 def swap(values, axis):
     return lax.all_to_all(values, axis, split_axis=0, concat_axis=0, tiled=True)
 
@@ -288,11 +325,7 @@
 
 
 def gather_row(own):
-    left = lax.ppermute(own, "y", RIGHT)
-    right = lax.ppermute(own, "y", LEFT)
-    opp_lo = lax.ppermute(left[:HALF], "y", RIGHT)
-    opp_hi = lax.ppermute(right[HALF:], "y", LEFT)
-    return own, left, right, opp_lo, opp_hi
+    return own, lax.ppermute(own, "y", RIGHT), lax.ppermute(own, "y", LEFT), lax.ppermute(own, "y", OPPOSITE)
 
 
 def sum_kernel(count, *refs):
@@ -418,7 +451,7 @@
 
     kv = project_kv(feats, w_qkv)
     qg = project_qg(feats, cot, w_qkv, w_out)
-    kv_row = [gather_row(swap(v, "z").reshape(ROW, 128)) for v in kv]
+    kv_row = [gather_row(v) for v in split_heads(swap(kv, "z"))]
     qg_row = [swap(v, "z").reshape(ROW, 128) for v in qg]
     feats_late = hold(feats, qg_row[0])
     feats_row = lax.all_gather(feats_late, "z", axis=0, tiled=True)
@@ -446,9 +479,8 @@
     share = sum_parts([v.reshape(d // 2, 384) for v in (mine, theirs)], (kv_nodes_b,))
     share = share.reshape(16, d // 32, 384)
     share = jnp.sum(swap(share, ("x", "y")).astype(f32), axis=0)
-    share = swap(share.reshape(ZS, d // 256, 384), "z")
-    share = share.reshape(ZS, d // 256, 3, 128).transpose(1, 2, 0, 3)
-    grad_weights = share.reshape(d // 256, 3 * H * HD)
+    share = gate([share.reshape(ZS, d // 256, 384)], [attn_update, grad_nodes])[0]
+    grad_weights = spread(swap(share, "z"))
     return attn_update[None], grad_nodes[None], grad_weights
 
 

time: 256 us -> 250 us (0.977)
  blocking collectives: 40.8 us -> 12.1 us
  waiting for transfers between devices: 47.8 us -> 63.2 us
  starting transfers between devices: 52 us -> 59.8 us
  Pallas kernels: 85.1 us -> 88.9 us
  local copies, waits for them, and re-layouts: 12.9 us -> 9.97 us
    all_to_all x2 -> x1, blocking collectives: 40.8 us -> 12.1 us  [swap(): return lax.all_to_all(values, axis, split_axis=0, concat_axis=0, tiled=True)]
    all_to_all x7, waiting for transfers between devices: 27.3 us -> 43.6 us  [swap(): return lax.all_to_all(values, axis, split_axis=0, concat_axis=0, tiled=True)]
    ppermute x2, waiting for transfers between devices: 10.4 us -> 0.07 us  [send_row(): lax.ppermute(to_right, 'y', RIGHT)]
    ppermute x2, waiting for transfers between devices: 1.42 us -> 10.5 us  [send_row(): lax.ppermute(to_left, 'y', LEFT)]
    all_to_all x7, starting transfers between devices: 35.6 us -> 43.1 us  [swap(): return lax.all_to_all(values, axis, split_axis=0, concat_axis=0, tiled=True)]
    pallas_call x2 -> x4, Pallas kernels: 47.3 us -> 51.2 us  [the longest x2 47.7 us: attend(): pl.pallas_call(attend_kernel, in_specs=[smem] * 3 + [vmem] * 5 + [pl.Bloc...]
    ppermute x2, waiting for transfers between devices: 4.93 us -> 8.54 us  [send_row(): lax.ppermute(opp, 'y', OPPOSITE)]
    ppermute x8 -> x6, waiting for transfers between devices: 3.75 us -> 0.47 us  [the longest x2 0.46 us: gather_row(): lax.ppermute(own, 'y', OPPOSITE)]
  transfers between devices with their start and end apart: 23 -> 21, of which waited for: 10 -> 8; matrix products, arithmetic and copies ran while one was open for 2% -> 1% of each run, Pallas kernels for 31% -> 32%
where the time goes in v3:
time: 250 us; the launch traced here: 248 us
  Pallas kernels  88.9 us (36%)
  waiting for transfers between devices  63.2 us (25%)
  starting transfers between devices  59.8 us (24%)
  between operations  14.2 us (6%)
  blocking collectives  12.1 us (5%)
  local copies, waits for them, and re-layouts  9.97 us (4%)
    pallas_call x2, Pallas kernels, attend(): pl.pallas_call(attend_kernel, in_specs=[smem] * 3 + [vmem] * 5 + [pl.Bloc...  47.7 us
    all_to_all x7, waiting for transfers between devices, swap(): return lax.all_to_all(values, axis, split_axis=0, concat_axis=0, tiled=True)  43.6 us
    all_to_all x7, starting transfers between devices, swap(): return lax.all_to_all(values, axis, split_axis=0, concat_axis=0, tiled=True)  43.1 us
    all_to_all x1, blocking collectives, swap(): return lax.all_to_all(values, axis, split_axis=0, concat_axis=0, tiled=True)  12.1 us
    ppermute x2, waiting for transfers between devices, send_row(): lax.ppermute(to_left, 'y', LEFT)  10.5 us
    ppermute x2, waiting for transfers between devices, send_row(): lax.ppermute(opp, 'y', OPPOSITE)  8.54 us
    pallas_call x1, Pallas kernels, weight_share(): pl.pallas_call(weight_kernel, grid=(d // 256,), in_specs=[part, part, who...  7.8 us
    pallas_call x1, Pallas kernels, node_grads(): pl.pallas_call(nodes_kernel, grid=(steps,), in_specs=[tile, SECOND, tile,...  6.26 us
  transfers between devices with their start and end apart: 21, of which 8 were waited for; matrix products, arithmetic and copies ran while one was open for 1% of the time, Pallas kernels for 32%

profile of v3, /device:TPU:8, one launch (start us, length us, event | category | flops | bytes accessed | tf_op | source)
XLA Modules:
  0.0 248.3 jit_solution(12495570284150355780)
XLA Ops:
  7.2 5.1 %project_kv.1 = bf16[8,512,128]{2,1,0:T(8,128)(2,1)} custom-call(bf16[256,1024]{1,0:T(8,128)(2,1)} %bitcast.22, bf16[1024,3072]{1,0:T(8,128)(2,1)} %wv_ref.3, bf16[1024,3072]{1,0:T(8,128)(2,1)} %wv_ref.3), custom_call_target="tpu_custom_call" | custom-call | tf_op jit(solution)/shard_map/project_kv/pallas_call | solution.py:98
  12.3 8.5 %all-to-all-start = ((bf16[8,512,128]{2,1,0:T(8,128)(2,1)}), bf16[8,512,128]{2,1,0:T(8,128)(2,1)S(1)}, u32[]{:S(2)}, u32[]{:S(2)}) async-start(bf16[8,512,128]{2,1,0:T(8,128)(2,1)} %project_kv.1), calls=%async_computation | async-start | bytes 2097152 | tf_op jit(solution)/shard_map/all_to_all | solution.py:319
  20.8 5.3 %project_qg.1 = (bf16[8,256,128]{2,1,0:T(8,128)(2,1)}, bf16[8,256,128]{2,1,0:T(8,128)(2,1)}) custom-call(bf16[256,1024]{1,0:T(8,128)(2,1)} %bitcast.23, bf16[256,1024]{1,0:T(8,128)(2,1)} %bitcast.36, bf16[1024,3072]{1,0:T(8,128)(2,1)} %wv_ref.3, bf16[1024,1024]{1,0:T(8,128)(2,1)} %wo_ref.3), custom_call_target="tpu_custom_call" | custom-call | tf_op jit(solution)/shard_map/project_qg/pallas_call | solution.py:117
  26.1 23.4 %all-to-all-done.x_ref = bf16[8,512,128]{2,1,0:T(8,128)(2,1)S(1)} async-done(((bf16[8,512,128]{2,1,0:T(8,128)(2,1)}), bf16[8,512,128]{2,1,0:T(8,128)(2,1)S(1)}, u32[]{:S(2)}, u32[]{:S(2)}) %all-to-all-start) | async-done | bytes 1048608 | tf_op jit(solution)/shard_map/all_to_all | solution.py:319
  49.5 3.5 %all-to-all-start.1 = ((bf16[8,256,128]{2,1,0:T(8,128)(2,1)}), bf16[8,256,128]{2,1,0:T(8,128)(2,1)S(1)}, u32[]{:S(2)}, u32[]{:S(2)}) async-start(bf16[8,256,128]{2,1,0:T(8,128)(2,1)} %get-tuple-element.23), calls=%async_computation.1 | async-start | bytes 1048576 | tf_op jit(solution)/shard_map/all_to_all | solution.py:319
  53.0 2.0 split_heads.1
  55.1 1.6 collective-permute-start
  56.6 0.5 collective-permute-start.1
  57.1 2.3 collective-permute-start.2
  59.5 11.4 %all-to-all-done.1 = bf16[8,256,128]{2,1,0:T(8,128)(2,1)S(1)} async-done(((bf16[8,256,128]{2,1,0:T(8,128)(2,1)}), bf16[8,256,128]{2,1,0:T(8,128)(2,1)S(1)}, u32[]{:S(2)}, u32[]{:S(2)}) %all-to-all-start.1) | async-done | bytes 524320 | tf_op jit(solution)/shard_map/all_to_all | solution.py:319
  70.9 3.5 %all-to-all-start.2 = ((bf16[8,256,128]{2,1,0:T(8,128)(2,1)}), bf16[8,256,128]{2,1,0:T(8,128)(2,1)S(1)}, u32[]{:S(2)}, u32[]{:S(2)}) async-start(bf16[8,256,128]{2,1,0:T(8,128)(2,1)} %get-tuple-element.25), calls=%async_computation.2 | async-start | bytes 1048576 | tf_op jit(solution)/shard_map/all_to_all | solution.py:319
  74.4 1.9 hold.1.after_ref
  76.5 0.7 reshape.42.tab_ref
  77.1 0.6 fusion.cnt_ref
  77.7 1.6 collective-permute-start.6
  79.8 2.3 collective-permute-start.8
  82.1 0.5 collective-permute-done.2.opp_ref
  82.9 23.9 %attend.2 = (bf16[2048,128]{1,0:T(8,128)(2,1)}, bf16[2048,128]{1,0:T(8,128)(2,1)}, bf16[2048,128]{1,0:T(8,128)(2,1)}, bf16[2048,128]{1,0:T(8,128)(2,1)}, bf16[2048,128]{1,0:T(8,128)(2,1)}) custom-call(s32[192]{0:T(256)} %reshape.42.tab_ref, s32[16]{0:T(128)} %fusion.cnt_ref, s32[1]{0:T(128)} %bitcast.3.y_ref, bf16[2048,128]{1,0:T(8,128)(2,1)} %get-tuple-element.22.own_ref, ...), custom_call_target="tpu_custom_call" | custom-call | flops 25999998976 | bytes 6291456 | tf_op jit(solution)/shard_map/attend/pallas_call | solution.py:207
  106.8 0.8 copy-done.8
  107.5 7.1 %all-to-all-start.3 = ((bf16[8,256,128]{2,1,0:T(8,128)(2,1)}), bf16[8,256,128]{2,1,0:T(8,128)(2,1)S(1)}, u32[]{:S(2)}, u32[]{:S(2)}) async-start(bf16[8,256,128]{2,1,0:T(8,128)(2,1)} %bitcast.26), calls=%async_computation.3 | async-start | bytes 1048576 | tf_op jit(solution)/shard_map/all_to_all | solution.py:319
  114.6 0.6 collective-permute-start.3
  115.2 1.6 collective-permute-start.4
  116.8 0.8 copy-done.18
  117.6 2.0 collective-permute-start.5
  119.6 23.9 %attend.3 = (bf16[2048,128]{1,0:T(8,128)(2,1)}, bf16[2048,128]{1,0:T(8,128)(2,1)}, bf16[2048,128]{1,0:T(8,128)(2,1)}, bf16[2048,128]{1,0:T(8,128)(2,1)}, bf16[2048,128]{1,0:T(8,128)(2,1)}) custom-call(s32[192]{0:T(256)} %reshape.42.tab_ref, s32[16]{0:T(128)} %fusion.cnt_ref, s32[1]{0:T(128)} %bitcast.3.y_ref, bf16[2048,128]{1,0:T(8,128)(2,1)} %get-tuple-element.30.own_ref, ...), custom_call_target="tpu_custom_call" | custom-call | flops 25999998976 | bytes 6291456 | tf_op jit(solution)/shard_map/attend/pallas_call | solution.py:207
  143.5 0.7 copy-done.5
  144.8 2.7 %sum_join.1.ka_ref = bf16[8,512,128]{2,1,0:T(8,128)(2,1)} custom-call(bf16[2048,128]{1,0:T(8,128)(2,1)} %get-tuple-element.26.a_ref, bf16[2048,128]{1,0:T(8,128)(2,1)} %copy-done.5, bf16[2048,128]{1,0:T(8,128)(2,1)} %copy-done.6, bf16[2048,128]{1,0:T(8,128)(2,1)} %copy-done.7, bf16[2048,128]{1,0:T(8,128)(2,1)} %get-tuple-element.36.od_ref.ob_ref), custom_call_target="tpu_custom_call" | custom-call | tf_op jit(solution)/shard_map/sum_join/pallas_call | solution.py:361
  147.5 7.2 %all-to-all-start.4 = ((bf16[8,512,128]{2,1,0:T(8,128)(2,1)}), bf16[8,512,128]{2,1,0:T(8,128)(2,1)S(1)}, u32[]{:S(2)}, u32[]{:S(2)}) async-start(bf16[8,512,128]{2,1,0:T(8,128)(2,1)} %sum_join.1.ka_ref), calls=%async_computation.4 | async-start | bytes 2097152 | tf_op jit(solution)/shard_map/all_to_all | solution.py:319
  154.7 1.6 collective-permute-start.10
  156.3 2.3 collective-permute-start.11
  158.6 10.5 %collective-permute-done.10.refs_2_ = bf16[2048,128]{1,0:T(8,128)(2,1)S(1)} collective-permute-done((bf16[2048,128]{1,0:T(8,128)(2,1)S(1)}, bf16[2048,128]{1,0:T(8,128)(2,1)S(1)}, u32[]{:S(2)}, u32[]{:S(2)}) %collective-permute-start.10) | collective-permute-done | bytes 524320 | tf_op jit(solution)/shard_map/ppermute | solution.py:376
  169.1 8.5 %collective-permute-done.11.refs_3_ = bf16[2048,128]{1,0:T(8,128)(2,1)S(1)} collective-permute-done((bf16[2048,128]{1,0:T(8,128)(2,1)S(1)}, bf16[2048,128]{1,0:T(8,128)(2,1)S(1)}, u32[]{:S(2)}, u32[]{:S(2)}) %collective-permute-start.11) | collective-permute-done | bytes 524320 | tf_op jit(solution)/shard_map/ppermute | solution.py:377
  177.6 0.8 copy-done.14
  178.5 2.0 all-to-all-done.4.b_ref.refs_4_.ob_ref.ka_ref
  180.5 1.0 copy-done.1
  181.5 2.3 sum_parts.2.kb_ref
  183.9 4.8 %all-to-all-start.5 = ((bf16[8,256,128]{2,1,0:T(8,128)(2,1)}), bf16[8,256,128]{2,1,0:T(8,128)(2,1)S(1)}, u32[]{:S(2)}, u32[]{:S(2)}) async-start(bf16[8,256,128]{2,1,0:T(8,128)(2,1)} %bitcast.25), calls=%async_computation.5 | async-start | bytes 1048576 | tf_op jit(solution)/shard_map/all_to_all | solution.py:319
  188.7 7.8 %weight_share.1 = bf16[1024,384]{1,0:T(8,128)(2,1)} custom-call(bf16[2048,128]{1,0:T(8,128)(2,1)} %gate.3.after_ref.oa_ref, bf16[2048,128]{1,0:T(8,128)(2,1)} %get-tuple-element.36.od_ref.ob_ref, bf16[8,512,128]{2,1,0:T(8,128)(2,1)} %sum_join.1.ka_ref, bf16[2048,128]{1,0:T(8,128)(2,1)} %sum_parts.2.kb_ref, bf16[2048,1024]{1,0:T(8,128)(2,1)} %all-gather.2.cloned.1.call-done.f_ref), custom_call_target="tpu_custom_call" | custom-call | tf_op jit(solution)/shard_map/weight_share/pallas_call | solution.py:431
  196.5 1.9 dynamic-slice_bitcast_fusion
  198.5 6.7 %all-to-all-done.5.kb_ref.refs_2_ = bf16[8,256,128]{2,1,0:T(8,128)(2,1)S(1)} async-done(((bf16[8,256,128]{2,1,0:T(8,128)(2,1)}), bf16[8,256,128]{2,1,0:T(8,128)(2,1)S(1)}, u32[]{:S(2)}, u32[]{:S(2)}) %all-to-all-start.5) | async-done | bytes 524320 | tf_op jit(solution)/shard_map/all_to_all | solution.py:319
  205.2 0.8 copy-done.3
  206.1 2.0 sum_parts.3
  208.1 8.5 %all-to-all-start.6 = ((bf16[16,32,384]{2,1,0:T(8,128)(2,1)}), bf16[16,32,384]{2,1,0:T(8,128)(2,1)S(1)}, u32[]{:S(2)}, u32[]{:S(2)}) async-start(bf16[16,32,384]{2,1,0:T(8,128)(2,1)} %bitcast.34), calls=%async_computation.6 | async-start | bytes 786432 | tf_op jit(solution)/shard_map/all_to_all | solution.py:319
  216.6 4.4 %project_out.1.refs_1_ = bf16[256,1024]{1,0:T(8,128)(2,1)} custom-call(bf16[8,256,128]{2,1,0:T(8,128)(2,1)} %copy-done.2, bf16[8,512,128]{2,1,0:T(8,128)(2,1)} %copy-done.1, bf16[1024,1024]{1,0:T(8,128)(2,1)} %wo_ref.3), custom_call_target="tpu_custom_call" | custom-call | tf_op jit(solution)/shard_map/project_out/pallas_call | solution.py:247
  220.9 6.3 %node_grads.1.refs_2_ = bf16[256,1024]{1,0:T(8,128)(2,1)} custom-call(bf16[8,256,128]{2,1,0:T(8,128)(2,1)} %copy-done.2, bf16[8,512,128]{2,1,0:T(8,128)(2,1)} %copy-done.1, bf16[8,512,128]{2,1,0:T(8,128)(2,1)} %copy-done.1, bf16[8,256,128]{2,1,0:T(8,128)(2,1)} %copy-done.3, bf16[1024,3072]{1,0:T(8,128)(2,1)} %wv_ref.3, bf16[1024,3072]{1,0:T(8,128)(2,1)} %wv_ref.3, ...), custom_call_target="tpu_custom_call" | custom-call | tf_op jit(solution)/shard_map/node_grads/pallas_call | solution.py:286
  227.3 0.6 reshape.52.refs_0_
  227.9 12.1 %all_to_all.40.x_ref = f32[8,4,384]{2,1,0:T(4,128)} all-to-all(f32[8,4,384]{2,1,0:T(4,128)} %gate.5), channel_id=1, replica_groups=mesh['x'=4,'c'=2,'y'=4,'z'=8] {'z'}, dimensions={0} | all-to-all | bytes 98304 | tf_op jit(solution)/shard_map/all_to_all | solution.py:319
  240.0 1.4 spread.1
  (63 shorter events, 2.0 us)
Async XLA Ops:
  7.2 52.2 %copy-start = (s32[1,64,8]{1,2,0:T(8,128)S(1)}, s32[1,64,8]{1,2,0:T(8,128)}, u32[]{:S(2)}) copy-start(s32[1,64,8]{1,2,0:T(8,128)} %param.11) | copy-start | bytes 6148
  12.3 37.2 %all-to-all-start = ((bf16[8,512,128]{2,1,0:T(8,128)(2,1)}), bf16[8,512,128]{2,1,0:T(8,128)(2,1)S(1)}, u32[]{:S(2)}, u32[]{:S(2)}) async-start(bf16[8,512,128]{2,1,0:T(8,128)(2,1)} %project_kv.1), calls=%async_computation | async-start | bytes 2097152 | tf_op jit(solution)/shard_map/all_to_all | solution.py:319
  20.8 38.6 %copy-start.19 = (s32[1,4]{1,0:T(1,128)S(1)}, s32[1,4]{1,0:T(1,128)}, u32[]{:S(2)}) copy-start(s32[1,4]{1,0:T(1,128)} %param.13) | copy-start | bytes 52
  26.1 51.1 %copy-start.20 = (s32[1,64]{1,0:T(1,128)S(1)}, s32[1,64]{1,0:T(1,128)}, u32[]{:S(2)}) copy-start(s32[1,64]{1,0:T(1,128)} %param.12) | copy-start | bytes 772
  49.5 3.5 %copy-start.4 = (bf16[8,512,128]{2,1,0:T(8,128)(2,1)}, bf16[8,512,128]{2,1,0:T(8,128)(2,1)S(1)}, u32[]{:S(2)}) copy-start(bf16[8,512,128]{2,1,0:T(8,128)(2,1)S(1)} %all-to-all-done.x_ref) | copy-start | bytes 3145732
  49.5 21.4 %all-to-all-start.1 = ((bf16[8,256,128]{2,1,0:T(8,128)(2,1)}), bf16[8,256,128]{2,1,0:T(8,128)(2,1)S(1)}, u32[]{:S(2)}, u32[]{:S(2)}) async-start(bf16[8,256,128]{2,1,0:T(8,128)(2,1)} %get-tuple-element.23), calls=%async_computation.1 | async-start | bytes 1048576 | tf_op jit(solution)/shard_map/all_to_all | solution.py:319
  55.1 24.7 %collective-permute-start = (bf16[2048,128]{1,0:T(8,128)(2,1)}, bf16[2048,128]{1,0:T(8,128)(2,1)S(1)}, u32[]{:S(2)}, u32[]{:S(2)}) collective-permute-start(bf16[2048,128]{1,0:T(8,128)(2,1)} %get-tuple-element.22.own_ref), channel_id=1, source_target_pairs={{0,8},{8,16},{16,24},{24,0},{1,9},{9,17},{17,25},{25,1},{2,10},{10... | collective-permute-start | bytes 1572872 | tf_op jit(solution)/shard_map/ppermute | solution.py:328
  56.6 25.4 %collective-permute-start.1 = (bf16[2048,128]{1,0:T(8,128)(2,1)}, bf16[2048,128]{1,0:T(8,128)(2,1)S(1)}, u32[]{:S(2)}, u32[]{:S(2)}) collective-permute-start(bf16[2048,128]{1,0:T(8,128)(2,1)} %get-tuple-element.22.own_ref), channel_id=1, source_target_pairs={{0,24},{8,0},{16,8},{24,16},{1,25},{9,1},{17,9},{25,17},{2,26},{10... | collective-permute-start | bytes 1572872 | tf_op jit(solution)/shard_map/ppermute | solution.py:328
  57.1 25.4 %collective-permute-start.2 = (bf16[2048,128]{1,0:T(8,128)(2,1)}, bf16[2048,128]{1,0:T(8,128)(2,1)}, u32[]{:S(2)}, u32[]{:S(2)}) collective-permute-start(bf16[2048,128]{1,0:T(8,128)(2,1)} %get-tuple-element.22.own_ref), channel_id=1, source_target_pairs={{0,16},{8,24},{16,0},{24,8},{1,17},{9,25},{17,1},{25,9},{2,18},{10... | collective-permute-start | bytes 1572872 | tf_op jit(solution)/shard_map/ppermute | solution.py:328
  70.9 3.6 %copy-start.9 = (bf16[8,256,128]{2,1,0:T(8,128)(2,1)}, bf16[8,256,128]{2,1,0:T(8,128)(2,1)S(1)}, u32[]{:S(2)}) copy-start(bf16[8,256,128]{2,1,0:T(8,128)(2,1)S(1)} %all-to-all-done.1) | copy-start | bytes 1572868
  70.9 35.9 %all-to-all-start.2 = ((bf16[8,256,128]{2,1,0:T(8,128)(2,1)}), bf16[8,256,128]{2,1,0:T(8,128)(2,1)S(1)}, u32[]{:S(2)}, u32[]{:S(2)}) async-start(bf16[8,256,128]{2,1,0:T(8,128)(2,1)} %get-tuple-element.25), calls=%async_computation.2 | async-start | bytes 1048576 | tf_op jit(solution)/shard_map/all_to_all | solution.py:319
  74.4 114.4 %all-gather.2.cloned.1.call-start = ((), (), s32[]{:S(2)}) async-start(), calls=%async_computation.8 | async-start | bytes 4718592 | tf_op jit(solution)/shard_map/all_gather | solution.py:457
  77.7 39.0 %collective-permute-start.6 = (bf16[2048,128]{1,0:T(8,128)(2,1)}, bf16[2048,128]{1,0:T(8,128)(2,1)S(1)}, u32[]{:S(2)}, u32[]{:S(2)}) collective-permute-start(bf16[2048,128]{1,0:T(8,128)(2,1)} %get-tuple-element.30.own_ref), channel_id=1, source_target_pairs={{0,8},{8,16},{16,24},{24,0},{1,9},{9,17},{17,25},{25,1},{2,10},{10... | collective-permute-start | bytes 1572872 | tf_op jit(solution)/shard_map/ppermute | solution.py:328
  79.3 40.3 %collective-permute-start.7 = (bf16[2048,128]{1,0:T(8,128)(2,1)}, bf16[2048,128]{1,0:T(8,128)(2,1)}, u32[]{:S(2)}, u32[]{:S(2)}) collective-permute-start(bf16[2048,128]{1,0:T(8,128)(2,1)} %get-tuple-element.30.own_ref), channel_id=1, source_target_pairs={{0,24},{8,0},{16,8},{24,16},{1,25},{9,1},{17,9},{25,17},{2,26},{10... | collective-permute-start | bytes 1572872 | tf_op jit(solution)/shard_map/ppermute | solution.py:328
  79.8 2.8 %copy-start.16 = (bf16[2048,128]{1,0:T(8,128)(2,1)}, bf16[2048,128]{1,0:T(8,128)(2,1)S(1)}, u32[]{:S(2)}) copy-start(bf16[2048,128]{1,0:T(8,128)(2,1)S(1)} %collective-permute-done.left_ref) | copy-start | bytes 1572868
  79.8 39.8 %collective-permute-start.8 = (bf16[2048,128]{1,0:T(8,128)(2,1)}, bf16[2048,128]{1,0:T(8,128)(2,1)}, u32[]{:S(2)}, u32[]{:S(2)}) collective-permute-start(bf16[2048,128]{1,0:T(8,128)(2,1)} %get-tuple-element.30.own_ref), channel_id=1, source_target_pairs={{0,16},{8,24},{16,0},{24,8},{1,17},{9,25},{17,1},{25,9},{2,18},{10... | collective-permute-start | bytes 1572872 | tf_op jit(solution)/shard_map/ppermute | solution.py:328
  82.1 0.8 copy-start.17
  106.8 0.8 copy-start.8
  107.5 35.9 %all-to-all-start.3 = ((bf16[8,256,128]{2,1,0:T(8,128)(2,1)}), bf16[8,256,128]{2,1,0:T(8,128)(2,1)S(1)}, u32[]{:S(2)}, u32[]{:S(2)}) async-start(bf16[8,256,128]{2,1,0:T(8,128)(2,1)} %bitcast.26), calls=%async_computation.3 | async-start | bytes 1048576 | tf_op jit(solution)/shard_map/all_to_all | solution.py:319
  114.6 28.8 %collective-permute-start.3 = (bf16[2048,128]{1,0:T(8,128)(2,1)}, bf16[2048,128]{1,0:T(8,128)(2,1)S(1)}, u32[]{:S(2)}, u32[]{:S(2)}) collective-permute-start(bf16[2048,128]{1,0:T(8,128)(2,1)} %get-tuple-element.27), channel_id=1, source_target_pairs={{0,8},{8,16},{16,24},{24,0},{1,9},{9,17},{17,25},{25,1},{2,10},{10... | collective-permute-start | bytes 1572872 | tf_op jit(solution)/shard_map/ppermute | solution.py:375
  115.2 28.2 %collective-permute-start.4 = (bf16[2048,128]{1,0:T(8,128)(2,1)}, bf16[2048,128]{1,0:T(8,128)(2,1)S(1)}, u32[]{:S(2)}, u32[]{:S(2)}) collective-permute-start(bf16[2048,128]{1,0:T(8,128)(2,1)} %get-tuple-element.28), channel_id=1, source_target_pairs={{0,24},{8,0},{16,8},{24,16},{1,25},{9,1},{17,9},{25,17},{2,26},{10... | collective-permute-start | bytes 1572872 | tf_op jit(solution)/shard_map/ppermute | solution.py:376
  116.8 0.8 copy-start.18
  117.6 25.9 %collective-permute-start.5 = (bf16[2048,128]{1,0:T(8,128)(2,1)}, bf16[2048,128]{1,0:T(8,128)(2,1)S(1)}, u32[]{:S(2)}, u32[]{:S(2)}) collective-permute-start(bf16[2048,128]{1,0:T(8,128)(2,1)} %get-tuple-element.29), channel_id=1, source_target_pairs={{0,16},{8,24},{16,0},{24,8},{1,17},{9,25},{17,1},{25,9},{2,18},{10... | collective-permute-start | bytes 1572872 | tf_op jit(solution)/shard_map/ppermute | solution.py:377
  143.4 0.8 copy-start.5
  143.4 1.0 copy-start.6
  143.5 1.1 copy-start.7
  143.5 1.3 copy-start.2
  144.8 9.9 %copy-start.11 = (bf16[2048,128]{1,0:T(8,128)(2,1)S(1)}, bf16[2048,128]{1,0:T(8,128)(2,1)}, u32[]{:S(2)}) copy-start(bf16[2048,128]{1,0:T(8,128)(2,1)} %get-tuple-element.39) | copy-start | bytes 1572868
  144.8 11.5 %copy-start.12 = (bf16[2048,128]{1,0:T(8,128)(2,1)S(1)}, bf16[2048,128]{1,0:T(8,128)(2,1)}, u32[]{:S(2)}) copy-start(bf16[2048,128]{1,0:T(8,128)(2,1)} %get-tuple-element.40) | copy-start | bytes 1572868
  144.8 13.9 %copy-start.10 = (bf16[2048,128]{1,0:T(8,128)(2,1)S(1)}, bf16[2048,128]{1,0:T(8,128)(2,1)}, u32[]{:S(2)}) copy-start(bf16[2048,128]{1,0:T(8,128)(2,1)} %get-tuple-element.38) | copy-start | bytes 1572868
  147.5 33.0 %all-to-all-start.4 = ((bf16[8,512,128]{2,1,0:T(8,128)(2,1)}), bf16[8,512,128]{2,1,0:T(8,128)(2,1)S(1)}, u32[]{:S(2)}, u32[]{:S(2)}) async-start(bf16[8,512,128]{2,1,0:T(8,128)(2,1)} %sum_join.1.ka_ref), calls=%async_computation.4 | async-start | bytes 2097152 | tf_op jit(solution)/shard_map/all_to_all | solution.py:319
  154.7 14.4 %collective-permute-start.10 = (bf16[2048,128]{1,0:T(8,128)(2,1)S(1)}, bf16[2048,128]{1,0:T(8,128)(2,1)S(1)}, u32[]{:S(2)}, u32[]{:S(2)}) collective-permute-start(bf16[2048,128]{1,0:T(8,128)(2,1)S(1)} %copy-done.11), channel_id=1, source_target_pairs={{0,24},{8,0},{16,8},{24,16},{1,25},{9,1},{17,9},{25,17},{2,26},{10... | collective-permute-start | bytes 1572872 | tf_op jit(solution)/shard_map/ppermute | solution.py:376
  156.3 21.3 %collective-permute-start.11 = (bf16[2048,128]{1,0:T(8,128)(2,1)S(1)}, bf16[2048,128]{1,0:T(8,128)(2,1)S(1)}, u32[]{:S(2)}, u32[]{:S(2)}) collective-permute-start(bf16[2048,128]{1,0:T(8,128)(2,1)S(1)} %copy-done.12), channel_id=1, source_target_pairs={{0,16},{8,24},{16,0},{24,8},{1,17},{9,25},{17,1},{25,9},{2,18},{10... | collective-permute-start | bytes 1572872 | tf_op jit(solution)/shard_map/ppermute | solution.py:377
  158.6 19.9 %collective-permute-start.9 = (bf16[2048,128]{1,0:T(8,128)(2,1)S(1)}, bf16[2048,128]{1,0:T(8,128)(2,1)}, u32[]{:S(2)}, u32[]{:S(2)}) collective-permute-start(bf16[2048,128]{1,0:T(8,128)(2,1)S(1)} %copy-done.10), channel_id=1, source_target_pairs={{0,8},{8,16},{16,24},{24,0},{1,9},{9,17},{17,25},{25,1},{2,10},{10... | collective-permute-start | bytes 1572872 | tf_op jit(solution)/shard_map/ppermute | solution.py:375
  169.1 11.4 %copy-start.13 = (bf16[2048,128]{1,0:T(8,128)(2,1)}, bf16[2048,128]{1,0:T(8,128)(2,1)S(1)}, u32[]{:S(2)}) copy-start(bf16[2048,128]{1,0:T(8,128)(2,1)S(1)} %collective-permute-done.10.refs_2_) | copy-start | bytes 1572868
  177.6 0.8 copy-start.14
  180.5 1.0 copy-start.1
  183.9 21.3 %all-to-all-start.5 = ((bf16[8,256,128]{2,1,0:T(8,128)(2,1)}), bf16[8,256,128]{2,1,0:T(8,128)(2,1)S(1)}, u32[]{:S(2)}, u32[]{:S(2)}) async-start(bf16[8,256,128]{2,1,0:T(8,128)(2,1)} %bitcast.25), calls=%async_computation.5 | async-start | bytes 1048576 | tf_op jit(solution)/shard_map/all_to_all | solution.py:319
  198.5 6.7 %collective-permute-start.12 = (bf16[4,128,384]{2,1,0:T(8,128)(2,1)S(1)}, bf16[4,128,384]{2,1,0:T(8,128)(2,1)S(1)}, u32[]{:S(2)}, u32[]{:S(2)}) collective-permute-start(bf16[4,128,384]{2,1,0:T(8,128)(2,1)S(1)} %get-tuple-element.41), channel_id=1, source_target_pairs={{0,32},{32,0},{1,33},{33,1},{2,34},{34,2},{3,35},{35,3},{4,36},{36... | collective-permute-start | bytes 1179656 | tf_op jit(solution)/shard_map/ppermute | solution.py:478
  205.2 0.8 copy-start.3
  205.2 0.9 copy-start.15
  208.1 19.1 %all-to-all-start.6 = ((bf16[16,32,384]{2,1,0:T(8,128)(2,1)}), bf16[16,32,384]{2,1,0:T(8,128)(2,1)S(1)}, u32[]{:S(2)}, u32[]{:S(2)}) async-start(bf16[16,32,384]{2,1,0:T(8,128)(2,1)} %bitcast.34), calls=%async_computation.6 | async-start | bytes 786432 | tf_op jit(solution)/shard_map/all_to_all | solution.py:319
Sparse Core Ops, SparseCore 0:
  77.0 67.5 all-gather.1

commit v4 on v3

--- a/solution.py
+++ b/solution.py
@@ -22,7 +22,8 @@
 ROW = NODE_DEV * ZS
 QBLK = ROW // BLOCK
 NODES = ROW * YS
-HALF = ROW // 2
+TURNED = (ZS, 2 * HD, NODE_DEV)
+PIECES = YS * ZS
 SCALE = HD**-0.5
 LOG2E = math.log2(math.e)
 MASKED = -3.0e38
@@ -44,6 +45,13 @@
     )
 
 
+def pair_rows(first, second):
+    return (
+        jnp.concatenate([first[:HD], second[:HD]], axis=0),
+        jnp.concatenate([first[HD:], second[HD:]], axis=0),
+    )
+
+
 def nt(a, b):
     return lax.dot_general(a, b, (((1,), (1,)), ((), ())), preferred_element_type=f32)
 
@@ -61,25 +69,27 @@
 
 
 def kv_kernel(f_ref, wk_ref, wv_ref, o_ref):
-    a_ref, b_ref = o_ref.at[:, :NODE_DEV], o_ref.at[:, NODE_DEV:]
-    put_pairs(nn(f_ref[...], wk_ref[...]), nn(f_ref[...], wv_ref[...]), a_ref, b_ref)
+    k = nn(f_ref[...], wk_ref[...])
+    v = nn(f_ref[...], wv_ref[...])
+    for u in (0, 1):
+        cols = slice(u * 128, (u + 1) * 128)
+        a, b = pair_rows(k[:, cols].T, v[:, cols].T)
+        o_ref[u, :128, :] = a.astype(bf16)
+        o_ref[u, 128:, :] = b.astype(bf16)
 
 
 def split_kernel(x_ref, a_ref, b_ref):
-    for u in range(x_ref.shape[0]):
-        rows = slice(u * NODE_DEV, (u + 1) * NODE_DEV)
-        a_ref[rows, :] = x_ref[u, :NODE_DEV, :]
-        b_ref[rows, :] = x_ref[u, NODE_DEV:, :]
+    a_ref[...] = x_ref[:, :128, :]
+    b_ref[...] = x_ref[:, 128:, :]
 
 
 def split_heads(both):
-    tile = pl.BlockSpec((HALF, 128), lambda i: (i, 0))
     return pl.pallas_call(
         split_kernel,
         grid=(2,),
-        in_specs=[pl.BlockSpec((ZS // 2, 2 * NODE_DEV, 128), lambda i: (i, 0, 0))],
-        out_specs=[tile, tile],
-        out_shape=[jax.ShapeDtypeStruct((ROW, 128), bf16)] * 2,
+        in_specs=[pl.BlockSpec((ZS // 2, 256, NODE_DEV), lambda i: (i, 0, 0))],
+        out_specs=[pl.BlockSpec((ZS // 2, 128, NODE_DEV), lambda i: (i, 0, 0))] * 2,
+        out_shape=[jax.ShapeDtypeStruct(TURNED, bf16)] * 2,
         compiler_params=VMEM,
         name="split_heads",
     )(both)
@@ -103,8 +113,8 @@
             pl.BlockSpec((d, 256), lambda i: (0, ZS // 2 + i)),
             pl.BlockSpec((d, 256), lambda i: (0, ZS + i)),
         ],
-        out_specs=pl.BlockSpec((2, 2 * NODE_DEV, 128), lambda i: (i, 0, 0)),
-        out_shape=jax.ShapeDtypeStruct((ZS, 2 * NODE_DEV, 128), bf16),
+        out_specs=pl.BlockSpec((2, 256, NODE_DEV), lambda i: (i, 0, 0)),
+        out_shape=jax.ShapeDtypeStruct((ZS, 256, NODE_DEV), bf16),
         compiler_params=VMEM,
         name="project_kv",
     )(feats, w_qkv, w_qkv)
@@ -131,30 +141,28 @@
 
 
 def attend_kernel(
-    tab_ref, cnt_ref, y_ref, own_ref, left_ref, right_ref, opp_ref, qg_ref, after_ref,
+    tab_ref, cnt_ref, order_ref, y_ref, own_ref, left_ref, right_ref, opp_ref, qg_ref, after_ref,
     od_ref, sum_own_ref, sum_right_ref, sum_left_ref, sum_opp_ref,
-    kv_s, acc, sc, xs,
+    kv_s, acc, sc0, sc1, xs0, xs1,
 ):
     y = y_ref[0]
-    at = lambda step: lax.rem(y + step, YS) * ROW
-
-    kv_s[pl.ds(pl.multiple_of(at(0), ROW), ROW), :] = own_ref[...]
-    kv_s[pl.ds(pl.multiple_of(at(YS - 1), ROW), ROW), :] = left_ref[...]
-    kv_s[pl.ds(pl.multiple_of(at(1), ROW), ROW), :] = right_ref[...]
-    kv_s[pl.ds(pl.multiple_of(at(2), ROW), ROW), :] = opp_ref[...]
-
-    @pl.loop(0, NODES // 512)
+    at = lambda step: lax.rem(y + step, YS) * ZS
+
+    for step, ref in ((0, own_ref), (YS - 1, left_ref), (1, right_ref), (2, opp_ref)):
+        kv_s[pl.ds(at(step), ZS)] = ref[...]
+
+    @pl.loop(0, PIECES)
     def _(t):
-        acc[:, pl.ds(pl.multiple_of(t * 512, 512), 512)] = jnp.zeros((128, 512), f32)
+        acc[t] = jnp.zeros((128, NODE_DEV), f32)
+
+    def cols(block):
+        return pl.ds(pl.multiple_of(lax.rem(block, 2) * BLOCK, BLOCK), BLOCK)
 
     def keys(ids, t):
-        rows = [kv_s[pl.ds(pl.multiple_of(ids[2 * t + u] * BLOCK, BLOCK), BLOCK), :] for u in (0, 1)]
-        return jnp.concatenate(rows, axis=0)
-
-    def row_block(i, pairs):
-        width = pairs * 256
+        return jnp.concatenate([kv_s[lax.div(ids[2 * t + u], 2), :, cols(ids[2 * t + u])] for u in (0, 1)], axis=1)
+
+    def score(i, pairs, sc):
         ids = [tab_ref[i * SLOTS + t] for t in range(2 * pairs)]
-        odd = lax.rem(cnt_ref[i], 2) == 1
         rows = pl.ds(pl.multiple_of(i * BLOCK, BLOCK), BLOCK)
         qg = qg_ref[rows, :].astype(f32)
         low = low_half(qg.shape)
@@ -162,57 +170,77 @@
         wide32 = jnp.concatenate([jnp.where(low, qg, zero), jnp.where(low, zero, qg)], axis=0)
         wide = wide32.astype(bf16)
         for t in range(pairs):
-            sc[:, t * 256 : (t + 1) * 256] = nt(wide, keys(ids, t))
+            sc[:, t * 256 : (t + 1) * 256] = nn(wide, keys(ids, t))
+        return i, ids, wide32.T.astype(bf16)
+
+    def soften(i, pairs, sc, xs):
+        width = pairs * 256
+        count = cnt_ref[i]
         step = 16
         for r in range(BLOCK // step):
             s = sc[r * step : (r + 1) * step, :width]
             dp = sc[BLOCK + r * step : BLOCK + (r + 1) * step, :width]
-            last = jnp.where(odd, MASKED, s[:, width - BLOCK :])
-            s = jnp.concatenate([s[:, : width - BLOCK], last], axis=1)
+            kept = [s[:, : (NGLOB + 1) * BLOCK]]
+            for t in range(NGLOB + 1, 2 * pairs):
+                kept.append(jnp.where(t - NGLOB < count, s[:, t * BLOCK : (t + 1) * BLOCK], MASKED))
+            s = jnp.concatenate(kept, axis=1)
             e = jnp.exp2((s - jnp.max(s, axis=1, keepdims=True)) * (SCALE * LOG2E))
             p = e * (1.0 / jnp.sum(e, axis=1, keepdims=True))
             delta = jnp.sum(p * dp, axis=1, keepdims=True)
             ds = p * (dp - delta) * SCALE
             xs[r * step : (r + 1) * step, :width] = ds.astype(bf16)
             xs[BLOCK + r * step : BLOCK + (r + 1) * step, :width] = p.astype(bf16)
-        every = jnp.concatenate([keys(ids, t) for t in range(pairs)], axis=0)
-        mixed = nn(xs[:, :width], every)
-        od_ref[rows, :] = jnp.where(low, mixed[:BLOCK], mixed[BLOCK:]).astype(bf16)
-        wide_t = wide32.T.astype(bf16)
+
+    def mix(state, pairs, xs):
+        i, ids, wide_t = state
+        every = jnp.concatenate([keys(ids, t) for t in range(pairs)], axis=1)
+        mixed = nt(every, xs[:, : pairs * 256])
+        od = jnp.concatenate([mixed[:HD, :BLOCK], mixed[HD:, BLOCK:]], axis=0)
+        od_ref[lax.div(i, 2), :, cols(i)] = od.astype(bf16)
         for t in range(pairs):
             part = nn(wide_t, xs[:, t * 256 : (t + 1) * 256])
             for u in (0, 1):
-                at_key = pl.ds(pl.multiple_of(ids[2 * t + u] * BLOCK, BLOCK), BLOCK)
-                acc[:, at_key] += part[:, u * BLOCK : (u + 1) * BLOCK]
-
-    @pl.loop(0, QBLK)
-    def _(i):
-        pairs = NGLOB // 2 + (cnt_ref[i] + 1) // 2
+                block = ids[2 * t + u]
+                acc[lax.div(block, 2), :, cols(block)] += part[:, u * BLOCK : (u + 1) * BLOCK]
+
+    def two_blocks(i, k, pairs):
+        first = score(i, pairs, sc0)
+        second = score(k, pairs, sc1)
+        soften(i, pairs, sc0, xs0)
+        mix(first, pairs, xs0)
+        soften(k, pairs, sc1, xs1)
+        mix(second, pairs, xs1)
+
+    @pl.loop(0, QBLK // 2)
+    def _(t):
+        i, k = order_ref[2 * t], order_ref[2 * t + 1]
+        pairs = NGLOB // 2 + (jnp.maximum(cnt_ref[i], cnt_ref[k]) + 1) // 2
         for v in range(NGLOB // 2 + 1, SLOTS // 2 + 1):
-            pl.when(pairs == v)(functools.partial(row_block, i, v))
+            pl.when(pairs == v)(functools.partial(two_blocks, i, k, v))
 
     for step, out in ((0, sum_own_ref), (1, sum_right_ref), (YS - 1, sum_left_ref), (2, sum_opp_ref)):
         start = at(step)
 
-        @pl.loop(0, ROW // 256)
+        @pl.loop(0, ZS)
         def _(t):
-            cols = pl.ds(pl.multiple_of(start + t * 256, 256), 256)
-            out[pl.ds(pl.multiple_of(t * 256, 256), 256), :] = acc[:, cols].T.astype(bf16)
-
-
-def attend(table, counts, y, kv_parts, qg, after):
+            out[t] = acc[start + t].astype(bf16)
+
+
+def attend(table, counts, order, y, kv_parts, qg, after):
     vmem = pl.BlockSpec(memory_space=pltpu.VMEM)
     smem = pl.BlockSpec(memory_space=pltpu.SMEM)
-    row = jax.ShapeDtypeStruct((ROW, 128), bf16)
+    row = jax.ShapeDtypeStruct(TURNED, bf16)
     return pl.pallas_call(
         attend_kernel,
-        in_specs=[smem] * 3 + [vmem] * 5 + [pl.BlockSpec(memory_space=pl.ANY)],
+        in_specs=[smem] * 4 + [vmem] * 5 + [pl.BlockSpec(memory_space=pl.ANY)],
         out_specs=[vmem] * 5,
         out_shape=[row] * 5,
         scratch_shapes=[
-            pltpu.VMEM((NODES, 128), bf16),
-            pltpu.VMEM((128, NODES), f32),
+            pltpu.VMEM((PIECES, 128, NODE_DEV), bf16),
+            pltpu.VMEM((PIECES, 128, NODE_DEV), f32),
             pltpu.VMEM((256, SLOTS * BLOCK), f32),
+            pltpu.VMEM((256, SLOTS * BLOCK), f32),
+            pltpu.VMEM((256, SLOTS * BLOCK), bf16),
             pltpu.VMEM((256, SLOTS * BLOCK), bf16),
         ],
         compiler_params=VMEM,
@@ -220,7 +248,11 @@
             flops=26 * 10**9, bytes_accessed=6 << 20, transcendentals=0
         ),
         name="attend",
-    )(table, counts, y, *kv_parts, qg, after)
+    )(table, counts, order, y, *kv_parts, qg, after)
+
+
+def turn(tiles):
+    return jnp.concatenate(tiles, axis=0).astype(f32).T.astype(bf16)
 
 
 def out_kernel(a_ref, b_ref, wo_ref, o_ref, total):
@@ -230,20 +262,20 @@
     def _():
         total[...] = jnp.zeros_like(total)
 
-    cols = [pair_up(a_ref[u].astype(f32), b_ref[u].astype(f32))[1] for u in (0, 1)]
-    total[...] += nn(jnp.concatenate(cols, axis=1).astype(bf16), wo_ref[...])
+    att = [pair_rows(a_ref[u], b_ref[u])[1] for u in (0, 1)]
+    total[...] += nn(turn(att), wo_ref[...])
 
     @pl.when(step == pl.num_programs(0) - 1)
     def _():
         o_ref[...] = total[...].astype(bf16)
 
 
-SECOND = pl.BlockSpec((2, NODE_DEV, 128), lambda i: (i, 1, 0))
+SECOND = pl.BlockSpec((2, 128, NODE_DEV), lambda i: (i, 1, 0))
 
 
 def project_out(od_a, joint, w_out):
     d = w_out.shape[1]
-    tile = pl.BlockSpec((2, NODE_DEV, 128), lambda i: (i, 0, 0))
+    tile = pl.BlockSpec((2, 128, NODE_DEV), lambda i: (i, 0, 0))
     return pl.pallas_call(
         out_kernel,
         grid=(ZS // 2,),
@@ -265,13 +297,13 @@
 
     dq, dk, dv = [], [], []
     for u in (0, 1):
-        dq.append(pair_up(oa_ref[u].astype(f32), ob_ref[u].astype(f32))[0])
-        k, v = pair_up(ka_ref[u].astype(f32), kb_ref[u].astype(f32))
+        dq.append(pair_rows(oa_ref[u], ob_ref[u])[0])
+        k, v = pair_rows(ka_ref[u], kb_ref[u])
         dk.append(k)
         dv.append(v)
-    add = nt(jnp.concatenate(dq, axis=1).astype(bf16), wq_ref[...])
-    add += nt(jnp.concatenate(dk, axis=1).astype(bf16), wk_ref[...])
-    add += nt(jnp.concatenate(dv, axis=1).astype(bf16), wv_ref[...])
+    add = nt(turn(dq), wq_ref[...])
+    add += nt(turn(dk), wk_ref[...])
+    add += nt(turn(dv), wv_ref[...])
     total[...] += add
 
     @pl.when(step == pl.num_programs(0) - 1)
@@ -281,7 +313,7 @@
 
 def node_grads(od_a, joint, kv_b, w_qkv):
     d = w_qkv.shape[0]
-    tile = pl.BlockSpec((2, NODE_DEV, 128), lambda i: (i, 0, 0))
+    tile = pl.BlockSpec((2, 128, NODE_DEV), lambda i: (i, 0, 0))
     steps = ZS // 2
     return pl.pallas_call(
         nodes_kernel,
@@ -334,36 +366,32 @@
 
 
 def sum_parts(parts, after):
-    rows, cols = parts[0].shape
-    tile = pl.BlockSpec((rows // 2, cols), lambda i: (i, 0))
+    shape = parts[0].shape
+    tile = pl.BlockSpec((shape[0] // 2, *shape[1:]), lambda i: (i,) + (0,) * (len(shape) - 1))
     return pl.pallas_call(
         functools.partial(sum_kernel, len(parts)),
         grid=(2,),
         in_specs=[tile] * len(parts) + [pl.BlockSpec(memory_space=pl.ANY)] * len(after),
         out_specs=tile,
-        out_shape=jax.ShapeDtypeStruct((rows, cols), bf16),
+        out_shape=jax.ShapeDtypeStruct(shape, bf16),
         compiler_params=VMEM,
         name="sum_parts",
     )(*parts, *after)
 
 
 def sum_join_kernel(a_ref, b_ref, c_ref, d_ref, od_ref, o_ref):
-    total = sum(r[...].astype(f32) for r in (a_ref, b_ref, c_ref, d_ref)).astype(bf16)
-    pieces = o_ref.shape[0]
-    for u in range(pieces):
-        rows = slice(u * NODE_DEV, (u + 1) * NODE_DEV)
-        o_ref[u, :NODE_DEV, :] = total[rows]
-        o_ref[u, NODE_DEV:, :] = od_ref[rows, :]
+    o_ref[:, :128, :] = sum(r[...].astype(f32) for r in (a_ref, b_ref, c_ref, d_ref)).astype(bf16)
+    o_ref[:, 128:, :] = od_ref[...]
 
 
 def sum_join(parts, od):
-    tile = pl.BlockSpec((HALF, 128), lambda i: (i, 0))
+    tile = pl.BlockSpec((ZS // 2, 128, NODE_DEV), lambda i: (i, 0, 0))
     return pl.pallas_call(
         sum_join_kernel,
         grid=(2,),
         in_specs=[tile] * 5,
-        out_specs=pl.BlockSpec((ZS // 2, 2 * NODE_DEV, 128), lambda i: (i, 0, 0)),
-        out_shape=jax.ShapeDtypeStruct((ZS, 2 * NODE_DEV, 128), bf16),
+        out_specs=pl.BlockSpec((ZS // 2, 256, NODE_DEV), lambda i: (i, 0, 0)),
+        out_shape=jax.ShapeDtypeStruct((ZS, 256, NODE_DEV), bf16),
         compiler_params=VMEM,
         name="sum_join",
     )(*parts, od)
@@ -414,20 +442,19 @@
 def weight_kernel(oa_ref, ob_ref, ka_ref, kb_ref, f_ref, o_ref, grads):
     @pl.when(pl.program_id(0) == 0)
     def _():
-        @pl.loop(0, ZS)
-        def _(t):
-            rows = pl.ds(pl.multiple_of(t * NODE_DEV, NODE_DEV), NODE_DEV)
-            dq = pair_up(oa_ref[rows, :].astype(f32), ob_ref[rows, :].astype(f32))[0]
-            dk, dv = pair_up(ka_ref[t, :NODE_DEV, :].astype(f32), kb_ref[rows, :].astype(f32))
+        for t in range(ZS):
+            nodes = slice(t * NODE_DEV, (t + 1) * NODE_DEV)
+            dq = pair_rows(oa_ref[t], ob_ref[t])[0]
+            dk, dv = pair_rows(ka_ref[t, :128, :], kb_ref[t])
             for k, part in enumerate((dq, dk, dv)):
-                grads[k * 128 : (k + 1) * 128, rows] = part.T.astype(bf16)
+                grads[k * 128 : (k + 1) * 128, nodes] = part
 
     o_ref[...] = nn(grads[...], f_ref[...]).T.astype(bf16)
 
 
 def weight_share(od_a, od_b, joint, kv_b, feats_row):
     d = feats_row.shape[1]
-    part = whole((ROW, 128))
+    part = whole(TURNED)
     return pl.pallas_call(
         weight_kernel,
         grid=(d // 256,),
@@ -447,6 +474,10 @@
     neighbors = lax.dynamic_slice_in_dim(block_neighbors[0], y * QBLK, QBLK, 0)
     counts = lax.dynamic_slice_in_dim(block_counts[0], y * QBLK, QBLK, 0)
     table = jnp.concatenate([jnp.broadcast_to(global_blocks[0][None], (QBLK, NGLOB)), neighbors], axis=1).reshape(-1)
+    place = jnp.arange(QBLK, dtype=jnp.int32)
+    key = counts * QBLK + place
+    rank = jnp.sum((key[None, :] < key[:, None]).astype(jnp.int32), axis=1)
+    order = jnp.sum(jnp.where(rank[None, :] == place[:, None], place[None, :], 0), axis=1)
     y_arr = y.reshape(1).astype(jnp.int32)
 
     kv = project_kv(feats, w_qkv)
@@ -455,12 +486,12 @@
     qg_row = [swap(v, "z").reshape(ROW, 128) for v in qg]
     feats_late = hold(feats, qg_row[0])
     feats_row = lax.all_gather(feats_late, "z", axis=0, tiled=True)
-    od_a, *kv_a = attend(table, counts, y_arr, kv_row[0], qg_row[0], feats_late)
-    to_nodes = lambda v: swap(v.reshape(ZS, NODE_DEV, 128), "z")
+    od_a, *kv_a = attend(table, counts, order, y_arr, kv_row[0], qg_row[0], feats_late)
+    to_nodes = lambda v: swap(v, "z")
     (od_a_late,) = gate([od_a], [qg_row[1]])
     od_nodes_a = to_nodes(od_a_late)
     parts_a = send_row(*kv_a)
-    late = attend(table, counts, y_arr, kv_row[1], qg_row[1], od_a_late)
+    late = attend(table, counts, order, y_arr, kv_row[1], qg_row[1], od_a_late)
     od_b, *kv_b = gate(late, parts_a[1:] + [od_nodes_a])
     parts_b = send_row(*kv_b)
     joint = sum_join(parts_a, od_b)

time: 250 us -> 238 us (0.952)
  Pallas kernels: 88.9 us -> 71.8 us
  waiting for transfers between devices: 63.2 us -> 67.6 us
    pallas_call x2, Pallas kernels: 47.7 us -> 32 us  [attend(): pl.pallas_call(attend_kernel, in_specs=[smem] * 4 + [vmem] * 5 + [pl.Bloc...]
    ppermute x2, waiting for transfers between devices: 8.54 us -> 13.9 us  [send_row(): lax.ppermute(opp, 'y', OPPOSITE)]
    ppermute x2, starting transfers between devices: 0.55 us -> 3.69 us  [send_row(): lax.ppermute(to_right, 'y', RIGHT)]
  transfers between devices with their start and end apart: 21 -> 21, of which waited for: 8 -> 9; matrix products, arithmetic and copies ran while one was open for 1% -> 2% of each run, Pallas kernels for 32% -> 27%
where the time goes in v4:
time: 238 us; the launch traced here: 237 us
  Pallas kernels  71.8 us (30%)
  waiting for transfers between devices  67.6 us (28%)
  starting transfers between devices  61.9 us (26%)
  between operations  14.2 us (6%)
  blocking collectives  12.1 us (5%)
  local copies, waits for them, and re-layouts  7.98 us (3%)
    all_to_all x7, waiting for transfers between devices, swap(): return lax.all_to_all(values, axis, split_axis=0, concat_axis=0, tiled=True)  44.5 us
    all_to_all x7, starting transfers between devices, swap(): return lax.all_to_all(values, axis, split_axis=0, concat_axis=0, tiled=True)  43.3 us
    pallas_call x2, Pallas kernels, attend(): pl.pallas_call(attend_kernel, in_specs=[smem] * 4 + [vmem] * 5 + [pl.Bloc...  32 us
    ppermute x2, waiting for transfers between devices, send_row(): lax.ppermute(opp, 'y', OPPOSITE)  13.9 us
    all_to_all x1, blocking collectives, swap(): return lax.all_to_all(values, axis, split_axis=0, concat_axis=0, tiled=True)  12.1 us
    ppermute x2, waiting for transfers between devices, send_row(): lax.ppermute(to_left, 'y', LEFT)  8.01 us
    pallas_call x1, Pallas kernels, weight_share(): pl.pallas_call(weight_kernel, grid=(d // 256,), in_specs=[part, part, who...  6.27 us
    pallas_call x1, Pallas kernels, node_grads(): pl.pallas_call(nodes_kernel, grid=(steps,), in_specs=[tile, SECOND, tile,...  6.26 us
  transfers between devices with their start and end apart: 21, of which 9 were waited for; matrix products, arithmetic and copies ran while one was open for 2% of the time, Pallas kernels for 27%

profile of v4, /device:TPU:8, one launch (start us, length us, event | category | flops | bytes accessed | tf_op | source)
XLA Modules:
  0.0 237.4 jit_solution(3776154498145286035)
XLA Ops:
  7.2 5.2 %project_kv.1 = bf16[8,256,256]{2,1,0:T(8,128)(2,1)} custom-call(bf16[256,1024]{1,0:T(8,128)(2,1)} %bitcast.23, bf16[1024,3072]{1,0:T(8,128)(2,1)} %wv_ref.3, bf16[1024,3072]{1,0:T(8,128)(2,1)} %wv_ref.3), custom_call_target="tpu_custom_call" | custom-call | tf_op jit(solution)/shard_map/project_kv/pallas_call | solution.py:108
  12.4 8.5 %all-to-all-start = ((bf16[8,256,256]{2,1,0:T(8,128)(2,1)}), bf16[8,256,256]{2,1,0:T(8,128)(2,1)S(1)}, u32[]{:S(2)}, u32[]{:S(2)}) async-start(bf16[8,256,256]{2,1,0:T(8,128)(2,1)} %project_kv.1), calls=%async_computation | async-start | bytes 2097152 | tf_op jit(solution)/shard_map/all_to_all | solution.py:351
  20.9 5.3 %project_qg.1 = (bf16[8,256,128]{2,1,0:T(8,128)(2,1)}, bf16[8,256,128]{2,1,0:T(8,128)(2,1)}) custom-call(bf16[256,1024]{1,0:T(8,128)(2,1)} %bitcast.24, bf16[256,1024]{1,0:T(8,128)(2,1)} %bitcast.35, bf16[1024,3072]{1,0:T(8,128)(2,1)} %wv_ref.3, bf16[1024,1024]{1,0:T(8,128)(2,1)} %wo_ref.3), custom_call_target="tpu_custom_call" | custom-call | tf_op jit(solution)/shard_map/project_qg/pallas_call | solution.py:127
  26.2 23.4 %all-to-all-done.x_ref = bf16[8,256,256]{2,1,0:T(8,128)(2,1)S(1)} async-done(((bf16[8,256,256]{2,1,0:T(8,128)(2,1)}), bf16[8,256,256]{2,1,0:T(8,128)(2,1)S(1)}, u32[]{:S(2)}, u32[]{:S(2)}) %all-to-all-start) | async-done | bytes 1048608 | tf_op jit(solution)/shard_map/all_to_all | solution.py:351
  49.6 3.5 %all-to-all-start.1 = ((bf16[8,256,128]{2,1,0:T(8,128)(2,1)}), bf16[8,256,128]{2,1,0:T(8,128)(2,1)S(1)}, u32[]{:S(2)}, u32[]{:S(2)}) async-start(bf16[8,256,128]{2,1,0:T(8,128)(2,1)} %get-tuple-element.23), calls=%async_computation.1 | async-start | bytes 1048576 | tf_op jit(solution)/shard_map/all_to_all | solution.py:351
  53.8 2.0 split_heads.1
  55.8 1.6 collective-permute-start
  57.8 2.3 collective-permute-start.2
  60.2 10.7 %all-to-all-done.1 = bf16[8,256,128]{2,1,0:T(8,128)(2,1)S(1)} async-done(((bf16[8,256,128]{2,1,0:T(8,128)(2,1)}), bf16[8,256,128]{2,1,0:T(8,128)(2,1)S(1)}, u32[]{:S(2)}, u32[]{:S(2)}) %all-to-all-start.1) | async-done | bytes 524320 | tf_op jit(solution)/shard_map/all_to_all | solution.py:351
  70.9 3.5 %all-to-all-start.2 = ((bf16[8,256,128]{2,1,0:T(8,128)(2,1)}), bf16[8,256,128]{2,1,0:T(8,128)(2,1)S(1)}, u32[]{:S(2)}, u32[]{:S(2)}) async-start(bf16[8,256,128]{2,1,0:T(8,128)(2,1)} %get-tuple-element.25), calls=%async_computation.2 | async-start | bytes 1048576 | tf_op jit(solution)/shard_map/all_to_all | solution.py:351
  74.5 1.9 hold.1.after_ref
  76.5 0.7 reshape.47.tab_ref
  77.4 0.7 select_reduce_fusion.order_ref
  78.1 1.6 collective-permute-start.6
  80.1 2.3 collective-permute-start.8
  82.4 1.0 collective-permute-done.2.opp_ref
  83.4 16.0 %attend.2 = (bf16[8,128,256]{2,1,0:T(8,128)(2,1)}, bf16[8,128,256]{2,1,0:T(8,128)(2,1)}, bf16[8,128,256]{2,1,0:T(8,128)(2,1)}, bf16[8,128,256]{2,1,0:T(8,128)(2,1)}, bf16[8,128,256]{2,1,0:T(8,128)(2,1)}) custom-call(s32[192]{0:T(256)} %reshape.47.tab_ref, s32[16]{0:T(128)} %get-tuple-element.42.cnt_ref, s32[16]{0:T(128)} %select_reduce_fusion.order_ref, ...), custom_call_target="tpu_custom_call" | custom-call | flops 25999998976 | bytes 6291456 | tf_op jit(solution)/shard_map/attend/pallas_call | solution.py:233
  99.4 0.8 copy-done.9
  100.2 6.9 %all-to-all-start.3 = ((bf16[8,128,256]{2,1,0:T(8,128)(2,1)}), bf16[8,128,256]{2,1,0:T(8,128)(2,1)S(1)}, u32[]{:S(2)}, u32[]{:S(2)}) async-start(bf16[8,128,256]{2,1,0:T(8,128)(2,1)} %gate.3.after_ref.oa_ref), calls=%async_computation.3 | async-start | bytes 1048576 | tf_op jit(solution)/shard_map/all_to_all | solution.py:351
  107.1 1.2 collective-permute-start.3
  108.2 0.9 collective-permute-start.4
  109.1 2.6 %collective-permute-start.5 = (bf16[8,128,256]{2,1,0:T(8,128)(2,1)}, bf16[8,128,256]{2,1,0:T(8,128)(2,1)S(1)}, u32[]{:S(2)}, u32[]{:S(2)}) collective-permute-start(bf16[8,128,256]{2,1,0:T(8,128)(2,1)} %get-tuple-element.29), channel_id=1, source_target_pairs={{0,16},{8,24},{16,0},{24,8},{1,17},{9,25},{17,1},{25,9},{2,18},{10... | collective-permute-start | bytes 1572872 | tf_op jit(solution)/shard_map/ppermute | solution.py:405
  111.7 16.0 %attend.3 = (bf16[8,128,256]{2,1,0:T(8,128)(2,1)}, bf16[8,128,256]{2,1,0:T(8,128)(2,1)}, bf16[8,128,256]{2,1,0:T(8,128)(2,1)}, bf16[8,128,256]{2,1,0:T(8,128)(2,1)}, bf16[8,128,256]{2,1,0:T(8,128)(2,1)}) custom-call(s32[192]{0:T(256)} %reshape.47.tab_ref, s32[16]{0:T(128)} %get-tuple-element.42.cnt_ref, s32[16]{0:T(128)} %select_reduce_fusion.order_ref, ...), custom_call_target="tpu_custom_call" | custom-call | flops 25999998976 | bytes 6291456 | tf_op jit(solution)/shard_map/attend/pallas_call | solution.py:233
  127.8 4.4 %collective-permute-done.5.refs_7_.d_ref = bf16[8,128,256]{2,1,0:T(8,128)(2,1)S(1)} collective-permute-done((bf16[8,128,256]{2,1,0:T(8,128)(2,1)}, bf16[8,128,256]{2,1,0:T(8,128)(2,1)S(1)}, u32[]{:S(2)}, u32[]{:S(2)}) %collective-permute-start.5) | collective-permute-done | bytes 524320 | tf_op jit(solution)/shard_map/ppermute | solution.py:405
  132.2 0.8 copy-done.7
  133.3 2.8 %sum_join.1.ka_ref = bf16[8,256,256]{2,1,0:T(8,128)(2,1)} custom-call(bf16[8,128,256]{2,1,0:T(8,128)(2,1)} %get-tuple-element.26.a_ref, bf16[8,128,256]{2,1,0:T(8,128)(2,1)} %copy-done.5, bf16[8,128,256]{2,1,0:T(8,128)(2,1)} %copy-done.6, bf16[8,128,256]{2,1,0:T(8,128)(2,1)} %copy-done.7, bf16[8,128,256]{2,1,0:T(8,128)(2,1)} %get-tuple-element.36.od_ref.ob_ref), custom_call_target="tpu_custom_call" | custom-call | tf_op jit(solution)/shard_map/sum_join/pallas_call | solution.py:389
  136.1 6.9 %all-to-all-start.4 = ((bf16[8,256,256]{2,1,0:T(8,128)(2,1)}), bf16[8,256,256]{2,1,0:T(8,128)(2,1)S(1)}, u32[]{:S(2)}, u32[]{:S(2)}) async-start(bf16[8,256,256]{2,1,0:T(8,128)(2,1)} %sum_join.1.ka_ref), calls=%async_computation.4 | async-start | bytes 2097152 | tf_op jit(solution)/shard_map/all_to_all | solution.py:351
  143.0 1.0 collective-permute-start.10
  144.0 1.8 collective-permute-start.11
  145.8 2.5 %collective-permute-start.9 = (bf16[8,128,256]{2,1,0:T(8,128)(2,1)S(1)}, bf16[8,128,256]{2,1,0:T(8,128)(2,1)}, u32[]{:S(2)}, u32[]{:S(2)}) collective-permute-start(bf16[8,128,256]{2,1,0:T(8,128)(2,1)S(1)} %copy-done.10), channel_id=1, source_target_pairs={{0,8},{8,16},{16,24},{24,0},{1,9},{9,17},{17,25},{25,1},{2,10},{10... | collective-permute-start | bytes 1572872 | tf_op jit(solution)/shard_map/ppermute | solution.py:403
  148.3 8.0 %collective-permute-done.10.refs_2_ = bf16[8,128,256]{2,1,0:T(8,128)(2,1)S(1)} collective-permute-done((bf16[8,128,256]{2,1,0:T(8,128)(2,1)S(1)}, bf16[8,128,256]{2,1,0:T(8,128)(2,1)S(1)}, u32[]{:S(2)}, u32[]{:S(2)}) %collective-permute-start.10) | collective-permute-done | bytes 524320 | tf_op jit(solution)/shard_map/ppermute | solution.py:404
  156.3 9.5 %collective-permute-done.11.refs_3_ = bf16[8,128,256]{2,1,0:T(8,128)(2,1)S(1)} collective-permute-done((bf16[8,128,256]{2,1,0:T(8,128)(2,1)S(1)}, bf16[8,128,256]{2,1,0:T(8,128)(2,1)S(1)}, u32[]{:S(2)}, u32[]{:S(2)}) %collective-permute-start.11) | collective-permute-done | bytes 524320 | tf_op jit(solution)/shard_map/ppermute | solution.py:405
  165.8 0.8 copy-done.14
  166.9 2.1 all-to-all-done.4.b_ref.refs_4_.ob_ref.ka_ref
  168.9 1.0 copy-done.1
  169.9 2.3 sum_parts.2.kb_ref
  172.2 4.8 %all-to-all-start.5 = ((bf16[8,128,256]{2,1,0:T(8,128)(2,1)}), bf16[8,128,256]{2,1,0:T(8,128)(2,1)S(1)}, u32[]{:S(2)}, u32[]{:S(2)}) async-start(bf16[8,128,256]{2,1,0:T(8,128)(2,1)} %sum_parts.2.kb_ref), calls=%async_computation.5 | async-start | bytes 1048576 | tf_op jit(solution)/shard_map/all_to_all | solution.py:351
  177.0 6.3 %weight_share.1 = bf16[1024,384]{1,0:T(8,128)(2,1)} custom-call(bf16[8,128,256]{2,1,0:T(8,128)(2,1)} %gate.3.after_ref.oa_ref, bf16[8,128,256]{2,1,0:T(8,128)(2,1)} %get-tuple-element.36.od_ref.ob_ref, bf16[8,256,256]{2,1,0:T(8,128)(2,1)} %sum_join.1.ka_ref, bf16[8,128,256]{2,1,0:T(8,128)(2,1)} %sum_parts.2.kb_ref, ...), custom_call_target="tpu_custom_call" | custom-call | tf_op jit(solution)/shard_map/weight_share/pallas_call | solution.py:458
  183.3 1.9 dynamic-slice_bitcast_fusion
  185.3 8.3 %all-to-all-done.5.kb_ref.refs_2_ = bf16[8,128,256]{2,1,0:T(8,128)(2,1)S(1)} async-done(((bf16[8,128,256]{2,1,0:T(8,128)(2,1)}), bf16[8,128,256]{2,1,0:T(8,128)(2,1)S(1)}, u32[]{:S(2)}, u32[]{:S(2)}) %all-to-all-start.5) | async-done | bytes 524320 | tf_op jit(solution)/shard_map/all_to_all | solution.py:351
  193.5 0.8 copy-done.3
  194.4 1.9 sum_parts.3
  196.4 9.2 %all-to-all-start.6 = ((bf16[16,32,384]{2,1,0:T(8,128)(2,1)}), bf16[16,32,384]{2,1,0:T(8,128)(2,1)S(1)}, u32[]{:S(2)}, u32[]{:S(2)}) async-start(bf16[16,32,384]{2,1,0:T(8,128)(2,1)} %bitcast.33), calls=%async_computation.6 | async-start | bytes 786432 | tf_op jit(solution)/shard_map/all_to_all | solution.py:351
  205.6 4.4 %project_out.1.refs_1_ = bf16[256,1024]{1,0:T(8,128)(2,1)} custom-call(bf16[8,128,256]{2,1,0:T(8,128)(2,1)} %copy-done.2, bf16[8,256,256]{2,1,0:T(8,128)(2,1)} %copy-done.1, bf16[1024,1024]{1,0:T(8,128)(2,1)} %wo_ref.3), custom_call_target="tpu_custom_call" | custom-call | tf_op jit(solution)/shard_map/project_out/pallas_call | solution.py:279
  210.0 6.3 %node_grads.1.refs_2_ = bf16[256,1024]{1,0:T(8,128)(2,1)} custom-call(bf16[8,128,256]{2,1,0:T(8,128)(2,1)} %copy-done.2, bf16[8,256,256]{2,1,0:T(8,128)(2,1)} %copy-done.1, bf16[8,256,256]{2,1,0:T(8,128)(2,1)} %copy-done.1, bf16[8,128,256]{2,1,0:T(8,128)(2,1)} %copy-done.3, bf16[1024,3072]{1,0:T(8,128)(2,1)} %wv_ref.3, bf16[1024,3072]{1,0:T(8,128)(2,1)} %wv_ref.3, ...), custom_call_target="tpu_custom_call" | custom-call | tf_op jit(solution)/shard_map/node_grads/pallas_call | solution.py:318
  216.3 0.6 reshape.55.refs_0_
  217.0 12.1 %all_to_all.40.x_ref = f32[8,4,384]{2,1,0:T(4,128)} all-to-all(f32[8,4,384]{2,1,0:T(4,128)} %gate.5), channel_id=1, replica_groups=mesh['x'=4,'c'=2,'y'=4,'z'=8] {'z'}, dimensions={0} | all-to-all | bytes 98304 | tf_op jit(solution)/shard_map/all_to_all | solution.py:351
  229.1 1.4 spread.1
  (66 shorter events, 2.8 us)
Async XLA Ops:
  7.2 46.5 %copy-start = (s32[1,64,8]{1,2,0:T(8,128)S(1)}, s32[1,64,8]{1,2,0:T(8,128)}, u32[]{:S(2)}) copy-start(s32[1,64,8]{1,2,0:T(8,128)} %param.11) | copy-start | bytes 6148
  12.4 37.2 %all-to-all-start = ((bf16[8,256,256]{2,1,0:T(8,128)(2,1)}), bf16[8,256,256]{2,1,0:T(8,128)(2,1)S(1)}, u32[]{:S(2)}, u32[]{:S(2)}) async-start(bf16[8,256,256]{2,1,0:T(8,128)(2,1)} %project_kv.1), calls=%async_computation | async-start | bytes 2097152 | tf_op jit(solution)/shard_map/all_to_all | solution.py:351
  20.8 32.2 %copy-start.20 = (s32[1,4]{1,0:T(1,128)S(1)}, s32[1,4]{1,0:T(1,128)}, u32[]{:S(2)}) copy-start(s32[1,4]{1,0:T(1,128)} %param.13) | copy-start | bytes 52
  20.8 32.3 %copy-start.16 = (s32[1,64]{1,0:T(1,128)S(1)}, s32[1,64]{1,0:T(1,128)}, u32[]{:S(2)}) copy-start(s32[1,64]{1,0:T(1,128)} %param.12) | copy-start | bytes 772
  49.6 4.2 %copy-start.4 = (bf16[8,256,256]{2,1,0:T(8,128)(2,1)}, bf16[8,256,256]{2,1,0:T(8,128)(2,1)S(1)}, u32[]{:S(2)}) copy-start(bf16[8,256,256]{2,1,0:T(8,128)(2,1)S(1)} %all-to-all-done.x_ref) | copy-start | bytes 3145732
  49.6 21.4 %all-to-all-start.1 = ((bf16[8,256,128]{2,1,0:T(8,128)(2,1)}), bf16[8,256,128]{2,1,0:T(8,128)(2,1)S(1)}, u32[]{:S(2)}, u32[]{:S(2)}) async-start(bf16[8,256,128]{2,1,0:T(8,128)(2,1)} %get-tuple-element.23), calls=%async_computation.1 | async-start | bytes 1048576 | tf_op jit(solution)/shard_map/all_to_all | solution.py:351
  55.8 24.3 %collective-permute-start = (bf16[8,128,256]{2,1,0:T(8,128)(2,1)}, bf16[8,128,256]{2,1,0:T(8,128)(2,1)S(1)}, u32[]{:S(2)}, u32[]{:S(2)}) collective-permute-start(bf16[8,128,256]{2,1,0:T(8,128)(2,1)} %get-tuple-element.22.own_ref), channel_id=1, source_target_pairs={{0,8},{8,16},{16,24},{24,0},{1,9},{9,17},{17,25},{25,1},{2,10},{10... | collective-permute-start | bytes 1572872 | tf_op jit(solution)/shard_map/ppermute | solution.py:360
  57.4 25.0 %collective-permute-start.1 = (bf16[8,128,256]{2,1,0:T(8,128)(2,1)}, bf16[8,128,256]{2,1,0:T(8,128)(2,1)S(1)}, u32[]{:S(2)}, u32[]{:S(2)}) collective-permute-start(bf16[8,128,256]{2,1,0:T(8,128)(2,1)} %get-tuple-element.22.own_ref), channel_id=1, source_target_pairs={{0,24},{8,0},{16,8},{24,16},{1,25},{9,1},{17,9},{25,17},{2,26},{10... | collective-permute-start | bytes 1572872 | tf_op jit(solution)/shard_map/ppermute | solution.py:360
  57.8 25.5 %collective-permute-start.2 = (bf16[8,128,256]{2,1,0:T(8,128)(2,1)}, bf16[8,128,256]{2,1,0:T(8,128)(2,1)}, u32[]{:S(2)}, u32[]{:S(2)}) collective-permute-start(bf16[8,128,256]{2,1,0:T(8,128)(2,1)} %get-tuple-element.22.own_ref), channel_id=1, source_target_pairs={{0,16},{8,24},{16,0},{24,8},{1,17},{9,25},{17,1},{25,9},{2,18},{10... | collective-permute-start | bytes 1572872 | tf_op jit(solution)/shard_map/ppermute | solution.py:360
  70.9 3.6 %copy-start.8 = (bf16[8,256,128]{2,1,0:T(8,128)(2,1)}, bf16[8,256,128]{2,1,0:T(8,128)(2,1)S(1)}, u32[]{:S(2)}) copy-start(bf16[8,256,128]{2,1,0:T(8,128)(2,1)S(1)} %all-to-all-done.1) | copy-start | bytes 1572868
  70.9 28.5 %all-to-all-start.2 = ((bf16[8,256,128]{2,1,0:T(8,128)(2,1)}), bf16[8,256,128]{2,1,0:T(8,128)(2,1)S(1)}, u32[]{:S(2)}, u32[]{:S(2)}) async-start(bf16[8,256,128]{2,1,0:T(8,128)(2,1)} %get-tuple-element.25), calls=%async_computation.2 | async-start | bytes 1048576 | tf_op jit(solution)/shard_map/all_to_all | solution.py:351
  74.4 102.6 %all-gather.2.cloned.1.call-start = ((), (), s32[]{:S(2)}) async-start(), calls=%async_computation.8 | async-start | bytes 4718592 | tf_op jit(solution)/shard_map/all_gather | solution.py:488
  78.1 31.0 %collective-permute-start.6 = (bf16[8,128,256]{2,1,0:T(8,128)(2,1)}, bf16[8,128,256]{2,1,0:T(8,128)(2,1)S(1)}, u32[]{:S(2)}, u32[]{:S(2)}) collective-permute-start(bf16[8,128,256]{2,1,0:T(8,128)(2,1)} %get-tuple-element.30.own_ref), channel_id=1, source_target_pairs={{0,8},{8,16},{16,24},{24,0},{1,9},{9,17},{17,25},{25,1},{2,10},{10... | collective-permute-start | bytes 1572872 | tf_op jit(solution)/shard_map/ppermute | solution.py:360
  79.6 32.1 %collective-permute-start.7 = (bf16[8,128,256]{2,1,0:T(8,128)(2,1)}, bf16[8,128,256]{2,1,0:T(8,128)(2,1)}, u32[]{:S(2)}, u32[]{:S(2)}) collective-permute-start(bf16[8,128,256]{2,1,0:T(8,128)(2,1)} %get-tuple-element.30.own_ref), channel_id=1, source_target_pairs={{0,24},{8,0},{16,8},{24,16},{1,25},{9,1},{17,9},{25,17},{2,26},{10... | collective-permute-start | bytes 1572872 | tf_op jit(solution)/shard_map/ppermute | solution.py:360
  80.1 3.3 %copy-start.17 = (bf16[8,128,256]{2,1,0:T(8,128)(2,1)}, bf16[8,128,256]{2,1,0:T(8,128)(2,1)S(1)}, u32[]{:S(2)}) copy-start(bf16[8,128,256]{2,1,0:T(8,128)(2,1)S(1)} %collective-permute-done.left_ref) | copy-start | bytes 1572868
  80.1 31.6 %collective-permute-start.8 = (bf16[8,128,256]{2,1,0:T(8,128)(2,1)}, bf16[8,128,256]{2,1,0:T(8,128)(2,1)}, u32[]{:S(2)}, u32[]{:S(2)}) collective-permute-start(bf16[8,128,256]{2,1,0:T(8,128)(2,1)} %get-tuple-element.30.own_ref), channel_id=1, source_target_pairs={{0,16},{8,24},{16,0},{24,8},{1,17},{9,25},{17,1},{25,9},{2,18},{10... | collective-permute-start | bytes 1572872 | tf_op jit(solution)/shard_map/ppermute | solution.py:360
  82.4 1.0 copy-start.19
  99.4 0.8 copy-start.9
  100.2 32.0 %all-to-all-start.3 = ((bf16[8,128,256]{2,1,0:T(8,128)(2,1)}), bf16[8,128,256]{2,1,0:T(8,128)(2,1)S(1)}, u32[]{:S(2)}, u32[]{:S(2)}) async-start(bf16[8,128,256]{2,1,0:T(8,128)(2,1)} %gate.3.after_ref.oa_ref), calls=%async_computation.3 | async-start | bytes 1048576 | tf_op jit(solution)/shard_map/all_to_all | solution.py:351
  107.1 20.7 %collective-permute-start.3 = (bf16[8,128,256]{2,1,0:T(8,128)(2,1)}, bf16[8,128,256]{2,1,0:T(8,128)(2,1)S(1)}, u32[]{:S(2)}, u32[]{:S(2)}) collective-permute-start(bf16[8,128,256]{2,1,0:T(8,128)(2,1)} %get-tuple-element.27), channel_id=1, source_target_pairs={{0,8},{8,16},{16,24},{24,0},{1,9},{9,17},{17,25},{25,1},{2,10},{10... | collective-permute-start | bytes 1572872 | tf_op jit(solution)/shard_map/ppermute | solution.py:403
  108.2 19.5 %collective-permute-start.4 = (bf16[8,128,256]{2,1,0:T(8,128)(2,1)}, bf16[8,128,256]{2,1,0:T(8,128)(2,1)S(1)}, u32[]{:S(2)}, u32[]{:S(2)}) collective-permute-start(bf16[8,128,256]{2,1,0:T(8,128)(2,1)} %get-tuple-element.28), channel_id=1, source_target_pairs={{0,24},{8,0},{16,8},{24,16},{1,25},{9,1},{17,9},{25,17},{2,26},{10... | collective-permute-start | bytes 1572872 | tf_op jit(solution)/shard_map/ppermute | solution.py:404
  109.1 2.6 %copy-start.18 = (bf16[8,128,256]{2,1,0:T(8,128)(2,1)}, bf16[8,128,256]{2,1,0:T(8,128)(2,1)S(1)}, u32[]{:S(2)}) copy-start(bf16[8,128,256]{2,1,0:T(8,128)(2,1)S(1)} %collective-permute-done.6.left_ref) | copy-start | bytes 1572868
  109.1 23.1 %collective-permute-start.5 = (bf16[8,128,256]{2,1,0:T(8,128)(2,1)}, bf16[8,128,256]{2,1,0:T(8,128)(2,1)S(1)}, u32[]{:S(2)}, u32[]{:S(2)}) collective-permute-start(bf16[8,128,256]{2,1,0:T(8,128)(2,1)} %get-tuple-element.29), channel_id=1, source_target_pairs={{0,16},{8,24},{16,0},{24,8},{1,17},{9,25},{17,1},{25,9},{2,18},{10... | collective-permute-start | bytes 1572872 | tf_op jit(solution)/shard_map/ppermute | solution.py:405
  127.8 4.5 %copy-start.5 = (bf16[8,128,256]{2,1,0:T(8,128)(2,1)}, bf16[8,128,256]{2,1,0:T(8,128)(2,1)S(1)}, u32[]{:S(2)}) copy-start(bf16[8,128,256]{2,1,0:T(8,128)(2,1)S(1)} %collective-permute-done.3.refs_5_.b_ref) | copy-start | bytes 1572868
  127.8 4.5 %copy-start.6 = (bf16[8,128,256]{2,1,0:T(8,128)(2,1)}, bf16[8,128,256]{2,1,0:T(8,128)(2,1)S(1)}, u32[]{:S(2)}) copy-start(bf16[8,128,256]{2,1,0:T(8,128)(2,1)S(1)} %collective-permute-done.4.refs_6_.c_ref) | copy-start | bytes 1572868
  132.2 0.9 copy-start.7
  132.2 1.1 copy-start.2
  133.3 9.7 %copy-start.11 = (bf16[8,128,256]{2,1,0:T(8,128)(2,1)S(1)}, bf16[8,128,256]{2,1,0:T(8,128)(2,1)}, u32[]{:S(2)}) copy-start(bf16[8,128,256]{2,1,0:T(8,128)(2,1)} %get-tuple-element.39) | copy-start | bytes 1572868
  133.3 10.7 %copy-start.12 = (bf16[8,128,256]{2,1,0:T(8,128)(2,1)S(1)}, bf16[8,128,256]{2,1,0:T(8,128)(2,1)}, u32[]{:S(2)}) copy-start(bf16[8,128,256]{2,1,0:T(8,128)(2,1)} %get-tuple-element.40) | copy-start | bytes 1572868
  133.3 12.5 %copy-start.10 = (bf16[8,128,256]{2,1,0:T(8,128)(2,1)S(1)}, bf16[8,128,256]{2,1,0:T(8,128)(2,1)}, u32[]{:S(2)}) copy-start(bf16[8,128,256]{2,1,0:T(8,128)(2,1)} %get-tuple-element.38) | copy-start | bytes 1572868
  136.1 32.9 %all-to-all-start.4 = ((bf16[8,256,256]{2,1,0:T(8,128)(2,1)}), bf16[8,256,256]{2,1,0:T(8,128)(2,1)S(1)}, u32[]{:S(2)}, u32[]{:S(2)}) async-start(bf16[8,256,256]{2,1,0:T(8,128)(2,1)} %sum_join.1.ka_ref), calls=%async_computation.4 | async-start | bytes 2097152 | tf_op jit(solution)/shard_map/all_to_all | solution.py:351
  143.0 13.3 %collective-permute-start.10 = (bf16[8,128,256]{2,1,0:T(8,128)(2,1)S(1)}, bf16[8,128,256]{2,1,0:T(8,128)(2,1)S(1)}, u32[]{:S(2)}, u32[]{:S(2)}) collective-permute-start(bf16[8,128,256]{2,1,0:T(8,128)(2,1)S(1)} %copy-done.11), channel_id=1, source_target_pairs={{0,24},{8,0},{16,8},{24,16},{1,25},{9,1},{17,9},{25,17},{2,26},{10... | collective-permute-start | bytes 1572872 | tf_op jit(solution)/shard_map/ppermute | solution.py:404
  144.0 21.8 %collective-permute-start.11 = (bf16[8,128,256]{2,1,0:T(8,128)(2,1)S(1)}, bf16[8,128,256]{2,1,0:T(8,128)(2,1)S(1)}, u32[]{:S(2)}, u32[]{:S(2)}) collective-permute-start(bf16[8,128,256]{2,1,0:T(8,128)(2,1)S(1)} %copy-done.12), channel_id=1, source_target_pairs={{0,16},{8,24},{16,0},{24,8},{1,17},{9,25},{17,1},{25,9},{2,18},{10... | collective-permute-start | bytes 1572872 | tf_op jit(solution)/shard_map/ppermute | solution.py:405
  145.8 21.0 %collective-permute-start.9 = (bf16[8,128,256]{2,1,0:T(8,128)(2,1)S(1)}, bf16[8,128,256]{2,1,0:T(8,128)(2,1)}, u32[]{:S(2)}, u32[]{:S(2)}) collective-permute-start(bf16[8,128,256]{2,1,0:T(8,128)(2,1)S(1)} %copy-done.10), channel_id=1, source_target_pairs={{0,8},{8,16},{16,24},{24,0},{1,9},{9,17},{17,25},{25,1},{2,10},{10... | collective-permute-start | bytes 1572872 | tf_op jit(solution)/shard_map/ppermute | solution.py:403
  156.3 12.6 %copy-start.13 = (bf16[8,128,256]{2,1,0:T(8,128)(2,1)}, bf16[8,128,256]{2,1,0:T(8,128)(2,1)S(1)}, u32[]{:S(2)}) copy-start(bf16[8,128,256]{2,1,0:T(8,128)(2,1)S(1)} %collective-permute-done.10.refs_2_) | copy-start | bytes 1572868
  165.8 0.8 copy-start.14
  168.9 1.0 copy-start.1
  172.2 21.3 %all-to-all-start.5 = ((bf16[8,128,256]{2,1,0:T(8,128)(2,1)}), bf16[8,128,256]{2,1,0:T(8,128)(2,1)S(1)}, u32[]{:S(2)}, u32[]{:S(2)}) async-start(bf16[8,128,256]{2,1,0:T(8,128)(2,1)} %sum_parts.2.kb_ref), calls=%async_computation.5 | async-start | bytes 1048576 | tf_op jit(solution)/shard_map/all_to_all | solution.py:351
  185.3 8.3 %collective-permute-start.12 = (bf16[4,128,384]{2,1,0:T(8,128)(2,1)S(1)}, bf16[4,128,384]{2,1,0:T(8,128)(2,1)S(1)}, u32[]{:S(2)}, u32[]{:S(2)}) collective-permute-start(bf16[4,128,384]{2,1,0:T(8,128)(2,1)S(1)} %get-tuple-element.43), channel_id=1, source_target_pairs={{0,32},{32,0},{1,33},{33,1},{2,34},{34,2},{3,35},{35,3},{4,36},{36... | collective-permute-start | bytes 1179656 | tf_op jit(solution)/shard_map/ppermute | solution.py:509
  193.5 0.8 copy-start.3
  193.5 0.9 copy-start.15
  196.4 19.9 %all-to-all-start.6 = ((bf16[16,32,384]{2,1,0:T(8,128)(2,1)}), bf16[16,32,384]{2,1,0:T(8,128)(2,1)S(1)}, u32[]{:S(2)}, u32[]{:S(2)}) async-start(bf16[16,32,384]{2,1,0:T(8,128)(2,1)} %bitcast.33), calls=%async_computation.6 | async-start | bytes 786432 | tf_op jit(solution)/shard_map/all_to_all | solution.py:351
Sparse Core Ops, SparseCore 0:
  77.1 69.1 all-gather.1

commit v5 on v4

--- a/solution.py
+++ b/solution.py
@@ -95,7 +95,13 @@
     )(both)
 
 
-def qg_kernel(f_ref, c_ref, wq_ref, wo_ref, a_ref, b_ref):
+def qg_kernel(f_ref, c_ref, wq_ref, wo_ref, *refs):
+    a_ref, b_ref, copy_ref = refs[-3:]
+
+    @pl.when(pl.program_id(0) == 0)
+    def _():
+        copy_ref[...] = f_ref[...]
+
     put_pairs(nn(f_ref[...], wq_ref[...]), nt(c_ref[...], wo_ref[...]), a_ref, b_ref)
 
 
@@ -120,7 +126,7 @@
     )(feats, w_qkv, w_qkv)
 
 
-def project_qg(feats, cot, w_qkv, w_out):
+def project_qg(feats, cot, w_qkv, w_out, before):
     d = feats.shape[1]
     out = jax.ShapeDtypeStruct((ZS, NODE_DEV, 128), bf16)
     tile = pl.BlockSpec((2, NODE_DEV, 128), lambda i: (i, 0, 0))
@@ -132,12 +138,13 @@
             whole((NODE_DEV, d)),
             pl.BlockSpec((d, 256), lambda i: (0, i)),
             pl.BlockSpec((256, d), lambda i: (i, 0)),
-        ],
-        out_specs=[tile, tile],
-        out_shape=[out, out],
+        ]
+        + [pl.BlockSpec(memory_space=pl.ANY)] * len(before),
+        out_specs=[tile, tile, whole((NODE_DEV, d))],
+        out_shape=[out, out, jax.ShapeDtypeStruct((NODE_DEV, d), bf16)],
         compiler_params=VMEM,
         name="project_qg",
-    )(feats, cot, w_qkv, w_out)
+    )(feats, cot, w_qkv, w_out, *before)
 
 
 def attend_kernel(
@@ -328,23 +335,26 @@
     )(od_a, joint, joint, kv_b, w_qkv, w_qkv, w_qkv)
 
 
-def spread_kernel(x_ref, o_ref):
+def spread_kernel(x_ref, *refs):
+    o_ref = refs[-1]
+    parts = x_ref[...].astype(f32).reshape(x_ref.shape[0] // ZS, ZS, *x_ref.shape[1:])
+    total = jnp.sum(parts, axis=0)
     for z in range(ZS):
         for third in range(3):
             cols = third * H * HD + z * 128
-            o_ref[:, cols : cols + 128] = x_ref[z, :, third * 128 : (third + 1) * 128]
-
-
-def spread(share):
+            o_ref[:, cols : cols + 128] = total[z, :, third * 128 : (third + 1) * 128]
+
+
+def spread(share, after):
     vmem = pl.BlockSpec(memory_space=pltpu.VMEM)
     return pl.pallas_call(
         spread_kernel,
-        in_specs=[vmem],
+        in_specs=[vmem] + [pl.BlockSpec(memory_space=pl.ANY)] * len(after),
         out_specs=vmem,
         out_shape=jax.ShapeDtypeStruct((share.shape[1], 3 * H * HD), f32),
         compiler_params=VMEM,
         name="spread",
-    )(share)
+    )(share, *after)
 
 
 def swap(values, axis):
@@ -404,22 +414,6 @@
         lax.ppermute(to_left, "y", LEFT),
         lax.ppermute(opp, "y", OPPOSITE),
     ]
-
-
-def hold_kernel(x_ref, after_ref, o_ref):
-    o_ref[...] = x_ref[...]
-
-
-def hold(values, after):
-    vmem = pl.BlockSpec(memory_space=pltpu.VMEM)
-    return pl.pallas_call(
-        hold_kernel,
-        in_specs=[vmem, pl.BlockSpec(memory_space=pl.ANY)],
-        out_specs=vmem,
-        out_shape=jax.ShapeDtypeStruct(values.shape, values.dtype),
-        compiler_params=VMEM,
-        name="hold",
-    )(values, after)
 
 
 def gate_kernel(*refs):
@@ -481,10 +475,10 @@
     y_arr = y.reshape(1).astype(jnp.int32)
 
     kv = project_kv(feats, w_qkv)
-    qg = project_qg(feats, cot, w_qkv, w_out)
+    *qg, feats_copy = project_qg(feats, cot, w_qkv, w_out, (table, counts, order))
     kv_row = [gather_row(v) for v in split_heads(swap(kv, "z"))]
     qg_row = [swap(v, "z").reshape(ROW, 128) for v in qg]
-    feats_late = hold(feats, qg_row[0])
+    (feats_late,) = gate([feats_copy], [qg_row[0]])
     feats_row = lax.all_gather(feats_late, "z", axis=0, tiled=True)
     od_a, *kv_a = attend(table, counts, order, y_arr, kv_row[0], qg_row[0], feats_late)
     to_nodes = lambda v: swap(v, "z")
@@ -508,10 +502,8 @@
     mine, theirs = (lax.dynamic_index_in_dim(share, k, 1, keepdims=False) for k in (c, 1 - c))
     theirs = lax.ppermute(theirs, "c", [(0, 1), (1, 0)])
     share = sum_parts([v.reshape(d // 2, 384) for v in (mine, theirs)], (kv_nodes_b,))
-    share = share.reshape(16, d // 32, 384)
-    share = jnp.sum(swap(share, ("x", "y")).astype(f32), axis=0)
-    share = gate([share.reshape(ZS, d // 256, 384)], [attn_update, grad_nodes])[0]
-    grad_weights = spread(swap(share, "z"))
+    share = swap(share.reshape(16 * ZS, d // 256, 384), ("x", "y", "z"))
+    grad_weights = spread(share, (attn_update, grad_nodes))
     return attn_update[None], grad_nodes[None], grad_weights
 
 

time: 238 us -> 232 us (0.975)
  blocking collectives: 12.1 us -> 0 us
  local copies, waits for them, and re-layouts: 7.98 us -> 12.2 us
    all_to_all x1 -> x0, blocking collectives: 12.1 us -> none  [swap(): return lax.all_to_all(values, axis, split_axis=0, concat_axis=0, tiled=True)]
    ppermute x2, waiting for transfers between devices: 13.9 us -> 2.96 us  [send_row(): lax.ppermute(opp, 'y', OPPOSITE)]
    ppermute x2, waiting for transfers between devices: 8.01 us -> 15.3 us  [send_row(): lax.ppermute(to_left, 'y', LEFT)]
    ppermute x2, waiting for transfers between devices: 0.97 us -> 4.03 us  [gather_row(): lax.ppermute(own, 'y', OPPOSITE)]
    unnamed x42 -> x46, local copies, waits for them, and re-layouts: 4.58 us -> 7.55 us
    ppermute x2, starting transfers between devices: 4.45 us -> 2.01 us  [send_row(): lax.ppermute(opp, 'y', OPPOSITE)]
  transfers between devices with their start and end apart: 21 -> 21, of which waited for: 9 -> 9; matrix products, arithmetic and copies ran while one was open for 2% -> 2% of each run, Pallas kernels for 27% -> 28%
where the time goes in v5:
time: 232 us; the launch traced here: 229 us
  Pallas kernels  72.3 us (31%)
  waiting for transfers between devices  67.6 us (29%)
  starting transfers between devices  61.6 us (27%)
  between operations  14.2 us (6%)
  local copies, waits for them, and re-layouts  12.2 us (5%)
    all_to_all x7, starting transfers between devices, swap(): return lax.all_to_all(values, axis, split_axis=0, concat_axis=0, tiled=True)  44.7 us
    all_to_all x7, waiting for transfers between devices, swap(): return lax.all_to_all(values, axis, split_axis=0, concat_axis=0, tiled=True)  44.2 us
    pallas_call x2, Pallas kernels, attend(): pl.pallas_call(attend_kernel, in_specs=[smem] * 4 + [vmem] * 5 + [pl.Bloc...  34.1 us
    ppermute x2, waiting for transfers between devices, send_row(): lax.ppermute(to_left, 'y', LEFT)  15.3 us
    unnamed x46, local copies, waits for them, and re-layouts  7.55 us
    pallas_call x1, Pallas kernels, weight_share(): pl.pallas_call(weight_kernel, grid=(d // 256,), in_specs=[part, part, who...  6.27 us
    pallas_call x1, Pallas kernels, node_grads(): pl.pallas_call(nodes_kernel, grid=(steps,), in_specs=[tile, SECOND, tile,...  6.26 us
    pallas_call x1, Pallas kernels, project_qg(): pl.pallas_call(qg_kernel, grid=(ZS // 2,), in_specs=[whole((NODE_DEV, d))...  5.33 us
  transfers between devices with their start and end apart: 21, of which 9 were waited for; matrix products, arithmetic and copies ran while one was open for 2% of the time, Pallas kernels for 28%

profile of v5, /device:TPU:8, one launch (start us, length us, event | category | flops | bytes accessed | tf_op | source)
XLA Modules:
  0.0 229.4 jit_solution(4635776208867290273)
XLA Ops:
  7.2 5.2 %project_kv.1 = bf16[8,256,256]{2,1,0:T(8,128)(2,1)} custom-call(bf16[256,1024]{1,0:T(8,128)(2,1)} %bitcast.23, bf16[1024,3072]{1,0:T(8,128)(2,1)} %wv_ref.3, bf16[1024,3072]{1,0:T(8,128)(2,1)} %wv_ref.3), custom_call_target="tpu_custom_call" | custom-call | tf_op jit(solution)/shard_map/project_kv/pallas_call | solution.py:114
  12.4 8.5 %all-to-all-start = ((bf16[8,256,256]{2,1,0:T(8,128)(2,1)}), bf16[8,256,256]{2,1,0:T(8,128)(2,1)S(1)}, u32[]{:S(2)}, u32[]{:S(2)}) async-start(bf16[8,256,256]{2,1,0:T(8,128)(2,1)} %project_kv.1), calls=%async_computation | async-start | bytes 2097152 | tf_op jit(solution)/shard_map/all_to_all | solution.py:361
  21.1 0.7 reshape.44.refs_0_.tab_ref
  22.6 0.6 select_reduce_fusion.refs_2_.order_ref
  23.2 5.3 %project_qg.1 = (bf16[8,256,128]{2,1,0:T(8,128)(2,1)}, bf16[8,256,128]{2,1,0:T(8,128)(2,1)}, bf16[256,1024]{1,0:T(8,128)(2,1)}) custom-call(bf16[256,1024]{1,0:T(8,128)(2,1)} %bitcast.24, bf16[256,1024]{1,0:T(8,128)(2,1)} %bitcast.32, bf16[1024,3072]{1,0:T(8,128)(2,1)} %wv_ref.3, bf16[1024,1024]{1,0:T(8,128)(2,1)} %wo_ref.3, s32[192]{0:T(256)} %reshape.44.refs_0_.tab_ref, ...), custom_call_target="tpu_custom_call" | custom-call | tf_op jit(solution)/shard_map/project_qg/pallas_call | solution.py:133
  28.5 21.0 %all-to-all-done.x_ref = bf16[8,256,256]{2,1,0:T(8,128)(2,1)S(1)} async-done(((bf16[8,256,256]{2,1,0:T(8,128)(2,1)}), bf16[8,256,256]{2,1,0:T(8,128)(2,1)S(1)}, u32[]{:S(2)}, u32[]{:S(2)}) %all-to-all-start) | async-done | bytes 1048608 | tf_op jit(solution)/shard_map/all_to_all | solution.py:361
  49.6 3.5 %all-to-all-start.1 = ((bf16[8,256,128]{2,1,0:T(8,128)(2,1)}), bf16[8,256,128]{2,1,0:T(8,128)(2,1)S(1)}, u32[]{:S(2)}, u32[]{:S(2)}) async-start(bf16[8,256,128]{2,1,0:T(8,128)(2,1)} %get-tuple-element.24), calls=%async_computation.1 | async-start | bytes 1048576 | tf_op jit(solution)/shard_map/all_to_all | solution.py:361
  53.1 2.0 split_heads.1
  55.2 1.6 collective-permute-start
  57.2 2.3 %collective-permute-start.2 = (bf16[8,128,256]{2,1,0:T(8,128)(2,1)}, bf16[8,128,256]{2,1,0:T(8,128)(2,1)S(1)}, u32[]{:S(2)}, u32[]{:S(2)}) collective-permute-start(bf16[8,128,256]{2,1,0:T(8,128)(2,1)} %get-tuple-element.23.own_ref), channel_id=1, source_target_pairs={{0,16},{8,24},{16,0},{24,8},{1,17},{9,25},{17,1},{25,9},{2,18},{10... | collective-permute-start | bytes 1572872 | tf_op jit(solution)/shard_map/ppermute | solution.py:370
  59.5 11.4 %all-to-all-done.1 = bf16[8,256,128]{2,1,0:T(8,128)(2,1)S(1)} async-done(((bf16[8,256,128]{2,1,0:T(8,128)(2,1)}), bf16[8,256,128]{2,1,0:T(8,128)(2,1)S(1)}, u32[]{:S(2)}, u32[]{:S(2)}) %all-to-all-start.1) | async-done | bytes 524320 | tf_op jit(solution)/shard_map/all_to_all | solution.py:361
  70.9 0.9 copy-done.9
  71.8 3.5 %all-to-all-start.2 = ((bf16[8,256,128]{2,1,0:T(8,128)(2,1)}), bf16[8,256,128]{2,1,0:T(8,128)(2,1)S(1)}, u32[]{:S(2)}, u32[]{:S(2)}) async-start(bf16[8,256,128]{2,1,0:T(8,128)(2,1)} %get-tuple-element.27), calls=%async_computation.2 | async-start | bytes 1048576 | tf_op jit(solution)/shard_map/all_to_all | solution.py:361
  75.3 1.7 collective-permute-start.6
  77.4 2.3 %collective-permute-start.8 = (bf16[8,128,256]{2,1,0:T(8,128)(2,1)}, bf16[8,128,256]{2,1,0:T(8,128)(2,1)}, u32[]{:S(2)}, u32[]{:S(2)}) collective-permute-start(bf16[8,128,256]{2,1,0:T(8,128)(2,1)} %get-tuple-element.32.own_ref), channel_id=1, source_target_pairs={{0,16},{8,24},{16,0},{24,8},{1,17},{9,25},{17,1},{25,9},{2,18},{10... | collective-permute-start | bytes 1572872 | tf_op jit(solution)/shard_map/ppermute | solution.py:370
  79.8 4.0 %collective-permute-done.2.opp_ref = bf16[8,128,256]{2,1,0:T(8,128)(2,1)S(1)} collective-permute-done((bf16[8,128,256]{2,1,0:T(8,128)(2,1)}, bf16[8,128,256]{2,1,0:T(8,128)(2,1)S(1)}, u32[]{:S(2)}, u32[]{:S(2)}) %collective-permute-start.2) | collective-permute-done | bytes 524320 | tf_op jit(solution)/shard_map/ppermute | solution.py:370
  83.8 0.8 copy-done.21
  84.6 17.0 %attend.2 = (bf16[8,128,256]{2,1,0:T(8,128)(2,1)}, bf16[8,128,256]{2,1,0:T(8,128)(2,1)}, bf16[8,128,256]{2,1,0:T(8,128)(2,1)}, bf16[8,128,256]{2,1,0:T(8,128)(2,1)}, bf16[8,128,256]{2,1,0:T(8,128)(2,1)}) custom-call(s32[192]{0:T(256)} %reshape.44.refs_0_.tab_ref, s32[16]{0:T(128)} %get-tuple-element.44.refs_1_.cnt_ref, ...), custom_call_target="tpu_custom_call" | custom-call | flops 25999998976 | bytes 6291456 | tf_op jit(solution)/shard_map/attend/pallas_call | solution.py:240
  101.6 0.8 copy-done.8
  102.4 7.1 %all-to-all-start.3 = ((bf16[8,128,256]{2,1,0:T(8,128)(2,1)}), bf16[8,128,256]{2,1,0:T(8,128)(2,1)S(1)}, u32[]{:S(2)}, u32[]{:S(2)}) async-start(bf16[8,128,256]{2,1,0:T(8,128)(2,1)} %gate.4.after_ref.oa_ref), calls=%async_computation.3 | async-start | bytes 1048576 | tf_op jit(solution)/shard_map/all_to_all | solution.py:361
  109.5 2.0 collective-permute-start.4
  112.3 17.1 %attend.3 = (bf16[8,128,256]{2,1,0:T(8,128)(2,1)}, bf16[8,128,256]{2,1,0:T(8,128)(2,1)}, bf16[8,128,256]{2,1,0:T(8,128)(2,1)}, bf16[8,128,256]{2,1,0:T(8,128)(2,1)}, bf16[8,128,256]{2,1,0:T(8,128)(2,1)}) custom-call(s32[192]{0:T(256)} %reshape.44.refs_0_.tab_ref, s32[16]{0:T(128)} %get-tuple-element.44.refs_1_.cnt_ref, ...), custom_call_target="tpu_custom_call" | custom-call | flops 25999998976 | bytes 6291456 | tf_op jit(solution)/shard_map/attend/pallas_call | solution.py:240
  129.4 3.0 %collective-permute-done.5.refs_7_.d_ref = bf16[8,128,256]{2,1,0:T(8,128)(2,1)S(1)} collective-permute-done((bf16[8,128,256]{2,1,0:T(8,128)(2,1)}, bf16[8,128,256]{2,1,0:T(8,128)(2,1)S(1)}, u32[]{:S(2)}, u32[]{:S(2)}) %collective-permute-start.5) | collective-permute-done | bytes 524320 | tf_op jit(solution)/shard_map/ppermute | solution.py:415
  132.4 0.8 copy-done.7
  133.4 2.7 %sum_join.1.ka_ref = bf16[8,256,256]{2,1,0:T(8,128)(2,1)} custom-call(bf16[8,128,256]{2,1,0:T(8,128)(2,1)} %get-tuple-element.28.a_ref, bf16[8,128,256]{2,1,0:T(8,128)(2,1)} %copy-done.5, bf16[8,128,256]{2,1,0:T(8,128)(2,1)} %copy-done.6, bf16[8,128,256]{2,1,0:T(8,128)(2,1)} %copy-done.7, bf16[8,128,256]{2,1,0:T(8,128)(2,1)} %get-tuple-element.38.od_ref.ob_ref), custom_call_target="tpu_custom_call" | custom-call | tf_op jit(solution)/shard_map/sum_join/pallas_call | solution.py:399
  136.1 7.0 %all-to-all-start.4 = ((bf16[8,256,256]{2,1,0:T(8,128)(2,1)}), bf16[8,256,256]{2,1,0:T(8,128)(2,1)S(1)}, u32[]{:S(2)}, u32[]{:S(2)}) async-start(bf16[8,256,256]{2,1,0:T(8,128)(2,1)} %sum_join.1.ka_ref), calls=%async_computation.4 | async-start | bytes 2097152 | tf_op jit(solution)/shard_map/all_to_all | solution.py:361
  143.1 1.5 collective-permute-start.10
  144.6 1.7 collective-permute-start.11
  146.4 2.5 %collective-permute-start.9 = (bf16[8,128,256]{2,1,0:T(8,128)(2,1)S(1)}, bf16[8,128,256]{2,1,0:T(8,128)(2,1)}, u32[]{:S(2)}, u32[]{:S(2)}) collective-permute-start(bf16[8,128,256]{2,1,0:T(8,128)(2,1)S(1)} %copy-done.11), channel_id=1, source_target_pairs={{0,8},{8,16},{16,24},{24,0},{1,9},{9,17},{17,25},{25,1},{2,10},{10... | collective-permute-start | bytes 1572872 | tf_op jit(solution)/shard_map/ppermute | solution.py:413
  148.9 15.3 %collective-permute-done.10.refs_2_ = bf16[8,128,256]{2,1,0:T(8,128)(2,1)S(1)} collective-permute-done((bf16[8,128,256]{2,1,0:T(8,128)(2,1)S(1)}, bf16[8,128,256]{2,1,0:T(8,128)(2,1)S(1)}, u32[]{:S(2)}, u32[]{:S(2)}) %collective-permute-start.10) | collective-permute-done | bytes 524320 | tf_op jit(solution)/shard_map/ppermute | solution.py:414
  164.2 0.8 copy-done.15
  165.0 1.1 collective-permute-done.9.refs_1_
  166.1 2.1 all-to-all-done.4.b_ref.refs_4_.ob_ref.ka_ref
  168.3 1.0 copy-done.1
  169.2 2.3 %sum_parts.2.kb_ref = bf16[8,128,256]{2,1,0:T(8,128)(2,1)} custom-call(bf16[8,128,256]{2,1,0:T(8,128)(2,1)} %get-tuple-element.39.refs_0_, bf16[8,128,256]{2,1,0:T(8,128)(2,1)} %collective-permute-done.9.refs_1_, bf16[8,128,256]{2,1,0:T(8,128)(2,1)} %copy-done.14, bf16[8,128,256]{2,1,0:T(8,128)(2,1)} %copy-done.15, bf16[8,256,256]{2,1,0:T(8,128)(2,1)} %copy-done.1), custom_call_target="tpu_custom_call" | custom-call | tf_op jit(solution)/shard_map/sum_parts/pallas_call | solution.py:381
  171.6 4.7 %all-to-all-start.5 = ((bf16[8,128,256]{2,1,0:T(8,128)(2,1)}), bf16[8,128,256]{2,1,0:T(8,128)(2,1)S(1)}, u32[]{:S(2)}, u32[]{:S(2)}) async-start(bf16[8,128,256]{2,1,0:T(8,128)(2,1)} %sum_parts.2.kb_ref), calls=%async_computation.5 | async-start | bytes 1048576 | tf_op jit(solution)/shard_map/all_to_all | solution.py:361
  176.3 6.3 %weight_share.1 = bf16[1024,384]{1,0:T(8,128)(2,1)} custom-call(bf16[8,128,256]{2,1,0:T(8,128)(2,1)} %gate.4.after_ref.oa_ref, bf16[8,128,256]{2,1,0:T(8,128)(2,1)} %get-tuple-element.38.od_ref.ob_ref, bf16[8,256,256]{2,1,0:T(8,128)(2,1)} %sum_join.1.ka_ref, bf16[8,128,256]{2,1,0:T(8,128)(2,1)} %sum_parts.2.kb_ref, ...), custom_call_target="tpu_custom_call" | custom-call | tf_op jit(solution)/shard_map/weight_share/pallas_call | solution.py:452
  182.6 1.9 dynamic-slice_bitcast_fusion
  184.5 5.1 %all-to-all-done.5.kb_ref.refs_2_ = bf16[8,128,256]{2,1,0:T(8,128)(2,1)S(1)} async-done(((bf16[8,128,256]{2,1,0:T(8,128)(2,1)}), bf16[8,128,256]{2,1,0:T(8,128)(2,1)S(1)}, u32[]{:S(2)}, u32[]{:S(2)}) %all-to-all-start.5) | async-done | bytes 524320 | tf_op jit(solution)/shard_map/all_to_all | solution.py:361
  189.6 0.8 copy-done.3
  190.5 2.0 sum_parts.3
  192.5 1.8 reshape.51
  194.3 10.5 %all-to-all-start.6 = ((bf16[128,4,384]{2,1,0:T(4,128)(2,1)}), bf16[128,4,384]{2,1,0:T(4,128)(2,1)S(1)}, u32[]{:S(2)}, u32[]{:S(2)}) async-start(bf16[128,4,384]{2,1,0:T(4,128)(2,1)} %reshape.51), calls=%async_computation.6 | async-start | bytes 786432 | tf_op jit(solution)/shard_map/all_to_all | solution.py:361
  204.8 4.4 %project_out.1.refs_0_ = bf16[256,1024]{1,0:T(8,128)(2,1)} custom-call(bf16[8,128,256]{2,1,0:T(8,128)(2,1)} %copy-done.2, bf16[8,256,256]{2,1,0:T(8,128)(2,1)} %copy-done.1, bf16[1024,1024]{1,0:T(8,128)(2,1)} %wo_ref.3), custom_call_target="tpu_custom_call" | custom-call | tf_op jit(solution)/shard_map/project_out/pallas_call | solution.py:286
  209.2 6.3 %node_grads.1.refs_1_ = bf16[256,1024]{1,0:T(8,128)(2,1)} custom-call(bf16[8,128,256]{2,1,0:T(8,128)(2,1)} %copy-done.2, bf16[8,256,256]{2,1,0:T(8,128)(2,1)} %copy-done.1, bf16[8,256,256]{2,1,0:T(8,128)(2,1)} %copy-done.1, bf16[8,128,256]{2,1,0:T(8,128)(2,1)} %copy-done.3, bf16[1024,3072]{1,0:T(8,128)(2,1)} %wv_ref.3, bf16[1024,3072]{1,0:T(8,128)(2,1)} %wv_ref.3, ...), custom_call_target="tpu_custom_call" | custom-call | tf_op jit(solution)/shard_map/node_grads/pallas_call | solution.py:325
  215.4 4.6 %all-to-all-done.6.x_ref = bf16[128,4,384]{2,1,0:T(4,128)(2,1)S(1)} async-done(((bf16[128,4,384]{2,1,0:T(4,128)(2,1)}), bf16[128,4,384]{2,1,0:T(4,128)(2,1)S(1)}, u32[]{:S(2)}, u32[]{:S(2)}) %all-to-all-start.6) | async-done | bytes 393248 | tf_op jit(solution)/shard_map/all_to_all | solution.py:361
  220.0 0.8 copy-done.10
  220.7 1.8 spread.1
  (67 shorter events, 3.3 us)
Async XLA Ops:
  7.2 13.7 %copy-start = (s32[1,64,8]{1,2,0:T(8,128)S(1)}, s32[1,64,8]{1,2,0:T(8,128)}, u32[]{:S(2)}) copy-start(s32[1,64,8]{1,2,0:T(8,128)} %param.11) | copy-start | bytes 6148
  7.2 13.7 %copy-start.22 = (s32[1,4]{1,0:T(1,128)S(1)}, s32[1,4]{1,0:T(1,128)}, u32[]{:S(2)}) copy-start(s32[1,4]{1,0:T(1,128)} %param.13) | copy-start | bytes 52
  7.2 14.6 %copy-start.17 = (s32[1,64]{1,0:T(1,128)S(1)}, s32[1,64]{1,0:T(1,128)}, u32[]{:S(2)}) copy-start(s32[1,64]{1,0:T(1,128)} %param.12) | copy-start | bytes 772
  12.4 37.2 %all-to-all-start = ((bf16[8,256,256]{2,1,0:T(8,128)(2,1)}), bf16[8,256,256]{2,1,0:T(8,128)(2,1)S(1)}, u32[]{:S(2)}, u32[]{:S(2)}) async-start(bf16[8,256,256]{2,1,0:T(8,128)(2,1)} %project_kv.1), calls=%async_computation | async-start | bytes 2097152 | tf_op jit(solution)/shard_map/all_to_all | solution.py:361
  49.6 3.6 %copy-start.4 = (bf16[8,256,256]{2,1,0:T(8,128)(2,1)}, bf16[8,256,256]{2,1,0:T(8,128)(2,1)S(1)}, u32[]{:S(2)}) copy-start(bf16[8,256,256]{2,1,0:T(8,128)(2,1)S(1)} %all-to-all-done.x_ref) | copy-start | bytes 3145732
  49.6 21.4 %all-to-all-start.1 = ((bf16[8,256,128]{2,1,0:T(8,128)(2,1)}), bf16[8,256,128]{2,1,0:T(8,128)(2,1)S(1)}, u32[]{:S(2)}, u32[]{:S(2)}) async-start(bf16[8,256,128]{2,1,0:T(8,128)(2,1)} %get-tuple-element.24), calls=%async_computation.1 | async-start | bytes 1048576 | tf_op jit(solution)/shard_map/all_to_all | solution.py:361
  53.1 123.2 %all-gather.2.cloned.1.call-start = ((), (), s32[]{:S(2)}) async-start(), calls=%async_computation.7 | async-start | bytes 4718592 | tf_op jit(solution)/shard_map/all_gather | solution.py:482
  55.2 22.3 %collective-permute-start = (bf16[8,128,256]{2,1,0:T(8,128)(2,1)}, bf16[8,128,256]{2,1,0:T(8,128)(2,1)S(1)}, u32[]{:S(2)}, u32[]{:S(2)}) collective-permute-start(bf16[8,128,256]{2,1,0:T(8,128)(2,1)} %get-tuple-element.23.own_ref), channel_id=1, source_target_pairs={{0,8},{8,16},{16,24},{24,0},{1,9},{9,17},{17,25},{25,1},{2,10},{10... | collective-permute-start | bytes 1572872 | tf_op jit(solution)/shard_map/ppermute | solution.py:370
  56.8 23.0 %collective-permute-start.1 = (bf16[8,128,256]{2,1,0:T(8,128)(2,1)}, bf16[8,128,256]{2,1,0:T(8,128)(2,1)S(1)}, u32[]{:S(2)}, u32[]{:S(2)}) collective-permute-start(bf16[8,128,256]{2,1,0:T(8,128)(2,1)} %get-tuple-element.23.own_ref), channel_id=1, source_target_pairs={{0,24},{8,0},{16,8},{24,16},{1,25},{9,1},{17,9},{25,17},{2,26},{10... | collective-permute-start | bytes 1572872 | tf_op jit(solution)/shard_map/ppermute | solution.py:370
  57.2 26.6 %collective-permute-start.2 = (bf16[8,128,256]{2,1,0:T(8,128)(2,1)}, bf16[8,128,256]{2,1,0:T(8,128)(2,1)S(1)}, u32[]{:S(2)}, u32[]{:S(2)}) collective-permute-start(bf16[8,128,256]{2,1,0:T(8,128)(2,1)} %get-tuple-element.23.own_ref), channel_id=1, source_target_pairs={{0,16},{8,24},{16,0},{24,8},{1,17},{9,25},{17,1},{25,9},{2,18},{10... | collective-permute-start | bytes 1572872 | tf_op jit(solution)/shard_map/ppermute | solution.py:370
  70.9 0.9 copy-start.9
  71.8 29.8 %all-to-all-start.2 = ((bf16[8,256,128]{2,1,0:T(8,128)(2,1)}), bf16[8,256,128]{2,1,0:T(8,128)(2,1)S(1)}, u32[]{:S(2)}, u32[]{:S(2)}) async-start(bf16[8,256,128]{2,1,0:T(8,128)(2,1)} %get-tuple-element.27), calls=%async_computation.2 | async-start | bytes 1048576 | tf_op jit(solution)/shard_map/all_to_all | solution.py:361
  75.3 36.2 %collective-permute-start.6 = (bf16[8,128,256]{2,1,0:T(8,128)(2,1)}, bf16[8,128,256]{2,1,0:T(8,128)(2,1)S(1)}, u32[]{:S(2)}, u32[]{:S(2)}) collective-permute-start(bf16[8,128,256]{2,1,0:T(8,128)(2,1)} %get-tuple-element.32.own_ref), channel_id=1, source_target_pairs={{0,8},{8,16},{16,24},{24,0},{1,9},{9,17},{17,25},{25,1},{2,10},{10... | collective-permute-start | bytes 1572872 | tf_op jit(solution)/shard_map/ppermute | solution.py:370
  77.0 34.8 %collective-permute-start.7 = (bf16[8,128,256]{2,1,0:T(8,128)(2,1)}, bf16[8,128,256]{2,1,0:T(8,128)(2,1)}, u32[]{:S(2)}, u32[]{:S(2)}) collective-permute-start(bf16[8,128,256]{2,1,0:T(8,128)(2,1)} %get-tuple-element.32.own_ref), channel_id=1, source_target_pairs={{0,24},{8,0},{16,8},{24,16},{1,25},{9,1},{17,9},{25,17},{2,26},{10... | collective-permute-start | bytes 1572872 | tf_op jit(solution)/shard_map/ppermute | solution.py:370
  77.4 6.3 %copy-start.19 = (bf16[8,128,256]{2,1,0:T(8,128)(2,1)}, bf16[8,128,256]{2,1,0:T(8,128)(2,1)S(1)}, u32[]{:S(2)}) copy-start(bf16[8,128,256]{2,1,0:T(8,128)(2,1)S(1)} %collective-permute-done.left_ref) | copy-start | bytes 1572868
  77.4 34.4 %collective-permute-start.8 = (bf16[8,128,256]{2,1,0:T(8,128)(2,1)}, bf16[8,128,256]{2,1,0:T(8,128)(2,1)}, u32[]{:S(2)}, u32[]{:S(2)}) collective-permute-start(bf16[8,128,256]{2,1,0:T(8,128)(2,1)} %get-tuple-element.32.own_ref), channel_id=1, source_target_pairs={{0,16},{8,24},{16,0},{24,8},{1,17},{9,25},{17,1},{25,9},{2,18},{10... | collective-permute-start | bytes 1572872 | tf_op jit(solution)/shard_map/ppermute | solution.py:370
  79.7 4.0 %copy-start.20 = (bf16[8,128,256]{2,1,0:T(8,128)(2,1)}, bf16[8,128,256]{2,1,0:T(8,128)(2,1)S(1)}, u32[]{:S(2)}) copy-start(bf16[8,128,256]{2,1,0:T(8,128)(2,1)S(1)} %collective-permute-done.1.right_ref) | copy-start | bytes 1572868
  83.8 0.8 copy-start.21
  101.6 0.8 copy-start.8
  102.4 30.0 %all-to-all-start.3 = ((bf16[8,128,256]{2,1,0:T(8,128)(2,1)}), bf16[8,128,256]{2,1,0:T(8,128)(2,1)S(1)}, u32[]{:S(2)}, u32[]{:S(2)}) async-start(bf16[8,128,256]{2,1,0:T(8,128)(2,1)} %gate.4.after_ref.oa_ref), calls=%async_computation.3 | async-start | bytes 1048576 | tf_op jit(solution)/shard_map/all_to_all | solution.py:361
  109.5 19.9 %collective-permute-start.3 = (bf16[8,128,256]{2,1,0:T(8,128)(2,1)}, bf16[8,128,256]{2,1,0:T(8,128)(2,1)S(1)}, u32[]{:S(2)}, u32[]{:S(2)}) collective-permute-start(bf16[8,128,256]{2,1,0:T(8,128)(2,1)} %get-tuple-element.29), channel_id=1, source_target_pairs={{0,8},{8,16},{16,24},{24,0},{1,9},{9,17},{17,25},{25,1},{2,10},{10... | collective-permute-start | bytes 1572872 | tf_op jit(solution)/shard_map/ppermute | solution.py:413
  109.5 19.9 %collective-permute-start.4 = (bf16[8,128,256]{2,1,0:T(8,128)(2,1)}, bf16[8,128,256]{2,1,0:T(8,128)(2,1)S(1)}, u32[]{:S(2)}, u32[]{:S(2)}) collective-permute-start(bf16[8,128,256]{2,1,0:T(8,128)(2,1)} %get-tuple-element.30), channel_id=1, source_target_pairs={{0,24},{8,0},{16,8},{24,16},{1,25},{9,1},{17,9},{25,17},{2,26},{10... | collective-permute-start | bytes 1572872 | tf_op jit(solution)/shard_map/ppermute | solution.py:414
  111.5 0.8 copy-start.18
  111.5 20.9 %collective-permute-start.5 = (bf16[8,128,256]{2,1,0:T(8,128)(2,1)}, bf16[8,128,256]{2,1,0:T(8,128)(2,1)S(1)}, u32[]{:S(2)}, u32[]{:S(2)}) collective-permute-start(bf16[8,128,256]{2,1,0:T(8,128)(2,1)} %get-tuple-element.31), channel_id=1, source_target_pairs={{0,16},{8,24},{16,0},{24,8},{1,17},{9,25},{17,1},{25,9},{2,18},{10... | collective-permute-start | bytes 1572872 | tf_op jit(solution)/shard_map/ppermute | solution.py:415
  129.4 3.0 %copy-start.5 = (bf16[8,128,256]{2,1,0:T(8,128)(2,1)}, bf16[8,128,256]{2,1,0:T(8,128)(2,1)S(1)}, u32[]{:S(2)}) copy-start(bf16[8,128,256]{2,1,0:T(8,128)(2,1)S(1)} %collective-permute-done.3.refs_5_.b_ref) | copy-start | bytes 1572868
  129.4 3.0 %copy-start.6 = (bf16[8,128,256]{2,1,0:T(8,128)(2,1)}, bf16[8,128,256]{2,1,0:T(8,128)(2,1)S(1)}, u32[]{:S(2)}) copy-start(bf16[8,128,256]{2,1,0:T(8,128)(2,1)S(1)} %collective-permute-done.4.refs_6_.c_ref) | copy-start | bytes 1572868
  132.4 0.8 copy-start.7
  132.4 1.0 copy-start.2
  133.4 9.7 %copy-start.12 = (bf16[8,128,256]{2,1,0:T(8,128)(2,1)S(1)}, bf16[8,128,256]{2,1,0:T(8,128)(2,1)}, u32[]{:S(2)}) copy-start(bf16[8,128,256]{2,1,0:T(8,128)(2,1)} %get-tuple-element.41) | copy-start | bytes 1572868
  133.4 11.2 %copy-start.13 = (bf16[8,128,256]{2,1,0:T(8,128)(2,1)S(1)}, bf16[8,128,256]{2,1,0:T(8,128)(2,1)}, u32[]{:S(2)}) copy-start(bf16[8,128,256]{2,1,0:T(8,128)(2,1)} %get-tuple-element.42) | copy-start | bytes 1572868
  133.4 13.0 %copy-start.11 = (bf16[8,128,256]{2,1,0:T(8,128)(2,1)S(1)}, bf16[8,128,256]{2,1,0:T(8,128)(2,1)}, u32[]{:S(2)}) copy-start(bf16[8,128,256]{2,1,0:T(8,128)(2,1)} %get-tuple-element.40) | copy-start | bytes 1572868
  136.1 32.1 %all-to-all-start.4 = ((bf16[8,256,256]{2,1,0:T(8,128)(2,1)}), bf16[8,256,256]{2,1,0:T(8,128)(2,1)S(1)}, u32[]{:S(2)}, u32[]{:S(2)}) async-start(bf16[8,256,256]{2,1,0:T(8,128)(2,1)} %sum_join.1.ka_ref), calls=%async_computation.4 | async-start | bytes 2097152 | tf_op jit(solution)/shard_map/all_to_all | solution.py:361
  143.1 21.1 %collective-permute-start.10 = (bf16[8,128,256]{2,1,0:T(8,128)(2,1)S(1)}, bf16[8,128,256]{2,1,0:T(8,128)(2,1)S(1)}, u32[]{:S(2)}, u32[]{:S(2)}) collective-permute-start(bf16[8,128,256]{2,1,0:T(8,128)(2,1)S(1)} %copy-done.12), channel_id=1, source_target_pairs={{0,24},{8,0},{16,8},{24,16},{1,25},{9,1},{17,9},{25,17},{2,26},{10... | collective-permute-start | bytes 1572872 | tf_op jit(solution)/shard_map/ppermute | solution.py:414
  144.6 19.5 %collective-permute-start.11 = (bf16[8,128,256]{2,1,0:T(8,128)(2,1)S(1)}, bf16[8,128,256]{2,1,0:T(8,128)(2,1)S(1)}, u32[]{:S(2)}, u32[]{:S(2)}) collective-permute-start(bf16[8,128,256]{2,1,0:T(8,128)(2,1)S(1)} %copy-done.13), channel_id=1, source_target_pairs={{0,16},{8,24},{16,0},{24,8},{1,17},{9,25},{17,1},{25,9},{2,18},{10... | collective-permute-start | bytes 1572872 | tf_op jit(solution)/shard_map/ppermute | solution.py:415
  146.4 19.7 %collective-permute-start.9 = (bf16[8,128,256]{2,1,0:T(8,128)(2,1)S(1)}, bf16[8,128,256]{2,1,0:T(8,128)(2,1)}, u32[]{:S(2)}, u32[]{:S(2)}) collective-permute-start(bf16[8,128,256]{2,1,0:T(8,128)(2,1)S(1)} %copy-done.11), channel_id=1, source_target_pairs={{0,8},{8,16},{16,24},{24,0},{1,9},{9,17},{17,25},{25,1},{2,10},{10... | collective-permute-start | bytes 1572872 | tf_op jit(solution)/shard_map/ppermute | solution.py:413
  164.2 4.1 %copy-start.14 = (bf16[8,128,256]{2,1,0:T(8,128)(2,1)}, bf16[8,128,256]{2,1,0:T(8,128)(2,1)S(1)}, u32[]{:S(2)}) copy-start(bf16[8,128,256]{2,1,0:T(8,128)(2,1)S(1)} %collective-permute-done.10.refs_2_) | copy-start | bytes 1572868
  164.2 0.9 copy-start.15
  168.2 1.0 copy-start.1
  171.6 18.0 %all-to-all-start.5 = ((bf16[8,128,256]{2,1,0:T(8,128)(2,1)}), bf16[8,128,256]{2,1,0:T(8,128)(2,1)S(1)}, u32[]{:S(2)}, u32[]{:S(2)}) async-start(bf16[8,128,256]{2,1,0:T(8,128)(2,1)} %sum_parts.2.kb_ref), calls=%async_computation.5 | async-start | bytes 1048576 | tf_op jit(solution)/shard_map/all_to_all | solution.py:361
  184.5 5.1 %collective-permute-start.12 = (bf16[4,128,384]{2,1,0:T(8,128)(2,1)S(1)}, bf16[4,128,384]{2,1,0:T(8,128)(2,1)S(1)}, u32[]{:S(2)}, u32[]{:S(2)}) collective-permute-start(bf16[4,128,384]{2,1,0:T(8,128)(2,1)S(1)} %get-tuple-element.45), channel_id=1, source_target_pairs={{0,32},{32,0},{1,33},{33,1},{2,34},{34,2},{3,35},{35,3},{4,36},{36... | collective-permute-start | bytes 1179656 | tf_op jit(solution)/shard_map/ppermute | solution.py:503
  189.6 0.8 copy-start.3
  189.6 0.9 copy-start.16
  194.3 25.7 %all-to-all-start.6 = ((bf16[128,4,384]{2,1,0:T(4,128)(2,1)}), bf16[128,4,384]{2,1,0:T(4,128)(2,1)S(1)}, u32[]{:S(2)}, u32[]{:S(2)}) async-start(bf16[128,4,384]{2,1,0:T(4,128)(2,1)} %reshape.51), calls=%async_computation.6 | async-start | bytes 786432 | tf_op jit(solution)/shard_map/all_to_all | solution.py:361
  220.0 0.8 copy-start.10
Sparse Core Ops, SparseCore 0:
  71.9 69.7 all-gather.1

commit v6 on v5

--- a/solution.py
+++ b/solution.py
@@ -63,46 +63,40 @@
 def put_pairs(first, second, a_ref, b_ref):
     for u in (0, 1):
         cols = slice(u * 128, (u + 1) * 128)
-        a, b = pair_up(first[:, cols], second[:, cols])
+        a, b = pair_rows(first[:, cols].T, second[:, cols].T)
         a_ref[u] = a.astype(bf16)
         b_ref[u] = b.astype(bf16)
 
 
-def kv_kernel(f_ref, wk_ref, wv_ref, o_ref):
-    k = nn(f_ref[...], wk_ref[...])
-    v = nn(f_ref[...], wv_ref[...])
-    for u in (0, 1):
-        cols = slice(u * 128, (u + 1) * 128)
-        a, b = pair_rows(k[:, cols].T, v[:, cols].T)
-        o_ref[u, :128, :] = a.astype(bf16)
-        o_ref[u, 128:, :] = b.astype(bf16)
-
-
-def split_kernel(x_ref, a_ref, b_ref):
-    a_ref[...] = x_ref[:, :128, :]
-    b_ref[...] = x_ref[:, 128:, :]
-
-
-def split_heads(both):
-    return pl.pallas_call(
-        split_kernel,
+def kv_kernel(f_ref, wk_ref, wv_ref, a_ref, b_ref):
+    put_pairs(nn(f_ref[...], wk_ref[...]), nn(f_ref[...], wv_ref[...]), a_ref, b_ref)
+
+
+def first_kernel(x_ref, o_ref):
+    o_ref[...] = x_ref[...]
+
+
+def first_half(both):
+    return pl.pallas_call(
+        first_kernel,
         grid=(2,),
-        in_specs=[pl.BlockSpec((ZS // 2, 256, NODE_DEV), lambda i: (i, 0, 0))],
-        out_specs=[pl.BlockSpec((ZS // 2, 128, NODE_DEV), lambda i: (i, 0, 0))] * 2,
-        out_shape=[jax.ShapeDtypeStruct(TURNED, bf16)] * 2,
-        compiler_params=VMEM,
-        name="split_heads",
+        in_specs=[pl.BlockSpec((ZS // 2, 128, NODE_DEV), lambda i: (i, 0, 0))],
+        out_specs=pl.BlockSpec((ZS // 2, 128, NODE_DEV), lambda i: (i, 0, 0)),
+        out_shape=jax.ShapeDtypeStruct(TURNED, bf16),
+        compiler_params=VMEM,
+        name="first_half",
     )(both)
 
 
-def qg_kernel(f_ref, c_ref, wq_ref, wo_ref, *refs):
-    a_ref, b_ref, copy_ref = refs[-3:]
+def qg_kernel(f_ref, c_ref, wq_ref, wo_ref, kv_ref, *refs):
+    joint_ref, b_ref, copy_ref = refs[-3:]
 
     @pl.when(pl.program_id(0) == 0)
     def _():
         copy_ref[...] = f_ref[...]
 
-    put_pairs(nn(f_ref[...], wq_ref[...]), nt(c_ref[...], wo_ref[...]), a_ref, b_ref)
+    joint_ref[:, :128, :] = kv_ref[...]
+    put_pairs(nn(f_ref[...], wq_ref[...]), nt(c_ref[...], wo_ref[...]), joint_ref.at[:, 128:], b_ref)
 
 
 def whole(shape):
@@ -119,17 +113,16 @@
             pl.BlockSpec((d, 256), lambda i: (0, ZS // 2 + i)),
             pl.BlockSpec((d, 256), lambda i: (0, ZS + i)),
         ],
-        out_specs=pl.BlockSpec((2, 256, NODE_DEV), lambda i: (i, 0, 0)),
-        out_shape=jax.ShapeDtypeStruct((ZS, 256, NODE_DEV), bf16),
+        out_specs=[pl.BlockSpec((2, 128, NODE_DEV), lambda i: (i, 0, 0))] * 2,
+        out_shape=[jax.ShapeDtypeStruct(TURNED, bf16)] * 2,
         compiler_params=VMEM,
         name="project_kv",
     )(feats, w_qkv, w_qkv)
 
 
-def project_qg(feats, cot, w_qkv, w_out, before):
+def project_qg(feats, cot, w_qkv, w_out, kv, before):
     d = feats.shape[1]
-    out = jax.ShapeDtypeStruct((ZS, NODE_DEV, 128), bf16)
-    tile = pl.BlockSpec((2, NODE_DEV, 128), lambda i: (i, 0, 0))
+    tile = pl.BlockSpec((2, 128, NODE_DEV), lambda i: (i, 0, 0))
     return pl.pallas_call(
         qg_kernel,
         grid=(ZS // 2,),
@@ -138,17 +131,22 @@
             whole((NODE_DEV, d)),
             pl.BlockSpec((d, 256), lambda i: (0, i)),
             pl.BlockSpec((256, d), lambda i: (i, 0)),
+            tile,
         ]
         + [pl.BlockSpec(memory_space=pl.ANY)] * len(before),
-        out_specs=[tile, tile, whole((NODE_DEV, d))],
-        out_shape=[out, out, jax.ShapeDtypeStruct((NODE_DEV, d), bf16)],
+        out_specs=[pl.BlockSpec((2, 256, NODE_DEV), lambda i: (i, 0, 0)), tile, whole((NODE_DEV, d))],
+        out_shape=[
+            jax.ShapeDtypeStruct((ZS, 256, NODE_DEV), bf16),
+            jax.ShapeDtypeStruct(TURNED, bf16),
+            jax.ShapeDtypeStruct((NODE_DEV, d), bf16),
+        ],
         compiler_params=VMEM,
         name="project_qg",
-    )(feats, cot, w_qkv, w_out, *before)
+    )(feats, cot, w_qkv, w_out, kv, *before)
 
 
 def attend_kernel(
-    tab_ref, cnt_ref, order_ref, y_ref, own_ref, left_ref, right_ref, opp_ref, qg_ref, after_ref,
+    skip, tab_ref, cnt_ref, order_ref, y_ref, own_ref, left_ref, right_ref, opp_ref, qg_ref, after_ref,
     od_ref, sum_own_ref, sum_right_ref, sum_left_ref, sum_opp_ref,
     kv_s, acc, sc0, sc1, xs0, xs1,
 ):
@@ -170,15 +168,14 @@
 
     def score(i, pairs, sc):
         ids = [tab_ref[i * SLOTS + t] for t in range(2 * pairs)]
-        rows = pl.ds(pl.multiple_of(i * BLOCK, BLOCK), BLOCK)
-        qg = qg_ref[rows, :].astype(f32)
-        low = low_half(qg.shape)
+        qg = qg_ref[lax.div(i, 2), skip : skip + 128, cols(i)].astype(f32)
+        top = lax.broadcasted_iota(jnp.int32, qg.shape, 0) < HD
         zero = jnp.zeros_like(qg)
-        wide32 = jnp.concatenate([jnp.where(low, qg, zero), jnp.where(low, zero, qg)], axis=0)
-        wide = wide32.astype(bf16)
+        wide_t = jnp.concatenate([jnp.where(top, qg, zero), jnp.where(top, zero, qg)], axis=1)
+        wide = wide_t.T.astype(bf16)
         for t in range(pairs):
             sc[:, t * 256 : (t + 1) * 256] = nn(wide, keys(ids, t))
-        return i, ids, wide32.T.astype(bf16)
+        return i, ids, wide_t.astype(bf16)
 
     def soften(i, pairs, sc, xs):
         width = pairs * 256
@@ -238,7 +235,7 @@
     smem = pl.BlockSpec(memory_space=pltpu.SMEM)
     row = jax.ShapeDtypeStruct(TURNED, bf16)
     return pl.pallas_call(
-        attend_kernel,
+        functools.partial(attend_kernel, qg.shape[1] - 128),
         in_specs=[smem] * 4 + [vmem] * 5 + [pl.BlockSpec(memory_space=pl.ANY)],
         out_specs=[vmem] * 5,
         out_shape=[row] * 5,
@@ -433,7 +430,7 @@
     )(*values, *after)
 
 
-def weight_kernel(oa_ref, ob_ref, ka_ref, kb_ref, f_ref, o_ref, grads):
+def weight_kernel(c_ref, oa_ref, ob_ref, ka_ref, kb_ref, f_ref, mine_ref, theirs_ref, grads):
     @pl.when(pl.program_id(0) == 0)
     def _():
         for t in range(ZS):
@@ -443,22 +440,25 @@
             for k, part in enumerate((dq, dk, dv)):
                 grads[k * 128 : (k + 1) * 128, nodes] = part
 
-    o_ref[...] = nn(grads[...], f_ref[...]).T.astype(bf16)
-
-
-def weight_share(od_a, od_b, joint, kv_b, feats_row):
+    both = nn(grads[...], f_ref[...]).T.astype(bf16)
+    first = c_ref[0] == 0
+    mine_ref[...] = jnp.where(first, both[:128], both[128:])
+    theirs_ref[...] = jnp.where(first, both[128:], both[:128])
+
+
+def weight_share(c, od_a, od_b, joint, kv_b, feats_row):
     d = feats_row.shape[1]
     part = whole(TURNED)
     return pl.pallas_call(
         weight_kernel,
         grid=(d // 256,),
-        in_specs=[part, part, whole(joint.shape), part, pl.BlockSpec((ROW, 256), lambda i: (0, i))],
-        out_specs=pl.BlockSpec((256, 384), lambda i: (i, 0)),
-        out_shape=jax.ShapeDtypeStruct((d, 384), bf16),
+        in_specs=[pl.BlockSpec(memory_space=pltpu.SMEM), part, part, whole(joint.shape), part, pl.BlockSpec((ROW, 256), lambda i: (0, i))],
+        out_specs=[pl.BlockSpec((128, 384), lambda i: (i, 0))] * 2,
+        out_shape=[jax.ShapeDtypeStruct((d // 2, 384), bf16)] * 2,
         scratch_shapes=[pltpu.VMEM((384, ROW), bf16)],
         compiler_params=VMEM,
         name="weight_share",
-    )(od_a, od_b, joint, kv_b, feats_row)
+    )(c, od_a, od_b, joint, kv_b, feats_row)
 
 
 def on_device(node_feats, w_qkv, w_out, cotangent, block_neighbors, block_counts, global_blocks):
@@ -474,18 +474,20 @@
     order = jnp.sum(jnp.where(rank[None, :] == place[:, None], place[None, :], 0), axis=1)
     y_arr = y.reshape(1).astype(jnp.int32)
 
-    kv = project_kv(feats, w_qkv)
-    *qg, feats_copy = project_qg(feats, cot, w_qkv, w_out, (table, counts, order))
-    kv_row = [gather_row(v) for v in split_heads(swap(kv, "z"))]
-    qg_row = [swap(v, "z").reshape(ROW, 128) for v in qg]
-    (feats_late,) = gate([feats_copy], [qg_row[0]])
+    kv_a, kv_b = project_kv(feats, w_qkv)
+    joint, qg_b, feats_copy = project_qg(feats, cot, w_qkv, w_out, kv_b, (table, counts, order))
+    row_a = gather_row(swap(kv_a, "z"))
+    joint_row = swap(joint, "z")
+    row_b = gather_row(first_half(joint_row))
+    (feats_late, qg_b) = gate([feats_copy, qg_b], [joint_row])
+    qg_row_b = swap(qg_b, "z")
     feats_row = lax.all_gather(feats_late, "z", axis=0, tiled=True)
-    od_a, *kv_a = attend(table, counts, order, y_arr, kv_row[0], qg_row[0], feats_late)
+    od_a, *kv_a = attend(table, counts, order, y_arr, row_a, joint_row, feats_late)
     to_nodes = lambda v: swap(v, "z")
-    (od_a_late,) = gate([od_a], [qg_row[1]])
+    (od_a_late,) = gate([od_a], [qg_row_b])
     od_nodes_a = to_nodes(od_a_late)
     parts_a = send_row(*kv_a)
-    late = attend(table, counts, order, y_arr, kv_row[1], qg_row[1], od_a_late)
+    late = attend(table, counts, order, y_arr, row_b, qg_row_b, od_a_late)
     od_b, *kv_b = gate(late, parts_a[1:] + [od_nodes_a])
     parts_b = send_row(*kv_b)
     joint = sum_join(parts_a, od_b)
@@ -495,14 +497,13 @@
     attn_update = project_out(od_nodes_a, joint_nodes, w_out)
     grad_nodes = node_grads(od_nodes_a, joint_nodes, kv_nodes_b, w_qkv)
 
-    share = weight_share(od_a_late, od_b, joint, sum_b, feats_row)
-    d = share.shape[0]
-    share = share.reshape(4, 2, d // 8, 384)
-    c = lax.axis_index("c")
-    mine, theirs = (lax.dynamic_index_in_dim(share, k, 1, keepdims=False) for k in (c, 1 - c))
+    d = feats.shape[1]
+    c_arr = lax.axis_index("c").reshape(1).astype(jnp.int32)
+    mine, theirs = weight_share(c_arr, od_a_late, od_b, joint, sum_b, feats_row)
     theirs = lax.ppermute(theirs, "c", [(0, 1), (1, 0)])
-    share = sum_parts([v.reshape(d // 2, 384) for v in (mine, theirs)], (kv_nodes_b,))
-    share = swap(share.reshape(16 * ZS, d // 256, 384), ("x", "y", "z"))
+    share = sum_parts([mine, theirs], ()).reshape(16 * ZS, d // 256, 384)
+    (share,) = gate([share], [kv_nodes_b])
+    share = swap(share, ("x", "y", "z"))
     grad_weights = spread(share, (attn_update, grad_nodes))
     return attn_update[None], grad_nodes[None], grad_weights
 

time: 232 us -> 233 us (level)
  waiting for transfers between devices: 67.6 us -> 76.4 us
  starting transfers between devices: 61.6 us -> 55.8 us
  local copies, waits for them, and re-layouts: 12.2 us -> 9.39 us
    all_to_all x7, waiting for transfers between devices: 44.2 us -> 54 us  [swap(): return lax.all_to_all(values, axis, split_axis=0, concat_axis=0, tiled=True)]
    ppermute x2, waiting for transfers between devices: 2.96 us -> 9.5 us  [send_row(): lax.ppermute(opp, 'y', OPPOSITE)]
    all_to_all x7, starting transfers between devices: 44.7 us -> 39.5 us  [swap(): return lax.all_to_all(values, axis, split_axis=0, concat_axis=0, tiled=True)]
    ppermute x2, waiting for transfers between devices: 15.3 us -> 10.8 us  [send_row(): lax.ppermute(to_left, 'y', LEFT)]
    ppermute x2, waiting for transfers between devices: 4.03 us -> 0.01 us  [gather_row(): lax.ppermute(own, 'y', OPPOSITE)]
    unnamed x46 -> x42, local copies, waits for them, and re-layouts: 7.55 us -> 6.74 us
  transfers between devices with their start and end apart: 21 -> 21, of which waited for: 9 -> 11; matrix products, arithmetic and copies ran while one was open for 2% -> 2% of each run, Pallas kernels for 28% -> 28%
where the time goes in v6:
time: 233 us; the launch traced here: 230 us
  waiting for transfers between devices  76.4 us (33%)
  Pallas kernels  72.3 us (31%)
  starting transfers between devices  55.8 us (24%)
  between operations  14.3 us (6%)
  local copies, waits for them, and re-layouts  9.39 us (4%)
    all_to_all x7, waiting for transfers between devices, swap(): return lax.all_to_all(values, axis, split_axis=0, concat_axis=0, tiled=True)  54 us
    all_to_all x7, starting transfers between devices, swap(): return lax.all_to_all(values, axis, split_axis=0, concat_axis=0, tiled=True)  39.5 us
    pallas_call x2, Pallas kernels, attend(): pl.pallas_call(functools.partial(attend_kernel, qg.shape[1] - 128), in_sp...  34 us
    ppermute x2, waiting for transfers between devices, send_row(): lax.ppermute(to_left, 'y', LEFT)  10.8 us
    ppermute x2, waiting for transfers between devices, send_row(): lax.ppermute(opp, 'y', OPPOSITE)  9.5 us
    unnamed x42, local copies, waits for them, and re-layouts  6.74 us
    pallas_call x1, Pallas kernels, weight_share(): pl.pallas_call(weight_kernel, grid=(d // 256,), in_specs=[pl.BlockSpec(me...  6.29 us
    pallas_call x1, Pallas kernels, node_grads(): pl.pallas_call(nodes_kernel, grid=(steps,), in_specs=[tile, SECOND, tile,...  6.26 us
  transfers between devices with their start and end apart: 21, of which 11 were waited for; matrix products, arithmetic and copies ran while one was open for 2% of the time, Pallas kernels for 28%

profile of v6, /device:TPU:8, one launch (start us, length us, event | category | flops | bytes accessed | tf_op | source)
XLA Modules:
  0.0 229.7 jit_solution(11886844643676169158)
XLA Ops:
  7.2 5.2 %project_kv.1 = (bf16[8,128,256]{2,1,0:T(8,128)(2,1)}, bf16[8,128,256]{2,1,0:T(8,128)(2,1)}) custom-call(bf16[256,1024]{1,0:T(8,128)(2,1)} %bitcast.16, bf16[1024,3072]{1,0:T(8,128)(2,1)} %wv_ref.3, bf16[1024,3072]{1,0:T(8,128)(2,1)} %wv_ref.3), custom_call_target="tpu_custom_call" | custom-call | tf_op jit(solution)/shard_map/project_kv/pallas_call | solution.py:108
  12.4 8.5 %all-to-all-start = ((bf16[8,128,256]{2,1,0:T(8,128)(2,1)}), bf16[8,128,256]{2,1,0:T(8,128)(2,1)S(1)}, u32[]{:S(2)}, u32[]{:S(2)}) async-start(bf16[8,128,256]{2,1,0:T(8,128)(2,1)} %get-tuple-element.27), calls=%async_computation | async-start | bytes 1048576 | tf_op jit(solution)/shard_map/all_to_all | solution.py:358
  21.1 0.7 reshape.31.refs_0_.tab_ref
  22.6 0.6 select_reduce_fusion.refs_2_.order_ref
  23.2 5.7 %project_qg.1 = (bf16[8,256,256]{2,1,0:T(8,128)(2,1)}, bf16[8,128,256]{2,1,0:T(8,128)(2,1)}, bf16[256,1024]{1,0:T(8,128)(2,1)}) custom-call(bf16[256,1024]{1,0:T(8,128)(2,1)} %bitcast.17, bf16[256,1024]{1,0:T(8,128)(2,1)} %bitcast.18, bf16[1024,3072]{1,0:T(8,128)(2,1)} %wv_ref.3, bf16[1024,1024]{1,0:T(8,128)(2,1)} %wo_ref.3, ...), custom_call_target="tpu_custom_call" | custom-call | tf_op jit(solution)/shard_map/project_qg/pallas_call | solution.py:126
  28.9 9.4 %all-to-all-done.own_ref = bf16[8,128,256]{2,1,0:T(8,128)(2,1)S(1)} async-done(((bf16[8,128,256]{2,1,0:T(8,128)(2,1)}), bf16[8,128,256]{2,1,0:T(8,128)(2,1)S(1)}, u32[]{:S(2)}, u32[]{:S(2)}) %all-to-all-start) | async-done | bytes 524320 | tf_op jit(solution)/shard_map/all_to_all | solution.py:358
  38.3 3.6 %all-to-all-start.1 = ((bf16[8,256,256]{2,1,0:T(8,128)(2,1)}), bf16[8,256,256]{2,1,0:T(8,128)(2,1)S(1)}, u32[]{:S(2)}, u32[]{:S(2)}) async-start(bf16[8,256,256]{2,1,0:T(8,128)(2,1)} %get-tuple-element.29), calls=%async_computation.1 | async-start | bytes 2097152 | tf_op jit(solution)/shard_map/all_to_all | solution.py:358
  41.9 1.7 collective-permute-start
  44.0 2.3 collective-permute-start.2
  46.3 24.7 %all-to-all-done.1.refs_2_.qg_ref.x_ref = bf16[8,256,256]{2,1,0:T(8,128)(2,1)S(1)} async-done(((bf16[8,256,256]{2,1,0:T(8,128)(2,1)}), bf16[8,256,256]{2,1,0:T(8,128)(2,1)S(1)}, u32[]{:S(2)}, u32[]{:S(2)}) %all-to-all-start.1) | async-done | bytes 1048608 | tf_op jit(solution)/shard_map/all_to_all | solution.py:358
  71.0 1.0 copy-done.2
  72.1 1.8 first_half.1.own_ref
  73.8 1.6 collective-permute-start.6
  75.9 3.5 %all-to-all-start.2 = ((bf16[8,128,256]{2,1,0:T(8,128)(2,1)}), bf16[8,128,256]{2,1,0:T(8,128)(2,1)S(1)}, u32[]{:S(2)}, u32[]{:S(2)}) async-start(bf16[8,128,256]{2,1,0:T(8,128)(2,1)} %get-tuple-element.34), calls=%async_computation.2 | async-start | bytes 1048576 | tf_op jit(solution)/shard_map/all_to_all | solution.py:358
  79.4 2.4 %collective-permute-start.8 = (bf16[8,128,256]{2,1,0:T(8,128)(2,1)}, bf16[8,128,256]{2,1,0:T(8,128)(2,1)}, u32[]{:S(2)}, u32[]{:S(2)}) collective-permute-start(bf16[8,128,256]{2,1,0:T(8,128)(2,1)} %first_half.1.own_ref), channel_id=1, source_target_pairs={{0,16},{8,24},{16,0},{24,8},{1,17},{9,25},{17,1},{25,9},{2,18},{10... | collective-permute-start | bytes 1572872 | tf_op jit(solution)/shard_map/ppermute | solution.py:367
  81.8 17.1 %attend.2 = (bf16[8,128,256]{2,1,0:T(8,128)(2,1)}, bf16[8,128,256]{2,1,0:T(8,128)(2,1)}, bf16[8,128,256]{2,1,0:T(8,128)(2,1)}, bf16[8,128,256]{2,1,0:T(8,128)(2,1)}, bf16[8,128,256]{2,1,0:T(8,128)(2,1)}) custom-call(s32[192]{0:T(256)} %reshape.31.refs_0_.tab_ref, s32[16]{0:T(128)} %get-tuple-element.52.refs_1_.cnt_ref, ...), custom_call_target="tpu_custom_call" | custom-call | flops 25999998976 | bytes 6291456 | tf_op jit(solution)/shard_map/attend/pallas_call | solution.py:237
  99.3 1.6 collective-permute-start.4
  100.9 1.7 all-to-all-done.2.refs_1_.qg_ref
  102.6 0.8 copy-done.8
  103.4 5.4 %all-to-all-start.3 = ((bf16[8,128,256]{2,1,0:T(8,128)(2,1)}), bf16[8,128,256]{2,1,0:T(8,128)(2,1)S(1)}, u32[]{:S(2)}, u32[]{:S(2)}) async-start(bf16[8,128,256]{2,1,0:T(8,128)(2,1)} %gate.5.after_ref.oa_ref), calls=%async_computation.3 | async-start | bytes 1048576 | tf_op jit(solution)/shard_map/all_to_all | solution.py:358
  108.8 1.1 collective-permute-start.5
  109.9 16.9 %attend.3 = (bf16[8,128,256]{2,1,0:T(8,128)(2,1)}, bf16[8,128,256]{2,1,0:T(8,128)(2,1)}, bf16[8,128,256]{2,1,0:T(8,128)(2,1)}, bf16[8,128,256]{2,1,0:T(8,128)(2,1)}, bf16[8,128,256]{2,1,0:T(8,128)(2,1)}) custom-call(s32[192]{0:T(256)} %reshape.31.refs_0_.tab_ref, s32[16]{0:T(128)} %get-tuple-element.52.refs_1_.cnt_ref, ...), custom_call_target="tpu_custom_call" | custom-call | flops 25999998976 | bytes 6291456 | tf_op jit(solution)/shard_map/attend/pallas_call | solution.py:237
  126.9 4.4 %all-to-all-done.3.refs_8_.a_ref.oa_ref = bf16[8,128,256]{2,1,0:T(8,128)(2,1)S(1)} async-done(((bf16[8,128,256]{2,1,0:T(8,128)(2,1)}), bf16[8,128,256]{2,1,0:T(8,128)(2,1)S(1)}, u32[]{:S(2)}, u32[]{:S(2)}) %all-to-all-start.3) | async-done | bytes 524320 | tf_op jit(solution)/shard_map/all_to_all | solution.py:358
  131.3 0.8 copy-done.3
  132.1 2.8 %sum_join.1.ka_ref = bf16[8,256,256]{2,1,0:T(8,128)(2,1)} custom-call(bf16[8,128,256]{2,1,0:T(8,128)(2,1)} %get-tuple-element.35.a_ref, bf16[8,128,256]{2,1,0:T(8,128)(2,1)} %copy-done.5, bf16[8,128,256]{2,1,0:T(8,128)(2,1)} %copy-done.6, bf16[8,128,256]{2,1,0:T(8,128)(2,1)} %copy-done.7, bf16[8,128,256]{2,1,0:T(8,128)(2,1)} %get-tuple-element.44.od_ref.ob_ref), custom_call_target="tpu_custom_call" | custom-call | tf_op jit(solution)/shard_map/sum_join/pallas_call | solution.py:396
  134.9 3.6 %all-to-all-start.4 = ((bf16[8,256,256]{2,1,0:T(8,128)(2,1)}), bf16[8,256,256]{2,1,0:T(8,128)(2,1)S(1)}, u32[]{:S(2)}, u32[]{:S(2)}) async-start(bf16[8,256,256]{2,1,0:T(8,128)(2,1)} %sum_join.1.ka_ref), calls=%async_computation.4 | async-start | bytes 2097152 | tf_op jit(solution)/shard_map/all_to_all | solution.py:358
  138.5 2.7 %collective-permute-start.10 = (bf16[8,128,256]{2,1,0:T(8,128)(2,1)S(1)}, bf16[8,128,256]{2,1,0:T(8,128)(2,1)S(1)}, u32[]{:S(2)}, u32[]{:S(2)}) collective-permute-start(bf16[8,128,256]{2,1,0:T(8,128)(2,1)S(1)} %copy-done.11), channel_id=1, source_target_pairs={{0,24},{8,0},{16,8},{24,16},{1,25},{9,1},{17,9},{25,17},{2,26},{10... | collective-permute-start | bytes 1572872 | tf_op jit(solution)/shard_map/ppermute | solution.py:411
  141.8 1.0 collective-permute-start.9
  142.8 10.8 %collective-permute-done.10.refs_2_ = bf16[8,128,256]{2,1,0:T(8,128)(2,1)S(1)} collective-permute-done((bf16[8,128,256]{2,1,0:T(8,128)(2,1)S(1)}, bf16[8,128,256]{2,1,0:T(8,128)(2,1)S(1)}, u32[]{:S(2)}, u32[]{:S(2)}) %collective-permute-start.10) | collective-permute-done | bytes 524320 | tf_op jit(solution)/shard_map/ppermute | solution.py:411
  153.6 9.5 %collective-permute-done.11.refs_3_ = bf16[8,128,256]{2,1,0:T(8,128)(2,1)S(1)} collective-permute-done((bf16[8,128,256]{2,1,0:T(8,128)(2,1)S(1)}, bf16[8,128,256]{2,1,0:T(8,128)(2,1)S(1)}, u32[]{:S(2)}, u32[]{:S(2)}) %collective-permute-start.11) | collective-permute-done | bytes 524320 | tf_op jit(solution)/shard_map/ppermute | solution.py:412
  163.1 0.8 copy-done.14
  163.9 5.8 %all-to-all-done.4.b_ref.refs_4_.ob_ref.ka_ref = bf16[8,256,256]{2,1,0:T(8,128)(2,1)S(1)} async-done(((bf16[8,256,256]{2,1,0:T(8,128)(2,1)}), bf16[8,256,256]{2,1,0:T(8,128)(2,1)S(1)}, u32[]{:S(2)}, u32[]{:S(2)}) %all-to-all-start.4) | async-done | bytes 1048608 | tf_op jit(solution)/shard_map/all_to_all | solution.py:358
  169.8 1.0 copy-done.1
  170.8 2.3 %sum_parts.2.kb_ref = bf16[8,128,256]{2,1,0:T(8,128)(2,1)} custom-call(bf16[8,128,256]{2,1,0:T(8,128)(2,1)} %get-tuple-element.45.refs_0_, bf16[8,128,256]{2,1,0:T(8,128)(2,1)} %collective-permute-done.9.refs_1_, bf16[8,128,256]{2,1,0:T(8,128)(2,1)} %copy-done.13, bf16[8,128,256]{2,1,0:T(8,128)(2,1)} %copy-done.14, bf16[8,256,256]{2,1,0:T(8,128)(2,1)} %copy-done.1), custom_call_target="tpu_custom_call" | custom-call | tf_op jit(solution)/shard_map/sum_parts/pallas_call | solution.py:378
  173.1 3.5 %all-to-all-start.5 = ((bf16[8,128,256]{2,1,0:T(8,128)(2,1)}), bf16[8,128,256]{2,1,0:T(8,128)(2,1)S(1)}, u32[]{:S(2)}, u32[]{:S(2)}) async-start(bf16[8,128,256]{2,1,0:T(8,128)(2,1)} %sum_parts.2.kb_ref), calls=%async_computation.5 | async-start | bytes 1048576 | tf_op jit(solution)/shard_map/all_to_all | solution.py:358
  176.6 6.3 %weight_share.1 = (bf16[512,384]{1,0:T(8,128)(2,1)}, bf16[512,384]{1,0:T(8,128)(2,1)}) custom-call(s32[1]{0:T(128)} %bitcast.9.c_ref, bf16[8,128,256]{2,1,0:T(8,128)(2,1)} %gate.5.after_ref.oa_ref, bf16[8,128,256]{2,1,0:T(8,128)(2,1)} %get-tuple-element.44.od_ref.ob_ref, bf16[8,256,256]{2,1,0:T(8,128)(2,1)} %sum_join.1.ka_ref, ...), custom_call_target="tpu_custom_call" | custom-call | tf_op jit(solution)/shard_map/weight_share/pallas_call | solution.py:452
  182.9 1.9 collective-permute-done.12.refs_1_
  184.8 0.7 copy-done.16
  185.6 1.9 sum_parts.3
  187.5 1.8 reshape.34.refs_0_
  189.4 2.5 %all-to-all-done.5.kb_ref.refs_1_ = bf16[8,128,256]{2,1,0:T(8,128)(2,1)S(1)} async-done(((bf16[8,128,256]{2,1,0:T(8,128)(2,1)}), bf16[8,128,256]{2,1,0:T(8,128)(2,1)S(1)}, u32[]{:S(2)}, u32[]{:S(2)}) %all-to-all-start.5) | async-done | bytes 524320 | tf_op jit(solution)/shard_map/all_to_all | solution.py:358
  191.9 0.8 copy-done.4
  192.7 11.5 %all-to-all-start.6 = ((bf16[128,4,384]{2,1,0:T(4,128)(2,1)}), bf16[128,4,384]{2,1,0:T(4,128)(2,1)S(1)}, u32[]{:S(2)}, u32[]{:S(2)}) async-start(bf16[128,4,384]{2,1,0:T(4,128)(2,1)} %gate.7), calls=%async_computation.6 | async-start | bytes 786432 | tf_op jit(solution)/shard_map/all_to_all | solution.py:358
  204.2 4.4 %project_out.1.refs_0_ = bf16[256,1024]{1,0:T(8,128)(2,1)} custom-call(bf16[8,128,256]{2,1,0:T(8,128)(2,1)} %copy-done.3, bf16[8,256,256]{2,1,0:T(8,128)(2,1)} %copy-done.1, bf16[1024,1024]{1,0:T(8,128)(2,1)} %wo_ref.3), custom_call_target="tpu_custom_call" | custom-call | tf_op jit(solution)/shard_map/project_out/pallas_call | solution.py:283
  208.5 6.3 %node_grads.1.refs_1_ = bf16[256,1024]{1,0:T(8,128)(2,1)} custom-call(bf16[8,128,256]{2,1,0:T(8,128)(2,1)} %copy-done.3, bf16[8,256,256]{2,1,0:T(8,128)(2,1)} %copy-done.1, bf16[8,256,256]{2,1,0:T(8,128)(2,1)} %copy-done.1, bf16[8,128,256]{2,1,0:T(8,128)(2,1)} %copy-done.4, bf16[1024,3072]{1,0:T(8,128)(2,1)} %wv_ref.3, bf16[1024,3072]{1,0:T(8,128)(2,1)} %wv_ref.3, ...), custom_call_target="tpu_custom_call" | custom-call | tf_op jit(solution)/shard_map/node_grads/pallas_call | solution.py:322
  214.8 5.5 %all-to-all-done.6.x_ref = bf16[128,4,384]{2,1,0:T(4,128)(2,1)S(1)} async-done(((bf16[128,4,384]{2,1,0:T(4,128)(2,1)}), bf16[128,4,384]{2,1,0:T(4,128)(2,1)S(1)}, u32[]{:S(2)}, u32[]{:S(2)}) %all-to-all-start.6) | async-done | bytes 393248 | tf_op jit(solution)/shard_map/all_to_all | solution.py:358
  220.3 0.7 copy-done.9
  221.0 1.8 spread.1
  (63 shorter events, 3.3 us)
Async XLA Ops:
  7.2 13.7 %copy-start = (s32[1,64,8]{1,2,0:T(8,128)S(1)}, s32[1,64,8]{1,2,0:T(8,128)}, u32[]{:S(2)}) copy-start(s32[1,64,8]{1,2,0:T(8,128)} %param.11) | copy-start | bytes 6148
  7.2 13.6 %copy-start.20 = (s32[1,4]{1,0:T(1,128)S(1)}, s32[1,4]{1,0:T(1,128)}, u32[]{:S(2)}) copy-start(s32[1,4]{1,0:T(1,128)} %param.13) | copy-start | bytes 52
  7.2 14.6 %copy-start.17 = (s32[1,64]{1,0:T(1,128)S(1)}, s32[1,64]{1,0:T(1,128)}, u32[]{:S(2)}) copy-start(s32[1,64]{1,0:T(1,128)} %param.12) | copy-start | bytes 772
  12.4 26.0 %all-to-all-start = ((bf16[8,128,256]{2,1,0:T(8,128)(2,1)}), bf16[8,128,256]{2,1,0:T(8,128)(2,1)S(1)}, u32[]{:S(2)}, u32[]{:S(2)}) async-start(bf16[8,128,256]{2,1,0:T(8,128)(2,1)} %get-tuple-element.27), calls=%async_computation | async-start | bytes 1048576 | tf_op jit(solution)/shard_map/all_to_all | solution.py:358
  38.3 43.5 %copy-start.15 = (bf16[8,128,256]{2,1,0:T(8,128)(2,1)}, bf16[8,128,256]{2,1,0:T(8,128)(2,1)S(1)}, u32[]{:S(2)}) copy-start(bf16[8,128,256]{2,1,0:T(8,128)(2,1)S(1)} %all-to-all-done.own_ref) | copy-start | bytes 1572868
  38.3 32.7 %all-to-all-start.1 = ((bf16[8,256,256]{2,1,0:T(8,128)(2,1)}), bf16[8,256,256]{2,1,0:T(8,128)(2,1)S(1)}, u32[]{:S(2)}, u32[]{:S(2)}) async-start(bf16[8,256,256]{2,1,0:T(8,128)(2,1)} %get-tuple-element.29), calls=%async_computation.1 | async-start | bytes 2097152 | tf_op jit(solution)/shard_map/all_to_all | solution.py:358
  41.9 134.7 %all-gather.2.cloned.1.call-start = ((), (), s32[]{:S(2)}) async-start(), calls=%async_computation.7 | async-start | bytes 4718592 | tf_op jit(solution)/shard_map/all_gather | solution.py:484
  41.9 37.4 %collective-permute-start = (bf16[8,128,256]{2,1,0:T(8,128)(2,1)S(1)}, bf16[8,128,256]{2,1,0:T(8,128)(2,1)S(1)}, u32[]{:S(2)}, u32[]{:S(2)}) collective-permute-start(bf16[8,128,256]{2,1,0:T(8,128)(2,1)S(1)} %all-to-all-done.own_ref), channel_id=1, source_target_pairs={{0,8},{8,16},{16,24},{24,0},{1,9},{9,17},{17,25},{25,1},{2,10},{10... | collective-permute-start | bytes 1572872 | tf_op jit(solution)/shard_map/ppermute | solution.py:367
  43.6 38.2 %collective-permute-start.1 = (bf16[8,128,256]{2,1,0:T(8,128)(2,1)S(1)}, bf16[8,128,256]{2,1,0:T(8,128)(2,1)}, u32[]{:S(2)}, u32[]{:S(2)}) collective-permute-start(bf16[8,128,256]{2,1,0:T(8,128)(2,1)S(1)} %all-to-all-done.own_ref), channel_id=1, source_target_pairs={{0,24},{8,0},{16,8},{24,16},{1,25},{9,1},{17,9},{25,17},{2,26},{10... | collective-permute-start | bytes 1572872 | tf_op jit(solution)/shard_map/ppermute | solution.py:367
  44.0 37.8 %collective-permute-start.2 = (bf16[8,128,256]{2,1,0:T(8,128)(2,1)S(1)}, bf16[8,128,256]{2,1,0:T(8,128)(2,1)}, u32[]{:S(2)}, u32[]{:S(2)}) collective-permute-start(bf16[8,128,256]{2,1,0:T(8,128)(2,1)S(1)} %all-to-all-done.own_ref), channel_id=1, source_target_pairs={{0,16},{8,24},{16,0},{24,8},{1,17},{9,25},{17,1},{25,9},{2,18},{10... | collective-permute-start | bytes 1572872 | tf_op jit(solution)/shard_map/ppermute | solution.py:367
  71.0 1.0 copy-start.2
  73.8 35.0 %collective-permute-start.6 = (bf16[8,128,256]{2,1,0:T(8,128)(2,1)}, bf16[8,128,256]{2,1,0:T(8,128)(2,1)S(1)}, u32[]{:S(2)}, u32[]{:S(2)}) collective-permute-start(bf16[8,128,256]{2,1,0:T(8,128)(2,1)} %first_half.1.own_ref), channel_id=1, source_target_pairs={{0,8},{8,16},{16,24},{24,0},{1,9},{9,17},{17,25},{25,1},{2,10},{10... | collective-permute-start | bytes 1572872 | tf_op jit(solution)/shard_map/ppermute | solution.py:367
  75.4 34.5 %collective-permute-start.7 = (bf16[8,128,256]{2,1,0:T(8,128)(2,1)}, bf16[8,128,256]{2,1,0:T(8,128)(2,1)}, u32[]{:S(2)}, u32[]{:S(2)}) collective-permute-start(bf16[8,128,256]{2,1,0:T(8,128)(2,1)} %first_half.1.own_ref), channel_id=1, source_target_pairs={{0,24},{8,0},{16,8},{24,16},{1,25},{9,1},{17,9},{25,17},{2,26},{10... | collective-permute-start | bytes 1572872 | tf_op jit(solution)/shard_map/ppermute | solution.py:367
  75.9 26.7 %all-to-all-start.2 = ((bf16[8,128,256]{2,1,0:T(8,128)(2,1)}), bf16[8,128,256]{2,1,0:T(8,128)(2,1)S(1)}, u32[]{:S(2)}, u32[]{:S(2)}) async-start(bf16[8,128,256]{2,1,0:T(8,128)(2,1)} %get-tuple-element.34), calls=%async_computation.2 | async-start | bytes 1048576 | tf_op jit(solution)/shard_map/all_to_all | solution.py:358
  79.4 2.4 %copy-start.19 = (bf16[8,128,256]{2,1,0:T(8,128)(2,1)}, bf16[8,128,256]{2,1,0:T(8,128)(2,1)S(1)}, u32[]{:S(2)}) copy-start(bf16[8,128,256]{2,1,0:T(8,128)(2,1)S(1)} %collective-permute-done.left_ref) | copy-start | bytes 1572868
  79.4 30.5 %collective-permute-start.8 = (bf16[8,128,256]{2,1,0:T(8,128)(2,1)}, bf16[8,128,256]{2,1,0:T(8,128)(2,1)}, u32[]{:S(2)}, u32[]{:S(2)}) collective-permute-start(bf16[8,128,256]{2,1,0:T(8,128)(2,1)} %first_half.1.own_ref), channel_id=1, source_target_pairs={{0,16},{8,24},{16,0},{24,8},{1,17},{9,25},{17,1},{25,9},{2,18},{10... | collective-permute-start | bytes 1572872 | tf_op jit(solution)/shard_map/ppermute | solution.py:367
  98.9 28.0 %collective-permute-start.3 = (bf16[8,128,256]{2,1,0:T(8,128)(2,1)}, bf16[8,128,256]{2,1,0:T(8,128)(2,1)S(1)}, u32[]{:S(2)}, u32[]{:S(2)}) collective-permute-start(bf16[8,128,256]{2,1,0:T(8,128)(2,1)} %get-tuple-element.36), channel_id=1, source_target_pairs={{0,8},{8,16},{16,24},{24,0},{1,9},{9,17},{17,25},{25,1},{2,10},{10... | collective-permute-start | bytes 1572872 | tf_op jit(solution)/shard_map/ppermute | solution.py:410
  99.3 27.5 %collective-permute-start.4 = (bf16[8,128,256]{2,1,0:T(8,128)(2,1)}, bf16[8,128,256]{2,1,0:T(8,128)(2,1)S(1)}, u32[]{:S(2)}, u32[]{:S(2)}) collective-permute-start(bf16[8,128,256]{2,1,0:T(8,128)(2,1)} %get-tuple-element.37), channel_id=1, source_target_pairs={{0,24},{8,0},{16,8},{24,16},{1,25},{9,1},{17,9},{25,17},{2,26},{10... | collective-permute-start | bytes 1572872 | tf_op jit(solution)/shard_map/ppermute | solution.py:411
  102.6 0.8 copy-start.8
  103.4 28.0 %all-to-all-start.3 = ((bf16[8,128,256]{2,1,0:T(8,128)(2,1)}), bf16[8,128,256]{2,1,0:T(8,128)(2,1)S(1)}, u32[]{:S(2)}, u32[]{:S(2)}) async-start(bf16[8,128,256]{2,1,0:T(8,128)(2,1)} %gate.5.after_ref.oa_ref), calls=%async_computation.3 | async-start | bytes 1048576 | tf_op jit(solution)/shard_map/all_to_all | solution.py:358
  108.8 1.1 copy-start.18
  108.8 18.0 %collective-permute-start.5 = (bf16[8,128,256]{2,1,0:T(8,128)(2,1)}, bf16[8,128,256]{2,1,0:T(8,128)(2,1)S(1)}, u32[]{:S(2)}, u32[]{:S(2)}) collective-permute-start(bf16[8,128,256]{2,1,0:T(8,128)(2,1)} %get-tuple-element.38), channel_id=1, source_target_pairs={{0,16},{8,24},{16,0},{24,8},{1,17},{9,25},{17,1},{25,9},{2,18},{10... | collective-permute-start | bytes 1572872 | tf_op jit(solution)/shard_map/ppermute | solution.py:412
  126.8 4.5 %copy-start.5 = (bf16[8,128,256]{2,1,0:T(8,128)(2,1)}, bf16[8,128,256]{2,1,0:T(8,128)(2,1)S(1)}, u32[]{:S(2)}) copy-start(bf16[8,128,256]{2,1,0:T(8,128)(2,1)S(1)} %collective-permute-done.3.refs_5_.b_ref) | copy-start | bytes 1572868
  126.8 4.5 %copy-start.6 = (bf16[8,128,256]{2,1,0:T(8,128)(2,1)}, bf16[8,128,256]{2,1,0:T(8,128)(2,1)S(1)}, u32[]{:S(2)}) copy-start(bf16[8,128,256]{2,1,0:T(8,128)(2,1)S(1)} %collective-permute-done.4.refs_6_.c_ref) | copy-start | bytes 1572868
  126.9 4.5 %copy-start.7 = (bf16[8,128,256]{2,1,0:T(8,128)(2,1)}, bf16[8,128,256]{2,1,0:T(8,128)(2,1)S(1)}, u32[]{:S(2)}) copy-start(bf16[8,128,256]{2,1,0:T(8,128)(2,1)S(1)} %collective-permute-done.5.refs_7_.d_ref) | copy-start | bytes 1572868
  131.3 0.8 copy-start.3
  132.1 6.3 %copy-start.11 = (bf16[8,128,256]{2,1,0:T(8,128)(2,1)S(1)}, bf16[8,128,256]{2,1,0:T(8,128)(2,1)}, u32[]{:S(2)}) copy-start(bf16[8,128,256]{2,1,0:T(8,128)(2,1)} %get-tuple-element.47) | copy-start | bytes 1572868
  132.1 9.1 %copy-start.12 = (bf16[8,128,256]{2,1,0:T(8,128)(2,1)S(1)}, bf16[8,128,256]{2,1,0:T(8,128)(2,1)}, u32[]{:S(2)}) copy-start(bf16[8,128,256]{2,1,0:T(8,128)(2,1)} %get-tuple-element.48) | copy-start | bytes 1572868
  132.1 9.7 %copy-start.10 = (bf16[8,128,256]{2,1,0:T(8,128)(2,1)S(1)}, bf16[8,128,256]{2,1,0:T(8,128)(2,1)}, u32[]{:S(2)}) copy-start(bf16[8,128,256]{2,1,0:T(8,128)(2,1)} %get-tuple-element.46) | copy-start | bytes 1572868
  134.9 34.9 %all-to-all-start.4 = ((bf16[8,256,256]{2,1,0:T(8,128)(2,1)}), bf16[8,256,256]{2,1,0:T(8,128)(2,1)S(1)}, u32[]{:S(2)}, u32[]{:S(2)}) async-start(bf16[8,256,256]{2,1,0:T(8,128)(2,1)} %sum_join.1.ka_ref), calls=%async_computation.4 | async-start | bytes 2097152 | tf_op jit(solution)/shard_map/all_to_all | solution.py:358
  138.5 15.1 %collective-permute-start.10 = (bf16[8,128,256]{2,1,0:T(8,128)(2,1)S(1)}, bf16[8,128,256]{2,1,0:T(8,128)(2,1)S(1)}, u32[]{:S(2)}, u32[]{:S(2)}) collective-permute-start(bf16[8,128,256]{2,1,0:T(8,128)(2,1)S(1)} %copy-done.11), channel_id=1, source_target_pairs={{0,24},{8,0},{16,8},{24,16},{1,25},{9,1},{17,9},{25,17},{2,26},{10... | collective-permute-start | bytes 1572872 | tf_op jit(solution)/shard_map/ppermute | solution.py:411
  141.2 21.9 %collective-permute-start.11 = (bf16[8,128,256]{2,1,0:T(8,128)(2,1)S(1)}, bf16[8,128,256]{2,1,0:T(8,128)(2,1)S(1)}, u32[]{:S(2)}, u32[]{:S(2)}) collective-permute-start(bf16[8,128,256]{2,1,0:T(8,128)(2,1)S(1)} %copy-done.12), channel_id=1, source_target_pairs={{0,16},{8,24},{16,0},{24,8},{1,17},{9,25},{17,1},{25,9},{2,18},{10... | collective-permute-start | bytes 1572872 | tf_op jit(solution)/shard_map/ppermute | solution.py:412
  141.8 22.1 %collective-permute-start.9 = (bf16[8,128,256]{2,1,0:T(8,128)(2,1)S(1)}, bf16[8,128,256]{2,1,0:T(8,128)(2,1)}, u32[]{:S(2)}, u32[]{:S(2)}) collective-permute-start(bf16[8,128,256]{2,1,0:T(8,128)(2,1)S(1)} %copy-done.10), channel_id=1, source_target_pairs={{0,8},{8,16},{16,24},{24,0},{1,9},{9,17},{17,25},{25,1},{2,10},{10... | collective-permute-start | bytes 1572872 | tf_op jit(solution)/shard_map/ppermute | solution.py:410
  153.6 16.2 %copy-start.13 = (bf16[8,128,256]{2,1,0:T(8,128)(2,1)}, bf16[8,128,256]{2,1,0:T(8,128)(2,1)S(1)}, u32[]{:S(2)}) copy-start(bf16[8,128,256]{2,1,0:T(8,128)(2,1)S(1)} %collective-permute-done.10.refs_2_) | copy-start | bytes 1572868
  163.1 0.8 copy-start.14
  169.8 1.0 copy-start.1
  173.1 18.8 %all-to-all-start.5 = ((bf16[8,128,256]{2,1,0:T(8,128)(2,1)}), bf16[8,128,256]{2,1,0:T(8,128)(2,1)S(1)}, u32[]{:S(2)}, u32[]{:S(2)}) async-start(bf16[8,128,256]{2,1,0:T(8,128)(2,1)} %sum_parts.2.kb_ref), calls=%async_computation.5 | async-start | bytes 1048576 | tf_op jit(solution)/shard_map/all_to_all | solution.py:358
  182.9 1.9 collective-permute-start.12
  184.8 0.7 copy-start.16
  191.9 0.8 copy-start.4
  192.7 27.6 %all-to-all-start.6 = ((bf16[128,4,384]{2,1,0:T(4,128)(2,1)}), bf16[128,4,384]{2,1,0:T(4,128)(2,1)S(1)}, u32[]{:S(2)}, u32[]{:S(2)}) async-start(bf16[128,4,384]{2,1,0:T(4,128)(2,1)} %gate.7), calls=%async_computation.6 | async-start | bytes 786432 | tf_op jit(solution)/shard_map/all_to_all | solution.py:358
  220.3 0.8 copy-start.9
Sparse Core Ops, SparseCore 0:
  72.2 83.4 all-gather.1

commit v7 on v6

--- a/solution.py
+++ b/solution.py
@@ -330,6 +330,26 @@
         compiler_params=VMEM,
         name="node_grads",
     )(od_a, joint, joint, kv_b, w_qkv, w_qkv, w_qkv)
+
+
+def rows_kernel(x_ref, *refs):
+    o_ref = refs[-1]
+    total = jnp.sum(x_ref[...].astype(f32), axis=0)
+    step = total.shape[0] // ZS
+    for z in range(ZS):
+        o_ref[z] = total[z * step : (z + 1) * step]
+
+
+def sum_rows(parts, after):
+    vmem = pl.BlockSpec(memory_space=pltpu.VMEM)
+    return pl.pallas_call(
+        rows_kernel,
+        in_specs=[vmem] + [pl.BlockSpec(memory_space=pl.ANY)] * len(after),
+        out_specs=vmem,
+        out_shape=jax.ShapeDtypeStruct((ZS, parts.shape[1] // ZS, parts.shape[2]), f32),
+        compiler_params=VMEM,
+        name="sum_rows",
+    )(parts, *after)
 
 
 def spread_kernel(x_ref, *refs):
@@ -501,10 +521,10 @@
     c_arr = lax.axis_index("c").reshape(1).astype(jnp.int32)
     mine, theirs = weight_share(c_arr, od_a_late, od_b, joint, sum_b, feats_row)
     theirs = lax.ppermute(theirs, "c", [(0, 1), (1, 0)])
-    share = sum_parts([mine, theirs], ()).reshape(16 * ZS, d // 256, 384)
+    share = sum_parts([mine, theirs], ()).reshape(16, d // 32, 384)
     (share,) = gate([share], [kv_nodes_b])
-    share = swap(share, ("x", "y", "z"))
-    grad_weights = spread(share, (attn_update, grad_nodes))
+    share = sum_rows(swap(share, ("x", "y")), (grad_nodes,))
+    grad_weights = spread(swap(share, "z"), (attn_update,))
     return attn_update[None], grad_nodes[None], grad_weights
 
 

time: 233 us -> 232 us (level)
  waiting for transfers between devices: 76.4 us -> 79 us
    ppermute x2, waiting for transfers between devices: 9.5 us -> 0.01 us  [send_row(): lax.ppermute(opp, 'y', OPPOSITE)]
    ppermute x2, waiting for transfers between devices: 10.8 us -> 19.9 us  [send_row(): lax.ppermute(to_left, 'y', LEFT)]
    all_to_all x7 -> x8, waiting for transfers between devices: 54 us -> 56.1 us  [swap(): return lax.all_to_all(values, axis, split_axis=0, concat_axis=0, tiled=True)]
    all_to_all x7 -> x8, starting transfers between devices: 39.5 us -> 38.3 us  [swap(): return lax.all_to_all(values, axis, split_axis=0, concat_axis=0, tiled=True)]
    unnamed x42 -> x44, local copies, waits for them, and re-layouts: 6.74 us -> 7.49 us
  transfers between devices with their start and end apart: 21 -> 22, of which waited for: 11 -> 11; matrix products, arithmetic and copies ran while one was open for 2% -> 1% of each run, Pallas kernels for 28% -> 28%
where the time goes in v7:
time: 232 us; the launch traced here: 231 us
  waiting for transfers between devices  79 us (34%)
  Pallas kernels  72.6 us (31%)
  starting transfers between devices  55.1 us (24%)
  between operations  14.2 us (6%)
  local copies, waits for them, and re-layouts  8.31 us (4%)
    all_to_all x8, waiting for transfers between devices, swap(): return lax.all_to_all(values, axis, split_axis=0, concat_axis=0, tiled=True)  56.1 us
    all_to_all x8, starting transfers between devices, swap(): return lax.all_to_all(values, axis, split_axis=0, concat_axis=0, tiled=True)  38.3 us
    pallas_call x2, Pallas kernels, attend(): pl.pallas_call(functools.partial(attend_kernel, qg.shape[1] - 128), in_sp...  32.9 us
    ppermute x2, waiting for transfers between devices, send_row(): lax.ppermute(to_left, 'y', LEFT)  19.9 us
    unnamed x44, local copies, waits for them, and re-layouts  7.49 us
    pallas_call x1, Pallas kernels, weight_share(): pl.pallas_call(weight_kernel, grid=(d // 256,), in_specs=[pl.BlockSpec(me...  6.29 us
    pallas_call x1, Pallas kernels, node_grads(): pl.pallas_call(nodes_kernel, grid=(steps,), in_specs=[tile, SECOND, tile,...  6.28 us
    pallas_call x1, Pallas kernels, project_qg(): pl.pallas_call(qg_kernel, grid=(ZS // 2,), in_specs=[whole((NODE_DEV, d))...  5.7 us
  transfers between devices with their start and end apart: 22, of which 11 were waited for; matrix products, arithmetic and copies ran while one was open for 1% of the time, Pallas kernels for 28%

profile of v7, /device:TPU:8, one launch (start us, length us, event | category | flops | bytes accessed | tf_op | source)
XLA Modules:
  0.0 230.9 jit_solution(6086519624570437635)
XLA Ops:
  7.2 5.2 %project_kv.1 = (bf16[8,128,256]{2,1,0:T(8,128)(2,1)}, bf16[8,128,256]{2,1,0:T(8,128)(2,1)}) custom-call(bf16[256,1024]{1,0:T(8,128)(2,1)} %bitcast.18, bf16[1024,3072]{1,0:T(8,128)(2,1)} %wv_ref.3, bf16[1024,3072]{1,0:T(8,128)(2,1)} %wv_ref.3), custom_call_target="tpu_custom_call" | custom-call | tf_op jit(solution)/shard_map/project_kv/pallas_call | solution.py:108
  12.4 8.5 %all-to-all-start = ((bf16[8,128,256]{2,1,0:T(8,128)(2,1)}), bf16[8,128,256]{2,1,0:T(8,128)(2,1)S(1)}, u32[]{:S(2)}, u32[]{:S(2)}) async-start(bf16[8,128,256]{2,1,0:T(8,128)(2,1)} %get-tuple-element.27), calls=%async_computation | async-start | bytes 1048576 | tf_op jit(solution)/shard_map/all_to_all | solution.py:378
  23.3 5.7 %project_qg.1 = (bf16[8,256,256]{2,1,0:T(8,128)(2,1)}, bf16[8,128,256]{2,1,0:T(8,128)(2,1)}, bf16[256,1024]{1,0:T(8,128)(2,1)}) custom-call(bf16[256,1024]{1,0:T(8,128)(2,1)} %bitcast.19, bf16[256,1024]{1,0:T(8,128)(2,1)} %bitcast.20, bf16[1024,3072]{1,0:T(8,128)(2,1)} %wv_ref.3, bf16[1024,1024]{1,0:T(8,128)(2,1)} %wo_ref.3, ...), custom_call_target="tpu_custom_call" | custom-call | tf_op jit(solution)/shard_map/project_qg/pallas_call | solution.py:126
  29.0 9.3 %all-to-all-done.own_ref = bf16[8,128,256]{2,1,0:T(8,128)(2,1)S(1)} async-done(((bf16[8,128,256]{2,1,0:T(8,128)(2,1)}), bf16[8,128,256]{2,1,0:T(8,128)(2,1)S(1)}, u32[]{:S(2)}, u32[]{:S(2)}) %all-to-all-start) | async-done | bytes 524320 | tf_op jit(solution)/shard_map/all_to_all | solution.py:378
  38.3 3.6 %all-to-all-start.1 = ((bf16[8,256,256]{2,1,0:T(8,128)(2,1)}), bf16[8,256,256]{2,1,0:T(8,128)(2,1)S(1)}, u32[]{:S(2)}, u32[]{:S(2)}) async-start(bf16[8,256,256]{2,1,0:T(8,128)(2,1)} %get-tuple-element.29), calls=%async_computation.1 | async-start | bytes 2097152 | tf_op jit(solution)/shard_map/all_to_all | solution.py:378
  41.9 1.7 collective-permute-start
  44.0 2.3 collective-permute-start.2
  46.3 24.7 %all-to-all-done.1.refs_2_.qg_ref.x_ref = bf16[8,256,256]{2,1,0:T(8,128)(2,1)S(1)} async-done(((bf16[8,256,256]{2,1,0:T(8,128)(2,1)}), bf16[8,256,256]{2,1,0:T(8,128)(2,1)S(1)}, u32[]{:S(2)}, u32[]{:S(2)}) %all-to-all-start.1) | async-done | bytes 1048608 | tf_op jit(solution)/shard_map/all_to_all | solution.py:378
  71.0 1.1 copy-done.2
  72.1 1.8 first_half.1.own_ref
  73.9 1.6 collective-permute-start.6
  75.9 3.5 %all-to-all-start.2 = ((bf16[8,128,256]{2,1,0:T(8,128)(2,1)}), bf16[8,128,256]{2,1,0:T(8,128)(2,1)S(1)}, u32[]{:S(2)}, u32[]{:S(2)}) async-start(bf16[8,128,256]{2,1,0:T(8,128)(2,1)} %get-tuple-element.34), calls=%async_computation.2 | async-start | bytes 1048576 | tf_op jit(solution)/shard_map/all_to_all | solution.py:378
  79.4 2.4 %collective-permute-start.8 = (bf16[8,128,256]{2,1,0:T(8,128)(2,1)}, bf16[8,128,256]{2,1,0:T(8,128)(2,1)}, u32[]{:S(2)}, u32[]{:S(2)}) collective-permute-start(bf16[8,128,256]{2,1,0:T(8,128)(2,1)} %first_half.1.own_ref), channel_id=1, source_target_pairs={{0,16},{8,24},{16,0},{24,8},{1,17},{9,25},{17,1},{25,9},{2,18},{10... | collective-permute-start | bytes 1572872 | tf_op jit(solution)/shard_map/ppermute | solution.py:387
  81.8 16.5 %attend.2 = (bf16[8,128,256]{2,1,0:T(8,128)(2,1)}, bf16[8,128,256]{2,1,0:T(8,128)(2,1)}, bf16[8,128,256]{2,1,0:T(8,128)(2,1)}, bf16[8,128,256]{2,1,0:T(8,128)(2,1)}, bf16[8,128,256]{2,1,0:T(8,128)(2,1)}) custom-call(s32[192]{0:T(256)} %reshape.31.refs_0_.tab_ref, s32[16]{0:T(128)} %get-tuple-element.52.refs_1_.cnt_ref, ...), custom_call_target="tpu_custom_call" | custom-call | flops 25999998976 | bytes 6291456 | tf_op jit(solution)/shard_map/attend/pallas_call | solution.py:237
  98.3 1.4 collective-permute-start.3
  100.4 2.3 all-to-all-done.2.refs_1_.qg_ref
  102.6 0.8 copy-done.8
  103.4 4.9 %all-to-all-start.3 = ((bf16[8,128,256]{2,1,0:T(8,128)(2,1)}), bf16[8,128,256]{2,1,0:T(8,128)(2,1)S(1)}, u32[]{:S(2)}, u32[]{:S(2)}) async-start(bf16[8,128,256]{2,1,0:T(8,128)(2,1)} %gate.5.after_ref.oa_ref), calls=%async_computation.3 | async-start | bytes 1048576 | tf_op jit(solution)/shard_map/all_to_all | solution.py:378
  108.3 2.0 collective-permute-start.5
  110.3 16.4 %attend.3 = (bf16[8,128,256]{2,1,0:T(8,128)(2,1)}, bf16[8,128,256]{2,1,0:T(8,128)(2,1)}, bf16[8,128,256]{2,1,0:T(8,128)(2,1)}, bf16[8,128,256]{2,1,0:T(8,128)(2,1)}, bf16[8,128,256]{2,1,0:T(8,128)(2,1)}) custom-call(s32[192]{0:T(256)} %reshape.31.refs_0_.tab_ref, s32[16]{0:T(128)} %get-tuple-element.52.refs_1_.cnt_ref, ...), custom_call_target="tpu_custom_call" | custom-call | flops 25999998976 | bytes 6291456 | tf_op jit(solution)/shard_map/attend/pallas_call | solution.py:237
  126.7 5.1 %all-to-all-done.3.refs_8_.a_ref.oa_ref = bf16[8,128,256]{2,1,0:T(8,128)(2,1)S(1)} async-done(((bf16[8,128,256]{2,1,0:T(8,128)(2,1)}), bf16[8,128,256]{2,1,0:T(8,128)(2,1)S(1)}, u32[]{:S(2)}, u32[]{:S(2)}) %all-to-all-start.3) | async-done | bytes 524320 | tf_op jit(solution)/shard_map/all_to_all | solution.py:378
  131.9 0.8 copy-done.3
  132.7 2.8 %sum_join.1.ka_ref = bf16[8,256,256]{2,1,0:T(8,128)(2,1)} custom-call(bf16[8,128,256]{2,1,0:T(8,128)(2,1)} %get-tuple-element.35.a_ref, bf16[8,128,256]{2,1,0:T(8,128)(2,1)} %copy-done.5, bf16[8,128,256]{2,1,0:T(8,128)(2,1)} %copy-done.6, bf16[8,128,256]{2,1,0:T(8,128)(2,1)} %copy-done.7, bf16[8,128,256]{2,1,0:T(8,128)(2,1)} %get-tuple-element.44.od_ref.ob_ref), custom_call_target="tpu_custom_call" | custom-call | tf_op jit(solution)/shard_map/sum_join/pallas_call | solution.py:416
  135.4 3.6 %all-to-all-start.4 = ((bf16[8,256,256]{2,1,0:T(8,128)(2,1)}), bf16[8,256,256]{2,1,0:T(8,128)(2,1)S(1)}, u32[]{:S(2)}, u32[]{:S(2)}) async-start(bf16[8,256,256]{2,1,0:T(8,128)(2,1)} %sum_join.1.ka_ref), calls=%async_computation.4 | async-start | bytes 2097152 | tf_op jit(solution)/shard_map/all_to_all | solution.py:378
  139.0 1.9 collective-permute-start.10
  140.9 1.4 collective-permute-start.11
  143.0 19.9 %collective-permute-done.10.refs_2_ = bf16[8,128,256]{2,1,0:T(8,128)(2,1)S(1)} collective-permute-done((bf16[8,128,256]{2,1,0:T(8,128)(2,1)S(1)}, bf16[8,128,256]{2,1,0:T(8,128)(2,1)S(1)}, u32[]{:S(2)}, u32[]{:S(2)}) %collective-permute-start.10) | collective-permute-done | bytes 524320 | tf_op jit(solution)/shard_map/ppermute | solution.py:431
  162.9 0.8 copy-done.14
  163.8 1.1 collective-permute-done.9.refs_1_
  164.8 5.0 %all-to-all-done.4.b_ref.refs_4_.ob_ref.ka_ref = bf16[8,256,256]{2,1,0:T(8,128)(2,1)S(1)} async-done(((bf16[8,256,256]{2,1,0:T(8,128)(2,1)}), bf16[8,256,256]{2,1,0:T(8,128)(2,1)S(1)}, u32[]{:S(2)}, u32[]{:S(2)}) %all-to-all-start.4) | async-done | bytes 1048608 | tf_op jit(solution)/shard_map/all_to_all | solution.py:378
  169.8 1.0 copy-done.1
  170.9 2.3 %sum_parts.2.kb_ref = bf16[8,128,256]{2,1,0:T(8,128)(2,1)} custom-call(bf16[8,128,256]{2,1,0:T(8,128)(2,1)} %get-tuple-element.45.refs_0_, bf16[8,128,256]{2,1,0:T(8,128)(2,1)} %collective-permute-done.9.refs_1_, bf16[8,128,256]{2,1,0:T(8,128)(2,1)} %copy-done.13, bf16[8,128,256]{2,1,0:T(8,128)(2,1)} %copy-done.14, bf16[8,256,256]{2,1,0:T(8,128)(2,1)} %copy-done.1), custom_call_target="tpu_custom_call" | custom-call | tf_op jit(solution)/shard_map/sum_parts/pallas_call | solution.py:398
  173.2 3.5 %all-to-all-start.5 = ((bf16[8,128,256]{2,1,0:T(8,128)(2,1)}), bf16[8,128,256]{2,1,0:T(8,128)(2,1)S(1)}, u32[]{:S(2)}, u32[]{:S(2)}) async-start(bf16[8,128,256]{2,1,0:T(8,128)(2,1)} %sum_parts.2.kb_ref), calls=%async_computation.5 | async-start | bytes 1048576 | tf_op jit(solution)/shard_map/all_to_all | solution.py:378
  176.7 6.3 %weight_share.1 = (bf16[512,384]{1,0:T(8,128)(2,1)}, bf16[512,384]{1,0:T(8,128)(2,1)}) custom-call(s32[1]{0:T(128)} %bitcast.9.c_ref, bf16[8,128,256]{2,1,0:T(8,128)(2,1)} %gate.5.after_ref.oa_ref, bf16[8,128,256]{2,1,0:T(8,128)(2,1)} %get-tuple-element.44.od_ref.ob_ref, bf16[8,256,256]{2,1,0:T(8,128)(2,1)} %sum_join.1.ka_ref, ...), custom_call_target="tpu_custom_call" | custom-call | tf_op jit(solution)/shard_map/weight_share/pallas_call | solution.py:472
  183.0 1.9 collective-permute-done.12.refs_1_
  185.0 0.7 copy-done.16
  185.7 1.9 sum_parts.3
  187.6 4.6 %all-to-all-done.5.kb_ref.refs_1_ = bf16[8,128,256]{2,1,0:T(8,128)(2,1)S(1)} async-done(((bf16[8,128,256]{2,1,0:T(8,128)(2,1)}), bf16[8,128,256]{2,1,0:T(8,128)(2,1)S(1)}, u32[]{:S(2)}, u32[]{:S(2)}) %all-to-all-start.5) | async-done | bytes 524320 | tf_op jit(solution)/shard_map/all_to_all | solution.py:378
  192.2 0.8 copy-done.4
  193.0 7.2 %all-to-all-start.6 = ((bf16[16,32,384]{2,1,0:T(8,128)(2,1)}), bf16[16,32,384]{2,1,0:T(8,128)(2,1)S(1)}, u32[]{:S(2)}, u32[]{:S(2)}) async-start(bf16[16,32,384]{2,1,0:T(8,128)(2,1)} %gate.7), calls=%async_computation.6 | async-start | bytes 786432 | tf_op jit(solution)/shard_map/all_to_all | solution.py:378
  200.2 6.3 %node_grads.1.refs_0_ = bf16[256,1024]{1,0:T(8,128)(2,1)} custom-call(bf16[8,128,256]{2,1,0:T(8,128)(2,1)} %copy-done.3, bf16[8,256,256]{2,1,0:T(8,128)(2,1)} %copy-done.1, bf16[8,256,256]{2,1,0:T(8,128)(2,1)} %copy-done.1, bf16[8,128,256]{2,1,0:T(8,128)(2,1)} %copy-done.4, bf16[1024,3072]{1,0:T(8,128)(2,1)} %wv_ref.3, bf16[1024,3072]{1,0:T(8,128)(2,1)} %wv_ref.3, ...), custom_call_target="tpu_custom_call" | custom-call | tf_op jit(solution)/shard_map/node_grads/pallas_call | solution.py:322
  206.5 1.2 all-to-all-done.6.x_ref
  207.7 0.7 copy-done.9
  208.5 1.7 sum_rows.1
  210.1 3.7 %all-to-all-start.7 = ((f32[8,4,384]{2,1,0:T(4,128)}), f32[8,4,384]{2,1,0:T(4,128)S(1)}, u32[]{:S(2)}, u32[]{:S(2)}) async-start(f32[8,4,384]{2,1,0:T(4,128)} %sum_rows.1), calls=%async_computation.7 | async-start | bytes 98304 | tf_op jit(solution)/shard_map/all_to_all | solution.py:378
  213.8 4.4 %project_out.1.refs_0_ = bf16[256,1024]{1,0:T(8,128)(2,1)} custom-call(bf16[8,128,256]{2,1,0:T(8,128)(2,1)} %copy-done.3, bf16[8,256,256]{2,1,0:T(8,128)(2,1)} %copy-done.1, bf16[1024,1024]{1,0:T(8,128)(2,1)} %wo_ref.3), custom_call_target="tpu_custom_call" | custom-call | tf_op jit(solution)/shard_map/project_out/pallas_call | solution.py:283
  218.2 3.8 %all-to-all-done.7.x_ref = f32[8,4,384]{2,1,0:T(4,128)S(1)} async-done(((f32[8,4,384]{2,1,0:T(4,128)}), f32[8,4,384]{2,1,0:T(4,128)S(1)}, u32[]{:S(2)}, u32[]{:S(2)}) %all-to-all-start.7) | async-done | bytes 49184 | tf_op jit(solution)/shard_map/all_to_all | solution.py:378
  222.7 1.4 spread.1
  (67 shorter events, 5.5 us)
Async XLA Ops:
  7.2 13.7 %copy-start = (s32[1,64,8]{1,2,0:T(8,128)S(1)}, s32[1,64,8]{1,2,0:T(8,128)}, u32[]{:S(2)}) copy-start(s32[1,64,8]{1,2,0:T(8,128)} %param.11) | copy-start | bytes 6148
  7.2 13.6 %copy-start.21 = (s32[1,4]{1,0:T(1,128)S(1)}, s32[1,4]{1,0:T(1,128)}, u32[]{:S(2)}) copy-start(s32[1,4]{1,0:T(1,128)} %param.13) | copy-start | bytes 52
  7.2 14.6 %copy-start.18 = (s32[1,64]{1,0:T(1,128)S(1)}, s32[1,64]{1,0:T(1,128)}, u32[]{:S(2)}) copy-start(s32[1,64]{1,0:T(1,128)} %param.12) | copy-start | bytes 772
  12.4 26.0 %all-to-all-start = ((bf16[8,128,256]{2,1,0:T(8,128)(2,1)}), bf16[8,128,256]{2,1,0:T(8,128)(2,1)S(1)}, u32[]{:S(2)}, u32[]{:S(2)}) async-start(bf16[8,128,256]{2,1,0:T(8,128)(2,1)} %get-tuple-element.27), calls=%async_computation | async-start | bytes 1048576 | tf_op jit(solution)/shard_map/all_to_all | solution.py:378
  38.3 43.5 %copy-start.15 = (bf16[8,128,256]{2,1,0:T(8,128)(2,1)}, bf16[8,128,256]{2,1,0:T(8,128)(2,1)S(1)}, u32[]{:S(2)}) copy-start(bf16[8,128,256]{2,1,0:T(8,128)(2,1)S(1)} %all-to-all-done.own_ref) | copy-start | bytes 1572868
  38.3 32.7 %all-to-all-start.1 = ((bf16[8,256,256]{2,1,0:T(8,128)(2,1)}), bf16[8,256,256]{2,1,0:T(8,128)(2,1)S(1)}, u32[]{:S(2)}, u32[]{:S(2)}) async-start(bf16[8,256,256]{2,1,0:T(8,128)(2,1)} %get-tuple-element.29), calls=%async_computation.1 | async-start | bytes 2097152 | tf_op jit(solution)/shard_map/all_to_all | solution.py:378
  41.9 134.8 %all-gather.2.cloned.1.call-start = ((), (), s32[]{:S(2)}) async-start(), calls=%async_computation.8 | async-start | bytes 4718592 | tf_op jit(solution)/shard_map/all_gather | solution.py:504
  41.9 37.5 %collective-permute-start = (bf16[8,128,256]{2,1,0:T(8,128)(2,1)S(1)}, bf16[8,128,256]{2,1,0:T(8,128)(2,1)S(1)}, u32[]{:S(2)}, u32[]{:S(2)}) collective-permute-start(bf16[8,128,256]{2,1,0:T(8,128)(2,1)S(1)} %all-to-all-done.own_ref), channel_id=1, source_target_pairs={{0,8},{8,16},{16,24},{24,0},{1,9},{9,17},{17,25},{25,1},{2,10},{10... | collective-permute-start | bytes 1572872 | tf_op jit(solution)/shard_map/ppermute | solution.py:387
  43.6 38.2 %collective-permute-start.1 = (bf16[8,128,256]{2,1,0:T(8,128)(2,1)S(1)}, bf16[8,128,256]{2,1,0:T(8,128)(2,1)}, u32[]{:S(2)}, u32[]{:S(2)}) collective-permute-start(bf16[8,128,256]{2,1,0:T(8,128)(2,1)S(1)} %all-to-all-done.own_ref), channel_id=1, source_target_pairs={{0,24},{8,0},{16,8},{24,16},{1,25},{9,1},{17,9},{25,17},{2,26},{10... | collective-permute-start | bytes 1572872 | tf_op jit(solution)/shard_map/ppermute | solution.py:387
  44.0 37.8 %collective-permute-start.2 = (bf16[8,128,256]{2,1,0:T(8,128)(2,1)S(1)}, bf16[8,128,256]{2,1,0:T(8,128)(2,1)}, u32[]{:S(2)}, u32[]{:S(2)}) collective-permute-start(bf16[8,128,256]{2,1,0:T(8,128)(2,1)S(1)} %all-to-all-done.own_ref), channel_id=1, source_target_pairs={{0,16},{8,24},{16,0},{24,8},{1,17},{9,25},{17,1},{25,9},{2,18},{10... | collective-permute-start | bytes 1572872 | tf_op jit(solution)/shard_map/ppermute | solution.py:387
  71.0 1.1 copy-start.2
  73.9 34.4 %collective-permute-start.6 = (bf16[8,128,256]{2,1,0:T(8,128)(2,1)}, bf16[8,128,256]{2,1,0:T(8,128)(2,1)S(1)}, u32[]{:S(2)}, u32[]{:S(2)}) collective-permute-start(bf16[8,128,256]{2,1,0:T(8,128)(2,1)} %first_half.1.own_ref), channel_id=1, source_target_pairs={{0,8},{8,16},{16,24},{24,0},{1,9},{9,17},{17,25},{25,1},{2,10},{10... | collective-permute-start | bytes 1572872 | tf_op jit(solution)/shard_map/ppermute | solution.py:387
  75.5 34.8 %collective-permute-start.7 = (bf16[8,128,256]{2,1,0:T(8,128)(2,1)}, bf16[8,128,256]{2,1,0:T(8,128)(2,1)}, u32[]{:S(2)}, u32[]{:S(2)}) collective-permute-start(bf16[8,128,256]{2,1,0:T(8,128)(2,1)} %first_half.1.own_ref), channel_id=1, source_target_pairs={{0,24},{8,0},{16,8},{24,16},{1,25},{9,1},{17,9},{25,17},{2,26},{10... | collective-permute-start | bytes 1572872 | tf_op jit(solution)/shard_map/ppermute | solution.py:387
  75.9 26.7 %all-to-all-start.2 = ((bf16[8,128,256]{2,1,0:T(8,128)(2,1)}), bf16[8,128,256]{2,1,0:T(8,128)(2,1)S(1)}, u32[]{:S(2)}, u32[]{:S(2)}) async-start(bf16[8,128,256]{2,1,0:T(8,128)(2,1)} %get-tuple-element.34), calls=%async_computation.2 | async-start | bytes 1048576 | tf_op jit(solution)/shard_map/all_to_all | solution.py:378
  79.4 2.4 %copy-start.20 = (bf16[8,128,256]{2,1,0:T(8,128)(2,1)}, bf16[8,128,256]{2,1,0:T(8,128)(2,1)S(1)}, u32[]{:S(2)}) copy-start(bf16[8,128,256]{2,1,0:T(8,128)(2,1)S(1)} %collective-permute-done.left_ref) | copy-start | bytes 1572868
  79.4 30.8 %collective-permute-start.8 = (bf16[8,128,256]{2,1,0:T(8,128)(2,1)}, bf16[8,128,256]{2,1,0:T(8,128)(2,1)}, u32[]{:S(2)}, u32[]{:S(2)}) collective-permute-start(bf16[8,128,256]{2,1,0:T(8,128)(2,1)} %first_half.1.own_ref), channel_id=1, source_target_pairs={{0,16},{8,24},{16,0},{24,8},{1,17},{9,25},{17,1},{25,9},{2,18},{10... | collective-permute-start | bytes 1572872 | tf_op jit(solution)/shard_map/ppermute | solution.py:387
  98.3 28.4 %collective-permute-start.3 = (bf16[8,128,256]{2,1,0:T(8,128)(2,1)}, bf16[8,128,256]{2,1,0:T(8,128)(2,1)S(1)}, u32[]{:S(2)}, u32[]{:S(2)}) collective-permute-start(bf16[8,128,256]{2,1,0:T(8,128)(2,1)} %get-tuple-element.36), channel_id=1, source_target_pairs={{0,8},{8,16},{16,24},{24,0},{1,9},{9,17},{17,25},{25,1},{2,10},{10... | collective-permute-start | bytes 1572872 | tf_op jit(solution)/shard_map/ppermute | solution.py:430
  99.8 26.9 %collective-permute-start.4 = (bf16[8,128,256]{2,1,0:T(8,128)(2,1)}, bf16[8,128,256]{2,1,0:T(8,128)(2,1)S(1)}, u32[]{:S(2)}, u32[]{:S(2)}) collective-permute-start(bf16[8,128,256]{2,1,0:T(8,128)(2,1)} %get-tuple-element.37), channel_id=1, source_target_pairs={{0,24},{8,0},{16,8},{24,16},{1,25},{9,1},{17,9},{25,17},{2,26},{10... | collective-permute-start | bytes 1572872 | tf_op jit(solution)/shard_map/ppermute | solution.py:431
  102.6 0.8 copy-start.8
  103.4 28.5 %all-to-all-start.3 = ((bf16[8,128,256]{2,1,0:T(8,128)(2,1)}), bf16[8,128,256]{2,1,0:T(8,128)(2,1)S(1)}, u32[]{:S(2)}, u32[]{:S(2)}) async-start(bf16[8,128,256]{2,1,0:T(8,128)(2,1)} %gate.5.after_ref.oa_ref), calls=%async_computation.3 | async-start | bytes 1048576 | tf_op jit(solution)/shard_map/all_to_all | solution.py:378
  108.3 2.0 copy-start.19
  108.3 18.4 %collective-permute-start.5 = (bf16[8,128,256]{2,1,0:T(8,128)(2,1)}, bf16[8,128,256]{2,1,0:T(8,128)(2,1)S(1)}, u32[]{:S(2)}, u32[]{:S(2)}) collective-permute-start(bf16[8,128,256]{2,1,0:T(8,128)(2,1)} %get-tuple-element.38), channel_id=1, source_target_pairs={{0,16},{8,24},{16,0},{24,8},{1,17},{9,25},{17,1},{25,9},{2,18},{10... | collective-permute-start | bytes 1572872 | tf_op jit(solution)/shard_map/ppermute | solution.py:432
  126.7 5.2 %copy-start.5 = (bf16[8,128,256]{2,1,0:T(8,128)(2,1)}, bf16[8,128,256]{2,1,0:T(8,128)(2,1)S(1)}, u32[]{:S(2)}) copy-start(bf16[8,128,256]{2,1,0:T(8,128)(2,1)S(1)} %collective-permute-done.3.refs_5_.b_ref) | copy-start | bytes 1572868
  126.7 5.2 %copy-start.6 = (bf16[8,128,256]{2,1,0:T(8,128)(2,1)}, bf16[8,128,256]{2,1,0:T(8,128)(2,1)S(1)}, u32[]{:S(2)}) copy-start(bf16[8,128,256]{2,1,0:T(8,128)(2,1)S(1)} %collective-permute-done.4.refs_6_.c_ref) | copy-start | bytes 1572868
  126.7 5.2 %copy-start.7 = (bf16[8,128,256]{2,1,0:T(8,128)(2,1)}, bf16[8,128,256]{2,1,0:T(8,128)(2,1)S(1)}, u32[]{:S(2)}) copy-start(bf16[8,128,256]{2,1,0:T(8,128)(2,1)S(1)} %collective-permute-done.5.refs_7_.d_ref) | copy-start | bytes 1572868
  131.9 0.8 copy-start.3
  132.7 6.3 %copy-start.11 = (bf16[8,128,256]{2,1,0:T(8,128)(2,1)S(1)}, bf16[8,128,256]{2,1,0:T(8,128)(2,1)}, u32[]{:S(2)}) copy-start(bf16[8,128,256]{2,1,0:T(8,128)(2,1)} %get-tuple-element.47) | copy-start | bytes 1572868
  132.7 8.2 %copy-start.12 = (bf16[8,128,256]{2,1,0:T(8,128)(2,1)S(1)}, bf16[8,128,256]{2,1,0:T(8,128)(2,1)}, u32[]{:S(2)}) copy-start(bf16[8,128,256]{2,1,0:T(8,128)(2,1)} %get-tuple-element.48) | copy-start | bytes 1572868
  132.7 9.6 %copy-start.10 = (bf16[8,128,256]{2,1,0:T(8,128)(2,1)S(1)}, bf16[8,128,256]{2,1,0:T(8,128)(2,1)}, u32[]{:S(2)}) copy-start(bf16[8,128,256]{2,1,0:T(8,128)(2,1)} %get-tuple-element.46) | copy-start | bytes 1572868
  135.4 34.4 %all-to-all-start.4 = ((bf16[8,256,256]{2,1,0:T(8,128)(2,1)}), bf16[8,256,256]{2,1,0:T(8,128)(2,1)S(1)}, u32[]{:S(2)}, u32[]{:S(2)}) async-start(bf16[8,256,256]{2,1,0:T(8,128)(2,1)} %sum_join.1.ka_ref), calls=%async_computation.4 | async-start | bytes 2097152 | tf_op jit(solution)/shard_map/all_to_all | solution.py:378
  139.0 23.9 %collective-permute-start.10 = (bf16[8,128,256]{2,1,0:T(8,128)(2,1)S(1)}, bf16[8,128,256]{2,1,0:T(8,128)(2,1)S(1)}, u32[]{:S(2)}, u32[]{:S(2)}) collective-permute-start(bf16[8,128,256]{2,1,0:T(8,128)(2,1)S(1)} %copy-done.11), channel_id=1, source_target_pairs={{0,24},{8,0},{16,8},{24,16},{1,25},{9,1},{17,9},{25,17},{2,26},{10... | collective-permute-start | bytes 1572872 | tf_op jit(solution)/shard_map/ppermute | solution.py:431
  140.9 22.0 %collective-permute-start.11 = (bf16[8,128,256]{2,1,0:T(8,128)(2,1)S(1)}, bf16[8,128,256]{2,1,0:T(8,128)(2,1)S(1)}, u32[]{:S(2)}, u32[]{:S(2)}) collective-permute-start(bf16[8,128,256]{2,1,0:T(8,128)(2,1)S(1)} %copy-done.12), channel_id=1, source_target_pairs={{0,16},{8,24},{16,0},{24,8},{1,17},{9,25},{17,1},{25,9},{2,18},{10... | collective-permute-start | bytes 1572872 | tf_op jit(solution)/shard_map/ppermute | solution.py:432
  142.3 22.5 %collective-permute-start.9 = (bf16[8,128,256]{2,1,0:T(8,128)(2,1)S(1)}, bf16[8,128,256]{2,1,0:T(8,128)(2,1)}, u32[]{:S(2)}, u32[]{:S(2)}) collective-permute-start(bf16[8,128,256]{2,1,0:T(8,128)(2,1)S(1)} %copy-done.10), channel_id=1, source_target_pairs={{0,8},{8,16},{16,24},{24,0},{1,9},{9,17},{17,25},{25,1},{2,10},{10... | collective-permute-start | bytes 1572872 | tf_op jit(solution)/shard_map/ppermute | solution.py:430
  162.9 6.9 %copy-start.13 = (bf16[8,128,256]{2,1,0:T(8,128)(2,1)}, bf16[8,128,256]{2,1,0:T(8,128)(2,1)S(1)}, u32[]{:S(2)}) copy-start(bf16[8,128,256]{2,1,0:T(8,128)(2,1)S(1)} %collective-permute-done.10.refs_2_) | copy-start | bytes 1572868
  162.9 0.9 copy-start.14
  169.8 1.1 copy-start.1
  173.2 19.0 %all-to-all-start.5 = ((bf16[8,128,256]{2,1,0:T(8,128)(2,1)}), bf16[8,128,256]{2,1,0:T(8,128)(2,1)S(1)}, u32[]{:S(2)}, u32[]{:S(2)}) async-start(bf16[8,128,256]{2,1,0:T(8,128)(2,1)} %sum_parts.2.kb_ref), calls=%async_computation.5 | async-start | bytes 1048576 | tf_op jit(solution)/shard_map/all_to_all | solution.py:378
  183.0 1.9 collective-permute-start.12
  185.0 0.7 copy-start.16
  192.2 0.8 copy-start.4
  193.0 14.7 %all-to-all-start.6 = ((bf16[16,32,384]{2,1,0:T(8,128)(2,1)}), bf16[16,32,384]{2,1,0:T(8,128)(2,1)S(1)}, u32[]{:S(2)}, u32[]{:S(2)}) async-start(bf16[16,32,384]{2,1,0:T(8,128)(2,1)} %gate.7), calls=%async_computation.6 | async-start | bytes 786432 | tf_op jit(solution)/shard_map/all_to_all | solution.py:378
  207.7 0.7 copy-start.9
  210.1 11.9 %all-to-all-start.7 = ((f32[8,4,384]{2,1,0:T(4,128)}), f32[8,4,384]{2,1,0:T(4,128)S(1)}, u32[]{:S(2)}, u32[]{:S(2)}) async-start(f32[8,4,384]{2,1,0:T(4,128)} %sum_rows.1), calls=%async_computation.7 | async-start | bytes 98304 | tf_op jit(solution)/shard_map/all_to_all | solution.py:378
  222.0 0.6 copy-start.17
Sparse Core Ops, SparseCore 0:
  72.2 79.6 all-gather.1

commit v8 on v7

--- a/solution.py
+++ b/solution.py
@@ -79,9 +79,9 @@
 def first_half(both):
     return pl.pallas_call(
         first_kernel,
-        grid=(2,),
-        in_specs=[pl.BlockSpec((ZS // 2, 128, NODE_DEV), lambda i: (i, 0, 0))],
-        out_specs=pl.BlockSpec((ZS // 2, 128, NODE_DEV), lambda i: (i, 0, 0)),
+        grid=(4,),
+        in_specs=[pl.BlockSpec((ZS // 4, 128, NODE_DEV), lambda i: (i, 0, 0))],
+        out_specs=pl.BlockSpec((ZS // 4, 128, NODE_DEV), lambda i: (i, 0, 0)),
         out_shape=jax.ShapeDtypeStruct(TURNED, bf16),
         compiler_params=VMEM,
         name="first_half",
@@ -394,10 +394,10 @@
 
 def sum_parts(parts, after):
     shape = parts[0].shape
-    tile = pl.BlockSpec((shape[0] // 2, *shape[1:]), lambda i: (i,) + (0,) * (len(shape) - 1))
+    tile = pl.BlockSpec((shape[0] // 4, *shape[1:]), lambda i: (i,) + (0,) * (len(shape) - 1))
     return pl.pallas_call(
         functools.partial(sum_kernel, len(parts)),
-        grid=(2,),
+        grid=(4,),
         in_specs=[tile] * len(parts) + [pl.BlockSpec(memory_space=pl.ANY)] * len(after),
         out_specs=tile,
         out_shape=jax.ShapeDtypeStruct(shape, bf16),
@@ -412,12 +412,12 @@
 
 
 def sum_join(parts, od):
-    tile = pl.BlockSpec((ZS // 2, 128, NODE_DEV), lambda i: (i, 0, 0))
+    tile = pl.BlockSpec((ZS // 4, 128, NODE_DEV), lambda i: (i, 0, 0))
     return pl.pallas_call(
         sum_join_kernel,
-        grid=(2,),
+        grid=(4,),
         in_specs=[tile] * 5,
-        out_specs=pl.BlockSpec((ZS // 2, 256, NODE_DEV), lambda i: (i, 0, 0)),
+        out_specs=pl.BlockSpec((ZS // 4, 256, NODE_DEV), lambda i: (i, 0, 0)),
         out_shape=jax.ShapeDtypeStruct((ZS, 256, NODE_DEV), bf16),
         compiler_params=VMEM,
         name="sum_join",

time: 232 us -> 236 us (1.017)
  Pallas kernels: 72.6 us -> 77.5 us
    ppermute x2, waiting for transfers between devices: 0.01 us -> 9.71 us  [send_row(): lax.ppermute(opp, 'y', OPPOSITE)]
    ppermute x2, waiting for transfers between devices: 19.9 us -> 10.7 us  [send_row(): lax.ppermute(to_left, 'y', LEFT)]
    pallas_call x4, Pallas kernels: 8.82 us -> 14 us  [the longest x2 6.84 us: sum_parts(): pl.pallas_call(functools.partial(sum_kernel, len(parts)), grid=(4,), in_s...]
  transfers between devices with their start and end apart: 22 -> 22, of which waited for: 11 -> 12; matrix products, arithmetic and copies ran while one was open for 1% -> 1% of each run, Pallas kernels for 28% -> 29%
where the time goes in v8:
time: 236 us; the launch traced here: 235 us
  Pallas kernels  77.5 us (33%)
  waiting for transfers between devices  76.8 us (33%)
  starting transfers between devices  56.6 us (24%)
  between operations  14.2 us (6%)
  local copies, waits for them, and re-layouts  8.25 us (3%)
    all_to_all x8, waiting for transfers between devices, swap(): return lax.all_to_all(values, axis, split_axis=0, concat_axis=0, tiled=True)  54.3 us
    all_to_all x8, starting transfers between devices, swap(): return lax.all_to_all(values, axis, split_axis=0, concat_axis=0, tiled=True)  39 us
    pallas_call x2, Pallas kernels, attend(): pl.pallas_call(functools.partial(attend_kernel, qg.shape[1] - 128), in_sp...  32.6 us
    ppermute x2, waiting for transfers between devices, send_row(): lax.ppermute(to_left, 'y', LEFT)  10.7 us
    ppermute x2, waiting for transfers between devices, send_row(): lax.ppermute(opp, 'y', OPPOSITE)  9.71 us
    unnamed x44, local copies, waits for them, and re-layouts  7.44 us
    pallas_call x2, Pallas kernels, sum_parts(): pl.pallas_call(functools.partial(sum_kernel, len(parts)), grid=(4,), in_s...  6.84 us
    pallas_call x1, Pallas kernels, weight_share(): pl.pallas_call(weight_kernel, grid=(d // 256,), in_specs=[pl.BlockSpec(me...  6.29 us
  transfers between devices with their start and end apart: 22, of which 12 were waited for; matrix products, arithmetic and copies ran while one was open for 1% of the time, Pallas kernels for 29%

profile of v8, /device:TPU:8, one launch (start us, length us, event | category | flops | bytes accessed | tf_op | source)
XLA Modules:
  0.0 235.0 jit_solution(15584126879916734170)
XLA Ops:
  7.2 5.2 %project_kv.1 = (bf16[8,128,256]{2,1,0:T(8,128)(2,1)}, bf16[8,128,256]{2,1,0:T(8,128)(2,1)}) custom-call(bf16[256,1024]{1,0:T(8,128)(2,1)} %bitcast.18, bf16[1024,3072]{1,0:T(8,128)(2,1)} %wv_ref.3, bf16[1024,3072]{1,0:T(8,128)(2,1)} %wv_ref.3), custom_call_target="tpu_custom_call" | custom-call | tf_op jit(solution)/shard_map/project_kv/pallas_call | solution.py:108
  12.4 8.5 %all-to-all-start = ((bf16[8,128,256]{2,1,0:T(8,128)(2,1)}), bf16[8,128,256]{2,1,0:T(8,128)(2,1)S(1)}, u32[]{:S(2)}, u32[]{:S(2)}) async-start(bf16[8,128,256]{2,1,0:T(8,128)(2,1)} %get-tuple-element.27), calls=%async_computation | async-start | bytes 1048576 | tf_op jit(solution)/shard_map/all_to_all | solution.py:378
  23.3 5.7 %project_qg.1 = (bf16[8,256,256]{2,1,0:T(8,128)(2,1)}, bf16[8,128,256]{2,1,0:T(8,128)(2,1)}, bf16[256,1024]{1,0:T(8,128)(2,1)}) custom-call(bf16[256,1024]{1,0:T(8,128)(2,1)} %bitcast.19, bf16[256,1024]{1,0:T(8,128)(2,1)} %bitcast.20, bf16[1024,3072]{1,0:T(8,128)(2,1)} %wv_ref.3, bf16[1024,1024]{1,0:T(8,128)(2,1)} %wo_ref.3, ...), custom_call_target="tpu_custom_call" | custom-call | tf_op jit(solution)/shard_map/project_qg/pallas_call | solution.py:126
  29.0 9.3 %all-to-all-done.own_ref = bf16[8,128,256]{2,1,0:T(8,128)(2,1)S(1)} async-done(((bf16[8,128,256]{2,1,0:T(8,128)(2,1)}), bf16[8,128,256]{2,1,0:T(8,128)(2,1)S(1)}, u32[]{:S(2)}, u32[]{:S(2)}) %all-to-all-start) | async-done | bytes 524320 | tf_op jit(solution)/shard_map/all_to_all | solution.py:378
  38.3 3.6 %all-to-all-start.1 = ((bf16[8,256,256]{2,1,0:T(8,128)(2,1)}), bf16[8,256,256]{2,1,0:T(8,128)(2,1)S(1)}, u32[]{:S(2)}, u32[]{:S(2)}) async-start(bf16[8,256,256]{2,1,0:T(8,128)(2,1)} %get-tuple-element.29), calls=%async_computation.1 | async-start | bytes 2097152 | tf_op jit(solution)/shard_map/all_to_all | solution.py:378
  41.9 1.7 collective-permute-start
  44.0 2.3 collective-permute-start.2
  46.3 24.7 %all-to-all-done.1.refs_2_.qg_ref.x_ref = bf16[8,256,256]{2,1,0:T(8,128)(2,1)S(1)} async-done(((bf16[8,256,256]{2,1,0:T(8,128)(2,1)}), bf16[8,256,256]{2,1,0:T(8,128)(2,1)S(1)}, u32[]{:S(2)}, u32[]{:S(2)}) %all-to-all-start.1) | async-done | bytes 1048608 | tf_op jit(solution)/shard_map/all_to_all | solution.py:378
  71.0 1.1 copy-done.2
  72.1 3.2 %first_half.1.own_ref = bf16[8,128,256]{2,1,0:T(8,128)(2,1)} custom-call(bf16[8,256,256]{2,1,0:T(8,128)(2,1)} %copy-done.2), custom_call_target="tpu_custom_call" | custom-call | tf_op jit(solution)/shard_map/first_half/pallas_call | solution.py:80
  75.3 1.6 collective-permute-start.6
  77.3 3.5 %all-to-all-start.2 = ((bf16[8,128,256]{2,1,0:T(8,128)(2,1)}), bf16[8,128,256]{2,1,0:T(8,128)(2,1)S(1)}, u32[]{:S(2)}, u32[]{:S(2)}) async-start(bf16[8,128,256]{2,1,0:T(8,128)(2,1)} %get-tuple-element.34), calls=%async_computation.2 | async-start | bytes 1048576 | tf_op jit(solution)/shard_map/all_to_all | solution.py:378
  80.9 2.4 %collective-permute-start.8 = (bf16[8,128,256]{2,1,0:T(8,128)(2,1)}, bf16[8,128,256]{2,1,0:T(8,128)(2,1)}, u32[]{:S(2)}, u32[]{:S(2)}) collective-permute-start(bf16[8,128,256]{2,1,0:T(8,128)(2,1)} %first_half.1.own_ref), channel_id=1, source_target_pairs={{0,16},{8,24},{16,0},{24,8},{1,17},{9,25},{17,1},{25,9},{2,18},{10... | collective-permute-start | bytes 1572872 | tf_op jit(solution)/shard_map/ppermute | solution.py:387
  83.3 16.4 %attend.2 = (bf16[8,128,256]{2,1,0:T(8,128)(2,1)}, bf16[8,128,256]{2,1,0:T(8,128)(2,1)}, bf16[8,128,256]{2,1,0:T(8,128)(2,1)}, bf16[8,128,256]{2,1,0:T(8,128)(2,1)}, bf16[8,128,256]{2,1,0:T(8,128)(2,1)}) custom-call(s32[192]{0:T(256)} %reshape.31.refs_0_.tab_ref, s32[16]{0:T(128)} %get-tuple-element.52.refs_1_.cnt_ref, ...), custom_call_target="tpu_custom_call" | custom-call | flops 25999998976 | bytes 6291456 | tf_op jit(solution)/shard_map/attend/pallas_call | solution.py:237
  99.6 1.9 collective-permute-start.3
  101.7 2.5 %all-to-all-done.2.refs_1_.qg_ref = bf16[8,128,256]{2,1,0:T(8,128)(2,1)S(1)} async-done(((bf16[8,128,256]{2,1,0:T(8,128)(2,1)}), bf16[8,128,256]{2,1,0:T(8,128)(2,1)S(1)}, u32[]{:S(2)}, u32[]{:S(2)}) %all-to-all-start.2) | async-done | bytes 524320 | tf_op jit(solution)/shard_map/all_to_all | solution.py:378
  104.2 0.8 copy-done.8
  105.0 4.6 %all-to-all-start.3 = ((bf16[8,128,256]{2,1,0:T(8,128)(2,1)}), bf16[8,128,256]{2,1,0:T(8,128)(2,1)S(1)}, u32[]{:S(2)}, u32[]{:S(2)}) async-start(bf16[8,128,256]{2,1,0:T(8,128)(2,1)} %gate.5.after_ref.oa_ref), calls=%async_computation.3 | async-start | bytes 1048576 | tf_op jit(solution)/shard_map/all_to_all | solution.py:378
  109.7 2.1 collective-permute-start.5
  111.8 16.3 %attend.3 = (bf16[8,128,256]{2,1,0:T(8,128)(2,1)}, bf16[8,128,256]{2,1,0:T(8,128)(2,1)}, bf16[8,128,256]{2,1,0:T(8,128)(2,1)}, bf16[8,128,256]{2,1,0:T(8,128)(2,1)}, bf16[8,128,256]{2,1,0:T(8,128)(2,1)}) custom-call(s32[192]{0:T(256)} %reshape.31.refs_0_.tab_ref, s32[16]{0:T(128)} %get-tuple-element.52.refs_1_.cnt_ref, ...), custom_call_target="tpu_custom_call" | custom-call | flops 25999998976 | bytes 6291456 | tf_op jit(solution)/shard_map/attend/pallas_call | solution.py:237
  128.1 4.8 %all-to-all-done.3.refs_8_.a_ref.oa_ref = bf16[8,128,256]{2,1,0:T(8,128)(2,1)S(1)} async-done(((bf16[8,128,256]{2,1,0:T(8,128)(2,1)}), bf16[8,128,256]{2,1,0:T(8,128)(2,1)S(1)}, u32[]{:S(2)}, u32[]{:S(2)}) %all-to-all-start.3) | async-done | bytes 524320 | tf_op jit(solution)/shard_map/all_to_all | solution.py:378
  132.9 0.8 copy-done.3
  133.7 3.9 %sum_join.1.ka_ref = bf16[8,256,256]{2,1,0:T(8,128)(2,1)} custom-call(bf16[8,128,256]{2,1,0:T(8,128)(2,1)} %get-tuple-element.35.a_ref, bf16[8,128,256]{2,1,0:T(8,128)(2,1)} %copy-done.5, bf16[8,128,256]{2,1,0:T(8,128)(2,1)} %copy-done.6, bf16[8,128,256]{2,1,0:T(8,128)(2,1)} %copy-done.7, bf16[8,128,256]{2,1,0:T(8,128)(2,1)} %get-tuple-element.44.od_ref.ob_ref), custom_call_target="tpu_custom_call" | custom-call | tf_op jit(solution)/shard_map/sum_join/pallas_call | solution.py:416
  137.7 3.6 %all-to-all-start.4 = ((bf16[8,256,256]{2,1,0:T(8,128)(2,1)}), bf16[8,256,256]{2,1,0:T(8,128)(2,1)S(1)}, u32[]{:S(2)}, u32[]{:S(2)}) async-start(bf16[8,256,256]{2,1,0:T(8,128)(2,1)} %sum_join.1.ka_ref), calls=%async_computation.4 | async-start | bytes 2097152 | tf_op jit(solution)/shard_map/all_to_all | solution.py:378
  141.2 2.9 %collective-permute-start.10 = (bf16[8,128,256]{2,1,0:T(8,128)(2,1)S(1)}, bf16[8,128,256]{2,1,0:T(8,128)(2,1)S(1)}, u32[]{:S(2)}, u32[]{:S(2)}) collective-permute-start(bf16[8,128,256]{2,1,0:T(8,128)(2,1)S(1)} %copy-done.11), channel_id=1, source_target_pairs={{0,24},{8,0},{16,8},{24,16},{1,25},{9,1},{17,9},{25,17},{2,26},{10... | collective-permute-start | bytes 1572872 | tf_op jit(solution)/shard_map/ppermute | solution.py:431
  144.1 1.7 collective-permute-start.11
  145.8 10.7 %collective-permute-done.10.refs_2_ = bf16[8,128,256]{2,1,0:T(8,128)(2,1)S(1)} collective-permute-done((bf16[8,128,256]{2,1,0:T(8,128)(2,1)S(1)}, bf16[8,128,256]{2,1,0:T(8,128)(2,1)S(1)}, u32[]{:S(2)}, u32[]{:S(2)}) %collective-permute-start.10) | collective-permute-done | bytes 524320 | tf_op jit(solution)/shard_map/ppermute | solution.py:431
  156.5 9.7 %collective-permute-done.11.refs_3_ = bf16[8,128,256]{2,1,0:T(8,128)(2,1)S(1)} collective-permute-done((bf16[8,128,256]{2,1,0:T(8,128)(2,1)S(1)}, bf16[8,128,256]{2,1,0:T(8,128)(2,1)S(1)}, u32[]{:S(2)}, u32[]{:S(2)}) %collective-permute-start.11) | collective-permute-done | bytes 524320 | tf_op jit(solution)/shard_map/ppermute | solution.py:432
  166.2 0.8 copy-done.14
  167.1 3.0 %all-to-all-done.4.b_ref.refs_4_.ob_ref.ka_ref = bf16[8,256,256]{2,1,0:T(8,128)(2,1)S(1)} async-done(((bf16[8,256,256]{2,1,0:T(8,128)(2,1)}), bf16[8,256,256]{2,1,0:T(8,128)(2,1)S(1)}, u32[]{:S(2)}, u32[]{:S(2)}) %all-to-all-start.4) | async-done | bytes 1048608 | tf_op jit(solution)/shard_map/all_to_all | solution.py:378
  170.1 1.0 copy-done.1
  171.1 3.6 %sum_parts.2.kb_ref = bf16[8,128,256]{2,1,0:T(8,128)(2,1)} custom-call(bf16[8,128,256]{2,1,0:T(8,128)(2,1)} %get-tuple-element.45.refs_0_, bf16[8,128,256]{2,1,0:T(8,128)(2,1)} %collective-permute-done.9.refs_1_, bf16[8,128,256]{2,1,0:T(8,128)(2,1)} %copy-done.13, bf16[8,128,256]{2,1,0:T(8,128)(2,1)} %copy-done.14, bf16[8,256,256]{2,1,0:T(8,128)(2,1)} %copy-done.1), custom_call_target="tpu_custom_call" | custom-call | tf_op jit(solution)/shard_map/sum_parts/pallas_call | solution.py:398
  174.7 3.8 %all-to-all-start.5 = ((bf16[8,128,256]{2,1,0:T(8,128)(2,1)}), bf16[8,128,256]{2,1,0:T(8,128)(2,1)S(1)}, u32[]{:S(2)}, u32[]{:S(2)}) async-start(bf16[8,128,256]{2,1,0:T(8,128)(2,1)} %sum_parts.2.kb_ref), calls=%async_computation.5 | async-start | bytes 1048576 | tf_op jit(solution)/shard_map/all_to_all | solution.py:378
  178.6 6.3 %weight_share.1 = (bf16[512,384]{1,0:T(8,128)(2,1)}, bf16[512,384]{1,0:T(8,128)(2,1)}) custom-call(s32[1]{0:T(128)} %bitcast.9.c_ref, bf16[8,128,256]{2,1,0:T(8,128)(2,1)} %gate.5.after_ref.oa_ref, bf16[8,128,256]{2,1,0:T(8,128)(2,1)} %get-tuple-element.44.od_ref.ob_ref, bf16[8,256,256]{2,1,0:T(8,128)(2,1)} %sum_join.1.ka_ref, ...), custom_call_target="tpu_custom_call" | custom-call | tf_op jit(solution)/shard_map/weight_share/pallas_call | solution.py:472
  184.9 1.9 collective-permute-done.12.refs_1_
  186.8 0.7 copy-done.16
  187.6 3.2 %sum_parts.3 = bf16[512,384]{1,0:T(8,128)(2,1)} custom-call(bf16[512,384]{1,0:T(8,128)(2,1)} %get-tuple-element.49.refs_0_, bf16[512,384]{1,0:T(8,128)(2,1)} %copy-done.16), custom_call_target="tpu_custom_call" | custom-call | tf_op jit(solution)/shard_map/sum_parts/pallas_call | solution.py:398
  190.8 4.1 %all-to-all-done.5.kb_ref.refs_1_ = bf16[8,128,256]{2,1,0:T(8,128)(2,1)S(1)} async-done(((bf16[8,128,256]{2,1,0:T(8,128)(2,1)}), bf16[8,128,256]{2,1,0:T(8,128)(2,1)S(1)}, u32[]{:S(2)}, u32[]{:S(2)}) %all-to-all-start.5) | async-done | bytes 524320 | tf_op jit(solution)/shard_map/all_to_all | solution.py:378
  194.9 0.8 copy-done.4
  195.7 8.1 %all-to-all-start.6 = ((bf16[16,32,384]{2,1,0:T(8,128)(2,1)}), bf16[16,32,384]{2,1,0:T(8,128)(2,1)S(1)}, u32[]{:S(2)}, u32[]{:S(2)}) async-start(bf16[16,32,384]{2,1,0:T(8,128)(2,1)} %gate.7), calls=%async_computation.6 | async-start | bytes 786432 | tf_op jit(solution)/shard_map/all_to_all | solution.py:378
  203.8 6.3 %node_grads.1.refs_0_ = bf16[256,1024]{1,0:T(8,128)(2,1)} custom-call(bf16[8,128,256]{2,1,0:T(8,128)(2,1)} %copy-done.3, bf16[8,256,256]{2,1,0:T(8,128)(2,1)} %copy-done.1, bf16[8,256,256]{2,1,0:T(8,128)(2,1)} %copy-done.1, bf16[8,128,256]{2,1,0:T(8,128)(2,1)} %copy-done.4, bf16[1024,3072]{1,0:T(8,128)(2,1)} %wv_ref.3, bf16[1024,3072]{1,0:T(8,128)(2,1)} %wv_ref.3, ...), custom_call_target="tpu_custom_call" | custom-call | tf_op jit(solution)/shard_map/node_grads/pallas_call | solution.py:322
  210.1 2.1 all-to-all-done.6.x_ref
  212.2 0.7 copy-done.9
  212.9 1.7 sum_rows.1
  214.6 3.3 %all-to-all-start.7 = ((f32[8,4,384]{2,1,0:T(4,128)}), f32[8,4,384]{2,1,0:T(4,128)S(1)}, u32[]{:S(2)}, u32[]{:S(2)}) async-start(f32[8,4,384]{2,1,0:T(4,128)} %sum_rows.1), calls=%async_computation.7 | async-start | bytes 98304 | tf_op jit(solution)/shard_map/all_to_all | solution.py:378
  217.9 4.4 %project_out.1.refs_0_ = bf16[256,1024]{1,0:T(8,128)(2,1)} custom-call(bf16[8,128,256]{2,1,0:T(8,128)(2,1)} %copy-done.3, bf16[8,256,256]{2,1,0:T(8,128)(2,1)} %copy-done.1, bf16[1024,1024]{1,0:T(8,128)(2,1)} %wo_ref.3), custom_call_target="tpu_custom_call" | custom-call | tf_op jit(solution)/shard_map/project_out/pallas_call | solution.py:283
  222.3 3.8 %all-to-all-done.7.x_ref = f32[8,4,384]{2,1,0:T(4,128)S(1)} async-done(((f32[8,4,384]{2,1,0:T(4,128)}), f32[8,4,384]{2,1,0:T(4,128)S(1)}, u32[]{:S(2)}, u32[]{:S(2)}) %all-to-all-start.7) | async-done | bytes 49184 | tf_op jit(solution)/shard_map/all_to_all | solution.py:378
  226.7 1.4 spread.1
  (67 shorter events, 4.4 us)
Async XLA Ops:
  7.2 13.7 %copy-start = (s32[1,64,8]{1,2,0:T(8,128)S(1)}, s32[1,64,8]{1,2,0:T(8,128)}, u32[]{:S(2)}) copy-start(s32[1,64,8]{1,2,0:T(8,128)} %param.11) | copy-start | bytes 6148
  7.2 13.6 %copy-start.21 = (s32[1,4]{1,0:T(1,128)S(1)}, s32[1,4]{1,0:T(1,128)}, u32[]{:S(2)}) copy-start(s32[1,4]{1,0:T(1,128)} %param.13) | copy-start | bytes 52
  7.2 14.6 %copy-start.18 = (s32[1,64]{1,0:T(1,128)S(1)}, s32[1,64]{1,0:T(1,128)}, u32[]{:S(2)}) copy-start(s32[1,64]{1,0:T(1,128)} %param.12) | copy-start | bytes 772
  12.4 26.0 %all-to-all-start = ((bf16[8,128,256]{2,1,0:T(8,128)(2,1)}), bf16[8,128,256]{2,1,0:T(8,128)(2,1)S(1)}, u32[]{:S(2)}, u32[]{:S(2)}) async-start(bf16[8,128,256]{2,1,0:T(8,128)(2,1)} %get-tuple-element.27), calls=%async_computation | async-start | bytes 1048576 | tf_op jit(solution)/shard_map/all_to_all | solution.py:378
  38.3 44.9 %copy-start.15 = (bf16[8,128,256]{2,1,0:T(8,128)(2,1)}, bf16[8,128,256]{2,1,0:T(8,128)(2,1)S(1)}, u32[]{:S(2)}) copy-start(bf16[8,128,256]{2,1,0:T(8,128)(2,1)S(1)} %all-to-all-done.own_ref) | copy-start | bytes 1572868
  38.3 32.7 %all-to-all-start.1 = ((bf16[8,256,256]{2,1,0:T(8,128)(2,1)}), bf16[8,256,256]{2,1,0:T(8,128)(2,1)S(1)}, u32[]{:S(2)}, u32[]{:S(2)}) async-start(bf16[8,256,256]{2,1,0:T(8,128)(2,1)} %get-tuple-element.29), calls=%async_computation.1 | async-start | bytes 2097152 | tf_op jit(solution)/shard_map/all_to_all | solution.py:378
  41.9 136.7 %all-gather.2.cloned.1.call-start = ((), (), s32[]{:S(2)}) async-start(), calls=%async_computation.8 | async-start | bytes 4718592 | tf_op jit(solution)/shard_map/all_gather | solution.py:504
  41.9 38.9 %collective-permute-start = (bf16[8,128,256]{2,1,0:T(8,128)(2,1)S(1)}, bf16[8,128,256]{2,1,0:T(8,128)(2,1)S(1)}, u32[]{:S(2)}, u32[]{:S(2)}) collective-permute-start(bf16[8,128,256]{2,1,0:T(8,128)(2,1)S(1)} %all-to-all-done.own_ref), channel_id=1, source_target_pairs={{0,8},{8,16},{16,24},{24,0},{1,9},{9,17},{17,25},{25,1},{2,10},{10... | collective-permute-start | bytes 1572872 | tf_op jit(solution)/shard_map/ppermute | solution.py:387
  43.6 39.7 %collective-permute-start.1 = (bf16[8,128,256]{2,1,0:T(8,128)(2,1)S(1)}, bf16[8,128,256]{2,1,0:T(8,128)(2,1)}, u32[]{:S(2)}, u32[]{:S(2)}) collective-permute-start(bf16[8,128,256]{2,1,0:T(8,128)(2,1)S(1)} %all-to-all-done.own_ref), channel_id=1, source_target_pairs={{0,24},{8,0},{16,8},{24,16},{1,25},{9,1},{17,9},{25,17},{2,26},{10... | collective-permute-start | bytes 1572872 | tf_op jit(solution)/shard_map/ppermute | solution.py:387
  44.0 39.2 %collective-permute-start.2 = (bf16[8,128,256]{2,1,0:T(8,128)(2,1)S(1)}, bf16[8,128,256]{2,1,0:T(8,128)(2,1)}, u32[]{:S(2)}, u32[]{:S(2)}) collective-permute-start(bf16[8,128,256]{2,1,0:T(8,128)(2,1)S(1)} %all-to-all-done.own_ref), channel_id=1, source_target_pairs={{0,16},{8,24},{16,0},{24,8},{1,17},{9,25},{17,1},{25,9},{2,18},{10... | collective-permute-start | bytes 1572872 | tf_op jit(solution)/shard_map/ppermute | solution.py:387
  71.0 1.1 copy-start.2
  75.3 34.3 %collective-permute-start.6 = (bf16[8,128,256]{2,1,0:T(8,128)(2,1)}, bf16[8,128,256]{2,1,0:T(8,128)(2,1)S(1)}, u32[]{:S(2)}, u32[]{:S(2)}) collective-permute-start(bf16[8,128,256]{2,1,0:T(8,128)(2,1)} %first_half.1.own_ref), channel_id=1, source_target_pairs={{0,8},{8,16},{16,24},{24,0},{1,9},{9,17},{17,25},{25,1},{2,10},{10... | collective-permute-start | bytes 1572872 | tf_op jit(solution)/shard_map/ppermute | solution.py:387
  76.9 34.9 %collective-permute-start.7 = (bf16[8,128,256]{2,1,0:T(8,128)(2,1)}, bf16[8,128,256]{2,1,0:T(8,128)(2,1)}, u32[]{:S(2)}, u32[]{:S(2)}) collective-permute-start(bf16[8,128,256]{2,1,0:T(8,128)(2,1)} %first_half.1.own_ref), channel_id=1, source_target_pairs={{0,24},{8,0},{16,8},{24,16},{1,25},{9,1},{17,9},{25,17},{2,26},{10... | collective-permute-start | bytes 1572872 | tf_op jit(solution)/shard_map/ppermute | solution.py:387
  77.3 26.9 %all-to-all-start.2 = ((bf16[8,128,256]{2,1,0:T(8,128)(2,1)}), bf16[8,128,256]{2,1,0:T(8,128)(2,1)S(1)}, u32[]{:S(2)}, u32[]{:S(2)}) async-start(bf16[8,128,256]{2,1,0:T(8,128)(2,1)} %get-tuple-element.34), calls=%async_computation.2 | async-start | bytes 1048576 | tf_op jit(solution)/shard_map/all_to_all | solution.py:378
  80.8 2.4 %copy-start.20 = (bf16[8,128,256]{2,1,0:T(8,128)(2,1)}, bf16[8,128,256]{2,1,0:T(8,128)(2,1)S(1)}, u32[]{:S(2)}) copy-start(bf16[8,128,256]{2,1,0:T(8,128)(2,1)S(1)} %collective-permute-done.left_ref) | copy-start | bytes 1572868
  80.9 30.9 %collective-permute-start.8 = (bf16[8,128,256]{2,1,0:T(8,128)(2,1)}, bf16[8,128,256]{2,1,0:T(8,128)(2,1)}, u32[]{:S(2)}, u32[]{:S(2)}) collective-permute-start(bf16[8,128,256]{2,1,0:T(8,128)(2,1)} %first_half.1.own_ref), channel_id=1, source_target_pairs={{0,16},{8,24},{16,0},{24,8},{1,17},{9,25},{17,1},{25,9},{2,18},{10... | collective-permute-start | bytes 1572872 | tf_op jit(solution)/shard_map/ppermute | solution.py:387
  99.6 28.5 %collective-permute-start.3 = (bf16[8,128,256]{2,1,0:T(8,128)(2,1)}, bf16[8,128,256]{2,1,0:T(8,128)(2,1)S(1)}, u32[]{:S(2)}, u32[]{:S(2)}) collective-permute-start(bf16[8,128,256]{2,1,0:T(8,128)(2,1)} %get-tuple-element.36), channel_id=1, source_target_pairs={{0,8},{8,16},{16,24},{24,0},{1,9},{9,17},{17,25},{25,1},{2,10},{10... | collective-permute-start | bytes 1572872 | tf_op jit(solution)/shard_map/ppermute | solution.py:430
  101.5 26.6 %collective-permute-start.4 = (bf16[8,128,256]{2,1,0:T(8,128)(2,1)}, bf16[8,128,256]{2,1,0:T(8,128)(2,1)S(1)}, u32[]{:S(2)}, u32[]{:S(2)}) collective-permute-start(bf16[8,128,256]{2,1,0:T(8,128)(2,1)} %get-tuple-element.37), channel_id=1, source_target_pairs={{0,24},{8,0},{16,8},{24,16},{1,25},{9,1},{17,9},{25,17},{2,26},{10... | collective-permute-start | bytes 1572872 | tf_op jit(solution)/shard_map/ppermute | solution.py:431
  104.2 0.8 copy-start.8
  105.0 27.9 %all-to-all-start.3 = ((bf16[8,128,256]{2,1,0:T(8,128)(2,1)}), bf16[8,128,256]{2,1,0:T(8,128)(2,1)S(1)}, u32[]{:S(2)}, u32[]{:S(2)}) async-start(bf16[8,128,256]{2,1,0:T(8,128)(2,1)} %gate.5.after_ref.oa_ref), calls=%async_computation.3 | async-start | bytes 1048576 | tf_op jit(solution)/shard_map/all_to_all | solution.py:378
  109.6 2.1 copy-start.19
  109.7 18.5 %collective-permute-start.5 = (bf16[8,128,256]{2,1,0:T(8,128)(2,1)}, bf16[8,128,256]{2,1,0:T(8,128)(2,1)S(1)}, u32[]{:S(2)}, u32[]{:S(2)}) collective-permute-start(bf16[8,128,256]{2,1,0:T(8,128)(2,1)} %get-tuple-element.38), channel_id=1, source_target_pairs={{0,16},{8,24},{16,0},{24,8},{1,17},{9,25},{17,1},{25,9},{2,18},{10... | collective-permute-start | bytes 1572872 | tf_op jit(solution)/shard_map/ppermute | solution.py:432
  128.1 4.9 %copy-start.5 = (bf16[8,128,256]{2,1,0:T(8,128)(2,1)}, bf16[8,128,256]{2,1,0:T(8,128)(2,1)S(1)}, u32[]{:S(2)}) copy-start(bf16[8,128,256]{2,1,0:T(8,128)(2,1)S(1)} %collective-permute-done.3.refs_5_.b_ref) | copy-start | bytes 1572868
  128.1 4.8 %copy-start.6 = (bf16[8,128,256]{2,1,0:T(8,128)(2,1)}, bf16[8,128,256]{2,1,0:T(8,128)(2,1)S(1)}, u32[]{:S(2)}) copy-start(bf16[8,128,256]{2,1,0:T(8,128)(2,1)S(1)} %collective-permute-done.4.refs_6_.c_ref) | copy-start | bytes 1572868
  128.1 4.8 %copy-start.7 = (bf16[8,128,256]{2,1,0:T(8,128)(2,1)}, bf16[8,128,256]{2,1,0:T(8,128)(2,1)S(1)}, u32[]{:S(2)}) copy-start(bf16[8,128,256]{2,1,0:T(8,128)(2,1)S(1)} %collective-permute-done.5.refs_7_.d_ref) | copy-start | bytes 1572868
  132.9 0.8 copy-start.3
  133.7 7.5 %copy-start.11 = (bf16[8,128,256]{2,1,0:T(8,128)(2,1)S(1)}, bf16[8,128,256]{2,1,0:T(8,128)(2,1)}, u32[]{:S(2)}) copy-start(bf16[8,128,256]{2,1,0:T(8,128)(2,1)} %get-tuple-element.47) | copy-start | bytes 1572868
  133.7 10.4 %copy-start.12 = (bf16[8,128,256]{2,1,0:T(8,128)(2,1)S(1)}, bf16[8,128,256]{2,1,0:T(8,128)(2,1)}, u32[]{:S(2)}) copy-start(bf16[8,128,256]{2,1,0:T(8,128)(2,1)} %get-tuple-element.48) | copy-start | bytes 1572868
  133.7 12.1 %copy-start.10 = (bf16[8,128,256]{2,1,0:T(8,128)(2,1)S(1)}, bf16[8,128,256]{2,1,0:T(8,128)(2,1)}, u32[]{:S(2)}) copy-start(bf16[8,128,256]{2,1,0:T(8,128)(2,1)} %get-tuple-element.46) | copy-start | bytes 1572868
  137.7 32.4 %all-to-all-start.4 = ((bf16[8,256,256]{2,1,0:T(8,128)(2,1)}), bf16[8,256,256]{2,1,0:T(8,128)(2,1)S(1)}, u32[]{:S(2)}, u32[]{:S(2)}) async-start(bf16[8,256,256]{2,1,0:T(8,128)(2,1)} %sum_join.1.ka_ref), calls=%async_computation.4 | async-start | bytes 2097152 | tf_op jit(solution)/shard_map/all_to_all | solution.py:378
  141.2 15.2 %collective-permute-start.10 = (bf16[8,128,256]{2,1,0:T(8,128)(2,1)S(1)}, bf16[8,128,256]{2,1,0:T(8,128)(2,1)S(1)}, u32[]{:S(2)}, u32[]{:S(2)}) collective-permute-start(bf16[8,128,256]{2,1,0:T(8,128)(2,1)S(1)} %copy-done.11), channel_id=1, source_target_pairs={{0,24},{8,0},{16,8},{24,16},{1,25},{9,1},{17,9},{25,17},{2,26},{10... | collective-permute-start | bytes 1572872 | tf_op jit(solution)/shard_map/ppermute | solution.py:431
  144.1 22.1 %collective-permute-start.11 = (bf16[8,128,256]{2,1,0:T(8,128)(2,1)S(1)}, bf16[8,128,256]{2,1,0:T(8,128)(2,1)S(1)}, u32[]{:S(2)}, u32[]{:S(2)}) collective-permute-start(bf16[8,128,256]{2,1,0:T(8,128)(2,1)S(1)} %copy-done.12), channel_id=1, source_target_pairs={{0,16},{8,24},{16,0},{24,8},{1,17},{9,25},{17,1},{25,9},{2,18},{10... | collective-permute-start | bytes 1572872 | tf_op jit(solution)/shard_map/ppermute | solution.py:432
  145.8 21.3 %collective-permute-start.9 = (bf16[8,128,256]{2,1,0:T(8,128)(2,1)S(1)}, bf16[8,128,256]{2,1,0:T(8,128)(2,1)}, u32[]{:S(2)}, u32[]{:S(2)}) collective-permute-start(bf16[8,128,256]{2,1,0:T(8,128)(2,1)S(1)} %copy-done.10), channel_id=1, source_target_pairs={{0,8},{8,16},{16,24},{24,0},{1,9},{9,17},{17,25},{25,1},{2,10},{10... | collective-permute-start | bytes 1572872 | tf_op jit(solution)/shard_map/ppermute | solution.py:430
  156.5 13.6 %copy-start.13 = (bf16[8,128,256]{2,1,0:T(8,128)(2,1)}, bf16[8,128,256]{2,1,0:T(8,128)(2,1)S(1)}, u32[]{:S(2)}) copy-start(bf16[8,128,256]{2,1,0:T(8,128)(2,1)S(1)} %collective-permute-done.10.refs_2_) | copy-start | bytes 1572868
  166.2 0.8 copy-start.14
  170.1 1.1 copy-start.1
  174.7 20.2 %all-to-all-start.5 = ((bf16[8,128,256]{2,1,0:T(8,128)(2,1)}), bf16[8,128,256]{2,1,0:T(8,128)(2,1)S(1)}, u32[]{:S(2)}, u32[]{:S(2)}) async-start(bf16[8,128,256]{2,1,0:T(8,128)(2,1)} %sum_parts.2.kb_ref), calls=%async_computation.5 | async-start | bytes 1048576 | tf_op jit(solution)/shard_map/all_to_all | solution.py:378
  184.9 1.9 collective-permute-start.12
  186.8 0.7 copy-start.16
  194.9 0.8 copy-start.4
  195.7 16.5 %all-to-all-start.6 = ((bf16[16,32,384]{2,1,0:T(8,128)(2,1)}), bf16[16,32,384]{2,1,0:T(8,128)(2,1)S(1)}, u32[]{:S(2)}, u32[]{:S(2)}) async-start(bf16[16,32,384]{2,1,0:T(8,128)(2,1)} %gate.7), calls=%async_computation.6 | async-start | bytes 786432 | tf_op jit(solution)/shard_map/all_to_all | solution.py:378
  212.2 0.7 copy-start.9
  214.6 11.5 %all-to-all-start.7 = ((f32[8,4,384]{2,1,0:T(4,128)}), f32[8,4,384]{2,1,0:T(4,128)S(1)}, u32[]{:S(2)}, u32[]{:S(2)}) async-start(f32[8,4,384]{2,1,0:T(4,128)} %sum_rows.1), calls=%async_computation.7 | async-start | bytes 98304 | tf_op jit(solution)/shard_map/all_to_all | solution.py:378
  226.1 0.6 copy-start.17
Sparse Core Ops, SparseCore 0:
  72.2 76.6 all-gather.1

commit v9 on v7

--- a/solution.py
+++ b/solution.py
@@ -508,9 +508,9 @@
     od_nodes_a = to_nodes(od_a_late)
     parts_a = send_row(*kv_a)
     late = attend(table, counts, order, y_arr, row_b, qg_row_b, od_a_late)
-    od_b, *kv_b = gate(late, parts_a[1:] + [od_nodes_a])
+    od_b, *kv_b = gate(late, parts_a[1:])
     parts_b = send_row(*kv_b)
-    joint = sum_join(parts_a, od_b)
+    (joint,) = gate([sum_join(parts_a, od_b)], [od_nodes_a])
     joint_nodes = swap(joint, "z")
     sum_b = sum_parts(parts_b, (joint_nodes,))
     kv_nodes_b = to_nodes(sum_b)

time: 232 us -> 232 us (level)
  waiting for transfers between devices: 79 us -> 73.5 us
  starting transfers between devices: 55.1 us -> 59.9 us
    ppermute x2, waiting for transfers between devices: 0.01 us -> 9.92 us  [send_row(): lax.ppermute(opp, 'y', OPPOSITE)]
    ppermute x2, waiting for transfers between devices: 19.9 us -> 10.3 us  [send_row(): lax.ppermute(to_left, 'y', LEFT)]
    all_to_all x8, waiting for transfers between devices: 56.1 us -> 50.5 us  [swap(): return lax.all_to_all(values, axis, split_axis=0, concat_axis=0, tiled=True)]
    all_to_all x8, starting transfers between devices: 38.3 us -> 42.3 us  [swap(): return lax.all_to_all(values, axis, split_axis=0, concat_axis=0, tiled=True)]
where the time goes in v9:
time: 232 us; the launch traced here: 231 us
  waiting for transfers between devices  73.5 us (32%)
  Pallas kernels  72.8 us (31%)
  starting transfers between devices  59.9 us (26%)
  between operations  14.2 us (6%)
  local copies, waits for them, and re-layouts  9.21 us (4%)
    all_to_all x8, waiting for transfers between devices, swap(): return lax.all_to_all(values, axis, split_axis=0, concat_axis=0, tiled=True)  50.5 us
    all_to_all x8, starting transfers between devices, swap(): return lax.all_to_all(values, axis, split_axis=0, concat_axis=0, tiled=True)  42.3 us
    pallas_call x2, Pallas kernels, attend(): pl.pallas_call(functools.partial(attend_kernel, qg.shape[1] - 128), in_sp...  33.1 us
    ppermute x2, waiting for transfers between devices, send_row(): lax.ppermute(to_left, 'y', LEFT)  10.3 us
    ppermute x2, waiting for transfers between devices, send_row(): lax.ppermute(opp, 'y', OPPOSITE)  9.92 us
    unnamed x44, local copies, waits for them, and re-layouts  8.39 us
    pallas_call x1, Pallas kernels, weight_share(): pl.pallas_call(weight_kernel, grid=(d // 256,), in_specs=[pl.BlockSpec(me...  6.29 us
    pallas_call x1, Pallas kernels, node_grads(): pl.pallas_call(nodes_kernel, grid=(steps,), in_specs=[tile, SECOND, tile,...  6.28 us
  transfers between devices with their start and end apart: 22, of which 11 were waited for; matrix products, arithmetic and copies ran while one was open for 1% of the time, Pallas kernels for 28%

profile of v9, /device:TPU:8, one launch (start us, length us, event | category | flops | bytes accessed | tf_op | source)
XLA Modules:
  0.0 231.1 jit_solution(15025572793781789535)
XLA Ops:
  7.2 5.2 %project_kv.1 = (bf16[8,128,256]{2,1,0:T(8,128)(2,1)}, bf16[8,128,256]{2,1,0:T(8,128)(2,1)}) custom-call(bf16[256,1024]{1,0:T(8,128)(2,1)} %bitcast.18, bf16[1024,3072]{1,0:T(8,128)(2,1)} %wv_ref.3, bf16[1024,3072]{1,0:T(8,128)(2,1)} %wv_ref.3), custom_call_target="tpu_custom_call" | custom-call | tf_op jit(solution)/shard_map/project_kv/pallas_call | solution.py:108
  12.4 8.5 %all-to-all-start = ((bf16[8,128,256]{2,1,0:T(8,128)(2,1)}), bf16[8,128,256]{2,1,0:T(8,128)(2,1)S(1)}, u32[]{:S(2)}, u32[]{:S(2)}) async-start(bf16[8,128,256]{2,1,0:T(8,128)(2,1)} %get-tuple-element.27), calls=%async_computation | async-start | bytes 1048576 | tf_op jit(solution)/shard_map/all_to_all | solution.py:378
  23.2 5.7 %project_qg.1 = (bf16[8,256,256]{2,1,0:T(8,128)(2,1)}, bf16[8,128,256]{2,1,0:T(8,128)(2,1)}, bf16[256,1024]{1,0:T(8,128)(2,1)}) custom-call(bf16[256,1024]{1,0:T(8,128)(2,1)} %bitcast.19, bf16[256,1024]{1,0:T(8,128)(2,1)} %bitcast.20, bf16[1024,3072]{1,0:T(8,128)(2,1)} %wv_ref.3, bf16[1024,1024]{1,0:T(8,128)(2,1)} %wo_ref.3, ...), custom_call_target="tpu_custom_call" | custom-call | tf_op jit(solution)/shard_map/project_qg/pallas_call | solution.py:126
  28.9 9.4 %all-to-all-done.own_ref = bf16[8,128,256]{2,1,0:T(8,128)(2,1)S(1)} async-done(((bf16[8,128,256]{2,1,0:T(8,128)(2,1)}), bf16[8,128,256]{2,1,0:T(8,128)(2,1)S(1)}, u32[]{:S(2)}, u32[]{:S(2)}) %all-to-all-start) | async-done | bytes 524320 | tf_op jit(solution)/shard_map/all_to_all | solution.py:378
  38.3 3.6 %all-to-all-start.1 = ((bf16[8,256,256]{2,1,0:T(8,128)(2,1)}), bf16[8,256,256]{2,1,0:T(8,128)(2,1)S(1)}, u32[]{:S(2)}, u32[]{:S(2)}) async-start(bf16[8,256,256]{2,1,0:T(8,128)(2,1)} %get-tuple-element.29), calls=%async_computation.1 | async-start | bytes 2097152 | tf_op jit(solution)/shard_map/all_to_all | solution.py:378
  41.9 1.7 collective-permute-start
  44.0 2.3 collective-permute-start.2
  46.3 24.7 %all-to-all-done.1.refs_2_.qg_ref.x_ref = bf16[8,256,256]{2,1,0:T(8,128)(2,1)S(1)} async-done(((bf16[8,256,256]{2,1,0:T(8,128)(2,1)}), bf16[8,256,256]{2,1,0:T(8,128)(2,1)S(1)}, u32[]{:S(2)}, u32[]{:S(2)}) %all-to-all-start.1) | async-done | bytes 1048608 | tf_op jit(solution)/shard_map/all_to_all | solution.py:378
  71.0 1.0 copy-done.2
  72.1 1.8 first_half.1.own_ref
  73.9 1.6 collective-permute-start.6
  75.9 3.5 %all-to-all-start.2 = ((bf16[8,128,256]{2,1,0:T(8,128)(2,1)}), bf16[8,128,256]{2,1,0:T(8,128)(2,1)S(1)}, u32[]{:S(2)}, u32[]{:S(2)}) async-start(bf16[8,128,256]{2,1,0:T(8,128)(2,1)} %get-tuple-element.34), calls=%async_computation.2 | async-start | bytes 1048576 | tf_op jit(solution)/shard_map/all_to_all | solution.py:378
  79.4 2.4 %collective-permute-start.8 = (bf16[8,128,256]{2,1,0:T(8,128)(2,1)}, bf16[8,128,256]{2,1,0:T(8,128)(2,1)}, u32[]{:S(2)}, u32[]{:S(2)}) collective-permute-start(bf16[8,128,256]{2,1,0:T(8,128)(2,1)} %first_half.1.own_ref), channel_id=1, source_target_pairs={{0,16},{8,24},{16,0},{24,8},{1,17},{9,25},{17,1},{25,9},{2,18},{10... | collective-permute-start | bytes 1572872 | tf_op jit(solution)/shard_map/ppermute | solution.py:387
  81.8 16.7 %attend.2 = (bf16[8,128,256]{2,1,0:T(8,128)(2,1)}, bf16[8,128,256]{2,1,0:T(8,128)(2,1)}, bf16[8,128,256]{2,1,0:T(8,128)(2,1)}, bf16[8,128,256]{2,1,0:T(8,128)(2,1)}, bf16[8,128,256]{2,1,0:T(8,128)(2,1)}) custom-call(s32[192]{0:T(256)} %reshape.31.refs_0_.tab_ref, s32[16]{0:T(128)} %get-tuple-element.52.refs_1_.cnt_ref, ...), custom_call_target="tpu_custom_call" | custom-call | flops 25999998976 | bytes 6291456 | tf_op jit(solution)/shard_map/attend/pallas_call | solution.py:237
  98.5 1.2 collective-permute-start.3
  99.7 0.8 collective-permute-start.4
  100.5 2.1 all-to-all-done.2.refs_1_.qg_ref
  102.6 0.8 copy-done.5
  103.4 5.0 %all-to-all-start.3 = ((bf16[8,128,256]{2,1,0:T(8,128)(2,1)}), bf16[8,128,256]{2,1,0:T(8,128)(2,1)S(1)}, u32[]{:S(2)}, u32[]{:S(2)}) async-start(bf16[8,128,256]{2,1,0:T(8,128)(2,1)} %gate.6.after_ref.oa_ref), calls=%async_computation.3 | async-start | bytes 1048576 | tf_op jit(solution)/shard_map/all_to_all | solution.py:378
  108.4 1.9 collective-permute-start.5
  110.3 0.8 copy-done.19
  111.1 16.5 %attend.3 = (bf16[8,128,256]{2,1,0:T(8,128)(2,1)}, bf16[8,128,256]{2,1,0:T(8,128)(2,1)}, bf16[8,128,256]{2,1,0:T(8,128)(2,1)}, bf16[8,128,256]{2,1,0:T(8,128)(2,1)}, bf16[8,128,256]{2,1,0:T(8,128)(2,1)}) custom-call(s32[192]{0:T(256)} %reshape.31.refs_0_.tab_ref, s32[16]{0:T(128)} %get-tuple-element.52.refs_1_.cnt_ref, ...), custom_call_target="tpu_custom_call" | custom-call | flops 25999998976 | bytes 6291456 | tf_op jit(solution)/shard_map/attend/pallas_call | solution.py:237
  127.6 0.7 copy-done.6
  128.7 2.7 %sum_join.1.refs_0_ = bf16[8,256,256]{2,1,0:T(8,128)(2,1)} custom-call(bf16[8,128,256]{2,1,0:T(8,128)(2,1)} %get-tuple-element.35.a_ref, bf16[8,128,256]{2,1,0:T(8,128)(2,1)} %copy-done.6, bf16[8,128,256]{2,1,0:T(8,128)(2,1)} %copy-done.7, bf16[8,128,256]{2,1,0:T(8,128)(2,1)} %copy-done.8, bf16[8,128,256]{2,1,0:T(8,128)(2,1)} %get-tuple-element.44.od_ref.ob_ref), custom_call_target="tpu_custom_call" | custom-call | tf_op jit(solution)/shard_map/sum_join/pallas_call | solution.py:416
  131.4 0.8 copy-done.3
  132.2 7.2 %all-to-all-start.4 = ((bf16[8,256,256]{2,1,0:T(8,128)(2,1)}), bf16[8,256,256]{2,1,0:T(8,128)(2,1)S(1)}, u32[]{:S(2)}, u32[]{:S(2)}) async-start(bf16[8,256,256]{2,1,0:T(8,128)(2,1)} %gate.8.ka_ref), calls=%async_computation.4 | async-start | bytes 2097152 | tf_op jit(solution)/shard_map/all_to_all | solution.py:378
  139.4 1.9 collective-permute-start.10
  141.3 2.6 %collective-permute-start.11 = (bf16[8,128,256]{2,1,0:T(8,128)(2,1)}, bf16[8,128,256]{2,1,0:T(8,128)(2,1)S(1)}, u32[]{:S(2)}, u32[]{:S(2)}) collective-permute-start(bf16[8,128,256]{2,1,0:T(8,128)(2,1)} %get-tuple-element.48), channel_id=1, source_target_pairs={{0,16},{8,24},{16,0},{24,8},{1,17},{9,25},{17,1},{25,9},{2,18},{10... | collective-permute-start | bytes 1572872 | tf_op jit(solution)/shard_map/ppermute | solution.py:432
  144.2 10.3 %collective-permute-done.10.refs_2_ = bf16[8,128,256]{2,1,0:T(8,128)(2,1)S(1)} collective-permute-done((bf16[8,128,256]{2,1,0:T(8,128)(2,1)}, bf16[8,128,256]{2,1,0:T(8,128)(2,1)S(1)}, u32[]{:S(2)}, u32[]{:S(2)}) %collective-permute-start.10) | collective-permute-done | bytes 524320 | tf_op jit(solution)/shard_map/ppermute | solution.py:431
  154.5 9.9 %collective-permute-done.11.refs_3_ = bf16[8,128,256]{2,1,0:T(8,128)(2,1)S(1)} collective-permute-done((bf16[8,128,256]{2,1,0:T(8,128)(2,1)}, bf16[8,128,256]{2,1,0:T(8,128)(2,1)S(1)}, u32[]{:S(2)}, u32[]{:S(2)}) %collective-permute-start.11) | collective-permute-done | bytes 524320 | tf_op jit(solution)/shard_map/ppermute | solution.py:432
  164.4 0.7 collective-permute-done.9.refs_1_
  165.2 4.6 %all-to-all-done.4.b_ref.refs_4_.ob_ref.ka_ref = bf16[8,256,256]{2,1,0:T(8,128)(2,1)S(1)} async-done(((bf16[8,256,256]{2,1,0:T(8,128)(2,1)}), bf16[8,256,256]{2,1,0:T(8,128)(2,1)S(1)}, u32[]{:S(2)}, u32[]{:S(2)}) %all-to-all-start.4) | async-done | bytes 1048608 | tf_op jit(solution)/shard_map/all_to_all | solution.py:378
  169.8 1.0 copy-done.1
  170.8 2.3 %sum_parts.2.kb_ref = bf16[8,128,256]{2,1,0:T(8,128)(2,1)} custom-call(bf16[8,128,256]{2,1,0:T(8,128)(2,1)} %get-tuple-element.45.refs_0_, bf16[8,128,256]{2,1,0:T(8,128)(2,1)} %copy-done.12, bf16[8,128,256]{2,1,0:T(8,128)(2,1)} %copy-done.10, bf16[8,128,256]{2,1,0:T(8,128)(2,1)} %copy-done.11, bf16[8,256,256]{2,1,0:T(8,128)(2,1)} %copy-done.1), custom_call_target="tpu_custom_call" | custom-call | tf_op jit(solution)/shard_map/sum_parts/pallas_call | solution.py:398
  173.1 3.5 %all-to-all-start.5 = ((bf16[8,128,256]{2,1,0:T(8,128)(2,1)}), bf16[8,128,256]{2,1,0:T(8,128)(2,1)S(1)}, u32[]{:S(2)}, u32[]{:S(2)}) async-start(bf16[8,128,256]{2,1,0:T(8,128)(2,1)} %sum_parts.2.kb_ref), calls=%async_computation.5 | async-start | bytes 1048576 | tf_op jit(solution)/shard_map/all_to_all | solution.py:378
  176.7 6.3 %weight_share.1 = (bf16[512,384]{1,0:T(8,128)(2,1)}, bf16[512,384]{1,0:T(8,128)(2,1)}) custom-call(s32[1]{0:T(128)} %bitcast.9.c_ref, bf16[8,128,256]{2,1,0:T(8,128)(2,1)} %gate.6.after_ref.oa_ref, bf16[8,128,256]{2,1,0:T(8,128)(2,1)} %get-tuple-element.44.od_ref.ob_ref, bf16[8,256,256]{2,1,0:T(8,128)(2,1)} %gate.8.ka_ref, ...), custom_call_target="tpu_custom_call" | custom-call | tf_op jit(solution)/shard_map/weight_share/pallas_call | solution.py:472
  183.0 1.9 collective-permute-done.12.refs_1_
  185.6 2.0 sum_parts.3
  187.6 4.3 %all-to-all-done.5.kb_ref.refs_1_ = bf16[8,128,256]{2,1,0:T(8,128)(2,1)S(1)} async-done(((bf16[8,128,256]{2,1,0:T(8,128)(2,1)}), bf16[8,128,256]{2,1,0:T(8,128)(2,1)S(1)}, u32[]{:S(2)}, u32[]{:S(2)}) %all-to-all-start.5) | async-done | bytes 524320 | tf_op jit(solution)/shard_map/all_to_all | solution.py:378
  191.9 0.8 copy-done.4
  192.7 7.8 %all-to-all-start.6 = ((bf16[16,32,384]{2,1,0:T(8,128)(2,1)}), bf16[16,32,384]{2,1,0:T(8,128)(2,1)S(1)}, u32[]{:S(2)}, u32[]{:S(2)}) async-start(bf16[16,32,384]{2,1,0:T(8,128)(2,1)} %gate.9), calls=%async_computation.6 | async-start | bytes 786432 | tf_op jit(solution)/shard_map/all_to_all | solution.py:378
  200.5 6.3 %node_grads.1.refs_0_ = bf16[256,1024]{1,0:T(8,128)(2,1)} custom-call(bf16[8,128,256]{2,1,0:T(8,128)(2,1)} %copy-done.3, bf16[8,256,256]{2,1,0:T(8,128)(2,1)} %copy-done.1, bf16[8,256,256]{2,1,0:T(8,128)(2,1)} %copy-done.1, bf16[8,128,256]{2,1,0:T(8,128)(2,1)} %copy-done.4, bf16[1024,3072]{1,0:T(8,128)(2,1)} %wv_ref.3, bf16[1024,3072]{1,0:T(8,128)(2,1)} %wv_ref.3, ...), custom_call_target="tpu_custom_call" | custom-call | tf_op jit(solution)/shard_map/node_grads/pallas_call | solution.py:322
  206.7 1.6 all-to-all-done.6.x_ref
  209.1 1.7 sum_rows.1
  210.8 3.3 %all-to-all-start.7 = ((f32[8,4,384]{2,1,0:T(4,128)}), f32[8,4,384]{2,1,0:T(4,128)S(1)}, u32[]{:S(2)}, u32[]{:S(2)}) async-start(f32[8,4,384]{2,1,0:T(4,128)} %sum_rows.1), calls=%async_computation.7 | async-start | bytes 98304 | tf_op jit(solution)/shard_map/all_to_all | solution.py:378
  214.1 4.4 %project_out.1.refs_0_ = bf16[256,1024]{1,0:T(8,128)(2,1)} custom-call(bf16[8,128,256]{2,1,0:T(8,128)(2,1)} %copy-done.3, bf16[8,256,256]{2,1,0:T(8,128)(2,1)} %copy-done.1, bf16[1024,1024]{1,0:T(8,128)(2,1)} %wo_ref.3), custom_call_target="tpu_custom_call" | custom-call | tf_op jit(solution)/shard_map/project_out/pallas_call | solution.py:283
  218.5 3.8 %all-to-all-done.7.x_ref = f32[8,4,384]{2,1,0:T(4,128)S(1)} async-done(((f32[8,4,384]{2,1,0:T(4,128)}), f32[8,4,384]{2,1,0:T(4,128)S(1)}, u32[]{:S(2)}, u32[]{:S(2)}) %all-to-all-start.7) | async-done | bytes 49184 | tf_op jit(solution)/shard_map/all_to_all | solution.py:378
  222.8 1.4 spread.1
  (68 shorter events, 6.2 us)
Async XLA Ops:
  7.2 13.7 %copy-start = (s32[1,64,8]{1,2,0:T(8,128)S(1)}, s32[1,64,8]{1,2,0:T(8,128)}, u32[]{:S(2)}) copy-start(s32[1,64,8]{1,2,0:T(8,128)} %param.11) | copy-start | bytes 6148
  7.2 13.6 %copy-start.21 = (s32[1,4]{1,0:T(1,128)S(1)}, s32[1,4]{1,0:T(1,128)}, u32[]{:S(2)}) copy-start(s32[1,4]{1,0:T(1,128)} %param.13) | copy-start | bytes 52
  7.2 14.6 %copy-start.17 = (s32[1,64]{1,0:T(1,128)S(1)}, s32[1,64]{1,0:T(1,128)}, u32[]{:S(2)}) copy-start(s32[1,64]{1,0:T(1,128)} %param.12) | copy-start | bytes 772
  12.4 26.0 %all-to-all-start = ((bf16[8,128,256]{2,1,0:T(8,128)(2,1)}), bf16[8,128,256]{2,1,0:T(8,128)(2,1)S(1)}, u32[]{:S(2)}, u32[]{:S(2)}) async-start(bf16[8,128,256]{2,1,0:T(8,128)(2,1)} %get-tuple-element.27), calls=%async_computation | async-start | bytes 1048576 | tf_op jit(solution)/shard_map/all_to_all | solution.py:378
  38.3 43.5 %copy-start.13 = (bf16[8,128,256]{2,1,0:T(8,128)(2,1)}, bf16[8,128,256]{2,1,0:T(8,128)(2,1)S(1)}, u32[]{:S(2)}) copy-start(bf16[8,128,256]{2,1,0:T(8,128)(2,1)S(1)} %all-to-all-done.own_ref) | copy-start | bytes 1572868
  38.3 32.7 %all-to-all-start.1 = ((bf16[8,256,256]{2,1,0:T(8,128)(2,1)}), bf16[8,256,256]{2,1,0:T(8,128)(2,1)S(1)}, u32[]{:S(2)}, u32[]{:S(2)}) async-start(bf16[8,256,256]{2,1,0:T(8,128)(2,1)} %get-tuple-element.29), calls=%async_computation.1 | async-start | bytes 2097152 | tf_op jit(solution)/shard_map/all_to_all | solution.py:378
  41.9 134.8 %all-gather.2.cloned.1.call-start = ((), (), s32[]{:S(2)}) async-start(), calls=%async_computation.8 | async-start | bytes 4718592 | tf_op jit(solution)/shard_map/all_gather | solution.py:504
  41.9 37.5 %collective-permute-start = (bf16[8,128,256]{2,1,0:T(8,128)(2,1)S(1)}, bf16[8,128,256]{2,1,0:T(8,128)(2,1)S(1)}, u32[]{:S(2)}, u32[]{:S(2)}) collective-permute-start(bf16[8,128,256]{2,1,0:T(8,128)(2,1)S(1)} %all-to-all-done.own_ref), channel_id=1, source_target_pairs={{0,8},{8,16},{16,24},{24,0},{1,9},{9,17},{17,25},{25,1},{2,10},{10... | collective-permute-start | bytes 1572872 | tf_op jit(solution)/shard_map/ppermute | solution.py:387
  43.6 38.2 %collective-permute-start.1 = (bf16[8,128,256]{2,1,0:T(8,128)(2,1)S(1)}, bf16[8,128,256]{2,1,0:T(8,128)(2,1)}, u32[]{:S(2)}, u32[]{:S(2)}) collective-permute-start(bf16[8,128,256]{2,1,0:T(8,128)(2,1)S(1)} %all-to-all-done.own_ref), channel_id=1, source_target_pairs={{0,24},{8,0},{16,8},{24,16},{1,25},{9,1},{17,9},{25,17},{2,26},{10... | collective-permute-start | bytes 1572872 | tf_op jit(solution)/shard_map/ppermute | solution.py:387
  44.0 37.8 %collective-permute-start.2 = (bf16[8,128,256]{2,1,0:T(8,128)(2,1)S(1)}, bf16[8,128,256]{2,1,0:T(8,128)(2,1)}, u32[]{:S(2)}, u32[]{:S(2)}) collective-permute-start(bf16[8,128,256]{2,1,0:T(8,128)(2,1)S(1)} %all-to-all-done.own_ref), channel_id=1, source_target_pairs={{0,16},{8,24},{16,0},{24,8},{1,17},{9,25},{17,1},{25,9},{2,18},{10... | collective-permute-start | bytes 1572872 | tf_op jit(solution)/shard_map/ppermute | solution.py:387
  71.0 1.0 copy-start.2
  73.9 34.6 %collective-permute-start.6 = (bf16[8,128,256]{2,1,0:T(8,128)(2,1)}, bf16[8,128,256]{2,1,0:T(8,128)(2,1)S(1)}, u32[]{:S(2)}, u32[]{:S(2)}) collective-permute-start(bf16[8,128,256]{2,1,0:T(8,128)(2,1)} %first_half.1.own_ref), channel_id=1, source_target_pairs={{0,8},{8,16},{16,24},{24,0},{1,9},{9,17},{17,25},{25,1},{2,10},{10... | collective-permute-start | bytes 1572872 | tf_op jit(solution)/shard_map/ppermute | solution.py:387
  75.5 34.8 %collective-permute-start.7 = (bf16[8,128,256]{2,1,0:T(8,128)(2,1)}, bf16[8,128,256]{2,1,0:T(8,128)(2,1)S(1)}, u32[]{:S(2)}, u32[]{:S(2)}) collective-permute-start(bf16[8,128,256]{2,1,0:T(8,128)(2,1)} %first_half.1.own_ref), channel_id=1, source_target_pairs={{0,24},{8,0},{16,8},{24,16},{1,25},{9,1},{17,9},{25,17},{2,26},{10... | collective-permute-start | bytes 1572872 | tf_op jit(solution)/shard_map/ppermute | solution.py:387
  75.9 26.7 %all-to-all-start.2 = ((bf16[8,128,256]{2,1,0:T(8,128)(2,1)}), bf16[8,128,256]{2,1,0:T(8,128)(2,1)S(1)}, u32[]{:S(2)}, u32[]{:S(2)}) async-start(bf16[8,128,256]{2,1,0:T(8,128)(2,1)} %get-tuple-element.34), calls=%async_computation.2 | async-start | bytes 1048576 | tf_op jit(solution)/shard_map/all_to_all | solution.py:378
  79.4 2.4 %copy-start.20 = (bf16[8,128,256]{2,1,0:T(8,128)(2,1)}, bf16[8,128,256]{2,1,0:T(8,128)(2,1)S(1)}, u32[]{:S(2)}) copy-start(bf16[8,128,256]{2,1,0:T(8,128)(2,1)S(1)} %collective-permute-done.left_ref) | copy-start | bytes 1572868
  79.4 30.9 %collective-permute-start.8 = (bf16[8,128,256]{2,1,0:T(8,128)(2,1)}, bf16[8,128,256]{2,1,0:T(8,128)(2,1)}, u32[]{:S(2)}, u32[]{:S(2)}) collective-permute-start(bf16[8,128,256]{2,1,0:T(8,128)(2,1)} %first_half.1.own_ref), channel_id=1, source_target_pairs={{0,16},{8,24},{16,0},{24,8},{1,17},{9,25},{17,1},{25,9},{2,18},{10... | collective-permute-start | bytes 1572872 | tf_op jit(solution)/shard_map/ppermute | solution.py:387
  98.5 29.1 %collective-permute-start.3 = (bf16[8,128,256]{2,1,0:T(8,128)(2,1)}, bf16[8,128,256]{2,1,0:T(8,128)(2,1)S(1)}, u32[]{:S(2)}, u32[]{:S(2)}) collective-permute-start(bf16[8,128,256]{2,1,0:T(8,128)(2,1)} %get-tuple-element.36), channel_id=1, source_target_pairs={{0,8},{8,16},{16,24},{24,0},{1,9},{9,17},{17,25},{25,1},{2,10},{10... | collective-permute-start | bytes 1572872 | tf_op jit(solution)/shard_map/ppermute | solution.py:430
  99.7 27.9 %collective-permute-start.4 = (bf16[8,128,256]{2,1,0:T(8,128)(2,1)}, bf16[8,128,256]{2,1,0:T(8,128)(2,1)S(1)}, u32[]{:S(2)}, u32[]{:S(2)}) collective-permute-start(bf16[8,128,256]{2,1,0:T(8,128)(2,1)} %get-tuple-element.37), channel_id=1, source_target_pairs={{0,24},{8,0},{16,8},{24,16},{1,25},{9,1},{17,9},{25,17},{2,26},{10... | collective-permute-start | bytes 1572872 | tf_op jit(solution)/shard_map/ppermute | solution.py:431
  102.6 0.8 copy-start.5
  103.4 28.0 %all-to-all-start.3 = ((bf16[8,128,256]{2,1,0:T(8,128)(2,1)}), bf16[8,128,256]{2,1,0:T(8,128)(2,1)S(1)}, u32[]{:S(2)}, u32[]{:S(2)}) async-start(bf16[8,128,256]{2,1,0:T(8,128)(2,1)} %gate.6.after_ref.oa_ref), calls=%async_computation.3 | async-start | bytes 1048576 | tf_op jit(solution)/shard_map/all_to_all | solution.py:378
  108.4 1.9 copy-start.18
  108.4 19.2 %collective-permute-start.5 = (bf16[8,128,256]{2,1,0:T(8,128)(2,1)}, bf16[8,128,256]{2,1,0:T(8,128)(2,1)S(1)}, u32[]{:S(2)}, u32[]{:S(2)}) collective-permute-start(bf16[8,128,256]{2,1,0:T(8,128)(2,1)} %get-tuple-element.38), channel_id=1, source_target_pairs={{0,16},{8,24},{16,0},{24,8},{1,17},{9,25},{17,1},{25,9},{2,18},{10... | collective-permute-start | bytes 1572872 | tf_op jit(solution)/shard_map/ppermute | solution.py:432
  110.3 0.8 copy-start.19
  127.6 0.8 copy-start.6
  127.6 1.0 copy-start.7
  127.6 1.1 copy-start.8
  128.7 15.1 %copy-start.14 = (bf16[8,128,256]{2,1,0:T(8,128)(2,1)S(1)}, bf16[8,128,256]{2,1,0:T(8,128)(2,1)}, u32[]{:S(2)}) copy-start(bf16[8,128,256]{2,1,0:T(8,128)(2,1)} %get-tuple-element.46) | copy-start | bytes 1572868
  131.4 0.8 copy-start.3
  132.2 37.6 %all-to-all-start.4 = ((bf16[8,256,256]{2,1,0:T(8,128)(2,1)}), bf16[8,256,256]{2,1,0:T(8,128)(2,1)S(1)}, u32[]{:S(2)}, u32[]{:S(2)}) async-start(bf16[8,256,256]{2,1,0:T(8,128)(2,1)} %gate.8.ka_ref), calls=%async_computation.4 | async-start | bytes 2097152 | tf_op jit(solution)/shard_map/all_to_all | solution.py:378
  139.4 15.1 %collective-permute-start.10 = (bf16[8,128,256]{2,1,0:T(8,128)(2,1)}, bf16[8,128,256]{2,1,0:T(8,128)(2,1)S(1)}, u32[]{:S(2)}, u32[]{:S(2)}) collective-permute-start(bf16[8,128,256]{2,1,0:T(8,128)(2,1)} %get-tuple-element.47), channel_id=1, source_target_pairs={{0,24},{8,0},{16,8},{24,16},{1,25},{9,1},{17,9},{25,17},{2,26},{10... | collective-permute-start | bytes 1572872 | tf_op jit(solution)/shard_map/ppermute | solution.py:431
  141.3 23.2 %collective-permute-start.11 = (bf16[8,128,256]{2,1,0:T(8,128)(2,1)}, bf16[8,128,256]{2,1,0:T(8,128)(2,1)S(1)}, u32[]{:S(2)}, u32[]{:S(2)}) collective-permute-start(bf16[8,128,256]{2,1,0:T(8,128)(2,1)} %get-tuple-element.48), channel_id=1, source_target_pairs={{0,16},{8,24},{16,0},{24,8},{1,17},{9,25},{17,1},{25,9},{2,18},{10... | collective-permute-start | bytes 1572872 | tf_op jit(solution)/shard_map/ppermute | solution.py:432
  143.8 21.4 %collective-permute-start.9 = (bf16[8,128,256]{2,1,0:T(8,128)(2,1)S(1)}, bf16[8,128,256]{2,1,0:T(8,128)(2,1)S(1)}, u32[]{:S(2)}, u32[]{:S(2)}) collective-permute-start(bf16[8,128,256]{2,1,0:T(8,128)(2,1)S(1)} %copy-done.14), channel_id=1, source_target_pairs={{0,8},{8,16},{16,24},{24,0},{1,9},{9,17},{17,25},{25,1},{2,10},{10... | collective-permute-start | bytes 1572872 | tf_op jit(solution)/shard_map/ppermute | solution.py:430
  154.5 15.3 %copy-start.10 = (bf16[8,128,256]{2,1,0:T(8,128)(2,1)}, bf16[8,128,256]{2,1,0:T(8,128)(2,1)S(1)}, u32[]{:S(2)}) copy-start(bf16[8,128,256]{2,1,0:T(8,128)(2,1)S(1)} %collective-permute-done.10.refs_2_) | copy-start | bytes 1572868
  164.4 5.4 %copy-start.11 = (bf16[8,128,256]{2,1,0:T(8,128)(2,1)}, bf16[8,128,256]{2,1,0:T(8,128)(2,1)S(1)}, u32[]{:S(2)}) copy-start(bf16[8,128,256]{2,1,0:T(8,128)(2,1)S(1)} %collective-permute-done.11.refs_3_) | copy-start | bytes 1572868
  165.2 4.6 %copy-start.12 = (bf16[8,128,256]{2,1,0:T(8,128)(2,1)}, bf16[8,128,256]{2,1,0:T(8,128)(2,1)S(1)}, u32[]{:S(2)}) copy-start(bf16[8,128,256]{2,1,0:T(8,128)(2,1)S(1)} %collective-permute-done.9.refs_1_) | copy-start | bytes 1572868
  169.8 1.0 copy-start.1
  173.1 18.8 %all-to-all-start.5 = ((bf16[8,128,256]{2,1,0:T(8,128)(2,1)}), bf16[8,128,256]{2,1,0:T(8,128)(2,1)S(1)}, u32[]{:S(2)}, u32[]{:S(2)}) async-start(bf16[8,128,256]{2,1,0:T(8,128)(2,1)} %sum_parts.2.kb_ref), calls=%async_computation.5 | async-start | bytes 1048576 | tf_op jit(solution)/shard_map/all_to_all | solution.py:378
  183.0 1.9 collective-permute-start.12
  184.9 0.7 copy-start.15
  191.9 0.8 copy-start.4
  192.7 15.6 %all-to-all-start.6 = ((bf16[16,32,384]{2,1,0:T(8,128)(2,1)}), bf16[16,32,384]{2,1,0:T(8,128)(2,1)S(1)}, u32[]{:S(2)}, u32[]{:S(2)}) async-start(bf16[16,32,384]{2,1,0:T(8,128)(2,1)} %gate.9), calls=%async_computation.6 | async-start | bytes 786432 | tf_op jit(solution)/shard_map/all_to_all | solution.py:378
  208.3 0.7 copy-start.9
  210.8 11.5 %all-to-all-start.7 = ((f32[8,4,384]{2,1,0:T(4,128)}), f32[8,4,384]{2,1,0:T(4,128)S(1)}, u32[]{:S(2)}, u32[]{:S(2)}) async-start(f32[8,4,384]{2,1,0:T(4,128)} %sum_rows.1), calls=%async_computation.7 | async-start | bytes 98304 | tf_op jit(solution)/shard_map/all_to_all | solution.py:378
  222.2 0.6 copy-start.16
Sparse Core Ops, SparseCore 0:
  72.2 81.2 all-gather.1
